TPU v7x, 512 devices: a whole 4x4x16 slice. The times are simulated.
512 devices in a mesh: seq: 32 (over x, z_lo, core), head: 16 (over y, z_hi).
Axes of the slice: x: 4, y: 4, z: 16 (z_hi: 4, z_lo: 4; z = z_hi * 4 + z_lo), core: 2. Of those that a mesh axis runs over, the one named last changes fastest.
Arguments:
- out_grad: bfloat16 [8192, 4096], P('seq', 'head'), may hold values from -7.2 to 7.2
- x_in: bfloat16 [8192, 4096], P('seq', 'head'), may hold values from -6 to 6
- b_in: bfloat16 [8192, 128], P('seq'), may hold values from -2.5 to 2.5
- c_in: bfloat16 [8192, 128], P('seq'), may hold values from -2.5 to 2.5
- dt_raw: float32 [64, 8192], P('head', 'seq'), may hold values from -5.1 to -0.7
- dt_bias: float32 [64], P('head'), may hold values from -0.5 to 0.5
- a_log: float32 [64], P('head'), may hold values from -7.5 to 2.2
- d_skip: float32 [64], P('head'), may hold values from 0.5 to 1.5
- states: bfloat16 [32, 4096, 128], P('seq', 'head'), may hold values from -6 to 6
- w_out: bfloat16 [4096, 4096], P('head'), may hold values from -0.09375 to 0.09375
- w_in: bfloat16 [4096, 4096], P(None, 'head'), may hold values from -0.125 to 0.125
Outputs:
- in_grad: bfloat16 [4096, 8192], P('head', 'seq')
- bc_grad: bfloat16 [256, 8192], P('head', 'seq')
- dt_grad: float32 [64, 8192], P('head', 'seq')
- param_grad: float32 [3, 64], P(None, 'head')
All inputs are finite; a program needn't handle non-finite values.
Results may differ from a plain program's by a relative error of at most 0.015.
Values may be sent and summed in bfloat16 or wider, within the bound.
No kernel may reach another device: no remote copies, remote signals or barrier semaphores. Data moves between devices by JAX's collectives and lax.ppermute only.
A program may use at most 64 MiB of HBM per device.

v0:
```python
import jax
import jax.numpy as jnp
from jax import lax
from jax.sharding import PartitionSpec as P


def passed_along(value, axis, steps):
    count = lax.axis_size(axis)
    initial, last = (max(0, -steps), min(count, count - steps))
    return lax.ppermute(value, axis, [(source, source + steps) for source in range(initial, last)])


def shards(out_grad, x_in, b_in, c_in, dt_raw, dt_bias, a_log, d_skip, states, w_out, w_in):
    tokens_here, inner_here = x_in.shape
    group_heads = dt_raw.shape[0]
    head_dim = inner_here // group_heads
    state_dim = b_in.shape[1]
    contract_last = (((1,), (1,)), ((), ()))
    head_sum = lax.dot_general(
        lax.all_gather(out_grad, "head", axis=1, tiled=True),
        w_out,
        contract_last,
        preferred_element_type=jnp.float32,
    )
    dy_heads = head_sum.astype(jnp.bfloat16).reshape(tokens_here, group_heads, head_dim)
    dy_wide = dy_heads.astype(jnp.float32)
    x_heads = x_in.reshape(tokens_here, group_heads, head_dim)
    x_wide = x_heads.astype(jnp.float32)
    decay_rate = jnp.exp(a_log)
    step_size = jax.nn.softplus(dt_raw + dt_bias[:, None])
    log_step = -decay_rate[:, None] * step_size
    cumlog = jnp.cumsum(log_step, axis=1)
    positions = jnp.arange(tokens_here)
    causal = positions[:, None] >= positions[None, :]
    log_gaps = cumlog[:, :, None] - cumlog[:, None, :]
    decay_mask = jnp.where(causal[None], jnp.exp(jnp.minimum(log_gaps, 0.0)), 0.0)
    scores = lax.dot_general(c_in, b_in, contract_last, preferred_element_type=jnp.float32)
    step_rows = step_size.T
    x_scaled = (x_wide * step_rows[:, :, None]).astype(jnp.bfloat16)
    pair_dots = jnp.einsum("ihp,jhp->hij", dy_heads, x_scaled, preferred_element_type=jnp.float32)
    kernel = (scores[None] * decay_mask).astype(jnp.bfloat16)
    intra_back = jnp.einsum("hij,ihp->jhp", kernel, dy_heads, preferred_element_type=jnp.float32)
    masked_dots = (pair_dots * decay_mask).astype(jnp.bfloat16)
    start_decay = jnp.exp(cumlog)
    dy_decay = (dy_wide * start_decay.T[:, :, None]).astype(jnp.bfloat16)
    local_state = jnp.einsum("ihp,in->hpn", dy_decay, c_in, preferred_element_type=jnp.float32)
    end_total = jnp.exp(cumlog[:, -1])
    entry_state = states.reshape(group_heads, head_dim, state_dim)
    db_intra = jnp.einsum("hij,in->nj", masked_dots, c_in, preferred_element_type=jnp.float32)
    dc_intra = jnp.einsum("hij,jn->ni", masked_dots, b_in, preferred_element_type=jnp.float32)
    dc_entry = jnp.einsum("ihp,hpn->ni", dy_decay, entry_state, preferred_element_type=jnp.float32)
    ystate = jnp.einsum("in,hpn->ihp", c_in, entry_state, preferred_element_type=jnp.float32)
    pair_weight = pair_dots * scores[None] * decay_mask
    state_terms = start_decay * jnp.sum(dy_wide * ystate, axis=2).T
    skip_terms = jnp.sum(dy_wide * x_wide, axis=(0, 2))

    def relay_turn(turn_index, held_state):
        return passed_along(end_total[:, None, None] * held_state + local_state, "seq", -1)

    carried = lax.fori_loop(0, lax.axis_size("seq") - 1, relay_turn, jnp.zeros_like(local_state))
    carried_bf = carried.astype(jnp.bfloat16)
    state_back = jnp.einsum("jn,hpn->jhp", b_in, carried_bf, preferred_element_type=jnp.float32)
    end_decay = jnp.exp(cumlog[:, -1:] - cumlog)
    end_weight = (step_size * end_decay).T
    x_grad = (
        (
            step_rows[:, :, None] * intra_back
            + end_weight[:, :, None] * state_back
            + d_skip[None, :, None] * dy_wide
        )
        .astype(jnp.bfloat16)
        .reshape(tokens_here, inner_here)
    )
    x_end = (x_wide * end_weight[:, :, None]).astype(jnp.bfloat16)
    db_entry = jnp.einsum("jhp,hpn->nj", x_end, carried_bf, preferred_element_type=jnp.float32)
    bc_part = jnp.concatenate([db_intra + db_entry, dc_intra + dc_entry], axis=0)
    end_terms = end_weight.T * jnp.sum(x_wide * state_back, axis=2).T
    cum_grad = pair_weight.sum(axis=2) - pair_weight.sum(axis=1) + state_terms - end_terms
    tail_grad = end_terms.sum(axis=1) + end_total * jnp.sum(
        entry_state.astype(jnp.float32) * carried, axis=(1, 2)
    )
    cum_grad = cum_grad.at[:, -1].add(tail_grad)
    step_grad = jnp.cumsum(cum_grad[:, ::-1], axis=1)[:, ::-1]
    dt_sum = (
        -decay_rate[:, None] * step_grad
        + jnp.sum(x_wide * (intra_back + end_decay.T[:, :, None] * state_back), axis=2).T
    )
    dt_grad = dt_sum * jax.nn.sigmoid(dt_raw + dt_bias[:, None])
    param_terms = jnp.stack(
        [jnp.sum(step_grad * log_step, axis=1), skip_terms, jnp.sum(dt_grad, axis=1)]
    )
    in_part = lax.psum_scatter(
        lax.dot_general(w_in, x_grad, contract_last, preferred_element_type=jnp.float32).astype(
            jnp.bfloat16
        ),
        "head",
        scatter_dimension=0,
        tiled=True,
    )
    bc_sum = lax.psum_scatter(bc_part.astype(jnp.bfloat16), "head", scatter_dimension=0, tiled=True)
    norm_scale = (lax.axis_size("seq") * tokens_here * head_dim) ** (-0.5)
    param_grad = lax.psum(param_terms, "seq") * norm_scale
    return (in_part, bc_sum, dt_grad, param_grad)


def solution(mesh):
    return jax.shard_map(
        shards,
        mesh=mesh,
        in_specs=(
            P("seq", "head"),
            P("seq", "head"),
            P("seq", None),
            P("seq", None),
            P("head", "seq"),
            P("head"),
            P("head"),
            P("head"),
            P("seq", "head", None),
            P("head", None),
            P(None, "head"),
        ),
        out_specs=(P("head", "seq"), P("head", "seq"), P("head", "seq"), P(None, "head")),
        check_vma=False,
    )
```

profile of v0, /device:TPU:1, one launch (start us, length us, event | category | flops | bytes accessed | tf_op | source)
XLA Modules:
  0.0 641.7 jit_solution(2640681701304499436)
XLA Ops:
  14.1 101.5 %all-gather.2.cloned.1.call-done = bf16[256,4096]{1,0:T(8,128)(2,1)} async-done(((bf16[256,256]{1,0:T(8,128)(2,1)}), bf16[256,4096]{1,0:T(8,128)(2,1)}) %all-gather.2.cloned.1.call-update) | async-done | bytes 2097168 | tf_op jit(solution)/shard_map/all_gather | solution.py:20
  120.1 254.0 %while.11 = (s32[]{:T(128)}, f32[4,64,128]{2,1,0:T(8,128)S(1)}, f32[4]{0:T(128)S(1)}, f32[4,64,128]{2,1,0:T(8,128)S(1)}, s32[]{:T(128)}) while((s32[]{:T(128)}, f32[4,64,128]{2,1,0:T(8,128)S(1)}, f32[4]{0:T(128)S(1)}, f32[4,64,128]{2,1,0:T(8,128)S(1)}, s32[]{:T(128)}) %tuple.42), condition=%wide.region_3.4_spmd, body=%wide.region_2.3_spmd.sunk | while | flops 65538 | bytes 917621 | solution.py:60
  120.2 5.0 collective-permute-start
  128.5 4.4 collective-permute-done
  134.9 4.4 collective-permute-done
  147.6 4.4 collective-permute-done
  154.0 4.4 collective-permute-done
  160.4 4.4 collective-permute-done
  185.8 6.9 %collective-permute-done = f32[4,64,128]{2,1,0:T(8,128)S(1)} collective-permute-done((f32[4,64,128]{2,1,0:T(8,128)S(1)}, f32[4,64,128]{2,1,0:T(8,128)S(1)}, u32[]{:S(2)}, u32[]{:S(2)}) %collective-permute-start) | collective-permute-done | bytes 131104 | tf_op jit(solution)/shard_map/while/body/eval_jaxpr/ppermute | solution.py:10
  194.8 7.1 %collective-permute-done = f32[4,64,128]{2,1,0:T(8,128)S(1)} collective-permute-done((f32[4,64,128]{2,1,0:T(8,128)S(1)}, f32[4,64,128]{2,1,0:T(8,128)S(1)}, u32[]{:S(2)}, u32[]{:S(2)}) %collective-permute-start) | collective-permute-done | bytes 131104 | tf_op jit(solution)/shard_map/while/body/eval_jaxpr/ppermute | solution.py:10
  203.9 7.1 %collective-permute-done = f32[4,64,128]{2,1,0:T(8,128)S(1)} collective-permute-done((f32[4,64,128]{2,1,0:T(8,128)S(1)}, f32[4,64,128]{2,1,0:T(8,128)S(1)}, u32[]{:S(2)}, u32[]{:S(2)}) %collective-permute-start) | collective-permute-done | bytes 131104 | tf_op jit(solution)/shard_map/while/body/eval_jaxpr/ppermute | solution.py:10
  212.9 7.1 %collective-permute-done = f32[4,64,128]{2,1,0:T(8,128)S(1)} collective-permute-done((f32[4,64,128]{2,1,0:T(8,128)S(1)}, f32[4,64,128]{2,1,0:T(8,128)S(1)}, u32[]{:S(2)}, u32[]{:S(2)}) %collective-permute-start) | collective-permute-done | bytes 131104 | tf_op jit(solution)/shard_map/while/body/eval_jaxpr/ppermute | solution.py:10
  222.0 7.1 %collective-permute-done = f32[4,64,128]{2,1,0:T(8,128)S(1)} collective-permute-done((f32[4,64,128]{2,1,0:T(8,128)S(1)}, f32[4,64,128]{2,1,0:T(8,128)S(1)}, u32[]{:S(2)}, u32[]{:S(2)}) %collective-permute-start) | collective-permute-done | bytes 131104 | tf_op jit(solution)/shard_map/while/body/eval_jaxpr/ppermute | solution.py:10
  231.1 7.1 %collective-permute-done = f32[4,64,128]{2,1,0:T(8,128)S(1)} collective-permute-done((f32[4,64,128]{2,1,0:T(8,128)S(1)}, f32[4,64,128]{2,1,0:T(8,128)S(1)}, u32[]{:S(2)}, u32[]{:S(2)}) %collective-permute-start) | collective-permute-done | bytes 131104 | tf_op jit(solution)/shard_map/while/body/eval_jaxpr/ppermute | solution.py:10
  240.1 7.1 %collective-permute-done = f32[4,64,128]{2,1,0:T(8,128)S(1)} collective-permute-done((f32[4,64,128]{2,1,0:T(8,128)S(1)}, f32[4,64,128]{2,1,0:T(8,128)S(1)}, u32[]{:S(2)}, u32[]{:S(2)}) %collective-permute-start) | collective-permute-done | bytes 131104 | tf_op jit(solution)/shard_map/while/body/eval_jaxpr/ppermute | solution.py:10
  249.2 7.1 %collective-permute-done = f32[4,64,128]{2,1,0:T(8,128)S(1)} collective-permute-done((f32[4,64,128]{2,1,0:T(8,128)S(1)}, f32[4,64,128]{2,1,0:T(8,128)S(1)}, u32[]{:S(2)}, u32[]{:S(2)}) %collective-permute-start) | collective-permute-done | bytes 131104 | tf_op jit(solution)/shard_map/while/body/eval_jaxpr/ppermute | solution.py:10
  258.3 7.1 %collective-permute-done = f32[4,64,128]{2,1,0:T(8,128)S(1)} collective-permute-done((f32[4,64,128]{2,1,0:T(8,128)S(1)}, f32[4,64,128]{2,1,0:T(8,128)S(1)}, u32[]{:S(2)}, u32[]{:S(2)}) %collective-permute-start) | collective-permute-done | bytes 131104 | tf_op jit(solution)/shard_map/while/body/eval_jaxpr/ppermute | solution.py:10
  267.3 7.1 %collective-permute-done = f32[4,64,128]{2,1,0:T(8,128)S(1)} collective-permute-done((f32[4,64,128]{2,1,0:T(8,128)S(1)}, f32[4,64,128]{2,1,0:T(8,128)S(1)}, u32[]{:S(2)}, u32[]{:S(2)}) %collective-permute-start) | collective-permute-done | bytes 131104 | tf_op jit(solution)/shard_map/while/body/eval_jaxpr/ppermute | solution.py:10
  276.4 7.1 %collective-permute-done = f32[4,64,128]{2,1,0:T(8,128)S(1)} collective-permute-done((f32[4,64,128]{2,1,0:T(8,128)S(1)}, f32[4,64,128]{2,1,0:T(8,128)S(1)}, u32[]{:S(2)}, u32[]{:S(2)}) %collective-permute-start) | collective-permute-done | bytes 131104 | tf_op jit(solution)/shard_map/while/body/eval_jaxpr/ppermute | solution.py:10
  285.5 7.1 %collective-permute-done = f32[4,64,128]{2,1,0:T(8,128)S(1)} collective-permute-done((f32[4,64,128]{2,1,0:T(8,128)S(1)}, f32[4,64,128]{2,1,0:T(8,128)S(1)}, u32[]{:S(2)}, u32[]{:S(2)}) %collective-permute-start) | collective-permute-done | bytes 131104 | tf_op jit(solution)/shard_map/while/body/eval_jaxpr/ppermute | solution.py:10
  294.6 7.1 %collective-permute-done = f32[4,64,128]{2,1,0:T(8,128)S(1)} collective-permute-done((f32[4,64,128]{2,1,0:T(8,128)S(1)}, f32[4,64,128]{2,1,0:T(8,128)S(1)}, u32[]{:S(2)}, u32[]{:S(2)}) %collective-permute-start) | collective-permute-done | bytes 131104 | tf_op jit(solution)/shard_map/while/body/eval_jaxpr/ppermute | solution.py:10
  303.6 7.1 %collective-permute-done = f32[4,64,128]{2,1,0:T(8,128)S(1)} collective-permute-done((f32[4,64,128]{2,1,0:T(8,128)S(1)}, f32[4,64,128]{2,1,0:T(8,128)S(1)}, u32[]{:S(2)}, u32[]{:S(2)}) %collective-permute-start) | collective-permute-done | bytes 131104 | tf_op jit(solution)/shard_map/while/body/eval_jaxpr/ppermute | solution.py:10
  312.7 7.1 %collective-permute-done = f32[4,64,128]{2,1,0:T(8,128)S(1)} collective-permute-done((f32[4,64,128]{2,1,0:T(8,128)S(1)}, f32[4,64,128]{2,1,0:T(8,128)S(1)}, u32[]{:S(2)}, u32[]{:S(2)}) %collective-permute-start) | collective-permute-done | bytes 131104 | tf_op jit(solution)/shard_map/while/body/eval_jaxpr/ppermute | solution.py:10
  321.8 7.1 %collective-permute-done = f32[4,64,128]{2,1,0:T(8,128)S(1)} collective-permute-done((f32[4,64,128]{2,1,0:T(8,128)S(1)}, f32[4,64,128]{2,1,0:T(8,128)S(1)}, u32[]{:S(2)}, u32[]{:S(2)}) %collective-permute-start) | collective-permute-done | bytes 131104 | tf_op jit(solution)/shard_map/while/body/eval_jaxpr/ppermute | solution.py:10
  330.8 7.1 %collective-permute-done = f32[4,64,128]{2,1,0:T(8,128)S(1)} collective-permute-done((f32[4,64,128]{2,1,0:T(8,128)S(1)}, f32[4,64,128]{2,1,0:T(8,128)S(1)}, u32[]{:S(2)}, u32[]{:S(2)}) %collective-permute-start) | collective-permute-done | bytes 131104 | tf_op jit(solution)/shard_map/while/body/eval_jaxpr/ppermute | solution.py:10
  339.9 7.1 %collective-permute-done = f32[4,64,128]{2,1,0:T(8,128)S(1)} collective-permute-done((f32[4,64,128]{2,1,0:T(8,128)S(1)}, f32[4,64,128]{2,1,0:T(8,128)S(1)}, u32[]{:S(2)}, u32[]{:S(2)}) %collective-permute-start) | collective-permute-done | bytes 131104 | tf_op jit(solution)/shard_map/while/body/eval_jaxpr/ppermute | solution.py:10
  349.0 7.1 %collective-permute-done = f32[4,64,128]{2,1,0:T(8,128)S(1)} collective-permute-done((f32[4,64,128]{2,1,0:T(8,128)S(1)}, f32[4,64,128]{2,1,0:T(8,128)S(1)}, u32[]{:S(2)}, u32[]{:S(2)}) %collective-permute-start) | collective-permute-done | bytes 131104 | tf_op jit(solution)/shard_map/while/body/eval_jaxpr/ppermute | solution.py:10
  358.0 7.1 %collective-permute-done = f32[4,64,128]{2,1,0:T(8,128)S(1)} collective-permute-done((f32[4,64,128]{2,1,0:T(8,128)S(1)}, f32[4,64,128]{2,1,0:T(8,128)S(1)}, u32[]{:S(2)}, u32[]{:S(2)}) %collective-permute-start) | collective-permute-done | bytes 131104 | tf_op jit(solution)/shard_map/while/body/eval_jaxpr/ppermute | solution.py:10
  367.1 7.1 %collective-permute-done = f32[4,64,128]{2,1,0:T(8,128)S(1)} collective-permute-done((f32[4,64,128]{2,1,0:T(8,128)S(1)}, f32[4,64,128]{2,1,0:T(8,128)S(1)}, u32[]{:S(2)}, u32[]{:S(2)}) %collective-permute-start) | collective-permute-done | bytes 131104 | tf_op jit(solution)/shard_map/while/body/eval_jaxpr/ppermute | solution.py:10
  384.6 78.0 %psum.7 = f32[3,4]{1,0:T(4,128)S(1)} all-reduce(f32[3,4]{1,0:T(4,128)S(1)} %pad_maximum_fusion.1), channel_id=1, replica_groups=mesh['seq'=32,'head'=16] {'seq'}, use_global_device_ids=true, to_apply=%region_20.21 | all-reduce | flops 12 | bytes 96 | tf_op jit(solution)/shard_map/psum | solution.py:102
  463.2 62.0 %reduce-scatter.3.cloned.1.call-done = bf16[256,256]{0,1:T(8,128)(2,1)} async-done(((bf16[4096,256]{0,1:T(8,128)(2,1)}), bf16[256,256]{0,1:T(8,128)(2,1)}) %reduce-scatter.3.cloned.1.call-update) | async-done | bytes 131088 | tf_op jit(solution)/shard_map/reduce_scatter | solution.py:92
  526.8 108.3 %reduce-scatter.5.cloned.1.call-done = bf16[16,256]{1,0:T(8,128)(2,1)} async-done(((bf16[256,256]{1,0:T(8,128)(2,1)}), bf16[16,256]{1,0:T(8,128)(2,1)}) %reduce-scatter.5.cloned.1.call-update) | async-done | bytes 8208 | tf_op jit(solution)/shard_map/reduce_scatter | solution.py:100
  (139 shorter events, 102.8 us)
Async XLA Ops:
  7.2 108.5 %all-gather.2.cloned.1.call-start = ((), (), s32[]{:S(2)}) async-start(), calls=%async_computation.2 | async-start | bytes 2228224 | tf_op jit(solution)/shard_map/all_gather | solution.py:20
  7.9 517.3 %reduce-scatter.3.cloned.1.call-start = ((), (), s32[]{:S(2)}) async-start(), calls=%async_computation.3 | async-start | bytes 2228224 | tf_op jit(solution)/shard_map/reduce_scatter | solution.py:92
  120.2 6.3 collective-permute-start
  126.6 6.3 collective-permute-start
  132.9 6.3 collective-permute-start
  139.3 6.3 collective-permute-start
  145.7 6.3 collective-permute-start
  152.1 6.3 collective-permute-start
  158.4 6.3 collective-permute-start
  171.2 6.3 collective-permute-start
  183.9 8.9 %collective-permute-start = (f32[4,64,128]{2,1,0:T(8,128)S(1)}, f32[4,64,128]{2,1,0:T(8,128)S(1)}, u32[]{:S(2)}, u32[]{:S(2)}) collective-permute-start(f32[4,64,128]{2,1,0:T(8,128)S(1)} %multiply_add_fusion.2), channel_id=1, source_target_pairs={{16,0},{32,16},{48,32},{64,48},{80,64},{96,80},{112,96},{128,112},... | collective-permute-start | bytes 393224 | tf_op jit(solution)/shard_map/while/body/eval_jaxpr/ppermute | solution.py:10
  192.9 9.0 %collective-permute-start = (f32[4,64,128]{2,1,0:T(8,128)S(1)}, f32[4,64,128]{2,1,0:T(8,128)S(1)}, u32[]{:S(2)}, u32[]{:S(2)}) collective-permute-start(f32[4,64,128]{2,1,0:T(8,128)S(1)} %multiply_add_fusion.2), channel_id=1, source_target_pairs={{16,0},{32,16},{48,32},{64,48},{80,64},{96,80},{112,96},{128,112},... | collective-permute-start | bytes 393224 | tf_op jit(solution)/shard_map/while/body/eval_jaxpr/ppermute | solution.py:10
  201.9 9.0 %collective-permute-start = (f32[4,64,128]{2,1,0:T(8,128)S(1)}, f32[4,64,128]{2,1,0:T(8,128)S(1)}, u32[]{:S(2)}, u32[]{:S(2)}) collective-permute-start(f32[4,64,128]{2,1,0:T(8,128)S(1)} %multiply_add_fusion.2), channel_id=1, source_target_pairs={{16,0},{32,16},{48,32},{64,48},{80,64},{96,80},{112,96},{128,112},... | collective-permute-start | bytes 393224 | tf_op jit(solution)/shard_map/while/body/eval_jaxpr/ppermute | solution.py:10
  211.0 9.0 %collective-permute-start = (f32[4,64,128]{2,1,0:T(8,128)S(1)}, f32[4,64,128]{2,1,0:T(8,128)S(1)}, u32[]{:S(2)}, u32[]{:S(2)}) collective-permute-start(f32[4,64,128]{2,1,0:T(8,128)S(1)} %multiply_add_fusion.2), channel_id=1, source_target_pairs={{16,0},{32,16},{48,32},{64,48},{80,64},{96,80},{112,96},{128,112},... | collective-permute-start | bytes 393224 | tf_op jit(solution)/shard_map/while/body/eval_jaxpr/ppermute | solution.py:10
  220.1 9.0 %collective-permute-start = (f32[4,64,128]{2,1,0:T(8,128)S(1)}, f32[4,64,128]{2,1,0:T(8,128)S(1)}, u32[]{:S(2)}, u32[]{:S(2)}) collective-permute-start(f32[4,64,128]{2,1,0:T(8,128)S(1)} %multiply_add_fusion.2), channel_id=1, source_target_pairs={{16,0},{32,16},{48,32},{64,48},{80,64},{96,80},{112,96},{128,112},... | collective-permute-start | bytes 393224 | tf_op jit(solution)/shard_map/while/body/eval_jaxpr/ppermute | solution.py:10
  229.1 9.0 %collective-permute-start = (f32[4,64,128]{2,1,0:T(8,128)S(1)}, f32[4,64,128]{2,1,0:T(8,128)S(1)}, u32[]{:S(2)}, u32[]{:S(2)}) collective-permute-start(f32[4,64,128]{2,1,0:T(8,128)S(1)} %multiply_add_fusion.2), channel_id=1, source_target_pairs={{16,0},{32,16},{48,32},{64,48},{80,64},{96,80},{112,96},{128,112},... | collective-permute-start | bytes 393224 | tf_op jit(solution)/shard_map/while/body/eval_jaxpr/ppermute | solution.py:10
  238.2 9.0 %collective-permute-start = (f32[4,64,128]{2,1,0:T(8,128)S(1)}, f32[4,64,128]{2,1,0:T(8,128)S(1)}, u32[]{:S(2)}, u32[]{:S(2)}) collective-permute-start(f32[4,64,128]{2,1,0:T(8,128)S(1)} %multiply_add_fusion.2), channel_id=1, source_target_pairs={{16,0},{32,16},{48,32},{64,48},{80,64},{96,80},{112,96},{128,112},... | collective-permute-start | bytes 393224 | tf_op jit(solution)/shard_map/while/body/eval_jaxpr/ppermute | solution.py:10
  247.3 9.0 %collective-permute-start = (f32[4,64,128]{2,1,0:T(8,128)S(1)}, f32[4,64,128]{2,1,0:T(8,128)S(1)}, u32[]{:S(2)}, u32[]{:S(2)}) collective-permute-start(f32[4,64,128]{2,1,0:T(8,128)S(1)} %multiply_add_fusion.2), channel_id=1, source_target_pairs={{16,0},{32,16},{48,32},{64,48},{80,64},{96,80},{112,96},{128,112},... | collective-permute-start | bytes 393224 | tf_op jit(solution)/shard_map/while/body/eval_jaxpr/ppermute | solution.py:10
  256.3 9.0 %collective-permute-start = (f32[4,64,128]{2,1,0:T(8,128)S(1)}, f32[4,64,128]{2,1,0:T(8,128)S(1)}, u32[]{:S(2)}, u32[]{:S(2)}) collective-permute-start(f32[4,64,128]{2,1,0:T(8,128)S(1)} %multiply_add_fusion.2), channel_id=1, source_target_pairs={{16,0},{32,16},{48,32},{64,48},{80,64},{96,80},{112,96},{128,112},... | collective-permute-start | bytes 393224 | tf_op jit(solution)/shard_map/while/body/eval_jaxpr/ppermute | solution.py:10
  265.4 9.0 %collective-permute-start = (f32[4,64,128]{2,1,0:T(8,128)S(1)}, f32[4,64,128]{2,1,0:T(8,128)S(1)}, u32[]{:S(2)}, u32[]{:S(2)}) collective-permute-start(f32[4,64,128]{2,1,0:T(8,128)S(1)} %multiply_add_fusion.2), channel_id=1, source_target_pairs={{16,0},{32,16},{48,32},{64,48},{80,64},{96,80},{112,96},{128,112},... | collective-permute-start | bytes 393224 | tf_op jit(solution)/shard_map/while/body/eval_jaxpr/ppermute | solution.py:10
  274.5 9.0 %collective-permute-start = (f32[4,64,128]{2,1,0:T(8,128)S(1)}, f32[4,64,128]{2,1,0:T(8,128)S(1)}, u32[]{:S(2)}, u32[]{:S(2)}) collective-permute-start(f32[4,64,128]{2,1,0:T(8,128)S(1)} %multiply_add_fusion.2), channel_id=1, source_target_pairs={{16,0},{32,16},{48,32},{64,48},{80,64},{96,80},{112,96},{128,112},... | collective-permute-start | bytes 393224 | tf_op jit(solution)/shard_map/while/body/eval_jaxpr/ppermute | solution.py:10
  283.6 9.0 %collective-permute-start = (f32[4,64,128]{2,1,0:T(8,128)S(1)}, f32[4,64,128]{2,1,0:T(8,128)S(1)}, u32[]{:S(2)}, u32[]{:S(2)}) collective-permute-start(f32[4,64,128]{2,1,0:T(8,128)S(1)} %multiply_add_fusion.2), channel_id=1, source_target_pairs={{16,0},{32,16},{48,32},{64,48},{80,64},{96,80},{112,96},{128,112},... | collective-permute-start | bytes 393224 | tf_op jit(solution)/shard_map/while/body/eval_jaxpr/ppermute | solution.py:10
  292.6 9.0 %collective-permute-start = (f32[4,64,128]{2,1,0:T(8,128)S(1)}, f32[4,64,128]{2,1,0:T(8,128)S(1)}, u32[]{:S(2)}, u32[]{:S(2)}) collective-permute-start(f32[4,64,128]{2,1,0:T(8,128)S(1)} %multiply_add_fusion.2), channel_id=1, source_target_pairs={{16,0},{32,16},{48,32},{64,48},{80,64},{96,80},{112,96},{128,112},... | collective-permute-start | bytes 393224 | tf_op jit(solution)/shard_map/while/body/eval_jaxpr/ppermute | solution.py:10
  301.7 9.0 %collective-permute-start = (f32[4,64,128]{2,1,0:T(8,128)S(1)}, f32[4,64,128]{2,1,0:T(8,128)S(1)}, u32[]{:S(2)}, u32[]{:S(2)}) collective-permute-start(f32[4,64,128]{2,1,0:T(8,128)S(1)} %multiply_add_fusion.2), channel_id=1, source_target_pairs={{16,0},{32,16},{48,32},{64,48},{80,64},{96,80},{112,96},{128,112},... | collective-permute-start | bytes 393224 | tf_op jit(solution)/shard_map/while/body/eval_jaxpr/ppermute | solution.py:10
  310.8 9.0 %collective-permute-start = (f32[4,64,128]{2,1,0:T(8,128)S(1)}, f32[4,64,128]{2,1,0:T(8,128)S(1)}, u32[]{:S(2)}, u32[]{:S(2)}) collective-permute-start(f32[4,64,128]{2,1,0:T(8,128)S(1)} %multiply_add_fusion.2), channel_id=1, source_target_pairs={{16,0},{32,16},{48,32},{64,48},{80,64},{96,80},{112,96},{128,112},... | collective-permute-start | bytes 393224 | tf_op jit(solution)/shard_map/while/body/eval_jaxpr/ppermute | solution.py:10
  319.8 9.0 %collective-permute-start = (f32[4,64,128]{2,1,0:T(8,128)S(1)}, f32[4,64,128]{2,1,0:T(8,128)S(1)}, u32[]{:S(2)}, u32[]{:S(2)}) collective-permute-start(f32[4,64,128]{2,1,0:T(8,128)S(1)} %multiply_add_fusion.2), channel_id=1, source_target_pairs={{16,0},{32,16},{48,32},{64,48},{80,64},{96,80},{112,96},{128,112},... | collective-permute-start | bytes 393224 | tf_op jit(solution)/shard_map/while/body/eval_jaxpr/ppermute | solution.py:10
  328.9 9.0 %collective-permute-start = (f32[4,64,128]{2,1,0:T(8,128)S(1)}, f32[4,64,128]{2,1,0:T(8,128)S(1)}, u32[]{:S(2)}, u32[]{:S(2)}) collective-permute-start(f32[4,64,128]{2,1,0:T(8,128)S(1)} %multiply_add_fusion.2), channel_id=1, source_target_pairs={{16,0},{32,16},{48,32},{64,48},{80,64},{96,80},{112,96},{128,112},... | collective-permute-start | bytes 393224 | tf_op jit(solution)/shard_map/while/body/eval_jaxpr/ppermute | solution.py:10
  338.0 9.0 %collective-permute-start = (f32[4,64,128]{2,1,0:T(8,128)S(1)}, f32[4,64,128]{2,1,0:T(8,128)S(1)}, u32[]{:S(2)}, u32[]{:S(2)}) collective-permute-start(f32[4,64,128]{2,1,0:T(8,128)S(1)} %multiply_add_fusion.2), channel_id=1, source_target_pairs={{16,0},{32,16},{48,32},{64,48},{80,64},{96,80},{112,96},{128,112},... | collective-permute-start | bytes 393224 | tf_op jit(solution)/shard_map/while/body/eval_jaxpr/ppermute | solution.py:10
  347.0 9.0 %collective-permute-start = (f32[4,64,128]{2,1,0:T(8,128)S(1)}, f32[4,64,128]{2,1,0:T(8,128)S(1)}, u32[]{:S(2)}, u32[]{:S(2)}) collective-permute-start(f32[4,64,128]{2,1,0:T(8,128)S(1)} %multiply_add_fusion.2), channel_id=1, source_target_pairs={{16,0},{32,16},{48,32},{64,48},{80,64},{96,80},{112,96},{128,112},... | collective-permute-start | bytes 393224 | tf_op jit(solution)/shard_map/while/body/eval_jaxpr/ppermute | solution.py:10
  356.1 9.0 %collective-permute-start = (f32[4,64,128]{2,1,0:T(8,128)S(1)}, f32[4,64,128]{2,1,0:T(8,128)S(1)}, u32[]{:S(2)}, u32[]{:S(2)}) collective-permute-start(f32[4,64,128]{2,1,0:T(8,128)S(1)} %multiply_add_fusion.2), channel_id=1, source_target_pairs={{16,0},{32,16},{48,32},{64,48},{80,64},{96,80},{112,96},{128,112},... | collective-permute-start | bytes 393224 | tf_op jit(solution)/shard_map/while/body/eval_jaxpr/ppermute | solution.py:10
  365.2 9.0 %collective-permute-start = (f32[4,64,128]{2,1,0:T(8,128)S(1)}, f32[4,64,128]{2,1,0:T(8,128)S(1)}, u32[]{:S(2)}, u32[]{:S(2)}) collective-permute-start(f32[4,64,128]{2,1,0:T(8,128)S(1)} %multiply_add_fusion.2), channel_id=1, source_target_pairs={{16,0},{32,16},{48,32},{64,48},{80,64},{96,80},{112,96},{128,112},... | collective-permute-start | bytes 393224 | tf_op jit(solution)/shard_map/while/body/eval_jaxpr/ppermute | solution.py:10
  377.6 257.6 %reduce-scatter.5.cloned.1.call-start = ((), (), s32[]{:S(2)}) async-start(), calls=%async_computation.4 | async-start | bytes 139264 | tf_op jit(solution)/shard_map/reduce_scatter | solution.py:100
  (9 other events, 898.7 us)
Sparse Core Ops, SparseCore 0:
  11.0 104.5 all-gather.1
  377.7 147.4 reduce-scatter.2
  530.3 104.7 reduce-scatter.4
where the time goes:
time: 644 us; the launch traced here: 642 us
  waiting for transfers between devices  461 us (72%)
  blocking collectives  78 us (12%)
  starting transfers between devices  62.7 us (10%)
  between operations  13.9 us (2%)
  matrix products  10.6 us (2%)
  other arithmetic  9.97 us (2%)
    ppermute x31, waiting for transfers between devices, passed_along(): lax.ppermute(value, axis, [(source, source + steps) for source in range(i...  188 us
    reduce_scatter x1, waiting for transfers between devices, shards(): lax.psum_scatter(bc_part.astype(jnp.bfloat16), 'head', scatter_dimension=...  108 us
    all_gather x1, waiting for transfers between devices, shards(): lax.all_gather(out_grad, 'head', axis=1, tiled=True)  102 us
    psum x1, blocking collectives, shards(): param_grad = lax.psum(param_terms, 'seq') * norm_scale  78 us
    ppermute x31, starting transfers between devices, passed_along(): lax.ppermute(value, axis, [(source, source + steps) for source in range(i...  62.6 us
    reduce_scatter x1, waiting for transfers between devices, shards(): lax.psum_scatter(lax.dot_general(w_in, x_grad, contract_last, preferred_e...  62 us
  transfers between devices with their start and end apart: 34, of which 34 were waited for; matrix products, arithmetic and copies ran while one was open for 2% of the time, Pallas kernels for 0%

commit v1 on v0

v1 whole, which is shorter than its diff:
```python
import jax
import jax.numpy as jnp
from jax import lax
from jax.experimental import pallas as pl
from jax.experimental.pallas import tpu as pltpu
from jax.sharding import Mesh, PartitionSpec as P

SEQ = ("x", "zl", "core")
HEAD = ("y", "zh")
f32, bf16 = jnp.float32, jnp.bfloat16


def scan_kernel(parts_ref, carried_ref):
    blocks = parts_ref.shape[0]
    held = jnp.zeros(carried_ref.shape[1:], f32)
    for k in range(blocks - 1, -1, -1):
        carried_ref[k] = held
        wide = parts_ref[k].astype(f32)
        total = wide[8:9] + wide[9:10] + wide[10:11]
        held = total * held + wide[:8]


def suffix_scan(parts):
    blocks, _, width = parts.shape
    return pl.pallas_call(
        scan_kernel,
        out_shape=jax.ShapeDtypeStruct((blocks, 8, width), f32),
        cost_estimate=pl.CostEstimate(flops=blocks * 3072, bytes_accessed=blocks * 8192, transcendentals=0),
    )(parts)


def three_parts(values):
    first = values.astype(bf16).astype(f32)
    second = (values - first).astype(bf16).astype(f32)
    return jnp.stack([first, second, values - first - second], axis=-1)


def shards(out_grad, x_in, b_in, c_in, dt_raw, dt_bias, a_log, d_skip, states, w_out, w_in):
    tokens_here, inner_here = x_in.shape
    group_heads = dt_raw.shape[0]
    head_dim = inner_here // group_heads
    state_dim = b_in.shape[1]
    blocks = lax.axis_size(SEQ)
    contract_last = (((1,), (1,)), ((), ()))
    near = lax.all_gather(out_grad, "zh", axis=1, tiled=True)
    whole = lax.all_to_all(jnp.broadcast_to(near[None], (4,) + near.shape), "y", 0, 0)
    head_sum = jnp.zeros((tokens_here, inner_here), f32)
    for y in range(4):
        head_sum = head_sum + lax.dot_general(
            whole[y], w_out[:, y * near.shape[1]:(y + 1) * near.shape[1]], contract_last, preferred_element_type=f32
        )
    dy_heads = head_sum.astype(bf16).reshape(tokens_here, group_heads, head_dim)
    dy_wide = dy_heads.astype(f32)
    x_heads = x_in.reshape(tokens_here, group_heads, head_dim)
    x_wide = x_heads.astype(f32)
    decay_rate = jnp.exp(a_log)
    step_size = jax.nn.softplus(dt_raw + dt_bias[:, None])
    log_step = -decay_rate[:, None] * step_size
    positions = jnp.arange(tokens_here)
    causal = positions[:, None] >= positions[None, :]
    triangle = causal.astype(f32)
    cumlog = jnp.dot(log_step, triangle.T, precision=lax.Precision.HIGHEST)
    log_gaps = cumlog[:, :, None] - cumlog[:, None, :]
    decay_mask = jnp.where(causal[None], jnp.exp(jnp.minimum(log_gaps, 0.0)), 0.0)
    scores = lax.dot_general(c_in, b_in, contract_last, preferred_element_type=f32)
    step_rows = step_size.T
    x_scaled = (x_wide * step_rows[:, :, None]).astype(bf16)
    start_decay = jnp.exp(cumlog)
    dy_decay = (dy_wide * start_decay.T[:, :, None]).astype(bf16)
    local_state = jnp.einsum("ihp,in->hpn", dy_decay, c_in, preferred_element_type=f32)
    end_total = jnp.exp(cumlog[:, -1])
    ends = jnp.pad(three_parts(end_total), ((0, 0), (0, 5)))
    ends = jnp.broadcast_to(ends[:, None, :, None], (group_heads, blocks // group_heads, 8, state_dim))
    sent = jnp.concatenate([local_state.reshape(blocks, 8, state_dim), ends.reshape(blocks, 8, state_dim)], axis=1)
    got = lax.all_to_all(sent.astype(bf16), SEQ, 0, 0)
    carried = lax.all_to_all(suffix_scan(got), SEQ, 0, 0).reshape(group_heads, head_dim, state_dim)

    pair_dots = jnp.einsum("ihp,jhp->hij", dy_heads, x_scaled, preferred_element_type=f32)
    kernel = (scores[None] * decay_mask).astype(bf16)
    intra_back = jnp.einsum("hij,ihp->jhp", kernel, dy_heads, preferred_element_type=f32)
    masked_dots = (pair_dots * decay_mask).astype(bf16)
    entry_state = states.reshape(group_heads, head_dim, state_dim)
    db_intra = jnp.einsum("hij,in->nj", masked_dots, c_in, preferred_element_type=f32)
    dc_intra = jnp.einsum("hij,jn->ni", masked_dots, b_in, preferred_element_type=f32)
    dc_entry = jnp.einsum("ihp,hpn->ni", dy_decay, entry_state, preferred_element_type=f32)
    ystate = jnp.einsum("in,hpn->ihp", c_in, entry_state, preferred_element_type=f32)
    pair_weight = pair_dots * scores[None] * decay_mask
    state_terms = start_decay * jnp.sum(dy_wide * ystate, axis=2).T
    skip_terms = jnp.sum(dy_wide * x_wide, axis=(0, 2))

    carried_bf = carried.astype(bf16)
    state_back = jnp.einsum("jn,hpn->jhp", b_in, carried_bf, preferred_element_type=f32)
    end_decay = jnp.exp(cumlog[:, -1:] - cumlog)
    end_weight = (step_size * end_decay).T
    x_grad = (
        (
            step_rows[:, :, None] * intra_back
            + end_weight[:, :, None] * state_back
            + d_skip[None, :, None] * dy_wide
        )
        .astype(bf16)
        .reshape(tokens_here, inner_here)
    )
    x_end = (x_wide * end_weight[:, :, None]).astype(bf16)
    db_entry = jnp.einsum("jhp,hpn->nj", x_end, carried_bf, preferred_element_type=f32)
    bc_part = jnp.concatenate([db_intra + db_entry, dc_intra + dc_entry], axis=0).astype(bf16)
    in_part = lax.dot_general(w_in, x_grad, contract_last, preferred_element_type=f32).astype(bf16)
    terms = jnp.concatenate(
        [in_part.reshape(4, 4, -1, tokens_here), bc_part.reshape(4, 4, -1, tokens_here)], axis=2
    )
    half = lax.all_to_all(terms, "y", 0, 0).astype(f32).sum(axis=0).astype(bf16)
    both = lax.all_to_all(half, "zh", 0, 0).astype(f32).sum(axis=0).astype(bf16)
    in_rows = in_part.shape[0] // 16

    end_terms = end_weight.T * jnp.sum(x_wide * state_back, axis=2).T
    cum_grad = pair_weight.sum(axis=2) - pair_weight.sum(axis=1) + state_terms - end_terms
    tail_grad = end_terms.sum(axis=1) + end_total * jnp.sum(entry_state.astype(f32) * carried, axis=(1, 2))
    step_grad = jnp.dot(cum_grad, triangle, precision=lax.Precision.HIGHEST) + tail_grad[:, None]
    dt_sum = (
        -decay_rate[:, None] * step_grad
        + jnp.sum(x_wide * (intra_back + end_decay.T[:, :, None] * state_back), axis=2).T
    )
    dt_grad = dt_sum * jax.nn.sigmoid(dt_raw + dt_bias[:, None])
    param_terms = jnp.stack([jnp.sum(step_grad * log_step, axis=1), skip_terms, jnp.sum(dt_grad, axis=1)])
    flat = jnp.pad(param_terms.reshape(1, -1), ((0, 0), (0, 128 - param_terms.size)))
    spread = lax.all_to_all(jnp.broadcast_to(flat[None], (blocks, 1, 128)), SEQ, 0, 0)
    norm_scale = (blocks * tokens_here * head_dim) ** (-0.5)
    param_grad = spread.sum(axis=0)[0, : param_terms.size].reshape(param_terms.shape) * norm_scale
    return (both[:in_rows], both[in_rows:], dt_grad, param_grad)


def solution(mesh):
    fine = Mesh(mesh.devices.reshape(4, 4, 2, 4, 4), ("x", "zl", "core", "y", "zh"))
    return jax.shard_map(
        shards,
        mesh=fine,
        in_specs=(
            P(SEQ, HEAD),
            P(SEQ, HEAD),
            P(SEQ, None),
            P(SEQ, None),
            P(HEAD, SEQ),
            P(HEAD),
            P(HEAD),
            P(HEAD),
            P(SEQ, HEAD, None),
            P(HEAD, None),
            P(None, HEAD),
        ),
        out_specs=(P(HEAD, SEQ), P(HEAD, SEQ), P(HEAD, SEQ), P(None, HEAD)),
        check_vma=False,
    )
```

time: 644 us -> 197 us (0.31)
  waiting for transfers between devices: 461 us -> 96.4 us
  blocking collectives: 78 us -> 31.5 us
  starting transfers between devices: 62.7 us -> 33.4 us
  between operations: 13.9 us -> 0.97 us
    ppermute x31 -> x0, waiting for transfers between devices: 188 us -> none  [passed_along(): lax.ppermute(value, axis, [(source, source + steps) for source in range(i...]
    reduce_scatter x2 -> x0, waiting for transfers between devices: 170 us -> none  [the longest x1 108 us: shards(): lax.psum_scatter(bc_part.astype(jnp.bfloat16), 'head', scatter_dimension=...]
    all_gather x1 -> x0, waiting for transfers between devices: 102 us -> none  [shards(): lax.all_gather(out_grad, 'head', axis=1, tiled=True)]
    all_to_all x0 -> x6, waiting for transfers between devices: none -> 96.4 us  [the longest x1 29.8 us: shards(): both = lax.all_to_all(half, 'zh', 0, 0).astype(f32).sum(axis=0).astype(bf16)]
    psum x1 -> x0, blocking collectives: 78 us -> none  [shards(): param_grad = lax.psum(param_terms, 'seq') * norm_scale]
    ppermute x31 -> x0, starting transfers between devices: 62.6 us -> none  [passed_along(): lax.ppermute(value, axis, [(source, source + steps) for source in range(i...]
    all_to_all x0 -> x6, starting transfers between devices: none -> 33.4 us  [the longest x1 9.44 us: shards(): got = lax.all_to_all(sent.astype(bf16), SEQ, 0, 0)]
    all_gather x0 -> x1, blocking collectives: none -> 31.5 us  [shards(): near = lax.all_gather(out_grad, 'zh', axis=1, tiled=True)]
  transfers between devices with their start and end apart: 34 -> 6, of which waited for: 34 -> 6; matrix products, arithmetic and copies ran while one was open for 2% -> 5% of each run, Pallas kernels for 0% -> 0%
where the time goes in v1:
time: 197 us; the launch traced here: 196 us
  waiting for transfers between devices  96.4 us (49%)
  starting transfers between devices  33.4 us (17%)
  blocking collectives  31.5 us (16%)
  matrix products  13.8 us (7%)
  local copies, waits for them, and re-layouts  9.57 us (5%)
  other arithmetic  8.64 us (4%)
    all_gather x1, blocking collectives, shards(): near = lax.all_gather(out_grad, 'zh', axis=1, tiled=True)  31.5 us
    all_to_all x1, waiting for transfers between devices, shards(): both = lax.all_to_all(half, 'zh', 0, 0).astype(f32).sum(axis=0).astype(bf16)  29.8 us
    all_to_all x1, waiting for transfers between devices, shards(): half = lax.all_to_all(terms, 'y', 0, 0).astype(f32).sum(axis=0).astype(bf16)  25.2 us
    all_to_all x1, waiting for transfers between devices, shards(): lax.all_to_all(jnp.broadcast_to(near[None], (4,) + near.shape), 'y', 0, 0)  22.2 us
    all_to_all x1, starting transfers between devices, shards(): got = lax.all_to_all(sent.astype(bf16), SEQ, 0, 0)  9.44 us
    all_to_all x1, waiting for transfers between devices, shards(): got = lax.all_to_all(sent.astype(bf16), SEQ, 0, 0)  7.61 us
    all_to_all x1, waiting for transfers between devices, shards(): lax.all_to_all(suffix_scan(got), SEQ, 0, 0)  7.21 us
    all_to_all x1, starting transfers between devices, shards(): both = lax.all_to_all(half, 'zh', 0, 0).astype(f32).sum(axis=0).astype(bf16)  6.36 us
  transfers between devices with their start and end apart: 6, of which 6 were waited for; matrix products, arithmetic and copies ran while one was open for 5% of the time, Pallas kernels for 0%

profile of v1, /device:TPU:1, one launch (start us, length us, event | category | flops | bytes accessed | tf_op | source)
XLA Modules:
  0.0 196.0 jit_solution(5205952468357359539)
XLA Ops:
  0.6 31.5 %all_gather.3 = bf16[256,1024]{1,0:T(8,128)(2,1)S(1)} all-gather(bf16[256,256]{1,0:T(8,128)(2,1)} %param.11), channel_id=1, replica_groups=mesh['x'=4,'zl'=4,'core'=2,'y'=4,'zh'=4] {'zh'}, dimensions={1}, use_global_device_ids=true | all-gather | bytes 655360 | tf_op jit(solution)/shard_map/all_gather | solution.py:45
  32.2 1.6 broadcast_in_dim.22
  33.8 4.6 %all-to-all-start = ((bf16[4,256,1024]{2,1,0:T(8,128)(2,1)}), bf16[4,256,1024]{2,1,0:T(8,128)(2,1)}, u32[]{:S(2)}, u32[]{:S(2)}) async-start(bf16[4,256,1024]{2,1,0:T(8,128)(2,1)} %broadcast_in_dim.22), calls=%async_computation | async-start | bytes 4194304 | tf_op jit(solution)/shard_map/all_to_all | solution.py:46
  39.4 22.2 %all-to-all-done = bf16[4,256,1024]{2,1,0:T(8,128)(2,1)} async-done(((bf16[4,256,1024]{2,1,0:T(8,128)(2,1)}), bf16[4,256,1024]{2,1,0:T(8,128)(2,1)}, u32[]{:S(2)}, u32[]{:S(2)}) %all-to-all-start) | async-done | bytes 2097184 | tf_op jit(solution)/shard_map/all_to_all | solution.py:46
  61.6 1.7 fusion.9
  63.3 1.6 convolution_add_fusion.2
  64.9 1.4 convolution_add_fusion.1
  66.3 1.4 fusion.21
  68.0 0.7 pad_maximum_fusion.1
  68.7 9.4 %all-to-all-start.1 = ((bf16[32,16,128]{2,1,0:T(8,128)(2,1)}), bf16[32,16,128]{2,1,0:T(8,128)(2,1)S(1)}, u32[]{:S(2)}, u32[]{:S(2)}) async-start(bf16[32,16,128]{2,1,0:T(8,128)(2,1)} %pad_maximum_fusion.1), calls=%async_computation.1 | async-start | bytes 262144 | tf_op jit(solution)/shard_map/all_to_all | solution.py:75
  78.6 0.7 fusion.7
  79.3 7.6 %all-to-all-done.1.parts_ref = bf16[32,16,128]{2,1,0:T(8,128)(2,1)S(1)} async-done(((bf16[32,16,128]{2,1,0:T(8,128)(2,1)}), bf16[32,16,128]{2,1,0:T(8,128)(2,1)S(1)}, u32[]{:S(2)}, u32[]{:S(2)}) %all-to-all-start.1) | async-done | bytes 131104 | tf_op jit(solution)/shard_map/all_to_all | solution.py:75
  86.9 0.7 copy-done.3
  87.5 1.6 shard_map.138
  89.2 3.9 %all-to-all-start.2 = ((f32[32,8,128]{2,1,0:T(8,128)}), f32[32,8,128]{2,1,0:T(8,128)S(1)}, u32[]{:S(2)}, u32[]{:S(2)}) async-start(f32[32,8,128]{2,1,0:T(8,128)} %shard_map.138), calls=%async_computation.2 | async-start | bytes 262144 | tf_op jit(solution)/shard_map/all_to_all | solution.py:76
  93.5 1.2 convolution_bitcast_fusion
  94.7 7.2 %all-to-all-done.2 = f32[32,8,128]{2,1,0:T(8,128)S(1)} async-done(((f32[32,8,128]{2,1,0:T(8,128)}), f32[32,8,128]{2,1,0:T(8,128)S(1)}, u32[]{:S(2)}, u32[]{:S(2)}) %all-to-all-start.2) | async-done | bytes 131104 | tf_op jit(solution)/shard_map/all_to_all | solution.py:76
  102.7 1.2 multiply_reduce_fusion.1
  103.9 2.1 %fusion = bf16[4096,256]{0,1:T(8,128)(2,1)} fusion(bf16[256,256]{0,1:T(8,128)(2,1)S(1)} %bitcast.140, bf16[4096,256]{1,0:T(8,128)(2,1)S(1)} %copy-done), kind=kOutput, calls=%fused_computation.1 | convolution fusion | flops 537919488 | bytes 4325376 | tf_op jit(solution)/shard_map/dot_general | solution.py:107
  106.0 4.1 %copy.56 = bf16[4096,256]{1,0:T(8,128)(2,1)} copy(bf16[4096,256]{0,1:T(8,128)(2,1)} %fusion) | data formatting | bytes 4194304 | tf_op jit(solution)/shard_map/reshape | solution.py:109
  110.1 3.1 %pad_maximum_fusion = bf16[4,4,272,256]{3,2,1,0:T(8,128)(2,1)} fusion(bf16[4,4,16,256]{3,2,1,0:T(8,128)(2,1)S(1)} %bitcast.134, bf16[4,4,256,256]{3,2,1,0:T(8,128)(2,1)} %bitcast.127), kind=kLoop, calls=%fused_computation.2 | loop fusion | flops 4456448 | bytes 4456448 | tf_op jit(solution)/shard_map/concatenate | solution.py:108
  113.2 4.5 %all-to-all-start.3 = ((bf16[4,4,272,256]{3,2,1,0:T(8,128)(2,1)}), bf16[4,4,272,256]{3,2,1,0:T(8,128)(2,1)}, u32[]{:S(2)}, u32[]{:S(2)}) async-start(bf16[4,4,272,256]{3,2,1,0:T(8,128)(2,1)} %pad_maximum_fusion), calls=%async_computation.3 | async-start | bytes 4456448 | tf_op jit(solution)/shard_map/all_to_all | solution.py:111
  118.8 1.0 fusion.50
  119.9 25.2 %all-to-all-done.3 = bf16[4,4,272,256]{3,2,1,0:T(8,128)(2,1)} async-done(((bf16[4,4,272,256]{3,2,1,0:T(8,128)(2,1)}), bf16[4,4,272,256]{3,2,1,0:T(8,128)(2,1)}, u32[]{:S(2)}, u32[]{:S(2)}) %all-to-all-start.3) | async-done | bytes 2228256 | tf_op jit(solution)/shard_map/all_to_all | solution.py:111
  145.2 0.6 broadcast_in_dim.28
  145.8 4.7 %all-to-all-start.5 = ((f32[32,1,128]{2,1,0:T(1,128)}), f32[32,1,128]{2,1,0:T(1,128)S(1)}, u32[]{:S(2)}, u32[]{:S(2)}) async-start(f32[32,1,128]{2,1,0:T(1,128)} %broadcast_in_dim.28), calls=%async_computation.5 | async-start | bytes 32768 | tf_op jit(solution)/shard_map/all_to_all | solution.py:126
  150.5 2.9 %reduce_sum.157 = bf16[4,272,256]{2,1,0:T(8,128)(2,1)} reduce(bf16[4,4,272,256]{3,2,1,0:T(8,128)(2,1)} %all-to-all-done.3, bf16[]{:T(256)} %constant.5.clone.1), dimensions={0}, to_apply=%region_1.2 | reduce | flops 835584 | bytes 2785282 | tf_op jit(solution)/shard_map/reduce_sum | solution.py:111
  153.4 4.3 %all-to-all-done.5 = f32[32,1,128]{2,1,0:T(1,128)S(1)} async-done(((f32[32,1,128]{2,1,0:T(1,128)}), f32[32,1,128]{2,1,0:T(1,128)S(1)}, u32[]{:S(2)}, u32[]{:S(2)}) %all-to-all-start.5) | async-done | bytes 16416 | tf_op jit(solution)/shard_map/all_to_all | solution.py:126
  157.7 6.4 %all-to-all-start.4 = ((bf16[4,272,256]{2,1,0:T(8,128)(2,1)}), bf16[4,272,256]{2,1,0:T(8,128)(2,1)S(1)}, u32[]{:S(2)}, u32[]{:S(2)}) async-start(bf16[4,272,256]{2,1,0:T(8,128)(2,1)} %reduce_sum.157), calls=%async_computation.4 | async-start | bytes 1114112 | tf_op jit(solution)/shard_map/all_to_all | solution.py:112
  164.1 0.7 mul.171
  164.8 29.8 %all-to-all-done.4 = bf16[4,272,256]{2,1,0:T(8,128)(2,1)S(1)} async-done(((bf16[4,272,256]{2,1,0:T(8,128)(2,1)}), bf16[4,272,256]{2,1,0:T(8,128)(2,1)S(1)}, u32[]{:S(2)}, u32[]{:S(2)}) %all-to-all-start.4) | async-done | bytes 557088 | tf_op jit(solution)/shard_map/all_to_all | solution.py:112
  194.7 0.7 slice.54
  (58 shorter events, 4.8 us)
Async XLA Ops:
  0.6 103.3 %copy-start = (bf16[4096,256]{1,0:T(8,128)(2,1)S(1)}, bf16[4096,256]{1,0:T(8,128)(2,1)}, u32[]{:S(2)}) copy-start(bf16[4096,256]{1,0:T(8,128)(2,1)} %param.21) | copy-start | bytes 6291460
  33.8 4.6 %copy-start.6 = (bf16[256,256]{1,0:T(8,128)(2,1)S(1)}, bf16[256,256]{1,0:T(8,128)(2,1)}, u32[]{:S(2)}) copy-start(bf16[256,256]{1,0:T(8,128)(2,1)} %param.12) | copy-start | bytes 393220
  33.8 4.7 %copy-start.7 = (f32[4,256]{1,0:T(4,128)S(1)}, f32[4,256]{1,0:T(4,128)}, u32[]{:S(2)}) copy-start(f32[4,256]{1,0:T(4,128)} %param.15) | copy-start | bytes 12292
  33.8 4.7 %copy-start.8 = (f32[4]{0:T(128)S(1)}, f32[4]{0:T(128)}, u32[]{:S(2)}) copy-start(f32[4]{0:T(128)} %param.16) | copy-start | bytes 52
  33.8 4.8 %copy-start.9 = (f32[4]{0:T(128)S(1)}, f32[4]{0:T(128)}, u32[]{:S(2)}) copy-start(f32[4]{0:T(128)} %param.17) | copy-start | bytes 52
  33.8 27.8 %all-to-all-start = ((bf16[4,256,1024]{2,1,0:T(8,128)(2,1)}), bf16[4,256,1024]{2,1,0:T(8,128)(2,1)}, u32[]{:S(2)}, u32[]{:S(2)}) async-start(bf16[4,256,1024]{2,1,0:T(8,128)(2,1)} %broadcast_in_dim.22), calls=%async_computation | async-start | bytes 4194304 | tf_op jit(solution)/shard_map/all_to_all | solution.py:46
  61.6 3.3 %copy-start.5 = (bf16[256,4096]{1,0:T(8,128)(2,1)S(1)}, bf16[256,4096]{1,0:T(8,128)(2,1)}, u32[]{:S(2)}) copy-start(bf16[256,4096]{1,0:T(8,128)(2,1)} %param.20) | copy-start | bytes 6291460
  63.3 4.4 %copy-start.1 = (bf16[256,128]{1,0:T(8,128)(2,1)S(1)}, bf16[256,128]{1,0:T(8,128)(2,1)}, u32[]{:S(2)}) copy-start(bf16[256,128]{1,0:T(8,128)(2,1)} %param.14) | copy-start | bytes 196612
  64.9 13.3 %copy-start.4 = (bf16[256,128]{1,0:T(8,128)(2,1)S(1)}, bf16[256,128]{1,0:T(8,128)(2,1)}, u32[]{:S(2)}) copy-start(bf16[256,128]{1,0:T(8,128)(2,1)} %param.13) | copy-start | bytes 196612
  68.7 18.2 %all-to-all-start.1 = ((bf16[32,16,128]{2,1,0:T(8,128)(2,1)}), bf16[32,16,128]{2,1,0:T(8,128)(2,1)S(1)}, u32[]{:S(2)}, u32[]{:S(2)}) async-start(bf16[32,16,128]{2,1,0:T(8,128)(2,1)} %pad_maximum_fusion.1), calls=%async_computation.1 | async-start | bytes 262144 | tf_op jit(solution)/shard_map/all_to_all | solution.py:75
  78.4 14.7 %copy-start.2 = (bf16[1,256,128]{2,1,0:T(8,128)(2,1)S(1)}, bf16[1,256,128]{2,1,0:T(8,128)(2,1)}, u32[]{:S(2)}) copy-start(bf16[1,256,128]{2,1,0:T(8,128)(2,1)} %param.19) | copy-start | bytes 196612
  79.3 23.4 %copy-start.10 = (f32[4]{0:T(128)S(1)}, f32[4]{0:T(128)}, u32[]{:S(2)}) copy-start(f32[4]{0:T(128)} %param.18) | copy-start | bytes 52
  86.9 0.7 copy-start.3
  89.2 12.7 %all-to-all-start.2 = ((f32[32,8,128]{2,1,0:T(8,128)}), f32[32,8,128]{2,1,0:T(8,128)S(1)}, u32[]{:S(2)}, u32[]{:S(2)}) async-start(f32[32,8,128]{2,1,0:T(8,128)} %shard_map.138), calls=%async_computation.2 | async-start | bytes 262144 | tf_op jit(solution)/shard_map/all_to_all | solution.py:76
  113.2 32.0 %all-to-all-start.3 = ((bf16[4,4,272,256]{3,2,1,0:T(8,128)(2,1)}), bf16[4,4,272,256]{3,2,1,0:T(8,128)(2,1)}, u32[]{:S(2)}, u32[]{:S(2)}) async-start(bf16[4,4,272,256]{3,2,1,0:T(8,128)(2,1)} %pad_maximum_fusion), calls=%async_computation.3 | async-start | bytes 4456448 | tf_op jit(solution)/shard_map/all_to_all | solution.py:111
  145.8 11.9 %all-to-all-start.5 = ((f32[32,1,128]{2,1,0:T(1,128)}), f32[32,1,128]{2,1,0:T(1,128)S(1)}, u32[]{:S(2)}, u32[]{:S(2)}) async-start(f32[32,1,128]{2,1,0:T(1,128)} %broadcast_in_dim.28), calls=%async_computation.5 | async-start | bytes 32768 | tf_op jit(solution)/shard_map/all_to_all | solution.py:126
  157.7 36.9 %all-to-all-start.4 = ((bf16[4,272,256]{2,1,0:T(8,128)(2,1)}), bf16[4,272,256]{2,1,0:T(8,128)(2,1)S(1)}, u32[]{:S(2)}, u32[]{:S(2)}) async-start(bf16[4,272,256]{2,1,0:T(8,128)(2,1)} %reduce_sum.157), calls=%async_computation.4 | async-start | bytes 1114112 | tf_op jit(solution)/shard_map/all_to_all | solution.py:112

commit v2 on v1

--- a/solution.py
+++ b/solution.py
@@ -25,7 +25,8 @@
     return pl.pallas_call(
         scan_kernel,
         out_shape=jax.ShapeDtypeStruct((blocks, 8, width), f32),
-        cost_estimate=pl.CostEstimate(flops=blocks * 3072, bytes_accessed=blocks * 8192, transcendentals=0),
+        compiler_params=small(),
+        cost_estimate=cost(blocks * 3072, blocks * 8192),
     )(parts)
 
 
@@ -33,6 +34,175 @@
     first = values.astype(bf16).astype(f32)
     second = (values - first).astype(bf16).astype(f32)
     return jnp.stack([first, second, values - first - second], axis=-1)
+
+
+def cost(flops, moved):
+    return pl.CostEstimate(flops=flops, bytes_accessed=moved, transcendentals=0)
+
+
+def small():
+    return pltpu.CompilerParams(vmem_limit_bytes=16 << 20)
+
+
+def dot_last(a, b):
+    return lax.dot_general(a, b, (((1,), (1,)), ((), ())), preferred_element_type=f32)
+
+
+def regroup_kernel(w_ref, out_ref):
+    out_ref[0] = w_ref[...]
+
+
+def regrouped(w):
+    rows, width = w.shape
+    part = width // 4
+    return pl.pallas_call(
+        regroup_kernel,
+        grid=(4,),
+        in_specs=[pl.BlockSpec((rows, part), lambda g: (0, g))],
+        out_specs=pl.BlockSpec((1, rows, part), lambda g: (g, 0, 0)),
+        out_shape=jax.ShapeDtypeStruct((4, rows, part), w.dtype),
+        cost_estimate=cost(0, 4 * rows * width),
+    )(w)
+
+
+def partial_kernel(near_ref, w_ref, out_ref):
+    out_ref[0] = dot_last(near_ref[...], w_ref[0]).astype(bf16)
+
+
+def partial_products(near, w_mine):
+    groups, inner, depth = w_mine.shape
+    tokens = near.shape[0]
+    return pl.pallas_call(
+        partial_kernel,
+        grid=(groups,),
+        in_specs=[
+            pl.BlockSpec((tokens, depth), lambda g: (0, 0)),
+            pl.BlockSpec((1, inner, depth), lambda g: (g, 0, 0)),
+        ],
+        out_specs=pl.BlockSpec((1, tokens, inner), lambda g: (g, 0, 0)),
+        out_shape=jax.ShapeDtypeStruct((groups, tokens, inner), bf16),
+        compiler_params=small(),
+        cost_estimate=cost(2 * groups * tokens * inner * depth, 4 << 20),
+    )(near, w_mine)
+
+
+def state_kernel(parts_ref, start_ref, c_ref, ends_ref, dy_ref, decayed_ref, sent_ref):
+    total = parts_ref[0].astype(f32)
+    for y in range(1, parts_ref.shape[0]):
+        total = total + parts_ref[y].astype(f32)
+    dy = total.astype(bf16)
+    dy_ref[...] = dy
+    decayed = (dy.astype(f32) * start_ref[...]).astype(bf16)
+    decayed_ref[...] = decayed
+    state = lax.dot_general(decayed, c_ref[...], (((0,), (0,)), ((), ())), preferred_element_type=f32)
+    blocks, rows, width = ends_ref.shape
+    state = state.reshape(blocks, rows, width)
+    sent_ref[...] = jnp.concatenate([state, ends_ref[...]], axis=1).astype(bf16)
+
+
+def local_states(parts, start, c_in, ends):
+    _, tokens, inner = parts.shape
+    blocks, rows, width = ends.shape
+    wide = jax.ShapeDtypeStruct((tokens, inner), bf16)
+    return pl.pallas_call(
+        state_kernel,
+        out_shape=(wide, wide, jax.ShapeDtypeStruct((blocks, 2 * rows, width), bf16)),
+        compiler_params=small(),
+        cost_estimate=cost(2 * tokens * inner * width, 2 << 20),
+    )(parts, start, c_in, ends)
+
+
+def x_grad_kernel(carried_ref, b_ref, base_ref, weight_ref, x_end_ref, bc_ref, sent_ref, back_ref):
+    blocks, rows, width = carried_ref.shape
+    carried = carried_ref[...].reshape(blocks * rows, width).astype(bf16)
+    back = dot_last(b_ref[...], carried)
+    back_ref[...] = back
+    x_grad = (base_ref[...] + weight_ref[...] * back).astype(bf16)
+    entry = jnp.dot(x_end_ref[...], carried, preferred_element_type=f32)
+    tokens = entry.shape[0]
+    rows = bc_ref.shape[0] // 4
+    db = (bc_ref[:width] + entry.T).astype(bf16)
+    dc = bc_ref[width:].astype(bf16)
+    for y in range(4):
+        sent_ref[y, :tokens] = x_grad
+        half = db if y < 2 else dc
+        sent_ref[y, tokens:] = half[(y % 2) * rows:(y % 2 + 1) * rows]
+
+
+def x_grads(carried, b_in, base, weight, x_end, bc_base):
+    tokens, inner = base.shape
+    rows = bc_base.shape[0] // 4
+    return pl.pallas_call(
+        x_grad_kernel,
+        out_shape=(
+            jax.ShapeDtypeStruct((4, tokens + rows, inner), bf16),
+            jax.ShapeDtypeStruct((tokens, inner), f32),
+        ),
+        compiler_params=small(),
+        cost_estimate=cost(4 * tokens * inner * 128, 2 << 20),
+    )(carried, b_in, base, weight, x_end, bc_base)
+
+
+def in_kernel(y_ref, got_ref, own_ref, *refs):
+    *held_refs, out_ref = refs
+    tokens = got_ref.shape[2]
+    feats = own_ref.shape[0]
+    y = y_ref[0]
+    total = dot_last(own_ref[...], got_ref[y, :tokens])
+    for s, w_ref in enumerate(held_refs):
+        total = total + dot_last(w_ref[...], got_ref[lax.rem(y + 3 - s, 4), :tokens])
+    out_ref[0, :feats] = total.astype(bf16)
+    rows = out_ref.shape[1] - feats
+    at = pl.ds(pl.multiple_of(tokens + pl.program_id(0) * rows, rows), rows)
+    bc = got_ref[0, at].astype(f32)
+    for other in range(1, 4):
+        bc = bc + got_ref[other, at].astype(f32)
+    out_ref[0, feats:] = bc.astype(bf16)
+
+
+def in_products(y, got, w_in, held):
+    features, inner = w_in.shape
+    _, height, tokens = got.shape
+    feats, rows = features // 16, (height - tokens) // 4
+    return pl.pallas_call(
+        in_kernel,
+        grid_spec=pltpu.PrefetchScalarGridSpec(
+            num_scalar_prefetch=1,
+            grid=(4,),
+            in_specs=[
+                pl.BlockSpec(got.shape, lambda z, y: (0, 0, 0)),
+                pl.BlockSpec((feats, inner), lambda z, y: (4 * y[0] + z, 0)),
+            ]
+            + [pl.BlockSpec((feats, inner), lambda z, y: (z, 0))] * 3,
+            out_specs=pl.BlockSpec((1, feats + rows, tokens), lambda z, y: (z, 0, 0)),
+        ),
+        out_shape=jax.ShapeDtypeStruct((4, feats + rows, tokens), bf16),
+        compiler_params=small(),
+        cost_estimate=cost(8 * features * inner * tokens // 4, 4 << 20),
+    )(y.reshape(1), got, w_in, *held)
+
+
+def sum_kernel(terms_ref, in_ref, bc_ref):
+    feats = in_ref.shape[0]
+    total = terms_ref[0].astype(f32)
+    for z in range(1, 4):
+        total = total + terms_ref[z].astype(f32)
+    total = total.astype(bf16)
+    in_ref[...] = total[:feats]
+    bc_ref[...] = total[feats:]
+
+
+def final_sums(terms, feats):
+    _, height, tokens = terms.shape
+    return pl.pallas_call(
+        sum_kernel,
+        out_shape=(
+            jax.ShapeDtypeStruct((feats, tokens), bf16),
+            jax.ShapeDtypeStruct((height - feats, tokens), bf16),
+        ),
+        compiler_params=small(),
+        cost_estimate=cost(4 * height * tokens, 1 << 20),
+    )(terms)
 
 
 def shards(out_grad, x_in, b_in, c_in, dt_raw, dt_bias, a_log, d_skip, states, w_out, w_in):
@@ -42,15 +212,9 @@
     state_dim = b_in.shape[1]
     blocks = lax.axis_size(SEQ)
     contract_last = (((1,), (1,)), ((), ()))
+    w_out_y = lax.all_to_all(regrouped(w_out), "y", 0, 0)
     near = lax.all_gather(out_grad, "zh", axis=1, tiled=True)
-    whole = lax.all_to_all(jnp.broadcast_to(near[None], (4,) + near.shape), "y", 0, 0)
-    head_sum = jnp.zeros((tokens_here, inner_here), f32)
-    for y in range(4):
-        head_sum = head_sum + lax.dot_general(
-            whole[y], w_out[:, y * near.shape[1]:(y + 1) * near.shape[1]], contract_last, preferred_element_type=f32
-        )
-    dy_heads = head_sum.astype(bf16).reshape(tokens_here, group_heads, head_dim)
-    dy_wide = dy_heads.astype(f32)
+    head_parts = lax.all_to_all(partial_products(near, w_out_y), "y", 0, 0)
     x_heads = x_in.reshape(tokens_here, group_heads, head_dim)
     x_wide = x_heads.astype(f32)
     decay_rate = jnp.exp(a_log)
@@ -66,14 +230,24 @@
     step_rows = step_size.T
     x_scaled = (x_wide * step_rows[:, :, None]).astype(bf16)
     start_decay = jnp.exp(cumlog)
-    dy_decay = (dy_wide * start_decay.T[:, :, None]).astype(bf16)
-    local_state = jnp.einsum("ihp,in->hpn", dy_decay, c_in, preferred_element_type=f32)
     end_total = jnp.exp(cumlog[:, -1])
     ends = jnp.pad(three_parts(end_total), ((0, 0), (0, 5)))
     ends = jnp.broadcast_to(ends[:, None, :, None], (group_heads, blocks // group_heads, 8, state_dim))
-    sent = jnp.concatenate([local_state.reshape(blocks, 8, state_dim), ends.reshape(blocks, 8, state_dim)], axis=1)
-    got = lax.all_to_all(sent.astype(bf16), SEQ, 0, 0)
-    carried = lax.all_to_all(suffix_scan(got), SEQ, 0, 0).reshape(group_heads, head_dim, state_dim)
+    y = lax.axis_index("y")
+    w_in_held, head_parts = lax.optimization_barrier((w_in, head_parts))
+    quarter = w_in.shape[0] // 4
+    held = []
+    for s in range(1, 4):
+        piece = lax.dynamic_slice_in_dim(w_in_held, lax.rem(y + s, 4) * quarter, quarter)
+        held.append(lax.ppermute(piece, "y", [(i, (i + s) % 4) for i in range(4)]))
+    start_wide = jnp.repeat(start_decay.T, head_dim, axis=1)
+    dy_flat, decayed_flat, sent = local_states(head_parts, start_wide, c_in, ends.reshape(blocks, 8, state_dim))
+    dy_heads = dy_flat.reshape(tokens_here, group_heads, head_dim)
+    dy_wide = dy_heads.astype(f32)
+    dy_decay = decayed_flat.reshape(tokens_here, group_heads, head_dim)
+    got = lax.all_to_all(sent, SEQ, 0, 0)
+    carried_rows = lax.all_to_all(suffix_scan(got), SEQ, 0, 0)
+    carried = carried_rows.reshape(group_heads, head_dim, state_dim)
 
     pair_dots = jnp.einsum("ihp,jhp->hij", dy_heads, x_scaled, preferred_element_type=f32)
     kernel = (scores[None] * decay_mask).astype(bf16)
@@ -88,29 +262,17 @@
     state_terms = start_decay * jnp.sum(dy_wide * ystate, axis=2).T
     skip_terms = jnp.sum(dy_wide * x_wide, axis=(0, 2))
 
-    carried_bf = carried.astype(bf16)
-    state_back = jnp.einsum("jn,hpn->jhp", b_in, carried_bf, preferred_element_type=f32)
     end_decay = jnp.exp(cumlog[:, -1:] - cumlog)
     end_weight = (step_size * end_decay).T
-    x_grad = (
-        (
-            step_rows[:, :, None] * intra_back
-            + end_weight[:, :, None] * state_back
-            + d_skip[None, :, None] * dy_wide
-        )
-        .astype(bf16)
-        .reshape(tokens_here, inner_here)
-    )
-    x_end = (x_wide * end_weight[:, :, None]).astype(bf16)
-    db_entry = jnp.einsum("jhp,hpn->nj", x_end, carried_bf, preferred_element_type=f32)
-    bc_part = jnp.concatenate([db_intra + db_entry, dc_intra + dc_entry], axis=0).astype(bf16)
-    in_part = lax.dot_general(w_in, x_grad, contract_last, preferred_element_type=f32).astype(bf16)
-    terms = jnp.concatenate(
-        [in_part.reshape(4, 4, -1, tokens_here), bc_part.reshape(4, 4, -1, tokens_here)], axis=2
-    )
-    half = lax.all_to_all(terms, "y", 0, 0).astype(f32).sum(axis=0).astype(bf16)
-    both = lax.all_to_all(half, "zh", 0, 0).astype(f32).sum(axis=0).astype(bf16)
-    in_rows = in_part.shape[0] // 16
+    flat = (tokens_here, inner_here)
+    base = (step_rows[:, :, None] * intra_back + d_skip[None, :, None] * dy_wide).reshape(flat)
+    weight_wide = jnp.repeat(end_weight, head_dim, axis=1)
+    x_end = (x_in.astype(f32) * weight_wide).astype(bf16)
+    bc_base = jnp.concatenate([db_intra, dc_intra + dc_entry], axis=0)
+    *held, carried_rows = lax.optimization_barrier((*held, carried_rows))
+    sent_y, back_flat = x_grads(carried_rows, b_in, base, weight_wide, x_end, bc_base)
+    state_back = back_flat.reshape(tokens_here, group_heads, head_dim)
+    terms = in_products(y, lax.all_to_all(sent_y, "y", 0, 0), w_in, held)
 
     end_terms = end_weight.T * jnp.sum(x_wide * state_back, axis=2).T
     cum_grad = pair_weight.sum(axis=2) - pair_weight.sum(axis=1) + state_terms - end_terms
@@ -122,11 +284,14 @@
     )
     dt_grad = dt_sum * jax.nn.sigmoid(dt_raw + dt_bias[:, None])
     param_terms = jnp.stack([jnp.sum(step_grad * log_step, axis=1), skip_terms, jnp.sum(dt_grad, axis=1)])
-    flat = jnp.pad(param_terms.reshape(1, -1), ((0, 0), (0, 128 - param_terms.size)))
-    spread = lax.all_to_all(jnp.broadcast_to(flat[None], (blocks, 1, 128)), SEQ, 0, 0)
+    row = jnp.pad(param_terms.reshape(1, -1), ((0, 0), (0, 128 - param_terms.size)))
+    row, terms = lax.optimization_barrier((row, terms))
+    for axis, flip in (("core", 1), ("zl", 1), ("zl", 2), ("x", 1), ("x", 2)):
+        row = row + lax.ppermute(row, axis, [(i, i ^ flip) for i in range(lax.axis_size(axis))])
+    in_grad, bc_grad = final_sums(lax.all_to_all(terms, "zh", 0, 0), w_in.shape[0] // 16)
     norm_scale = (blocks * tokens_here * head_dim) ** (-0.5)
-    param_grad = spread.sum(axis=0)[0, : param_terms.size].reshape(param_terms.shape) * norm_scale
-    return (both[:in_rows], both[in_rows:], dt_grad, param_grad)
+    param_grad = row[0, : param_terms.size].reshape(param_terms.shape) * norm_scale
+    return (in_grad, bc_grad, dt_grad, param_grad)
 
 
 def solution(mesh):

time: 197 us -> 173 us (0.88)
  the two profiles are of different devices: /device:TPU:1 before, /device:TPU:166 now
where the time goes in v2:
time: 173 us; the launch traced here: 171 us
  starting transfers between devices  59.3 us (34%)
  waiting for transfers between devices  46.6 us (27%)
  blocking collectives  28.2 us (16%)
  Pallas kernels  12.9 us (7%)
  matrix products  10.4 us (6%)
  local copies, waits for them, and re-layouts  7.53 us (4%)
  other arithmetic  5.37 us (3%)
    ppermute x5, waiting for transfers between devices, shards(): lax.ppermute(row, axis, [(i, i ^ flip) for i in range(lax.axis_size(axis))])  28.5 us
    all_gather x1, blocking collectives, shards(): near = lax.all_gather(out_grad, 'zh', axis=1, tiled=True)  28.2 us
    ppermute x5, starting transfers between devices, shards(): lax.ppermute(row, axis, [(i, i ^ flip) for i in range(lax.axis_size(axis))])  13.8 us
    ppermute x3, starting transfers between devices, shards(): held.append(lax.ppermute(piece, 'y', [(i, (i + s) % 4) for i in range(4)]))  8.97 us
    all_to_all x1, starting transfers between devices, shards(): lax.all_to_all(terms, 'zh', 0, 0)  8.41 us
    all_to_all x1, starting transfers between devices, shards(): got = lax.all_to_all(sent, SEQ, 0, 0)  7.73 us
    all_to_all x1, starting transfers between devices, shards(): carried_rows = lax.all_to_all(suffix_scan(got), SEQ, 0, 0)  7.69 us
    all_to_all x1, waiting for transfers between devices, shards(): head_parts = lax.all_to_all(partial_products(near, w_out_y), 'y', 0, 0)  6.53 us
  transfers between devices with their start and end apart: 14, of which 9 were waited for; matrix products, arithmetic and copies ran while one was open for 10% of the time, Pallas kernels for 0%

profile of v2, /device:TPU:166, one launch (start us, length us, event | category | flops | bytes accessed | tf_op | source)
XLA Modules:
  0.0 171.4 jit_solution(3603148846252406450)
XLA Ops:
  0.6 3.8 %shard_map.138 = bf16[4,256,1024]{2,1,0:T(8,128)(2,1)} custom-call(bf16[256,4096]{1,0:T(8,128)(2,1)} %w_ref.1), custom_call_target="tpu_custom_call" | custom-call | bytes 4194304 | tf_op jit(solution)/shard_map/pallas_call | solution.py:58
  4.4 4.6 %all-to-all-start = ((bf16[4,256,1024]{2,1,0:T(8,128)(2,1)}), bf16[4,256,1024]{2,1,0:T(8,128)(2,1)S(1)}, u32[]{:S(2)}, u32[]{:S(2)}) async-start(bf16[4,256,1024]{2,1,0:T(8,128)(2,1)} %shard_map.138), calls=%async_computation | async-start | bytes 4194304 | tf_op jit(solution)/shard_map/all_to_all | solution.py:215
  10.8 28.2 %all_gather.3.near_ref = bf16[256,1024]{1,0:T(8,128)(2,1)S(1)} all-gather(bf16[256,256]{1,0:T(8,128)(2,1)S(1)} %copy-done.8), channel_id=1, replica_groups=mesh['x'=4,'zl'=4,'core'=2,'y'=4,'zh'=4] {'zh'}, dimensions={1}, use_global_device_ids=true | all-gather | bytes 655360 | tf_op jit(solution)/shard_map/all_gather | solution.py:216
  39.1 2.4 %shard_map.139 = bf16[4,256,256]{2,1,0:T(8,128)(2,1)} custom-call(bf16[256,1024]{1,0:T(8,128)(2,1)S(1)} %all_gather.3.near_ref, bf16[4,256,1024]{2,1,0:T(8,128)(2,1)S(1)} %all-to-all-done.w_ref), custom_call_target="tpu_custom_call" | custom-call | flops 536870912 | bytes 4194304 | tf_op jit(solution)/shard_map/pallas_call | solution.py:75
  41.5 4.1 %all-to-all-start.1 = ((bf16[4,256,256]{2,1,0:T(8,128)(2,1)}), bf16[4,256,256]{2,1,0:T(8,128)(2,1)S(1)}, u32[]{:S(2)}, u32[]{:S(2)}) async-start(bf16[4,256,256]{2,1,0:T(8,128)(2,1)} %shard_map.139), calls=%async_computation.1 | async-start | bytes 1048576 | tf_op jit(solution)/shard_map/all_to_all | solution.py:217
  47.1 6.5 %all-to-all-done.1.parts_ref = bf16[4,256,256]{2,1,0:T(8,128)(2,1)S(1)} async-done(((bf16[4,256,256]{2,1,0:T(8,128)(2,1)}), bf16[4,256,256]{2,1,0:T(8,128)(2,1)S(1)}, u32[]{:S(2)}, u32[]{:S(2)}) %all-to-all-start.1) | async-done | bytes 524320 | tf_op jit(solution)/shard_map/all_to_all | solution.py:217
  54.8 2.4 %fusion.3 = (f32[4,256]{1,0:T(4,128)}, f32[4,256]{1,0:T(4,128)}, bf16[256,256]{1,0:T(8,128)(2,1)S(1)}) fusion(f32[4,256]{1,0:T(4,128)S(1)} %fusion.11, f32[256,256]{1,0:T(8,128)} %fusion.34, pred[256,256]{1,0:T(8,128)(4,1)S(1)} %iota_compare_fusion, bf16[256,4,64]{0,2,1:T(8,128)(2,1)S(1)} %bitcast.82, f32[256,4,64]{0,2,1:T(8,128)S(1)} %bitcast.77, ...), kind=kOutput, calls=%fused_computation.13 | convolution fusion | flops 36501504 | bytes 868352 | tf_op jit(solution)/shard_map/ihp,jhp->hij/dot_general | solution.py:252
  58.0 7.7 %all-to-all-start.2 = ((bf16[32,16,128]{2,1,0:T(8,128)(2,1)}), bf16[32,16,128]{2,1,0:T(8,128)(2,1)S(1)}, u32[]{:S(2)}, u32[]{:S(2)}) async-start(bf16[32,16,128]{2,1,0:T(8,128)(2,1)} %get-tuple-element.22), calls=%async_computation.2 | async-start | bytes 262144 | tf_op jit(solution)/shard_map/all_to_all | solution.py:248
  65.8 1.2 constant_dynamic-slice_fusion
  67.8 2.5 %collective-permute-start = (bf16[1024,256]{1,0:T(8,128)(2,1)}, bf16[1024,256]{1,0:T(8,128)(2,1)}, u32[]{:S(2)}, u32[]{:S(2)}) collective-permute-start(bf16[1024,256]{1,0:T(8,128)(2,1)} %get-tuple-element.43), channel_id=1, source_target_pairs={{0,4},{4,8},{8,12},{12,0},{1,5},{5,9},{9,13},{13,1},{2,6},{6,10},{... | collective-permute-start | bytes 1572872 | tf_op jit(solution)/shard_map/ppermute | solution.py:242
  70.2 4.0 %collective-permute-start.1 = (bf16[1024,256]{1,0:T(8,128)(2,1)}, bf16[1024,256]{1,0:T(8,128)(2,1)}, u32[]{:S(2)}, u32[]{:S(2)}) collective-permute-start(bf16[1024,256]{1,0:T(8,128)(2,1)} %get-tuple-element.42), channel_id=1, source_target_pairs={{0,8},{4,12},{8,0},{12,4},{1,9},{5,13},{9,1},{13,5},{2,10},{6,14},... | collective-permute-start | bytes 1572872 | tf_op jit(solution)/shard_map/ppermute | solution.py:242
  74.2 2.5 %collective-permute-start.2 = (bf16[1024,256]{1,0:T(8,128)(2,1)}, bf16[1024,256]{1,0:T(8,128)(2,1)}, u32[]{:S(2)}, u32[]{:S(2)}) collective-permute-start(bf16[1024,256]{1,0:T(8,128)(2,1)} %get-tuple-element.41), channel_id=1, source_target_pairs={{0,12},{4,0},{8,4},{12,8},{1,13},{5,1},{9,5},{13,9},{2,14},{6,2},{... | collective-permute-start | bytes 1572872 | tf_op jit(solution)/shard_map/ppermute | solution.py:242
  77.4 2.2 %fusion.10 = (f32[256,4,64]{0,2,1:T(8,128)}, f32[256,4,64]{0,2,1:T(8,128)}) fusion(f32[4]{0:T(128)S(1)} %copy-done.18, f32[256,4]{0,1:T(4,128)S(1)} %copy-done.15, bf16[256,256]{0,1:T(8,128)(2,1)S(1)} %copy.38, bf16[256,4,64]{0,2,1:T(8,128)(2,1)S(1)} %bitcast.83, f32[4,256]{1,0:T(4,128)S(1)} %fusion.11, f32[256,256]{1,0:T(8,128)} %fusion.34, ...), kind=kOutput, calls=%fused_computation.21 | convolution fusion | flops 35127296 | bytes 1122320 | tf_op jit(solution)/shard_map/hij,ihp->jhp/dot_general | solution.py:254
  80.3 7.7 %all-to-all-start.3 = ((f32[32,8,128]{2,1,0:T(8,128)}), f32[32,8,128]{2,1,0:T(8,128)S(1)}, u32[]{:S(2)}, u32[]{:S(2)}) async-start(f32[32,8,128]{2,1,0:T(8,128)} %shard_map.141), calls=%async_computation.3 | async-start | bytes 262144 | tf_op jit(solution)/shard_map/all_to_all | solution.py:249
  88.0 1.1 convolution_bitcast_fusion.1
  93.6 2.8 %collective-permute-done.refs_0_ = bf16[1024,256]{1,0:T(8,128)(2,1)} collective-permute-done((bf16[1024,256]{1,0:T(8,128)(2,1)}, bf16[1024,256]{1,0:T(8,128)(2,1)}, u32[]{:S(2)}, u32[]{:S(2)}) %collective-permute-start) | collective-permute-done | bytes 524320 | tf_op jit(solution)/shard_map/ppermute | solution.py:242
  96.4 2.5 %collective-permute-done.2.refs_2_ = bf16[1024,256]{1,0:T(8,128)(2,1)} collective-permute-done((bf16[1024,256]{1,0:T(8,128)(2,1)}, bf16[1024,256]{1,0:T(8,128)(2,1)}, u32[]{:S(2)}, u32[]{:S(2)}) %collective-permute-start.2) | collective-permute-done | bytes 524320 | tf_op jit(solution)/shard_map/ppermute | solution.py:242
  100.0 4.0 %all-to-all-start.4 = ((bf16[4,320,256]{2,1,0:T(8,128)(2,1)}), bf16[4,320,256]{2,1,0:T(8,128)(2,1)S(1)}, u32[]{:S(2)}, u32[]{:S(2)}) async-start(bf16[4,320,256]{2,1,0:T(8,128)(2,1)} %copy-done.2), calls=%async_computation.4 | async-start | bytes 1310720 | tf_op jit(solution)/shard_map/all_to_all | solution.py:275
  104.2 1.1 multiply_reduce_fusion.2
  107.0 1.7 %fusion.33 = (f32[4]{0:T(128)S(1)}, f32[4,256]{1,0:T(4,128)}, f32[4]{0:T(128)S(1)}) fusion(f32[4,256]{1,0:T(4,128)S(1)} %copy-done.9, f32[4]{0:T(128)S(1)} %copy-done.10, f32[256,4]{0,1:T(4,128)S(1)} %get-tuple-element.38, f32[4]{0:T(128)} %copy-done.19, f32[4,256]{1,0:T(4,128)} %copy-done.13, f32[4]{0:T(128)S(1)} %add_reduce_fusion, ...), kind=kOutput, calls=%fused_computation.72 | convolution fusion | flops 3230712 | bytes 36960 | tf_op jit(solution)/shard_map/dot_general | solution.py:280
  108.9 6.2 %all-to-all-done.4.got_ref = bf16[4,320,256]{2,1,0:T(8,128)(2,1)S(1)} async-done(((bf16[4,320,256]{2,1,0:T(8,128)(2,1)}), bf16[4,320,256]{2,1,0:T(8,128)(2,1)S(1)}, u32[]{:S(2)}, u32[]{:S(2)}) %all-to-all-start.4) | async-done | bytes 655392 | tf_op jit(solution)/shard_map/all_to_all | solution.py:275
  115.1 4.1 %shard_map.143 = bf16[4,272,256]{2,1,0:T(8,128)(2,1)} custom-call(s32[1]{0:T(128)} %bitcast.27.y_ref, bf16[4,320,256]{2,1,0:T(8,128)(2,1)S(1)} %all-to-all-done.4.got_ref, bf16[4096,256]{1,0:T(8,128)(2,1)S(1)} %copy-done, bf16[1024,256]{1,0:T(8,128)(2,1)} %collective-permute-done.refs_0_, bf16[1024,256]{1,0:T(8,128)(2,1)} %collective-permute-done.1.refs_1_, ...), custom_call_target="tpu_custom_call" | custom-call | flops 536870912 | bytes 4194304 | tf_op jit(solution)/shard_map/pallas_call | solution.py:167
  119.2 8.4 %all-to-all-start.5 = ((bf16[4,272,256]{2,1,0:T(8,128)(2,1)}), bf16[4,272,256]{2,1,0:T(8,128)(2,1)S(1)}, u32[]{:S(2)}, u32[]{:S(2)}) async-start(bf16[4,272,256]{2,1,0:T(8,128)(2,1)} %shard_map.143), calls=%async_computation.5 | async-start | bytes 1114112 | tf_op jit(solution)/shard_map/all_to_all | solution.py:291
  127.6 1.9 %collective-permute-start.3 = (f32[1,128]{1,0:T(1,128)S(1)}, f32[1,128]{1,0:T(1,128)S(1)}, u32[]{:S(2)}, u32[]{:S(2)}) collective-permute-start(f32[1,128]{1,0:T(1,128)S(1)} %pad.9), channel_id=1, source_target_pairs={{0,16},{16,0},{1,17},{17,1},{2,18},{18,2},{3,19},{19,3},{4,20},{20... | collective-permute-start | bytes 1544 | tf_op jit(solution)/shard_map/ppermute | solution.py:290
  130.6 2.4 %collective-permute-start.4 = (f32[1,128]{1,0:T(1,128)S(1)}, f32[1,128]{1,0:T(1,128)S(1)}, u32[]{:S(2)}, u32[]{:S(2)}) collective-permute-start(f32[1,128]{1,0:T(1,128)S(1)} %add.108), channel_id=1, source_target_pairs={{0,32},{32,0},{64,96},{96,64},{1,33},{33,1},{65,97},{97,65},{2,34}... | collective-permute-start | bytes 1544 | tf_op jit(solution)/shard_map/ppermute | solution.py:290
  133.1 18.3 %collective-permute-done.4 = f32[1,128]{1,0:T(1,128)S(1)} collective-permute-done((f32[1,128]{1,0:T(1,128)S(1)}, f32[1,128]{1,0:T(1,128)S(1)}, u32[]{:S(2)}, u32[]{:S(2)}) %collective-permute-start.4) | collective-permute-done | bytes 544 | tf_op jit(solution)/shard_map/ppermute | solution.py:290
  151.3 3.5 %collective-permute-start.5 = (f32[1,128]{1,0:T(1,128)S(1)}, f32[1,128]{1,0:T(1,128)S(1)}, u32[]{:S(2)}, u32[]{:S(2)}) collective-permute-start(f32[1,128]{1,0:T(1,128)S(1)} %add.109), channel_id=1, source_target_pairs={{0,64},{32,96},{64,0},{96,32},{1,65},{33,97},{65,1},{97,33},{2,66}... | collective-permute-start | bytes 1544 | tf_op jit(solution)/shard_map/ppermute | solution.py:290
  154.8 2.8 %collective-permute-done.5 = f32[1,128]{1,0:T(1,128)S(1)} collective-permute-done((f32[1,128]{1,0:T(1,128)S(1)}, f32[1,128]{1,0:T(1,128)S(1)}, u32[]{:S(2)}, u32[]{:S(2)}) %collective-permute-start.5) | collective-permute-done | bytes 544 | tf_op jit(solution)/shard_map/ppermute | solution.py:290
  157.6 2.7 %collective-permute-start.6 = (f32[1,128]{1,0:T(1,128)S(1)}, f32[1,128]{1,0:T(1,128)S(1)}, u32[]{:S(2)}, u32[]{:S(2)}) collective-permute-start(f32[1,128]{1,0:T(1,128)S(1)} %add.110), channel_id=1, source_target_pairs={{0,128},{128,0},{256,384},{384,256},{1,129},{129,1},{257,385},{385... | collective-permute-start | bytes 1544 | tf_op jit(solution)/shard_map/ppermute | solution.py:290
  160.4 2.7 %collective-permute-done.6 = f32[1,128]{1,0:T(1,128)S(1)} collective-permute-done((f32[1,128]{1,0:T(1,128)S(1)}, f32[1,128]{1,0:T(1,128)S(1)}, u32[]{:S(2)}, u32[]{:S(2)}) %collective-permute-start.6) | collective-permute-done | bytes 544 | tf_op jit(solution)/shard_map/ppermute | solution.py:290
  163.1 3.3 %collective-permute-start.7 = (f32[1,128]{1,0:T(1,128)S(1)}, f32[1,128]{1,0:T(1,128)S(1)}, u32[]{:S(2)}, u32[]{:S(2)}) collective-permute-start(f32[1,128]{1,0:T(1,128)S(1)} %add.111), channel_id=1, source_target_pairs={{0,256},{128,384},{256,0},{384,128},{1,257},{129,385},{257,1},{385... | collective-permute-start | bytes 1544 | tf_op jit(solution)/shard_map/ppermute | solution.py:290
  166.4 3.6 %collective-permute-done.7 = f32[1,128]{1,0:T(1,128)S(1)} collective-permute-done((f32[1,128]{1,0:T(1,128)S(1)}, f32[1,128]{1,0:T(1,128)S(1)}, u32[]{:S(2)}, u32[]{:S(2)}) %collective-permute-start.7) | collective-permute-done | bytes 544 | tf_op jit(solution)/shard_map/ppermute | solution.py:290
  (94 shorter events, 17.3 us)
Async XLA Ops:
  4.4 4.6 %copy-start.17 = (f32[4]{0:T(128)S(1)}, f32[4]{0:T(128)}, u32[]{:S(2)}) copy-start(f32[4]{0:T(128)} %param.17) | copy-start | bytes 52
  4.4 4.6 %copy-start.9 = (f32[4,256]{1,0:T(4,128)S(1)}, f32[4,256]{1,0:T(4,128)}, u32[]{:S(2)}) copy-start(f32[4,256]{1,0:T(4,128)} %param.15) | copy-start | bytes 12292
  4.4 4.6 %copy-start.10 = (f32[4]{0:T(128)S(1)}, f32[4]{0:T(128)}, u32[]{:S(2)}) copy-start(f32[4]{0:T(128)} %param.16) | copy-start | bytes 52
  4.4 6.3 %copy-start.8 = (bf16[256,256]{1,0:T(8,128)(2,1)S(1)}, bf16[256,256]{1,0:T(8,128)(2,1)}, u32[]{:S(2)}) copy-start(bf16[256,256]{1,0:T(8,128)(2,1)} %param.11) | copy-start | bytes 393220
  4.4 34.7 %all-to-all-start = ((bf16[4,256,1024]{2,1,0:T(8,128)(2,1)}), bf16[4,256,1024]{2,1,0:T(8,128)(2,1)S(1)}, u32[]{:S(2)}, u32[]{:S(2)}) async-start(bf16[4,256,1024]{2,1,0:T(8,128)(2,1)} %shard_map.138), calls=%async_computation | async-start | bytes 4194304 | tf_op jit(solution)/shard_map/all_to_all | solution.py:215
  10.7 28.4 %copy-start.11 = (f32[4]{0:T(128)}, f32[4]{0:T(128)S(1)}, u32[]{:S(2)}) copy-start(f32[4]{0:T(128)S(1)} %get-tuple-element.50) | copy-start | bytes 52
  39.1 6.7 %copy-start.7 = (bf16[256,256]{1,0:T(8,128)(2,1)S(1)}, bf16[256,256]{1,0:T(8,128)(2,1)}, u32[]{:S(2)}) copy-start(bf16[256,256]{1,0:T(8,128)(2,1)} %param.12) | copy-start | bytes 393220
  41.5 4.7 %copy-start.1 = (bf16[256,128]{1,0:T(8,128)(2,1)S(1)}, bf16[256,128]{1,0:T(8,128)(2,1)}, u32[]{:S(2)}) copy-start(bf16[256,128]{1,0:T(8,128)(2,1)} %c_ref.1) | copy-start | bytes 196612
  41.5 4.7 %copy-start.3 = (bf16[256,128]{1,0:T(8,128)(2,1)S(1)}, bf16[256,128]{1,0:T(8,128)(2,1)}, u32[]{:S(2)}) copy-start(bf16[256,128]{1,0:T(8,128)(2,1)} %b_ref.1) | copy-start | bytes 196612
  41.5 12.2 %all-to-all-start.1 = ((bf16[4,256,256]{2,1,0:T(8,128)(2,1)}), bf16[4,256,256]{2,1,0:T(8,128)(2,1)S(1)}, u32[]{:S(2)}, u32[]{:S(2)}) async-start(bf16[4,256,256]{2,1,0:T(8,128)(2,1)} %shard_map.139), calls=%async_computation.1 | async-start | bytes 1048576 | tf_op jit(solution)/shard_map/all_to_all | solution.py:217
  45.6 11.5 %copy-start.14 = (f32[256,4]{0,1:T(4,128)}, f32[256,4]{0,1:T(4,128)S(1)}, u32[]{:S(2)}) copy-start(f32[256,4]{0,1:T(4,128)S(1)} %fusion.46) | copy-start | bytes 12292
  45.9 11.2 %copy-start.4 = (f32[256,256]{0,1:T(8,128)}, f32[256,256]{0,1:T(8,128)S(1)}, u32[]{:S(2)}) copy-start(f32[256,256]{0,1:T(8,128)S(1)} %copy.39) | copy-start | bytes 786436
  54.7 11.1 %copy-start = (bf16[4096,256]{1,0:T(8,128)(2,1)S(1)}, bf16[4096,256]{1,0:T(8,128)(2,1)}, u32[]{:S(2)}) copy-start(bf16[4096,256]{1,0:T(8,128)(2,1)} %own_ref.1) | copy-start | bytes 6291460
  58.0 21.6 %all-to-all-start.2 = ((bf16[32,16,128]{2,1,0:T(8,128)(2,1)}), bf16[32,16,128]{2,1,0:T(8,128)(2,1)S(1)}, u32[]{:S(2)}, u32[]{:S(2)}) async-start(bf16[32,16,128]{2,1,0:T(8,128)(2,1)} %get-tuple-element.22), calls=%async_computation.2 | async-start | bytes 262144 | tf_op jit(solution)/shard_map/all_to_all | solution.py:248
  65.8 11.6 %copy-start.15 = (f32[256,4]{0,1:T(4,128)S(1)}, f32[256,4]{0,1:T(4,128)}, u32[]{:S(2)}) copy-start(f32[256,4]{0,1:T(4,128)} %copy-done.14) | copy-start | bytes 12292
  65.8 11.6 %copy-start.18 = (f32[4]{0:T(128)S(1)}, f32[4]{0:T(128)}, u32[]{:S(2)}) copy-start(f32[4]{0:T(128)} %param.18) | copy-start | bytes 52
  67.0 21.0 %copy-start.5 = (bf16[1,256,128]{2,1,0:T(8,128)(2,1)S(1)}, bf16[1,256,128]{2,1,0:T(8,128)(2,1)}, u32[]{:S(2)}) copy-start(bf16[1,256,128]{2,1,0:T(8,128)(2,1)} %param.19) | copy-start | bytes 196612
  67.8 28.6 %collective-permute-start = (bf16[1024,256]{1,0:T(8,128)(2,1)}, bf16[1024,256]{1,0:T(8,128)(2,1)}, u32[]{:S(2)}, u32[]{:S(2)}) collective-permute-start(bf16[1024,256]{1,0:T(8,128)(2,1)} %get-tuple-element.43), channel_id=1, source_target_pairs={{0,4},{4,8},{8,12},{12,0},{1,5},{5,9},{9,13},{13,1},{2,6},{6,10},{... | collective-permute-start | bytes 1572872 | tf_op jit(solution)/shard_map/ppermute | solution.py:242
  70.2 26.2 %collective-permute-start.1 = (bf16[1024,256]{1,0:T(8,128)(2,1)}, bf16[1024,256]{1,0:T(8,128)(2,1)}, u32[]{:S(2)}, u32[]{:S(2)}) collective-permute-start(bf16[1024,256]{1,0:T(8,128)(2,1)} %get-tuple-element.42), channel_id=1, source_target_pairs={{0,8},{4,12},{8,0},{12,4},{1,9},{5,13},{9,1},{13,5},{2,10},{6,14},... | collective-permute-start | bytes 1572872 | tf_op jit(solution)/shard_map/ppermute | solution.py:242
  74.2 24.7 %collective-permute-start.2 = (bf16[1024,256]{1,0:T(8,128)(2,1)}, bf16[1024,256]{1,0:T(8,128)(2,1)}, u32[]{:S(2)}, u32[]{:S(2)}) collective-permute-start(bf16[1024,256]{1,0:T(8,128)(2,1)} %get-tuple-element.41), channel_id=1, source_target_pairs={{0,12},{4,0},{8,4},{12,8},{1,13},{5,1},{9,5},{13,9},{2,14},{6,2},{... | collective-permute-start | bytes 1572872 | tf_op jit(solution)/shard_map/ppermute | solution.py:242
  80.3 18.6 %all-to-all-start.3 = ((f32[32,8,128]{2,1,0:T(8,128)}), f32[32,8,128]{2,1,0:T(8,128)S(1)}, u32[]{:S(2)}, u32[]{:S(2)}) async-start(f32[32,8,128]{2,1,0:T(8,128)} %shard_map.141), calls=%async_computation.3 | async-start | bytes 262144 | tf_op jit(solution)/shard_map/all_to_all | solution.py:249
  93.6 11.7 %copy-start.6 = (bf16[1,256,128]{2,1,0:T(8,128)(2,1)S(1)}, bf16[1,256,128]{2,1,0:T(8,128)(2,1)}, u32[]{:S(2)}) copy-start(bf16[1,256,128]{2,1,0:T(8,128)(2,1)} %param.19) | copy-start | bytes 196612
  99.2 0.8 copy-start.2
  100.0 7.0 %copy-start.12 = (f32[256,4]{0,1:T(4,128)S(1)}, f32[256,4]{0,1:T(4,128)}, u32[]{:S(2)}) copy-start(f32[256,4]{0,1:T(4,128)} %fusion) | copy-start | bytes 12292
  100.0 8.7 %copy-start.16 = (f32[4]{0:T(128)S(1)}, f32[4]{0:T(128)}, u32[]{:S(2)}) copy-start(f32[4]{0:T(128)} %reduce_sum.135) | copy-start | bytes 52
  100.0 15.1 %all-to-all-start.4 = ((bf16[4,320,256]{2,1,0:T(8,128)(2,1)}), bf16[4,320,256]{2,1,0:T(8,128)(2,1)S(1)}, u32[]{:S(2)}, u32[]{:S(2)}) async-start(bf16[4,320,256]{2,1,0:T(8,128)(2,1)} %copy-done.2), calls=%async_computation.4 | async-start | bytes 1310720 | tf_op jit(solution)/shard_map/all_to_all | solution.py:275
  119.2 51.5 %all-to-all-start.5 = ((bf16[4,272,256]{2,1,0:T(8,128)(2,1)}), bf16[4,272,256]{2,1,0:T(8,128)(2,1)S(1)}, u32[]{:S(2)}, u32[]{:S(2)}) async-start(bf16[4,272,256]{2,1,0:T(8,128)(2,1)} %shard_map.143), calls=%async_computation.5 | async-start | bytes 1114112 | tf_op jit(solution)/shard_map/all_to_all | solution.py:291
  127.6 3.0 %collective-permute-start.3 = (f32[1,128]{1,0:T(1,128)S(1)}, f32[1,128]{1,0:T(1,128)S(1)}, u32[]{:S(2)}, u32[]{:S(2)}) collective-permute-start(f32[1,128]{1,0:T(1,128)S(1)} %pad.9), channel_id=1, source_target_pairs={{0,16},{16,0},{1,17},{17,1},{2,18},{18,2},{3,19},{19,3},{4,20},{20... | collective-permute-start | bytes 1544 | tf_op jit(solution)/shard_map/ppermute | solution.py:290
  130.6 20.7 %collective-permute-start.4 = (f32[1,128]{1,0:T(1,128)S(1)}, f32[1,128]{1,0:T(1,128)S(1)}, u32[]{:S(2)}, u32[]{:S(2)}) collective-permute-start(f32[1,128]{1,0:T(1,128)S(1)} %add.108), channel_id=1, source_target_pairs={{0,32},{32,0},{64,96},{96,64},{1,33},{33,1},{65,97},{97,65},{2,34}... | collective-permute-start | bytes 1544 | tf_op jit(solution)/shard_map/ppermute | solution.py:290
  151.3 6.3 %collective-permute-start.5 = (f32[1,128]{1,0:T(1,128)S(1)}, f32[1,128]{1,0:T(1,128)S(1)}, u32[]{:S(2)}, u32[]{:S(2)}) collective-permute-start(f32[1,128]{1,0:T(1,128)S(1)} %add.109), channel_id=1, source_target_pairs={{0,64},{32,96},{64,0},{96,32},{1,65},{33,97},{65,1},{97,33},{2,66}... | collective-permute-start | bytes 1544 | tf_op jit(solution)/shard_map/ppermute | solution.py:290
  157.6 5.4 %collective-permute-start.6 = (f32[1,128]{1,0:T(1,128)S(1)}, f32[1,128]{1,0:T(1,128)S(1)}, u32[]{:S(2)}, u32[]{:S(2)}) collective-permute-start(f32[1,128]{1,0:T(1,128)S(1)} %add.110), channel_id=1, source_target_pairs={{0,128},{128,0},{256,384},{384,256},{1,129},{129,1},{257,385},{385... | collective-permute-start | bytes 1544 | tf_op jit(solution)/shard_map/ppermute | solution.py:290
  163.1 6.9 %collective-permute-start.7 = (f32[1,128]{1,0:T(1,128)S(1)}, f32[1,128]{1,0:T(1,128)S(1)}, u32[]{:S(2)}, u32[]{:S(2)}) collective-permute-start(f32[1,128]{1,0:T(1,128)S(1)} %add.111), channel_id=1, source_target_pairs={{0,256},{128,384},{256,0},{384,128},{1,257},{129,385},{257,1},{385... | collective-permute-start | bytes 1544 | tf_op jit(solution)/shard_map/ppermute | solution.py:290
  (2 other events, 1.2 us)

commit v3 on v2

--- a/solution.py
+++ b/solution.py
@@ -48,19 +48,25 @@
     return lax.dot_general(a, b, (((1,), (1,)), ((), ())), preferred_element_type=f32)
 
 
-def regroup_kernel(w_ref, out_ref):
-    out_ref[0] = w_ref[...]
+def regroup_kernel(w_ref, out_ref, sems):
+    part = out_ref.shape[2]
+    copies = [
+        pltpu.make_async_copy(w_ref.at[:, pl.ds(g * part, part)], out_ref.at[g], sems.at[g]) for g in range(4)
+    ]
+    for copy in copies:
+        copy.start()
+    for copy in copies:
+        copy.wait()
 
 
 def regrouped(w):
     rows, width = w.shape
-    part = width // 4
     return pl.pallas_call(
         regroup_kernel,
-        grid=(4,),
-        in_specs=[pl.BlockSpec((rows, part), lambda g: (0, g))],
-        out_specs=pl.BlockSpec((1, rows, part), lambda g: (g, 0, 0)),
-        out_shape=jax.ShapeDtypeStruct((4, rows, part), w.dtype),
+        in_specs=[pl.BlockSpec(memory_space=pl.ANY)],
+        out_specs=pl.BlockSpec(memory_space=pl.ANY),
+        out_shape=jax.ShapeDtypeStruct((4, rows, width // 4), w.dtype),
+        scratch_shapes=[pltpu.SemaphoreType.DMA((4,))],
         cost_estimate=cost(0, 4 * rows * width),
     )(w)
 
@@ -112,7 +118,157 @@
     )(parts, start, c_in, ends)
 
 
-def x_grad_kernel(carried_ref, b_ref, base_ref, weight_ref, x_end_ref, bc_ref, sent_ref, back_ref):
+def widened(columns, width):
+    tokens, heads = columns.shape
+    return jnp.concatenate(
+        [jnp.broadcast_to(columns[:, h:h + 1], (tokens, width // heads)) for h in range(heads)], axis=1
+    )
+
+
+def head_sums(values, heads):
+    width = values.shape[1] // heads
+    return [jnp.sum(values[:, h * width:(h + 1) * width], axis=1, keepdims=True) for h in range(heads)]
+
+
+def as_rows(columns):
+    tokens = columns[0].shape[0]
+    lanes = lax.broadcasted_iota(jnp.int32, (tokens, 128), 1)
+    spread = jnp.zeros((tokens, 128), f32)
+    for k, column in enumerate(columns):
+        spread = jnp.where(lanes == k, column, spread)
+    return spread.T[:8]
+
+
+def pre_kernel(rows_ref, x_ref, b_ref, c_ref, states_ref, start_ref, step_ref, weight_ref, scaled_ref, end_ref, scores_ref, y_ref):
+    tokens, width = x_ref.shape
+    rows = rows_ref[...]
+    last = rows[:4, tokens - 1:]
+    start = jnp.exp(rows[:4])
+    weight = rows[4:] * jnp.exp(last - rows[:4])
+    columns = jnp.concatenate([start, weight], axis=0).T
+    start_ref[...] = widened(columns[:, :4], width)
+    weight_wide = widened(columns[:, 4:], width)
+    weight_ref[...] = weight_wide
+    step_wide = widened(rows.T[:, 4:], width)
+    step_ref[...] = step_wide
+    x = x_ref[...].astype(f32)
+    scaled_ref[...] = (x * step_wide).astype(bf16)
+    end_ref[...] = (x * weight_wide).astype(bf16)
+    scores_ref[...] = dot_last(c_ref[...], b_ref[...])
+    y_ref[...] = dot_last(c_ref[...], states_ref[...])
+
+
+def prepared(rows, x_in, b_in, c_in, states):
+    tokens, width = x_in.shape
+    wide = jax.ShapeDtypeStruct((tokens, width), f32)
+    half = jax.ShapeDtypeStruct((tokens, width), bf16)
+    square = jax.ShapeDtypeStruct((tokens, tokens), f32)
+    return pl.pallas_call(
+        pre_kernel,
+        out_shape=(wide, wide, wide, half, half, square, wide),
+        compiler_params=small(),
+        cost_estimate=cost(4 * tokens * width * 128, 2 << 20),
+    )(rows, x_in, b_in, c_in, states)
+
+
+def intra_kernel(
+    dy_ref, decayed_ref, x_ref, scaled_ref, b_ref, c_ref, states_ref, rows_ref, skip_ref, start_ref, step_ref, scores_ref, y_ref,
+    base_ref, db_ref, dc_ref, part_ref, across_ref,
+):
+    tokens, width = dy_ref.shape
+    head_dim = width // 4
+    cum = rows_ref[:4]
+    columns = rows_ref[...].T
+    scores = scores_ref[...]
+    dy = dy_ref[...]
+    causal = lax.broadcasted_iota(jnp.int32, (tokens, tokens), 0) >= lax.broadcasted_iota(jnp.int32, (tokens, tokens), 1)
+    total = jnp.zeros((tokens, tokens), f32)
+    along, down, backs = [], [], []
+    for h in range(4):
+        mine = slice(h * head_dim, (h + 1) * head_dim)
+        dy_h = dy[:, mine]
+        gaps = jnp.minimum(columns[:, h:h + 1] - cum[h:h + 1], 0.0)
+        mask = jnp.where(causal, jnp.exp(gaps), 0.0)
+        weighed = (scores * mask).astype(bf16)
+        backs.append(lax.dot_general(weighed, dy_h, (((0,), (0,)), ((), ())), preferred_element_type=f32))
+        masked = dot_last(dy_h, scaled_ref[:, mine]) * mask
+        total = total + masked
+        pairs = masked * scores
+        along.append(jnp.sum(pairs, axis=1, keepdims=True))
+        down.append(jnp.sum(pairs, axis=0, keepdims=True))
+    total = total.astype(bf16)
+    db_ref[...] = lax.dot_general(total, c_ref[...], (((0,), (0,)), ((), ())), preferred_element_type=f32)
+    dc = jnp.dot(total, b_ref[...], preferred_element_type=f32)
+    dc = dc + jnp.dot(decayed_ref[...], states_ref[...], preferred_element_type=f32)
+    dc_ref[...] = dc.T.astype(bf16)
+    back = jnp.concatenate(backs, axis=1)
+    dy = dy.astype(f32)
+    x = x_ref[...].astype(f32)
+    base_ref[...] = step_ref[...] * back + skip_ref[...] * dy
+    entered = head_sums(start_ref[...] * dy * y_ref[...], 4)
+    rows = as_rows([a + e for a, e in zip(along, entered)] + head_sums(x * back, 4))
+    part_ref[...] = rows - jnp.concatenate(down + [jnp.zeros((4, tokens), f32)], axis=0)
+    across_ref[...] = jnp.sum(dy * x, axis=0, keepdims=True)
+
+
+def intra_terms(dy, decayed, x_in, scaled, b_in, c_in, states, rows, skip, start, step, scores, y_state):
+    tokens, width = dy.shape
+    state_dim = b_in.shape[1]
+    return pl.pallas_call(
+        intra_kernel,
+        out_shape=(
+            jax.ShapeDtypeStruct((tokens, width), f32),
+            jax.ShapeDtypeStruct((tokens, state_dim), f32),
+            jax.ShapeDtypeStruct((state_dim, tokens), bf16),
+            jax.ShapeDtypeStruct((8, tokens), f32),
+            jax.ShapeDtypeStruct((1, width), f32),
+        ),
+        compiler_params=small(),
+        cost_estimate=cost(12 * tokens * tokens * width, 4 << 20),
+    )(dy, decayed, x_in, scaled, b_in, c_in, states, rows, skip, start, step, scores, y_state)
+
+
+def dt_kernel(back_ref, x_ref, rows_ref, part_ref, across_ref, carried_ref, states_ref, raw_ref, scal_ref, dt_ref, param_ref):
+    tokens, width = x_ref.shape
+    head_dim = width // 4
+    cum, step = rows_ref[:4], rows_ref[4:]
+    last = cum[:, tokens - 1:]
+    rate, bias = scal_ref[:, 0:1], scal_ref[:, 1:2]
+    dots = as_rows(head_sums(x_ref[...].astype(f32) * back_ref[...], 4))[:4]
+    end_decay = jnp.exp(last - cum)
+    end_terms = step * end_decay * dots
+    carried = carried_ref[...].reshape(4, head_dim, -1)
+    held = jnp.sum(carried * states_ref[...].astype(f32).reshape(4, head_dim, -1), axis=1)
+    tail = jnp.sum(end_terms, axis=1, keepdims=True) + jnp.exp(last) * jnp.sum(held, axis=1, keepdims=True)
+    below = lax.broadcasted_iota(jnp.int32, (tokens, tokens), 0) >= lax.broadcasted_iota(jnp.int32, (tokens, tokens), 1)
+    step_grad = tail + jnp.dot(
+        part_ref[:4] - end_terms, below.astype(f32), precision=lax.Precision.HIGHEST, preferred_element_type=f32
+    )
+    dt_sum = part_ref[4:] + end_decay * dots - rate * step_grad
+    dt = dt_sum * jax.nn.sigmoid(raw_ref[...] + bias)
+    dt_ref[...] = dt
+    lanes = lax.broadcasted_iota(jnp.int32, (4, width), 1)
+    heads = lax.broadcasted_iota(jnp.int32, (4, width), 0)
+    skip = jnp.sum(jnp.where(lanes // head_dim == heads, across_ref[...], 0.0), axis=1, keepdims=True)
+    decays = jnp.sum(step_grad * (-rate * step), axis=1, keepdims=True)
+    biases = jnp.sum(dt, axis=1, keepdims=True)
+    lanes, heads = lanes[:, :128], heads[:, :128]
+    placed = jnp.where(lanes == heads, decays, 0.0)
+    placed = jnp.where(lanes == heads + 4, skip, placed)
+    placed = jnp.where(lanes == heads + 8, biases, placed)
+    param_ref[...] = jnp.sum(placed, axis=0, keepdims=True)
+
+
+def dt_terms(back, x_in, rows, part, across, carried, states, dt_raw, scalars):
+    return pl.pallas_call(
+        dt_kernel,
+        out_shape=(jax.ShapeDtypeStruct(dt_raw.shape, f32), jax.ShapeDtypeStruct((1, 128), f32)),
+        compiler_params=small(),
+        cost_estimate=cost(1 << 22, 1 << 20),
+    )(back, x_in, rows, part, across, carried, states, dt_raw, scalars)
+
+
+def x_grad_kernel(carried_ref, b_ref, base_ref, weight_ref, x_end_ref, db_ref, dc_ref, sent_ref, back_ref):
     blocks, rows, width = carried_ref.shape
     carried = carried_ref[...].reshape(blocks * rows, width).astype(bf16)
     back = dot_last(b_ref[...], carried)
@@ -120,18 +276,19 @@
     x_grad = (base_ref[...] + weight_ref[...] * back).astype(bf16)
     entry = jnp.dot(x_end_ref[...], carried, preferred_element_type=f32)
     tokens = entry.shape[0]
-    rows = bc_ref.shape[0] // 4
-    db = (bc_ref[:width] + entry.T).astype(bf16)
-    dc = bc_ref[width:].astype(bf16)
+    rows = width // 2
+    db = (db_ref[...] + entry).T.astype(bf16)
     for y in range(4):
         sent_ref[y, :tokens] = x_grad
-        half = db if y < 2 else dc
-        sent_ref[y, tokens:] = half[(y % 2) * rows:(y % 2 + 1) * rows]
-
-
-def x_grads(carried, b_in, base, weight, x_end, bc_base):
+        if y < 2:
+            sent_ref[y, tokens:] = db[y * rows:(y + 1) * rows]
+        else:
+            sent_ref[y, tokens:] = dc_ref[(y - 2) * rows:(y - 1) * rows]
+
+
+def x_grads(carried, b_in, base, weight, x_end, db, dc):
     tokens, inner = base.shape
-    rows = bc_base.shape[0] // 4
+    rows = db.shape[1] // 2
     return pl.pallas_call(
         x_grad_kernel,
         out_shape=(
@@ -140,7 +297,7 @@
         ),
         compiler_params=small(),
         cost_estimate=cost(4 * tokens * inner * 128, 2 << 20),
-    )(carried, b_in, base, weight, x_end, bc_base)
+    )(carried, b_in, base, weight, x_end, db, dc)
 
 
 def in_kernel(y_ref, got_ref, own_ref, *refs):
@@ -211,86 +368,52 @@
     head_dim = inner_here // group_heads
     state_dim = b_in.shape[1]
     blocks = lax.axis_size(SEQ)
-    contract_last = (((1,), (1,)), ((), ()))
+    y = lax.axis_index("y")
+    entry_state = states[0]
+
     w_out_y = lax.all_to_all(regrouped(w_out), "y", 0, 0)
     near = lax.all_gather(out_grad, "zh", axis=1, tiled=True)
     head_parts = lax.all_to_all(partial_products(near, w_out_y), "y", 0, 0)
-    x_heads = x_in.reshape(tokens_here, group_heads, head_dim)
-    x_wide = x_heads.astype(f32)
+
     decay_rate = jnp.exp(a_log)
     step_size = jax.nn.softplus(dt_raw + dt_bias[:, None])
     log_step = -decay_rate[:, None] * step_size
     positions = jnp.arange(tokens_here)
-    causal = positions[:, None] >= positions[None, :]
-    triangle = causal.astype(f32)
-    cumlog = jnp.dot(log_step, triangle.T, precision=lax.Precision.HIGHEST)
-    log_gaps = cumlog[:, :, None] - cumlog[:, None, :]
-    decay_mask = jnp.where(causal[None], jnp.exp(jnp.minimum(log_gaps, 0.0)), 0.0)
-    scores = lax.dot_general(c_in, b_in, contract_last, preferred_element_type=f32)
-    step_rows = step_size.T
-    x_scaled = (x_wide * step_rows[:, :, None]).astype(bf16)
-    start_decay = jnp.exp(cumlog)
-    end_total = jnp.exp(cumlog[:, -1])
-    ends = jnp.pad(three_parts(end_total), ((0, 0), (0, 5)))
+    upto = (positions[:, None] <= positions[None, :]).astype(f32)
+    cumlog = jnp.dot(log_step, upto, precision=lax.Precision.HIGHEST)
+    rows = jnp.concatenate([cumlog, step_size], axis=0)
+    ends = jnp.pad(three_parts(jnp.exp(cumlog[:, -1])), ((0, 0), (0, 5)))
     ends = jnp.broadcast_to(ends[:, None, :, None], (group_heads, blocks // group_heads, 8, state_dim))
-    y = lax.axis_index("y")
+    scalars = jnp.pad(jnp.stack([decay_rate, dt_bias], axis=1), ((0, 0), (0, 126)))
+    skip = jnp.repeat(d_skip, head_dim)[None]
+    start, step, weight, scaled, x_end, scores, y_state = prepared(rows, x_in, b_in, c_in, entry_state)
+
     w_in_held, head_parts = lax.optimization_barrier((w_in, head_parts))
     quarter = w_in.shape[0] // 4
-    held = []
-    for s in range(1, 4):
-        piece = lax.dynamic_slice_in_dim(w_in_held, lax.rem(y + s, 4) * quarter, quarter)
-        held.append(lax.ppermute(piece, "y", [(i, (i + s) % 4) for i in range(4)]))
-    start_wide = jnp.repeat(start_decay.T, head_dim, axis=1)
-    dy_flat, decayed_flat, sent = local_states(head_parts, start_wide, c_in, ends.reshape(blocks, 8, state_dim))
-    dy_heads = dy_flat.reshape(tokens_here, group_heads, head_dim)
-    dy_wide = dy_heads.astype(f32)
-    dy_decay = decayed_flat.reshape(tokens_here, group_heads, head_dim)
-    got = lax.all_to_all(sent, SEQ, 0, 0)
-    carried_rows = lax.all_to_all(suffix_scan(got), SEQ, 0, 0)
-    carried = carried_rows.reshape(group_heads, head_dim, state_dim)
-
-    pair_dots = jnp.einsum("ihp,jhp->hij", dy_heads, x_scaled, preferred_element_type=f32)
-    kernel = (scores[None] * decay_mask).astype(bf16)
-    intra_back = jnp.einsum("hij,ihp->jhp", kernel, dy_heads, preferred_element_type=f32)
-    masked_dots = (pair_dots * decay_mask).astype(bf16)
-    entry_state = states.reshape(group_heads, head_dim, state_dim)
-    db_intra = jnp.einsum("hij,in->nj", masked_dots, c_in, preferred_element_type=f32)
-    dc_intra = jnp.einsum("hij,jn->ni", masked_dots, b_in, preferred_element_type=f32)
-    dc_entry = jnp.einsum("ihp,hpn->ni", dy_decay, entry_state, preferred_element_type=f32)
-    ystate = jnp.einsum("in,hpn->ihp", c_in, entry_state, preferred_element_type=f32)
-    pair_weight = pair_dots * scores[None] * decay_mask
-    state_terms = start_decay * jnp.sum(dy_wide * ystate, axis=2).T
-    skip_terms = jnp.sum(dy_wide * x_wide, axis=(0, 2))
-
-    end_decay = jnp.exp(cumlog[:, -1:] - cumlog)
-    end_weight = (step_size * end_decay).T
-    flat = (tokens_here, inner_here)
-    base = (step_rows[:, :, None] * intra_back + d_skip[None, :, None] * dy_wide).reshape(flat)
-    weight_wide = jnp.repeat(end_weight, head_dim, axis=1)
-    x_end = (x_in.astype(f32) * weight_wide).astype(bf16)
-    bc_base = jnp.concatenate([db_intra, dc_intra + dc_entry], axis=0)
-    *held, carried_rows = lax.optimization_barrier((*held, carried_rows))
-    sent_y, back_flat = x_grads(carried_rows, b_in, base, weight_wide, x_end, bc_base)
-    state_back = back_flat.reshape(tokens_here, group_heads, head_dim)
-    terms = in_products(y, lax.all_to_all(sent_y, "y", 0, 0), w_in, held)
-
-    end_terms = end_weight.T * jnp.sum(x_wide * state_back, axis=2).T
-    cum_grad = pair_weight.sum(axis=2) - pair_weight.sum(axis=1) + state_terms - end_terms
-    tail_grad = end_terms.sum(axis=1) + end_total * jnp.sum(entry_state.astype(f32) * carried, axis=(1, 2))
-    step_grad = jnp.dot(cum_grad, triangle, precision=lax.Precision.HIGHEST) + tail_grad[:, None]
-    dt_sum = (
-        -decay_rate[:, None] * step_grad
-        + jnp.sum(x_wide * (intra_back + end_decay.T[:, :, None] * state_back), axis=2).T
+    pieces = [lax.dynamic_slice_in_dim(w_in_held, lax.rem(y + s, 4) * quarter, quarter) for s in range(1, 4)]
+    shift = [[(i, (i + s) % 4) for i in range(4)] for s in range(1, 4)]
+    dy, decayed, sent = local_states(head_parts, start, c_in, ends.reshape(blocks, 8, state_dim))
+    held = [lax.ppermute(pieces[1], "y", shift[1]), lax.ppermute(pieces[0], "y", shift[0])]
+    ahead = suffix_scan(lax.all_to_all(sent, SEQ, 0, 0))
+    ahead, dy, piece = lax.optimization_barrier((ahead, dy, pieces[2]))
+    held.append(lax.ppermute(piece, "y", shift[2]))
+    base, db, dc, part, across = intra_terms(
+        dy, decayed, x_in, scaled, b_in, c_in, entry_state, rows, skip, start, step, scores, y_state
     )
-    dt_grad = dt_sum * jax.nn.sigmoid(dt_raw + dt_bias[:, None])
-    param_terms = jnp.stack([jnp.sum(step_grad * log_step, axis=1), skip_terms, jnp.sum(dt_grad, axis=1)])
-    row = jnp.pad(param_terms.reshape(1, -1), ((0, 0), (0, 128 - param_terms.size)))
+    *held, carried, base = lax.optimization_barrier((*held, lax.all_to_all(ahead, SEQ, 0, 0), base))
+    sent_y, back = x_grads(carried, b_in, base, weight, x_end, db, dc)
+    got = lax.all_to_all(sent_y, "y", 0, 0)
+    dt_grad, row = dt_terms(back, x_in, rows, part, across, carried, entry_state, dt_raw, scalars)
+    for flip in (1, 2):
+        row = row + lax.ppermute(row, "zl", [(i, i ^ flip) for i in range(4)])
+    row, got = lax.optimization_barrier((row, got))
+    terms = in_products(y, got, w_in, (held[1], held[0], held[2]))
     row, terms = lax.optimization_barrier((row, terms))
-    for axis, flip in (("core", 1), ("zl", 1), ("zl", 2), ("x", 1), ("x", 2)):
+    for axis, flip in (("core", 1), ("x", 1), ("x", 2)):
         row = row + lax.ppermute(row, axis, [(i, i ^ flip) for i in range(lax.axis_size(axis))])
     in_grad, bc_grad = final_sums(lax.all_to_all(terms, "zh", 0, 0), w_in.shape[0] // 16)
     norm_scale = (blocks * tokens_here * head_dim) ** (-0.5)
-    param_grad = row[0, : param_terms.size].reshape(param_terms.shape) * norm_scale
+    param_grad = row[0, : 3 * group_heads].reshape(3, group_heads) * norm_scale
     return (in_grad, bc_grad, dt_grad, param_grad)
 
 

time: 173 us -> 223 us (1.29)
  the two profiles are of different devices: /device:TPU:166 before, /device:TPU:54 now
where the time goes in v3:
time: 223 us; the launch traced here: 222 us
  Pallas kernels  77.8 us (35%)
  starting transfers between devices  62.3 us (28%)
  blocking collectives  32 us (14%)
  waiting for transfers between devices  29 us (13%)
  local copies, waits for them, and re-layouts  19 us (9%)
    pallas_call x1, Pallas kernels, regrouped(): pl.pallas_call(regroup_kernel, in_specs=[pl.BlockSpec(memory_space=pl.ANY...  64.7 us
    all_gather x1, blocking collectives, shards(): near = lax.all_gather(out_grad, 'zh', axis=1, tiled=True)  32 us
    unnamed x68, local copies, waits for them, and re-layouts  15.4 us
    all_to_all x1, waiting for transfers between devices, shards(): lax.all_to_all(terms, 'zh', 0, 0)  13.8 us
    ppermute x3, starting transfers between devices, shards(): lax.ppermute(row, axis, [(i, i ^ flip) for i in range(lax.axis_size(axis))])  7.92 us
    all_to_all x1, starting transfers between devices, shards(): lax.all_to_all(ahead, SEQ, 0, 0)  7.7 us
    ppermute x3, waiting for transfers between devices, shards(): lax.ppermute(row, axis, [(i, i ^ flip) for i in range(lax.axis_size(axis))])  7.41 us
    all_to_all x1, starting transfers between devices, shards(): ahead = suffix_scan(lax.all_to_all(sent, SEQ, 0, 0))  7 us
  transfers between devices with their start and end apart: 14, of which 9 were waited for; matrix products, arithmetic and copies ran while one was open for 2% of the time, Pallas kernels for 2%

profile of v3, /device:TPU:54, one launch (start us, length us, event | category | flops | bytes accessed | tf_op | source)
XLA Modules:
  0.0 222.2 jit_solution(4014702364787549742)
XLA Ops:
  0.6 64.7 %shard_map.138 = bf16[4,256,1024]{2,1,0:T(8,128)(2,1)} custom-call(bf16[256,4096]{1,0:T(8,128)(2,1)} %w_ref.1), custom_call_target="tpu_custom_call" | custom-call | bytes 4194304 | tf_op jit(solution)/shard_map/pallas_call | solution.py:64
  65.4 4.9 %all-to-all-start = ((bf16[4,256,1024]{2,1,0:T(8,128)(2,1)}), bf16[4,256,1024]{2,1,0:T(8,128)(2,1)S(1)}, u32[]{:S(2)}, u32[]{:S(2)}) async-start(bf16[4,256,1024]{2,1,0:T(8,128)(2,1)} %shard_map.138), calls=%async_computation | async-start | bytes 4194304 | tf_op jit(solution)/shard_map/all_to_all | solution.py:374
  70.3 32.0 %all_gather.3.near_ref = bf16[256,1024]{1,0:T(8,128)(2,1)S(1)} all-gather(bf16[256,256]{1,0:T(8,128)(2,1)S(1)} %copy-done.30), channel_id=1, replica_groups=mesh['x'=4,'zl'=4,'core'=2,'y'=4,'zh'=4] {'zh'}, dimensions={1}, use_global_device_ids=true | all-gather | bytes 655360 | tf_op jit(solution)/shard_map/all_gather | solution.py:375
  103.2 2.4 %shard_map.139 = bf16[4,256,256]{2,1,0:T(8,128)(2,1)} custom-call(bf16[256,1024]{1,0:T(8,128)(2,1)S(1)} %all_gather.3.near_ref, bf16[4,256,1024]{2,1,0:T(8,128)(2,1)S(1)} %all-to-all-done.w_ref), custom_call_target="tpu_custom_call" | custom-call | flops 536870912 | bytes 4194304 | tf_op jit(solution)/shard_map/pallas_call | solution.py:81
  105.6 4.9 %all-to-all-start.1 = ((bf16[4,256,256]{2,1,0:T(8,128)(2,1)}), bf16[4,256,256]{2,1,0:T(8,128)(2,1)S(1)}, u32[]{:S(2)}, u32[]{:S(2)}) async-start(bf16[4,256,256]{2,1,0:T(8,128)(2,1)} %shard_map.139), calls=%async_computation.1 | async-start | bytes 1048576 | tf_op jit(solution)/shard_map/all_to_all | solution.py:376
  118.0 7.0 %all-to-all-start.2 = ((bf16[32,16,128]{2,1,0:T(8,128)(2,1)}), bf16[32,16,128]{2,1,0:T(8,128)(2,1)S(1)}, u32[]{:S(2)}, u32[]{:S(2)}) async-start(bf16[32,16,128]{2,1,0:T(8,128)(2,1)} %copy-done.20), calls=%async_computation.2 | async-start | bytes 262144 | tf_op jit(solution)/shard_map/all_to_all | solution.py:397
  125.0 1.2 constant_dynamic-slice_fusion
  126.2 4.9 %collective-permute-start = (bf16[1024,256]{1,0:T(8,128)(2,1)}, bf16[1024,256]{1,0:T(8,128)(2,1)}, u32[]{:S(2)}, u32[]{:S(2)}) collective-permute-start(bf16[1024,256]{1,0:T(8,128)(2,1)} %get-tuple-element.76), channel_id=1, source_target_pairs={{0,8},{4,12},{8,0},{12,4},{1,9},{5,13},{9,1},{13,5},{2,10},{6,14},... | collective-permute-start | bytes 1572872 | tf_op jit(solution)/shard_map/ppermute | solution.py:396
  131.1 3.1 %collective-permute-start.1 = (bf16[1024,256]{1,0:T(8,128)(2,1)}, bf16[1024,256]{1,0:T(8,128)(2,1)}, u32[]{:S(2)}, u32[]{:S(2)}) collective-permute-start(bf16[1024,256]{1,0:T(8,128)(2,1)} %get-tuple-element.75), channel_id=1, source_target_pairs={{0,4},{4,8},{8,12},{12,0},{1,5},{5,9},{9,13},{13,1},{2,6},{6,10},{... | collective-permute-start | bytes 1572872 | tf_op jit(solution)/shard_map/ppermute | solution.py:396
  134.9 2.8 %collective-permute-start.2 = (bf16[1024,256]{1,0:T(8,128)(2,1)}, bf16[1024,256]{1,0:T(8,128)(2,1)}, u32[]{:S(2)}, u32[]{:S(2)}) collective-permute-start(bf16[1024,256]{1,0:T(8,128)(2,1)} %get-tuple-element.44), channel_id=1, source_target_pairs={{0,12},{4,0},{8,4},{12,8},{1,13},{5,1},{9,5},{13,9},{2,14},{6,2},{... | collective-permute-start | bytes 1572872 | tf_op jit(solution)/shard_map/ppermute | solution.py:399
  137.7 7.7 %all-to-all-start.3 = ((f32[32,8,128]{2,1,0:T(8,128)}), f32[32,8,128]{2,1,0:T(8,128)S(1)}, u32[]{:S(2)}, u32[]{:S(2)}) async-start(f32[32,8,128]{2,1,0:T(8,128)} %shard_map.142), calls=%async_computation.3 | async-start | bytes 262144 | tf_op jit(solution)/shard_map/all_to_all | solution.py:403
  145.6 0.9 copy-done.9
  146.5 0.9 copy-done.11
  148.4 2.8 %shard_map.143 = (f32[256,256]{1,0:T(8,128)S(1)}, f32[256,128]{1,0:T(8,128)S(1)}, bf16[128,256]{1,0:T(8,128)(2,1)S(1)}, f32[8,256]{1,0:T(8,128)S(1)}, f32[1,256]{1,0:T(1,128)S(1)}) custom-call(bf16[256,256]{1,0:T(8,128)(2,1)S(1)} %copy-done.17, bf16[256,256]{1,0:T(8,128)(2,1)S(1)} %copy-done.19, bf16[256,256]{1,0:T(8,128)(2,1)S(1)} %copy-done.1, ...), custom_call_target="tpu_custom_call" | custom-call | flops 201326592 | bytes 4194304 | tf_op jit(solution)/shard_map/pallas_call | solution.py:217
  153.7 1.4 collective-permute-done.1.refs_0_
  155.8 0.9 copy-done.13
  156.7 0.9 copy-done.15
  160.6 5.8 %all-to-all-start.4 = ((bf16[4,320,256]{2,1,0:T(8,128)(2,1)}), bf16[4,320,256]{2,1,0:T(8,128)(2,1)S(1)}, u32[]{:S(2)}, u32[]{:S(2)}) async-start(bf16[4,320,256]{2,1,0:T(8,128)(2,1)} %copy-done.2), calls=%async_computation.4 | async-start | bytes 1310720 | tf_op jit(solution)/shard_map/all_to_all | solution.py:405
  168.0 1.2 shard_map.145
  169.1 2.4 %collective-permute-start.3 = (f32[1,128]{1,0:T(1,128)S(1)}, f32[1,128]{1,0:T(1,128)S(1)}, u32[]{:S(2)}, u32[]{:S(2)}) collective-permute-start(f32[1,128]{1,0:T(1,128)S(1)} %get-tuple-element.62), channel_id=1, source_target_pairs={{0,32},{32,0},{64,96},{96,64},{1,33},{33,1},{65,97},{97,65},{2,34}... | collective-permute-start | bytes 1544 | tf_op jit(solution)/shard_map/ppermute | solution.py:408
  171.6 3.0 %collective-permute-done.3 = f32[1,128]{1,0:T(1,128)S(1)} collective-permute-done((f32[1,128]{1,0:T(1,128)S(1)}, f32[1,128]{1,0:T(1,128)S(1)}, u32[]{:S(2)}, u32[]{:S(2)}) %collective-permute-start.3) | collective-permute-done | bytes 544 | tf_op jit(solution)/shard_map/ppermute | solution.py:408
  174.6 4.3 %collective-permute-start.4 = (f32[1,128]{1,0:T(1,128)S(1)}, f32[1,128]{1,0:T(1,128)S(1)}, u32[]{:S(2)}, u32[]{:S(2)}) collective-permute-start(f32[1,128]{1,0:T(1,128)S(1)} %add.58), channel_id=1, source_target_pairs={{0,64},{32,96},{64,0},{96,32},{1,65},{33,97},{65,1},{97,33},{2,66}... | collective-permute-start | bytes 1544 | tf_op jit(solution)/shard_map/ppermute | solution.py:408
  178.9 2.0 collective-permute-done.4
  180.9 4.1 %shard_map.146 = bf16[4,272,256]{2,1,0:T(8,128)(2,1)} custom-call(s32[1]{0:T(128)} %bitcast.4.y_ref, bf16[4,320,256]{2,1,0:T(8,128)(2,1)S(1)} %all-to-all-done.4.got_ref, bf16[4096,256]{1,0:T(8,128)(2,1)S(1)} %copy-done, bf16[1024,256]{1,0:T(8,128)(2,1)} %collective-permute-done.1.refs_0_, bf16[1024,256]{1,0:T(8,128)(2,1)} %collective-permute-done.refs_1_, ...), custom_call_target="tpu_custom_call" | custom-call | flops 536870912 | bytes 4194304 | tf_op jit(solution)/shard_map/pallas_call | solution.py:324
  185.0 6.6 %all-to-all-start.5 = ((bf16[4,272,256]{2,1,0:T(8,128)(2,1)}), bf16[4,272,256]{2,1,0:T(8,128)(2,1)S(1)}, u32[]{:S(2)}, u32[]{:S(2)}) async-start(bf16[4,272,256]{2,1,0:T(8,128)(2,1)} %shard_map.146), calls=%async_computation.5 | async-start | bytes 1114112 | tf_op jit(solution)/shard_map/all_to_all | solution.py:414
  191.6 1.9 collective-permute-start.5
  193.5 1.1 collective-permute-done.5
  194.6 2.7 %collective-permute-start.6 = (f32[1,128]{1,0:T(1,128)S(1)}, f32[1,128]{1,0:T(1,128)S(1)}, u32[]{:S(2)}, u32[]{:S(2)}) collective-permute-start(f32[1,128]{1,0:T(1,128)S(1)} %add.60), channel_id=1, source_target_pairs={{0,128},{128,0},{256,384},{384,256},{1,129},{129,1},{257,385},{385... | collective-permute-start | bytes 1544 | tf_op jit(solution)/shard_map/ppermute | solution.py:413
  197.3 2.7 %collective-permute-done.6 = f32[1,128]{1,0:T(1,128)S(1)} collective-permute-done((f32[1,128]{1,0:T(1,128)S(1)}, f32[1,128]{1,0:T(1,128)S(1)}, u32[]{:S(2)}, u32[]{:S(2)}) %collective-permute-start.6) | collective-permute-done | bytes 544 | tf_op jit(solution)/shard_map/ppermute | solution.py:413
  200.0 3.3 %collective-permute-start.7 = (f32[1,128]{1,0:T(1,128)S(1)}, f32[1,128]{1,0:T(1,128)S(1)}, u32[]{:S(2)}, u32[]{:S(2)}) collective-permute-start(f32[1,128]{1,0:T(1,128)S(1)} %add.61), channel_id=1, source_target_pairs={{0,256},{128,384},{256,0},{384,128},{1,257},{129,385},{257,1},{385... | collective-permute-start | bytes 1544 | tf_op jit(solution)/shard_map/ppermute | solution.py:413
  203.3 3.6 %collective-permute-done.7 = f32[1,128]{1,0:T(1,128)S(1)} collective-permute-done((f32[1,128]{1,0:T(1,128)S(1)}, f32[1,128]{1,0:T(1,128)S(1)}, u32[]{:S(2)}, u32[]{:S(2)}) %collective-permute-start.7) | collective-permute-done | bytes 544 | tf_op jit(solution)/shard_map/ppermute | solution.py:413
  207.6 13.8 %all-to-all-done.5.terms_ref = bf16[4,272,256]{2,1,0:T(8,128)(2,1)S(1)} async-done(((bf16[4,272,256]{2,1,0:T(8,128)(2,1)}), bf16[4,272,256]{2,1,0:T(8,128)(2,1)S(1)}, u32[]{:S(2)}, u32[]{:S(2)}) %all-to-all-start.5) | async-done | bytes 557088 | tf_op jit(solution)/shard_map/all_to_all | solution.py:414
  (96 shorter events, 19.2 us)
Async XLA Ops:
  65.3 5.0 %copy-start.30 = (bf16[256,256]{1,0:T(8,128)(2,1)S(1)}, bf16[256,256]{1,0:T(8,128)(2,1)}, u32[]{:S(2)}) copy-start(bf16[256,256]{1,0:T(8,128)(2,1)} %param.11) | copy-start | bytes 393220
  65.3 37.0 %copy-start.33 = (f32[4]{0:T(128)S(1)}, f32[4]{0:T(128)}, u32[]{:S(2)}) copy-start(f32[4]{0:T(128)} %param.17) | copy-start | bytes 52
  65.3 37.5 %copy-start.25 = (f32[4,256]{1,0:T(4,128)S(1)}, f32[4,256]{1,0:T(4,128)}, u32[]{:S(2)}) copy-start(f32[4,256]{1,0:T(4,128)} %raw_ref.1) | copy-start | bytes 12292
  65.3 37.5 %copy-start.31 = (f32[4]{0:T(128)S(1)}, f32[4]{0:T(128)}, u32[]{:S(2)}) copy-start(f32[4]{0:T(128)} %param.16) | copy-start | bytes 52
  65.4 37.9 %all-to-all-start = ((bf16[4,256,1024]{2,1,0:T(8,128)(2,1)}), bf16[4,256,1024]{2,1,0:T(8,128)(2,1)S(1)}, u32[]{:S(2)}, u32[]{:S(2)}) async-start(bf16[4,256,1024]{2,1,0:T(8,128)(2,1)} %shard_map.138), calls=%async_computation | async-start | bytes 4194304 | tf_op jit(solution)/shard_map/all_to_all | solution.py:374
  103.1 7.4 %copy-start.1 = (bf16[256,256]{1,0:T(8,128)(2,1)S(1)}, bf16[256,256]{1,0:T(8,128)(2,1)}, u32[]{:S(2)}) copy-start(bf16[256,256]{1,0:T(8,128)(2,1)} %x_ref.5) | copy-start | bytes 393220
  103.1 7.4 %copy-start.3 = (bf16[256,128]{1,0:T(8,128)(2,1)S(1)}, bf16[256,128]{1,0:T(8,128)(2,1)}, u32[]{:S(2)}) copy-start(bf16[256,128]{1,0:T(8,128)(2,1)} %b_ref.5) | copy-start | bytes 196612
  103.2 7.4 %copy-start.4 = (bf16[1,256,128]{2,1,0:T(8,128)(2,1)S(1)}, bf16[1,256,128]{2,1,0:T(8,128)(2,1)}, u32[]{:S(2)}) copy-start(bf16[1,256,128]{2,1,0:T(8,128)(2,1)} %param.19) | copy-start | bytes 196612
  103.2 7.4 %copy-start.5 = (bf16[256,128]{1,0:T(8,128)(2,1)S(1)}, bf16[256,128]{1,0:T(8,128)(2,1)}, u32[]{:S(2)}) copy-start(bf16[256,128]{1,0:T(8,128)(2,1)} %c_ref.5) | copy-start | bytes 196612
  105.6 19.4 %copy-start = (bf16[4096,256]{1,0:T(8,128)(2,1)S(1)}, bf16[4096,256]{1,0:T(8,128)(2,1)}, u32[]{:S(2)}) copy-start(bf16[4096,256]{1,0:T(8,128)(2,1)} %own_ref.1) | copy-start | bytes 6291460
  105.6 10.0 %all-to-all-start.1 = ((bf16[4,256,256]{2,1,0:T(8,128)(2,1)}), bf16[4,256,256]{2,1,0:T(8,128)(2,1)S(1)}, u32[]{:S(2)}, u32[]{:S(2)}) async-start(bf16[4,256,256]{2,1,0:T(8,128)(2,1)} %shard_map.139), calls=%async_computation.1 | async-start | bytes 1048576 | tf_op jit(solution)/shard_map/all_to_all | solution.py:376
  118.0 27.4 %copy-start.32 = (f32[4]{0:T(128)S(1)}, f32[4]{0:T(128)}, u32[]{:S(2)}) copy-start(f32[4]{0:T(128)} %param.18) | copy-start | bytes 52
  118.0 27.6 %copy-start.7 = (f32[256,256]{1,0:T(8,128)S(1)}, f32[256,256]{1,0:T(8,128)}, u32[]{:S(2)}) copy-start(f32[256,256]{1,0:T(8,128)} %copy-done.6) | copy-start | bytes 786436
  118.0 27.6 %copy-start.17 = (bf16[256,256]{1,0:T(8,128)(2,1)S(1)}, bf16[256,256]{1,0:T(8,128)(2,1)}, u32[]{:S(2)}) copy-start(bf16[256,256]{1,0:T(8,128)(2,1)} %copy-done.16) | copy-start | bytes 393220
  118.0 16.2 %all-to-all-start.2 = ((bf16[32,16,128]{2,1,0:T(8,128)(2,1)}), bf16[32,16,128]{2,1,0:T(8,128)(2,1)S(1)}, u32[]{:S(2)}, u32[]{:S(2)}) async-start(bf16[32,16,128]{2,1,0:T(8,128)(2,1)} %copy-done.20), calls=%async_computation.2 | async-start | bytes 262144 | tf_op jit(solution)/shard_map/all_to_all | solution.py:397
  126.2 27.5 %collective-permute-start = (bf16[1024,256]{1,0:T(8,128)(2,1)}, bf16[1024,256]{1,0:T(8,128)(2,1)}, u32[]{:S(2)}, u32[]{:S(2)}) collective-permute-start(bf16[1024,256]{1,0:T(8,128)(2,1)} %get-tuple-element.76), channel_id=1, source_target_pairs={{0,8},{4,12},{8,0},{12,4},{1,9},{5,13},{9,1},{13,5},{2,10},{6,14},... | collective-permute-start | bytes 1572872 | tf_op jit(solution)/shard_map/ppermute | solution.py:396
  131.1 24.0 %collective-permute-start.1 = (bf16[1024,256]{1,0:T(8,128)(2,1)}, bf16[1024,256]{1,0:T(8,128)(2,1)}, u32[]{:S(2)}, u32[]{:S(2)}) collective-permute-start(bf16[1024,256]{1,0:T(8,128)(2,1)} %get-tuple-element.75), channel_id=1, source_target_pairs={{0,4},{4,8},{8,12},{12,0},{1,5},{5,9},{9,13},{13,1},{2,6},{6,10},{... | collective-permute-start | bytes 1572872 | tf_op jit(solution)/shard_map/ppermute | solution.py:396
  134.9 20.9 %collective-permute-start.2 = (bf16[1024,256]{1,0:T(8,128)(2,1)}, bf16[1024,256]{1,0:T(8,128)(2,1)}, u32[]{:S(2)}, u32[]{:S(2)}) collective-permute-start(bf16[1024,256]{1,0:T(8,128)(2,1)} %get-tuple-element.44), channel_id=1, source_target_pairs={{0,12},{4,0},{8,4},{12,8},{1,13},{5,1},{9,5},{13,9},{2,14},{6,2},{... | collective-permute-start | bytes 1572872 | tf_op jit(solution)/shard_map/ppermute | solution.py:399
  137.7 17.5 %all-to-all-start.3 = ((f32[32,8,128]{2,1,0:T(8,128)}), f32[32,8,128]{2,1,0:T(8,128)S(1)}, u32[]{:S(2)}, u32[]{:S(2)}) async-start(f32[32,8,128]{2,1,0:T(8,128)} %shard_map.142), calls=%async_computation.3 | async-start | bytes 262144 | tf_op jit(solution)/shard_map/all_to_all | solution.py:403
  145.6 1.0 copy-start.9
  146.5 0.9 copy-start.11
  153.7 14.3 %copy-start.27 = (f32[8,256]{1,0:T(8,128)S(1)}, f32[8,256]{1,0:T(8,128)}, u32[]{:S(2)}) copy-start(f32[8,256]{1,0:T(8,128)} %copy-done.26) | copy-start | bytes 24580
  153.7 14.3 %copy-start.29 = (f32[1,256]{1,0:T(1,128)S(1)}, f32[1,256]{1,0:T(1,128)}, u32[]{:S(2)}) copy-start(f32[1,256]{1,0:T(1,128)} %copy-done.28) | copy-start | bytes 3076
  155.8 1.0 copy-start.13
  156.7 0.9 copy-start.15
  160.6 20.3 %all-to-all-start.4 = ((bf16[4,320,256]{2,1,0:T(8,128)(2,1)}), bf16[4,320,256]{2,1,0:T(8,128)(2,1)S(1)}, u32[]{:S(2)}, u32[]{:S(2)}) async-start(bf16[4,320,256]{2,1,0:T(8,128)(2,1)} %copy-done.2), calls=%async_computation.4 | async-start | bytes 1310720 | tf_op jit(solution)/shard_map/all_to_all | solution.py:405
  169.1 5.4 %collective-permute-start.3 = (f32[1,128]{1,0:T(1,128)S(1)}, f32[1,128]{1,0:T(1,128)S(1)}, u32[]{:S(2)}, u32[]{:S(2)}) collective-permute-start(f32[1,128]{1,0:T(1,128)S(1)} %get-tuple-element.62), channel_id=1, source_target_pairs={{0,32},{32,0},{64,96},{96,64},{1,33},{33,1},{65,97},{97,65},{2,34}... | collective-permute-start | bytes 1544 | tf_op jit(solution)/shard_map/ppermute | solution.py:408
  174.6 6.3 %collective-permute-start.4 = (f32[1,128]{1,0:T(1,128)S(1)}, f32[1,128]{1,0:T(1,128)S(1)}, u32[]{:S(2)}, u32[]{:S(2)}) collective-permute-start(f32[1,128]{1,0:T(1,128)S(1)} %add.58), channel_id=1, source_target_pairs={{0,64},{32,96},{64,0},{96,32},{1,65},{33,97},{65,1},{97,33},{2,66}... | collective-permute-start | bytes 1544 | tf_op jit(solution)/shard_map/ppermute | solution.py:408
  185.0 36.4 %all-to-all-start.5 = ((bf16[4,272,256]{2,1,0:T(8,128)(2,1)}), bf16[4,272,256]{2,1,0:T(8,128)(2,1)S(1)}, u32[]{:S(2)}, u32[]{:S(2)}) async-start(bf16[4,272,256]{2,1,0:T(8,128)(2,1)} %shard_map.146), calls=%async_computation.5 | async-start | bytes 1114112 | tf_op jit(solution)/shard_map/all_to_all | solution.py:414
  191.6 3.0 %collective-permute-start.5 = (f32[1,128]{1,0:T(1,128)S(1)}, f32[1,128]{1,0:T(1,128)S(1)}, u32[]{:S(2)}, u32[]{:S(2)}) collective-permute-start(f32[1,128]{1,0:T(1,128)S(1)} %add.59), channel_id=1, source_target_pairs={{0,16},{16,0},{1,17},{17,1},{2,18},{18,2},{3,19},{19,3},{4,20},{20... | collective-permute-start | bytes 1544 | tf_op jit(solution)/shard_map/ppermute | solution.py:413
  194.6 5.4 %collective-permute-start.6 = (f32[1,128]{1,0:T(1,128)S(1)}, f32[1,128]{1,0:T(1,128)S(1)}, u32[]{:S(2)}, u32[]{:S(2)}) collective-permute-start(f32[1,128]{1,0:T(1,128)S(1)} %add.60), channel_id=1, source_target_pairs={{0,128},{128,0},{256,384},{384,256},{1,129},{129,1},{257,385},{385... | collective-permute-start | bytes 1544 | tf_op jit(solution)/shard_map/ppermute | solution.py:413
  200.0 6.9 %collective-permute-start.7 = (f32[1,128]{1,0:T(1,128)S(1)}, f32[1,128]{1,0:T(1,128)S(1)}, u32[]{:S(2)}, u32[]{:S(2)}) collective-permute-start(f32[1,128]{1,0:T(1,128)S(1)} %add.61), channel_id=1, source_target_pairs={{0,256},{128,384},{256,0},{384,128},{1,257},{129,385},{257,1},{385... | collective-permute-start | bytes 1544 | tf_op jit(solution)/shard_map/ppermute | solution.py:413
  (16 other events, 11.6 us)

commit v4 on v3

v4 whole, which is shorter than its diff:
```python
import jax
import jax.numpy as jnp
from jax import lax
from jax.experimental import pallas as pl
from jax.experimental.pallas import tpu as pltpu
from jax.sharding import Mesh, PartitionSpec as P

SEQ = ("x", "zl", "core")
HEAD = ("y", "zh")
f32, bf16 = jnp.float32, jnp.bfloat16


def scan_kernel(parts_ref, carried_ref):
    blocks = parts_ref.shape[0]
    held = jnp.zeros(carried_ref.shape[1:], f32)
    for k in range(blocks - 1, -1, -1):
        carried_ref[k] = held
        wide = parts_ref[k].astype(f32)
        total = wide[8:9] + wide[9:10] + wide[10:11]
        held = total * held + wide[:8]


def suffix_scan(parts):
    blocks, _, width = parts.shape
    return pl.pallas_call(
        scan_kernel,
        out_shape=jax.ShapeDtypeStruct((blocks, 8, width), f32),
        compiler_params=small(),
        cost_estimate=cost(blocks * 3072, blocks * 8192),
    )(parts)


def three_parts(values):
    first = values.astype(bf16).astype(f32)
    second = (values - first).astype(bf16).astype(f32)
    return jnp.stack([first, second, values - first - second], axis=-1)


def cost(flops, moved):
    return pl.CostEstimate(flops=flops, bytes_accessed=moved, transcendentals=0)


def small(mib=16):
    return pltpu.CompilerParams(vmem_limit_bytes=mib << 20)


def dot_last(a, b):
    return lax.dot_general(a, b, (((1,), (1,)), ((), ())), preferred_element_type=f32)


def regroup_kernel(w_ref, out_ref, stage_ref, in_sems, out_sems):
    _, pieces, rows, part = stage_ref.shape
    steps = [(g, r) for g in range(4) for r in range(pieces)]

    def copy_in(g, r):
        source = w_ref.at[pl.ds(r * rows, rows), pl.ds(g * part, part)]
        return pltpu.make_async_copy(source, stage_ref.at[g, r], in_sems.at[g, r])

    def copy_out(g, r):
        return pltpu.make_async_copy(stage_ref.at[g, r], out_ref.at[g, pl.ds(r * rows, rows)], out_sems.at[g, r])

    for step in steps:
        copy_in(*step).start()
    for step in steps:
        copy_in(*step).wait()
        copy_out(*step).start()
    for step in steps:
        copy_out(*step).wait()


def regrouped(w):
    rows, width = w.shape
    pieces = 4
    return pl.pallas_call(
        regroup_kernel,
        in_specs=[pl.BlockSpec(memory_space=pl.ANY)],
        out_specs=pl.BlockSpec(memory_space=pl.ANY),
        out_shape=jax.ShapeDtypeStruct((4, rows, width // 4), w.dtype),
        scratch_shapes=[
            pltpu.VMEM((4, pieces, rows // pieces, width // 4), w.dtype),
            pltpu.SemaphoreType.DMA((4, pieces)),
            pltpu.SemaphoreType.DMA((4, pieces)),
        ],
        cost_estimate=cost(0, 4 * rows * width),
    )(w)


def partial_kernel(near_ref, w_ref, out_ref):
    out_ref[0] = dot_last(w_ref[0], near_ref[...]).astype(bf16)


def partial_products(near, w_mine):
    groups, inner, depth = w_mine.shape
    tokens = near.shape[0]
    return pl.pallas_call(
        partial_kernel,
        grid=(groups,),
        in_specs=[
            pl.BlockSpec((tokens, depth), lambda g: (0, 0)),
            pl.BlockSpec((1, inner, depth), lambda g: (g, 0, 0)),
        ],
        out_specs=pl.BlockSpec((1, inner, tokens), lambda g: (g, 0, 0)),
        out_shape=jax.ShapeDtypeStruct((groups, inner, tokens), bf16),
        compiler_params=small(),
        cost_estimate=cost(2 * groups * tokens * inner * depth, 4 << 20),
    )(near, w_mine)


def over_channels(rows, height):
    heads, tokens = rows.shape
    return jnp.concatenate(
        [jnp.broadcast_to(rows[h:h + 1], (height // heads, tokens)) for h in range(heads)], axis=0
    )


def state_kernel(parts_ref, rows_ref, c_ref, ends_ref, dy_ref, sent_ref):
    total = parts_ref[0].astype(f32)
    for y in range(1, parts_ref.shape[0]):
        total = total + parts_ref[y].astype(f32)
    dy = total.astype(bf16)
    dy_ref[...] = dy
    start = over_channels(jnp.exp(rows_ref[:4]), dy.shape[0])
    decayed = (dy.astype(f32) * start).astype(bf16)
    state = jnp.dot(decayed, c_ref[...], preferred_element_type=f32)
    blocks, rows, width = ends_ref.shape
    state = state.reshape(blocks, rows, width)
    sent_ref[...] = jnp.concatenate([state, ends_ref[...]], axis=1).astype(bf16)


def local_states(parts, rows, c_in, ends):
    _, inner, tokens = parts.shape
    blocks, height, width = ends.shape
    return pl.pallas_call(
        state_kernel,
        out_shape=(pltpu.HBM((inner, tokens), bf16), pltpu.HBM((blocks, 2 * height, width), bf16)),
        compiler_params=small(),
        cost_estimate=cost(2 * tokens * inner * width, 2 << 20),
    )(parts, rows, c_in, ends)


def widened(columns, width):
    tokens, heads = columns.shape
    return jnp.concatenate(
        [jnp.broadcast_to(columns[:, h:h + 1], (tokens, width // heads)) for h in range(heads)], axis=1
    )


def head_sums(values, heads):
    width = values.shape[1] // heads
    return [jnp.sum(values[:, h * width:(h + 1) * width], axis=1, keepdims=True) for h in range(heads)]


def as_rows(columns):
    tokens = columns[0].shape[0]
    lanes = lax.broadcasted_iota(jnp.int32, (tokens, 128), 1)
    spread = jnp.zeros((tokens, 128), f32)
    for k, column in enumerate(columns):
        spread = jnp.where(lanes == k, column, spread)
    return spread.T[:8]


def intra_kernel(dy_ref, x_ref, b_ref, c_ref, states_ref, rows_ref, skip_ref, wide_ref, half_ref, part_ref):
    width, tokens = dy_ref.shape
    head_dim = width // 4
    cum = rows_ref[:4]
    columns = rows_ref[...].T
    step = widened(columns[:, 4:], width)
    start = widened(jnp.exp(columns[:, :4]), width)
    b, c, states = b_ref[...], c_ref[...], states_ref[...]
    scores = dot_last(c, b)
    entered = dot_last(c, states)
    dy_wide = dy_ref[...].astype(f32).T
    dy = dy_wide.astype(bf16)
    x = x_ref[...].astype(f32)
    scaled = (x * step).astype(bf16)
    causal = lax.broadcasted_iota(jnp.int32, (tokens, tokens), 0) >= lax.broadcasted_iota(jnp.int32, (tokens, tokens), 1)
    total = jnp.zeros((tokens, tokens), f32)
    along, down, backs = [], [], []
    for h in range(4):
        mine = slice(h * head_dim, (h + 1) * head_dim)
        dy_h = dy[:, mine]
        gaps = jnp.minimum(columns[:, h:h + 1] - cum[h:h + 1], 0.0)
        mask = jnp.where(causal, jnp.exp(gaps), 0.0)
        weighed = (scores * mask).astype(bf16)
        backs.append(lax.dot_general(weighed, dy_h, (((0,), (0,)), ((), ())), preferred_element_type=f32))
        masked = dot_last(dy_h, scaled[:, mine]) * mask
        total = total + masked
        pairs = masked * scores
        along.append(jnp.sum(pairs, axis=1, keepdims=True))
        down.append(jnp.sum(pairs, axis=0, keepdims=True))
    total = total.astype(bf16)
    db = lax.dot_general(total, c, (((0,), (0,)), ((), ())), preferred_element_type=f32)
    dc = jnp.dot(total, b, preferred_element_type=f32)
    dc = dc + jnp.dot((dy_wide * start).astype(bf16), states, preferred_element_type=f32)
    back = jnp.concatenate(backs, axis=1)
    wide_ref[:width] = (step * back + skip_ref[...] * dy_wide).T
    wide_ref[width:] = db.T
    half_ref[:width] = x.T.astype(bf16)
    half_ref[width:] = dc.T.astype(bf16)
    entered = head_sums(start * dy_wide * entered, 4)
    rows = as_rows([a + e for a, e in zip(along, entered)] + head_sums(x * back, 4))
    part_ref[:8] = rows - jnp.concatenate(down + [jnp.zeros((4, tokens), f32)], axis=0)
    part_ref[8:] = jnp.broadcast_to(jnp.sum(dy_wide * x, axis=0, keepdims=True), (8, width))


def intra_terms(dy, x_in, b_in, c_in, states, rows, skip):
    width, tokens = dy.shape
    height = width + b_in.shape[1]
    return pl.pallas_call(
        intra_kernel,
        out_shape=(pltpu.HBM((height, tokens), f32), pltpu.HBM((height, tokens), bf16), pltpu.HBM((16, tokens), f32)),
        cost_estimate=cost(14 * tokens * tokens * width, 2 << 20),
    )(dy, x_in, b_in, c_in, states, rows, skip)


def dt_kernel(back_ref, half_ref, rows_ref, part_ref, carried_ref, states_ref, raw_ref, scal_ref, dt_ref, param_ref):
    width, tokens = back_ref.shape
    head_dim = width // 4
    cum, step = rows_ref[:4], rows_ref[4:]
    last = cum[:, tokens - 1:]
    rate, bias = scal_ref[:, 0:1], scal_ref[:, 1:2]
    dots = jnp.sum((half_ref[:width].astype(f32) * back_ref[...]).reshape(4, head_dim, tokens), axis=1)
    end_decay = jnp.exp(last - cum)
    end_terms = step * end_decay * dots
    carried = carried_ref[...].reshape(4, head_dim, -1)
    held = jnp.sum(carried * states_ref[...].astype(f32).reshape(4, head_dim, -1), axis=1)
    tail = jnp.sum(end_terms, axis=1, keepdims=True) + jnp.exp(last) * jnp.sum(held, axis=1, keepdims=True)
    below = lax.broadcasted_iota(jnp.int32, (tokens, tokens), 0) >= lax.broadcasted_iota(jnp.int32, (tokens, tokens), 1)
    step_grad = tail + jnp.dot(
        part_ref[:4] - end_terms, below.astype(f32), precision=lax.Precision.HIGHEST, preferred_element_type=f32
    )
    dt_sum = part_ref[4:8] + end_decay * dots - rate * step_grad
    dt = dt_sum * jax.nn.sigmoid(raw_ref[...] + bias)
    dt_ref[...] = dt
    lanes = lax.broadcasted_iota(jnp.int32, (4, width), 1)
    heads = lax.broadcasted_iota(jnp.int32, (4, width), 0)
    skip = jnp.sum(jnp.where(lanes // head_dim == heads, part_ref[8:9], 0.0), axis=1, keepdims=True)
    decays = jnp.sum(step_grad * (-rate * step), axis=1, keepdims=True)
    biases = jnp.sum(dt, axis=1, keepdims=True)
    lanes, heads = lanes[:, :128], heads[:, :128]
    placed = jnp.where(lanes == heads, decays, 0.0)
    placed = jnp.where(lanes == heads + 4, skip, placed)
    placed = jnp.where(lanes == heads + 8, biases, placed)
    param_ref[...] = jnp.sum(placed, axis=0, keepdims=True)


def dt_terms(back, half, rows, part, carried, states, dt_raw, scalars):
    return pl.pallas_call(
        dt_kernel,
        out_shape=(jax.ShapeDtypeStruct(dt_raw.shape, f32), jax.ShapeDtypeStruct((1, 128), f32)),
        compiler_params=small(),
        cost_estimate=cost(1 << 22, 1 << 20),
    )(back, half, rows, part, carried, states, dt_raw, scalars)


def x_grad_kernel(carried_ref, b_ref, wide_hbm, half_hbm, rows_ref, sent_ref, back_ref, wide_ref, half_ref, sems):
    fetches = [
        pltpu.make_async_copy(wide_hbm, wide_ref, sems.at[0]),
        pltpu.make_async_copy(half_hbm, half_ref, sems.at[1]),
    ]
    for fetch in fetches:
        fetch.start()
    blocks, height, state_dim = carried_ref.shape
    width = blocks * height
    tokens = b_ref.shape[0]
    carried = carried_ref[...].reshape(width, state_dim).astype(bf16)
    back = dot_last(carried, b_ref[...])
    back_ref[...] = back
    cum = rows_ref[:4]
    weight = over_channels(rows_ref[4:] * jnp.exp(cum[:, tokens - 1:] - cum), width)
    for fetch in fetches:
        fetch.wait()
    x_grad = (wide_ref[:width] + weight * back).astype(bf16)
    x_end = (half_ref[:width].astype(f32) * weight).astype(bf16)
    entry = lax.dot_general(carried, x_end, (((0,), (0,)), ((), ())), preferred_element_type=f32)
    db = (wide_ref[width:] + entry).astype(bf16)
    rows = state_dim // 2
    for y in range(4):
        sent_ref[y, :width] = x_grad
        if y < 2:
            sent_ref[y, width:] = db[y * rows:(y + 1) * rows]
        else:
            sent_ref[y, width:] = half_ref[width + (y - 2) * rows:width + (y - 1) * rows]


def x_grads(carried, b_in, wide, half, rows):
    tokens, state_dim = b_in.shape
    inner = wide.shape[0] - state_dim
    at_vmem, at_hbm = pl.BlockSpec(memory_space=pltpu.VMEM), pl.BlockSpec(memory_space=pltpu.HBM)
    return pl.pallas_call(
        x_grad_kernel,
        in_specs=[at_vmem, at_vmem, at_hbm, at_hbm, at_vmem],
        scratch_shapes=[
            pltpu.VMEM(wide.shape, wide.dtype),
            pltpu.VMEM(half.shape, half.dtype),
            pltpu.SemaphoreType.DMA((2,)),
        ],
        out_shape=(pltpu.HBM((4, inner + state_dim // 2, tokens), bf16), pltpu.HBM((inner, tokens), f32)),
        cost_estimate=cost(4 * tokens * inner * 128, 2 << 20),
    )(carried, b_in, wide, half, rows)


def in_kernel(y_ref, got_ref, own_hbm, *refs):
    *held_hbm, out_hbm, w_ref, out_ref, w_sems, out_sems = refs
    _, _, feats, inner = w_ref.shape
    rows = out_ref.shape[1] - feats
    y = y_ref[0]

    def fetch(z, s):
        at = pl.multiple_of((4 * y + z) * feats, feats) if s == 0 else z * feats
        source = own_hbm if s == 0 else held_hbm[s - 1]
        return pltpu.make_async_copy(source.at[pl.ds(at, feats)], w_ref.at[z, s], w_sems.at[z, s])

    def store(z):
        return pltpu.make_async_copy(out_ref.at[z], out_hbm.at[z], out_sems.at[z])

    for z in range(4):
        for s in range(4):
            fetch(z, s).start()
    for z in range(4):
        at = slice(inner + z * rows, inner + (z + 1) * rows)
        bc = got_ref[0, at].astype(f32)
        for other in range(1, 4):
            bc = bc + got_ref[other, at].astype(f32)
        out_ref[z, feats:] = bc.astype(bf16)
        total = jnp.zeros((feats, got_ref.shape[2]), f32)
        for s in range(4):
            fetch(z, s).wait()
            total = total + jnp.dot(w_ref[z, s], got_ref[lax.rem(y + 4 - s, 4), :inner], preferred_element_type=f32)
        out_ref[z, :feats] = total.astype(bf16)
        store(z).start()
    for z in range(4):
        store(z).wait()


def in_products(y, got, w_in, held):
    features, inner = w_in.shape
    _, height, tokens = got.shape
    feats, rows = features // 16, (height - inner) // 4
    out = (4, feats + rows, tokens)
    return pl.pallas_call(
        in_kernel,
        in_specs=[pl.BlockSpec(memory_space=pltpu.SMEM), pl.BlockSpec(memory_space=pltpu.VMEM)]
        + [pl.BlockSpec(memory_space=pltpu.HBM)] * 4,
        out_specs=pl.BlockSpec(memory_space=pltpu.HBM),
        out_shape=jax.ShapeDtypeStruct(out, bf16),
        scratch_shapes=[
            pltpu.VMEM((4, 4, feats, inner), w_in.dtype),
            pltpu.VMEM(out, bf16),
            pltpu.SemaphoreType.DMA((4, 4)),
            pltpu.SemaphoreType.DMA((4,)),
        ],
        cost_estimate=cost(8 * features * inner * tokens // 4, 4 << 20),
    )(y.reshape(1), got, w_in, *held)


def sum_kernel(terms_ref, in_ref, bc_ref):
    feats = in_ref.shape[0]
    total = terms_ref[0].astype(f32)
    for z in range(1, 4):
        total = total + terms_ref[z].astype(f32)
    total = total.astype(bf16)
    in_ref[...] = total[:feats]
    bc_ref[...] = total[feats:]


def final_sums(terms, feats):
    _, height, tokens = terms.shape
    return pl.pallas_call(
        sum_kernel,
        out_shape=(
            jax.ShapeDtypeStruct((feats, tokens), bf16),
            jax.ShapeDtypeStruct((height - feats, tokens), bf16),
        ),
        compiler_params=small(),
        cost_estimate=cost(4 * height * tokens, 1 << 20),
    )(terms)


def shards(out_grad, x_in, b_in, c_in, dt_raw, dt_bias, a_log, d_skip, states, w_out, w_in):
    tokens_here, inner_here = x_in.shape
    group_heads = dt_raw.shape[0]
    head_dim = inner_here // group_heads
    state_dim = b_in.shape[1]
    blocks = lax.axis_size(SEQ)
    y = lax.axis_index("y")
    entry_state = states[0]

    w_out_y = lax.all_to_all(regrouped(w_out), "y", 0, 0)
    near = lax.all_gather(out_grad, "zh", axis=1, tiled=True)
    head_parts = lax.all_to_all(partial_products(near, w_out_y), "y", 0, 0)

    decay_rate = jnp.exp(a_log)
    step_size = jax.nn.softplus(dt_raw + dt_bias[:, None])
    log_step = -decay_rate[:, None] * step_size
    positions = jnp.arange(tokens_here)
    upto = (positions[:, None] <= positions[None, :]).astype(f32)
    cumlog = jnp.dot(log_step, upto, precision=lax.Precision.HIGHEST)
    rows = jnp.concatenate([cumlog, step_size], axis=0)
    ends = jnp.pad(three_parts(jnp.exp(cumlog[:, -1])), ((0, 0), (0, 5)))
    ends = jnp.broadcast_to(ends[:, None, :, None], (group_heads, blocks // group_heads, 8, state_dim))
    scalars = jnp.pad(jnp.stack([decay_rate, dt_bias], axis=1), ((0, 0), (0, 126)))
    skip = jnp.repeat(d_skip, head_dim)[None]
    w_in_held, head_parts = lax.optimization_barrier((w_in, head_parts))
    quarter = w_in.shape[0] // 4
    pieces = [lax.dynamic_slice_in_dim(w_in_held, lax.rem(y + s, 4) * quarter, quarter) for s in range(1, 4)]
    shift = [[(i, (i + s) % 4) for i in range(4)] for s in range(1, 4)]
    dy, sent = local_states(head_parts, rows, c_in, ends.reshape(blocks, 8, state_dim))
    held = [lax.ppermute(pieces[1], "y", shift[1]), lax.ppermute(pieces[0], "y", shift[0])]
    ahead = suffix_scan(lax.all_to_all(sent, SEQ, 0, 0))
    ahead, dy, piece = lax.optimization_barrier((ahead, dy, pieces[2]))
    held.append(lax.ppermute(piece, "y", shift[2]))
    wide, half, part = intra_terms(dy, x_in, b_in, c_in, entry_state, rows, skip)
    *held, carried, wide = lax.optimization_barrier((*held, lax.all_to_all(ahead, SEQ, 0, 0), wide))
    sent_y, back = x_grads(carried, b_in, wide, half, rows)
    got = lax.all_to_all(sent_y, "y", 0, 0)
    dt_grad, row = dt_terms(back, half, rows, part, carried, entry_state, dt_raw, scalars)
    for flip in (1, 2):
        row = row + lax.ppermute(row, "zl", [(i, i ^ flip) for i in range(4)])
    row, got = lax.optimization_barrier((row, got))
    terms = in_products(y, got, w_in, (held[1], held[0], held[2]))
    row, terms = lax.optimization_barrier((row, terms))
    for axis, flip in (("core", 1), ("x", 1), ("x", 2)):
        row = row + lax.ppermute(row, axis, [(i, i ^ flip) for i in range(lax.axis_size(axis))])
    in_grad, bc_grad = final_sums(lax.all_to_all(terms, "zh", 0, 0), w_in.shape[0] // 16)
    norm_scale = (blocks * tokens_here * head_dim) ** (-0.5)
    param_grad = row[0, : 3 * group_heads].reshape(3, group_heads) * norm_scale
    return (in_grad, bc_grad, dt_grad, param_grad)


def solution(mesh):
    fine = Mesh(mesh.devices.reshape(4, 4, 2, 4, 4), ("x", "zl", "core", "y", "zh"))
    return jax.shard_map(
        shards,
        mesh=fine,
        in_specs=(
            P(SEQ, HEAD),
            P(SEQ, HEAD),
            P(SEQ, None),
            P(SEQ, None),
            P(HEAD, SEQ),
            P(HEAD),
            P(HEAD),
            P(HEAD),
            P(SEQ, HEAD, None),
            P(HEAD, None),
            P(None, HEAD),
        ),
        out_specs=(P(HEAD, SEQ), P(HEAD, SEQ), P(HEAD, SEQ), P(None, HEAD)),
        check_vma=False,
    )
```

time: 223 us -> 161 us (0.72)
  Pallas kernels: 77.8 us -> 21 us
  local copies, waits for them, and re-layouts: 19 us -> 5.5 us
  waiting for transfers between devices: 29 us -> 36.1 us
    pallas_call x1, Pallas kernels: 64.7 us -> 2.62 us  [regrouped(): pl.pallas_call(regroup_kernel, in_specs=[pl.BlockSpec(memory_space=pl.ANY...]
    unnamed x68 -> x38, local copies, waits for them, and re-layouts: 15.4 us -> 2.77 us
    pallas_call x5 -> x4, Pallas kernels: 8.19 us -> 13.6 us  [the longest x1 4.89 us: in_products(): pl.pallas_call(in_kernel, in_specs=[pl.BlockSpec(memory_space=pltpu.SMEM)...]
    all_to_all x1, waiting for transfers between devices: 0.74 us -> 5.01 us  [shards(): head_parts = lax.all_to_all(partial_products(near, w_out_y), 'y', 0, 0)]
    ppermute x1, waiting for transfers between devices: 1.43 us -> 4.26 us  [shards(): lax.ppermute(pieces[0], 'y', shift[0])]
  transfers between devices with their start and end apart: 14 -> 14, of which waited for: 9 -> 9; matrix products, arithmetic and copies ran while one was open for 2% -> 2% of each run, Pallas kernels for 2% -> 4%
where the time goes in v4:
time: 161 us; the launch traced here: 160 us
  starting transfers between devices  63.5 us (39%)
  waiting for transfers between devices  36.1 us (22%)
  blocking collectives  32 us (20%)
  Pallas kernels  21 us (13%)
  local copies, waits for them, and re-layouts  5.5 us (3%)
    all_gather x1, blocking collectives, shards(): near = lax.all_gather(out_grad, 'zh', axis=1, tiled=True)  32 us
    all_to_all x1, waiting for transfers between devices, shards(): lax.all_to_all(terms, 'zh', 0, 0)  13.8 us
    ppermute x3, starting transfers between devices, shards(): lax.ppermute(row, axis, [(i, i ^ flip) for i in range(lax.axis_size(axis))])  7.91 us
    all_to_all x1, starting transfers between devices, shards(): lax.all_to_all(ahead, SEQ, 0, 0)  7.7 us
    ppermute x3, waiting for transfers between devices, shards(): lax.ppermute(row, axis, [(i, i ^ flip) for i in range(lax.axis_size(axis))])  7.41 us
    all_to_all x1, starting transfers between devices, shards(): lax.all_to_all(terms, 'zh', 0, 0)  7.16 us
    all_to_all x1, starting transfers between devices, shards(): ahead = suffix_scan(lax.all_to_all(sent, SEQ, 0, 0))  6.99 us
    ppermute x2, starting transfers between devices, shards(): row = row + lax.ppermute(row, 'zl', [(i, i ^ flip) for i in range(4)])  6.73 us
  transfers between devices with their start and end apart: 14, of which 9 were waited for; matrix products, arithmetic and copies ran while one was open for 2% of the time, Pallas kernels for 4%

profile of v4, /device:TPU:54, one launch (start us, length us, event | category | flops | bytes accessed | tf_op | source)
XLA Modules:
  0.0 159.5 jit_solution(1663753082962514590)
XLA Ops:
  0.6 2.6 %shard_map.138 = bf16[4,256,1024]{2,1,0:T(8,128)(2,1)} custom-call(bf16[256,4096]{1,0:T(8,128)(2,1)} %w_ref.1), custom_call_target="tpu_custom_call" | custom-call | bytes 4194304 | tf_op jit(solution)/shard_map/pallas_call | solution.py:74
  3.3 4.9 %all-to-all-start = ((bf16[4,256,1024]{2,1,0:T(8,128)(2,1)}), bf16[4,256,1024]{2,1,0:T(8,128)(2,1)S(1)}, u32[]{:S(2)}, u32[]{:S(2)}) async-start(bf16[4,256,1024]{2,1,0:T(8,128)(2,1)} %shard_map.138), calls=%async_computation | async-start | bytes 4194304 | tf_op jit(solution)/shard_map/all_to_all | solution.py:389
  8.3 32.0 %all_gather.3.near_ref = bf16[256,1024]{1,0:T(8,128)(2,1)S(1)} all-gather(bf16[256,256]{1,0:T(8,128)(2,1)S(1)} %copy-done.15), channel_id=1, replica_groups=mesh['x'=4,'zl'=4,'core'=2,'y'=4,'zh'=4] {'zh'}, dimensions={1}, use_global_device_ids=true | all-gather | bytes 655360 | tf_op jit(solution)/shard_map/all_gather | solution.py:390
  40.6 2.4 %shard_map.139 = bf16[4,256,256]{2,1,0:T(8,128)(2,1)} custom-call(bf16[256,1024]{1,0:T(8,128)(2,1)S(1)} %all_gather.3.near_ref, bf16[4,256,1024]{2,1,0:T(8,128)(2,1)S(1)} %all-to-all-done.w_ref), custom_call_target="tpu_custom_call" | custom-call | flops 536870912 | bytes 4194304 | tf_op jit(solution)/shard_map/pallas_call | solution.py:95
  43.0 4.9 %all-to-all-start.1 = ((bf16[4,256,256]{2,1,0:T(8,128)(2,1)}), bf16[4,256,256]{2,1,0:T(8,128)(2,1)S(1)}, u32[]{:S(2)}, u32[]{:S(2)}) async-start(bf16[4,256,256]{2,1,0:T(8,128)(2,1)} %shard_map.139), calls=%async_computation.1 | async-start | bytes 1048576 | tf_op jit(solution)/shard_map/all_to_all | solution.py:391
  48.0 5.0 %all-to-all-done.1.parts_ref = bf16[4,256,256]{2,1,0:T(8,128)(2,1)S(1)} async-done(((bf16[4,256,256]{2,1,0:T(8,128)(2,1)}), bf16[4,256,256]{2,1,0:T(8,128)(2,1)S(1)}, u32[]{:S(2)}, u32[]{:S(2)}) %all-to-all-start.1) | async-done | bytes 524320 | tf_op jit(solution)/shard_map/all_to_all | solution.py:391
  54.0 7.0 %all-to-all-start.2 = ((bf16[32,16,128]{2,1,0:T(8,128)(2,1)}), bf16[32,16,128]{2,1,0:T(8,128)(2,1)S(1)}, u32[]{:S(2)}, u32[]{:S(2)}) async-start(bf16[32,16,128]{2,1,0:T(8,128)(2,1)} %get-tuple-element.31), calls=%async_computation.2 | async-start | bytes 262144 | tf_op jit(solution)/shard_map/all_to_all | solution.py:410
  61.1 1.1 constant_dynamic-slice_fusion
  62.2 5.0 %collective-permute-start = (bf16[1024,256]{1,0:T(8,128)(2,1)}, bf16[1024,256]{1,0:T(8,128)(2,1)S(1)}, u32[]{:S(2)}, u32[]{:S(2)}) collective-permute-start(bf16[1024,256]{1,0:T(8,128)(2,1)} %get-tuple-element.56), channel_id=1, source_target_pairs={{0,8},{4,12},{8,0},{12,4},{1,9},{5,13},{9,1},{13,5},{2,10},{6,14},... | collective-permute-start | bytes 1572872 | tf_op jit(solution)/shard_map/ppermute | solution.py:409
  67.2 3.1 %collective-permute-start.1 = (bf16[1024,256]{1,0:T(8,128)(2,1)}, bf16[1024,256]{1,0:T(8,128)(2,1)S(1)}, u32[]{:S(2)}, u32[]{:S(2)}) collective-permute-start(bf16[1024,256]{1,0:T(8,128)(2,1)} %get-tuple-element.55), channel_id=1, source_target_pairs={{0,4},{4,8},{8,12},{12,0},{1,5},{5,9},{9,13},{13,1},{2,6},{6,10},{... | collective-permute-start | bytes 1572872 | tf_op jit(solution)/shard_map/ppermute | solution.py:409
  71.0 2.8 %collective-permute-start.2 = (bf16[1024,256]{1,0:T(8,128)(2,1)S(1)}, bf16[1024,256]{1,0:T(8,128)(2,1)S(1)}, u32[]{:S(2)}, u32[]{:S(2)}) collective-permute-start(bf16[1024,256]{1,0:T(8,128)(2,1)S(1)} %get-tuple-element.33), channel_id=1, source_target_pairs={{0,12},{4,0},{8,4},{12,8},{1,13},{5,1},{9,5},{13,9},{2,14},{6,2},{... | collective-permute-start | bytes 1572872 | tf_op jit(solution)/shard_map/ppermute | solution.py:412
  73.7 7.7 %all-to-all-start.3 = ((f32[32,8,128]{2,1,0:T(8,128)}), f32[32,8,128]{2,1,0:T(8,128)S(1)}, u32[]{:S(2)}, u32[]{:S(2)}) async-start(f32[32,8,128]{2,1,0:T(8,128)} %shard_map.141), calls=%async_computation.3 | async-start | bytes 262144 | tf_op jit(solution)/shard_map/all_to_all | solution.py:414
  82.2 4.6 %shard_map.142 = (f32[384,256]{1,0:T(8,128)}, bf16[384,256]{1,0:T(8,128)(2,1)}, f32[16,256]{1,0:T(8,128)}) custom-call(bf16[256,256]{1,0:T(8,128)(2,1)} %get-tuple-element.35.dy_ref, bf16[256,256]{1,0:T(8,128)(2,1)} %x_ref.1, bf16[256,128]{1,0:T(8,128)(2,1)} %b_ref.3, bf16[256,128]{1,0:T(8,128)(2,1)} %c_ref.3, bf16[256,128]{1,0:T(8,128)(2,1)} %bitcast.7, ...), custom_call_target="tpu_custom_call" | custom-call | flops 234881024 | bytes 2097152 | tf_op jit(solution)/shard_map/pallas_call | solution.py:209
  86.8 4.3 %collective-permute-done.1.refs_0_ = bf16[1024,256]{1,0:T(8,128)(2,1)S(1)} collective-permute-done((bf16[1024,256]{1,0:T(8,128)(2,1)}, bf16[1024,256]{1,0:T(8,128)(2,1)S(1)}, u32[]{:S(2)}, u32[]{:S(2)}) %collective-permute-start.1) | collective-permute-done | bytes 524320 | tf_op jit(solution)/shard_map/ppermute | solution.py:409
  91.8 3.2 %shard_map.143 = (bf16[4,320,256]{2,1,0:T(8,128)(2,1)}, f32[256,256]{1,0:T(8,128)}) custom-call(f32[32,8,128]{2,1,0:T(8,128)} %copy-done, bf16[256,128]{1,0:T(8,128)(2,1)} %b_ref.3, f32[384,256]{1,0:T(8,128)} %get-tuple-element.38.wide_hbm, bf16[384,256]{1,0:T(8,128)(2,1)} %get-tuple-element.39.half_hbm.half_ref, f32[8,256]{1,0:T(8,128)} %copy-done.4), custom_call_target="tpu_custom_call" | custom-call | flops 33554432 | bytes 2097152 | tf_op jit(solution)/shard_map/pallas_call | solution.py:290
  95.0 6.3 %all-to-all-start.4 = ((bf16[4,320,256]{2,1,0:T(8,128)(2,1)}), bf16[4,320,256]{2,1,0:T(8,128)(2,1)S(1)}, u32[]{:S(2)}, u32[]{:S(2)}) async-start(bf16[4,320,256]{2,1,0:T(8,128)(2,1)} %get-tuple-element.43), calls=%async_computation.4 | async-start | bytes 1310720 | tf_op jit(solution)/shard_map/all_to_all | solution.py:416
  101.6 0.9 copy-done.1
  102.5 0.9 copy-done.3
  103.4 0.9 shard_map.144
  104.3 2.4 %collective-permute-start.3 = (f32[1,128]{1,0:T(1,128)S(1)}, f32[1,128]{1,0:T(1,128)S(1)}, u32[]{:S(2)}, u32[]{:S(2)}) collective-permute-start(f32[1,128]{1,0:T(1,128)S(1)} %get-tuple-element.42), channel_id=1, source_target_pairs={{0,32},{32,0},{64,96},{96,64},{1,33},{33,1},{65,97},{97,65},{2,34}... | collective-permute-start | bytes 1544 | tf_op jit(solution)/shard_map/ppermute | solution.py:419
  106.8 3.0 %collective-permute-done.3 = f32[1,128]{1,0:T(1,128)S(1)} collective-permute-done((f32[1,128]{1,0:T(1,128)S(1)}, f32[1,128]{1,0:T(1,128)S(1)}, u32[]{:S(2)}, u32[]{:S(2)}) %collective-permute-start.3) | collective-permute-done | bytes 544 | tf_op jit(solution)/shard_map/ppermute | solution.py:419
  109.7 4.3 %collective-permute-start.4 = (f32[1,128]{1,0:T(1,128)S(1)}, f32[1,128]{1,0:T(1,128)S(1)}, u32[]{:S(2)}, u32[]{:S(2)}) collective-permute-start(f32[1,128]{1,0:T(1,128)S(1)} %add.58), channel_id=1, source_target_pairs={{0,64},{32,96},{64,0},{96,32},{1,65},{33,97},{65,1},{97,33},{2,66}... | collective-permute-start | bytes 1544 | tf_op jit(solution)/shard_map/ppermute | solution.py:419
  114.0 2.0 %collective-permute-done.4 = f32[1,128]{1,0:T(1,128)S(1)} collective-permute-done((f32[1,128]{1,0:T(1,128)S(1)}, f32[1,128]{1,0:T(1,128)S(1)}, u32[]{:S(2)}, u32[]{:S(2)}) %collective-permute-start.4) | collective-permute-done | bytes 544 | tf_op jit(solution)/shard_map/ppermute | solution.py:419
  116.9 4.9 %shard_map.145 = bf16[4,272,256]{2,1,0:T(8,128)(2,1)} custom-call(s32[1]{0:T(128)} %bitcast.4.y_ref, bf16[4,320,256]{2,1,0:T(8,128)(2,1)} %copy-done.11, bf16[4096,256]{1,0:T(8,128)(2,1)} %own_hbm.1, bf16[1024,256]{1,0:T(8,128)(2,1)} %copy-done.13, bf16[1024,256]{1,0:T(8,128)(2,1)} %copy-done.12, bf16[1024,256]{1,0:T(8,128)(2,1)} %copy-done.14), custom_call_target="tpu_custom_call" | custom-call | flops 536870912 | bytes 4194304 | tf_op jit(solution)/shard_map/pallas_call | solution.py:341
  121.8 7.2 %all-to-all-start.5 = ((bf16[4,272,256]{2,1,0:T(8,128)(2,1)}), bf16[4,272,256]{2,1,0:T(8,128)(2,1)S(1)}, u32[]{:S(2)}, u32[]{:S(2)}) async-start(bf16[4,272,256]{2,1,0:T(8,128)(2,1)} %shard_map.145), calls=%async_computation.5 | async-start | bytes 1114112 | tf_op jit(solution)/shard_map/all_to_all | solution.py:425
  129.0 1.9 %collective-permute-start.5 = (f32[1,128]{1,0:T(1,128)S(1)}, f32[1,128]{1,0:T(1,128)S(1)}, u32[]{:S(2)}, u32[]{:S(2)}) collective-permute-start(f32[1,128]{1,0:T(1,128)S(1)} %add.59), channel_id=1, source_target_pairs={{0,16},{16,0},{1,17},{17,1},{2,18},{18,2},{3,19},{19,3},{4,20},{20... | collective-permute-start | bytes 1544 | tf_op jit(solution)/shard_map/ppermute | solution.py:424
  130.9 1.1 collective-permute-done.5
  132.0 2.7 %collective-permute-start.6 = (f32[1,128]{1,0:T(1,128)S(1)}, f32[1,128]{1,0:T(1,128)S(1)}, u32[]{:S(2)}, u32[]{:S(2)}) collective-permute-start(f32[1,128]{1,0:T(1,128)S(1)} %add.60), channel_id=1, source_target_pairs={{0,128},{128,0},{256,384},{384,256},{1,129},{129,1},{257,385},{385... | collective-permute-start | bytes 1544 | tf_op jit(solution)/shard_map/ppermute | solution.py:424
  134.7 2.7 %collective-permute-done.6 = f32[1,128]{1,0:T(1,128)S(1)} collective-permute-done((f32[1,128]{1,0:T(1,128)S(1)}, f32[1,128]{1,0:T(1,128)S(1)}, u32[]{:S(2)}, u32[]{:S(2)}) %collective-permute-start.6) | collective-permute-done | bytes 544 | tf_op jit(solution)/shard_map/ppermute | solution.py:424
  137.4 3.3 %collective-permute-start.7 = (f32[1,128]{1,0:T(1,128)S(1)}, f32[1,128]{1,0:T(1,128)S(1)}, u32[]{:S(2)}, u32[]{:S(2)}) collective-permute-start(f32[1,128]{1,0:T(1,128)S(1)} %add.61), channel_id=1, source_target_pairs={{0,256},{128,384},{256,0},{384,128},{1,257},{129,385},{257,1},{385... | collective-permute-start | bytes 1544 | tf_op jit(solution)/shard_map/ppermute | solution.py:424
  140.7 3.6 %collective-permute-done.7 = f32[1,128]{1,0:T(1,128)S(1)} collective-permute-done((f32[1,128]{1,0:T(1,128)S(1)}, f32[1,128]{1,0:T(1,128)S(1)}, u32[]{:S(2)}, u32[]{:S(2)}) %collective-permute-start.7) | collective-permute-done | bytes 544 | tf_op jit(solution)/shard_map/ppermute | solution.py:424
  145.0 13.8 %all-to-all-done.5.terms_ref = bf16[4,272,256]{2,1,0:T(8,128)(2,1)S(1)} async-done(((bf16[4,272,256]{2,1,0:T(8,128)(2,1)}), bf16[4,272,256]{2,1,0:T(8,128)(2,1)S(1)}, u32[]{:S(2)}, u32[]{:S(2)}) %all-to-all-start.5) | async-done | bytes 557088 | tf_op jit(solution)/shard_map/all_to_all | solution.py:425
  (65 shorter events, 6.1 us)
Async XLA Ops:
  3.3 5.0 %copy-start.15 = (bf16[256,256]{1,0:T(8,128)(2,1)S(1)}, bf16[256,256]{1,0:T(8,128)(2,1)}, u32[]{:S(2)}) copy-start(bf16[256,256]{1,0:T(8,128)(2,1)} %param.11) | copy-start | bytes 393220
  3.3 37.0 %copy-start.18 = (f32[4]{0:T(128)S(1)}, f32[4]{0:T(128)}, u32[]{:S(2)}) copy-start(f32[4]{0:T(128)} %param.17) | copy-start | bytes 52
  3.3 37.0 %copy-start.8 = (f32[4,256]{1,0:T(4,128)S(1)}, f32[4,256]{1,0:T(4,128)}, u32[]{:S(2)}) copy-start(f32[4,256]{1,0:T(4,128)} %raw_ref.1) | copy-start | bytes 12292
  3.3 37.0 %copy-start.16 = (f32[4]{0:T(128)S(1)}, f32[4]{0:T(128)}, u32[]{:S(2)}) copy-start(f32[4]{0:T(128)} %param.16) | copy-start | bytes 52
  3.3 37.3 %all-to-all-start = ((bf16[4,256,1024]{2,1,0:T(8,128)(2,1)}), bf16[4,256,1024]{2,1,0:T(8,128)(2,1)S(1)}, u32[]{:S(2)}, u32[]{:S(2)}) async-start(bf16[4,256,1024]{2,1,0:T(8,128)(2,1)} %shard_map.138), calls=%async_computation | async-start | bytes 4194304 | tf_op jit(solution)/shard_map/all_to_all | solution.py:389
  40.6 12.5 %copy-start.6 = (bf16[256,128]{1,0:T(8,128)(2,1)S(1)}, bf16[256,128]{1,0:T(8,128)(2,1)}, u32[]{:S(2)}) copy-start(bf16[256,128]{1,0:T(8,128)(2,1)} %c_ref.3) | copy-start | bytes 196612
  43.0 18.1 %copy-start.10 = (bf16[4096,256]{1,0:T(8,128)(2,1)S(1)}, bf16[4096,256]{1,0:T(8,128)(2,1)}, u32[]{:S(2)}) copy-start(bf16[4096,256]{1,0:T(8,128)(2,1)} %own_hbm.1) | copy-start | bytes 6291460
  43.0 10.0 %all-to-all-start.1 = ((bf16[4,256,256]{2,1,0:T(8,128)(2,1)}), bf16[4,256,256]{2,1,0:T(8,128)(2,1)S(1)}, u32[]{:S(2)}, u32[]{:S(2)}) async-start(bf16[4,256,256]{2,1,0:T(8,128)(2,1)} %shard_map.139), calls=%async_computation.1 | async-start | bytes 1048576 | tf_op jit(solution)/shard_map/all_to_all | solution.py:391
  48.0 14.1 %copy-start.4 = (f32[8,256]{1,0:T(8,128)}, f32[8,256]{1,0:T(8,128)S(1)}, u32[]{:S(2)}) copy-start(f32[8,256]{1,0:T(8,128)S(1)} %pad_maximum_fusion.rows_ref) | copy-start | bytes 24580
  54.0 27.4 %copy-start.17 = (f32[4]{0:T(128)S(1)}, f32[4]{0:T(128)}, u32[]{:S(2)}) copy-start(f32[4]{0:T(128)} %param.18) | copy-start | bytes 52
  54.0 16.2 %all-to-all-start.2 = ((bf16[32,16,128]{2,1,0:T(8,128)(2,1)}), bf16[32,16,128]{2,1,0:T(8,128)(2,1)S(1)}, u32[]{:S(2)}, u32[]{:S(2)}) async-start(bf16[32,16,128]{2,1,0:T(8,128)(2,1)} %get-tuple-element.31), calls=%async_computation.2 | async-start | bytes 262144 | tf_op jit(solution)/shard_map/all_to_all | solution.py:410
  62.1 39.4 %copy-start.7 = (bf16[1,256,128]{2,1,0:T(8,128)(2,1)S(1)}, bf16[1,256,128]{2,1,0:T(8,128)(2,1)}, u32[]{:S(2)}) copy-start(bf16[1,256,128]{2,1,0:T(8,128)(2,1)} %param.19) | copy-start | bytes 196612
  62.1 39.4 %copy-start.5 = (f32[8,256]{1,0:T(8,128)S(1)}, f32[8,256]{1,0:T(8,128)}, u32[]{:S(2)}) copy-start(f32[8,256]{1,0:T(8,128)} %copy-done.4) | copy-start | bytes 24580
  62.2 24.7 %collective-permute-start = (bf16[1024,256]{1,0:T(8,128)(2,1)}, bf16[1024,256]{1,0:T(8,128)(2,1)S(1)}, u32[]{:S(2)}, u32[]{:S(2)}) collective-permute-start(bf16[1024,256]{1,0:T(8,128)(2,1)} %get-tuple-element.56), channel_id=1, source_target_pairs={{0,8},{4,12},{8,0},{12,4},{1,9},{5,13},{9,1},{13,5},{2,10},{6,14},... | collective-permute-start | bytes 1572872 | tf_op jit(solution)/shard_map/ppermute | solution.py:409
  67.2 23.9 %collective-permute-start.1 = (bf16[1024,256]{1,0:T(8,128)(2,1)}, bf16[1024,256]{1,0:T(8,128)(2,1)S(1)}, u32[]{:S(2)}, u32[]{:S(2)}) collective-permute-start(bf16[1024,256]{1,0:T(8,128)(2,1)} %get-tuple-element.55), channel_id=1, source_target_pairs={{0,4},{4,8},{8,12},{12,0},{1,5},{5,9},{9,13},{13,1},{2,6},{6,10},{... | collective-permute-start | bytes 1572872 | tf_op jit(solution)/shard_map/ppermute | solution.py:409
  71.0 20.8 %collective-permute-start.2 = (bf16[1024,256]{1,0:T(8,128)(2,1)S(1)}, bf16[1024,256]{1,0:T(8,128)(2,1)S(1)}, u32[]{:S(2)}, u32[]{:S(2)}) collective-permute-start(bf16[1024,256]{1,0:T(8,128)(2,1)S(1)} %get-tuple-element.33), channel_id=1, source_target_pairs={{0,12},{4,0},{8,4},{12,8},{1,13},{5,1},{9,5},{13,9},{2,14},{6,2},{... | collective-permute-start | bytes 1572872 | tf_op jit(solution)/shard_map/ppermute | solution.py:412
  73.7 17.4 %all-to-all-start.3 = ((f32[32,8,128]{2,1,0:T(8,128)}), f32[32,8,128]{2,1,0:T(8,128)S(1)}, u32[]{:S(2)}, u32[]{:S(2)}) async-start(f32[32,8,128]{2,1,0:T(8,128)} %shard_map.141), calls=%async_computation.3 | async-start | bytes 262144 | tf_op jit(solution)/shard_map/all_to_all | solution.py:414
  86.8 14.7 %copy-start.2 = (bf16[384,256]{1,0:T(8,128)(2,1)S(1)}, bf16[384,256]{1,0:T(8,128)(2,1)}, u32[]{:S(2)}) copy-start(bf16[384,256]{1,0:T(8,128)(2,1)} %get-tuple-element.39.half_hbm.half_ref) | copy-start | bytes 589828
  86.8 14.8 %copy-start.9 = (f32[16,256]{1,0:T(8,128)S(1)}, f32[16,256]{1,0:T(8,128)}, u32[]{:S(2)}) copy-start(f32[16,256]{1,0:T(8,128)} %get-tuple-element.41.part_ref) | copy-start | bytes 49156
  86.8 29.3 %copy-start.12 = (bf16[1024,256]{1,0:T(8,128)(2,1)}, bf16[1024,256]{1,0:T(8,128)(2,1)S(1)}, u32[]{:S(2)}) copy-start(bf16[1024,256]{1,0:T(8,128)(2,1)S(1)} %collective-permute-done.refs_1_) | copy-start | bytes 1572868
  91.1 25.0 %copy-start.13 = (bf16[1024,256]{1,0:T(8,128)(2,1)}, bf16[1024,256]{1,0:T(8,128)(2,1)S(1)}, u32[]{:S(2)}) copy-start(bf16[1024,256]{1,0:T(8,128)(2,1)S(1)} %collective-permute-done.1.refs_0_) | copy-start | bytes 1572868
  91.7 24.4 %copy-start.14 = (bf16[1024,256]{1,0:T(8,128)(2,1)}, bf16[1024,256]{1,0:T(8,128)(2,1)S(1)}, u32[]{:S(2)}) copy-start(bf16[1024,256]{1,0:T(8,128)(2,1)S(1)} %collective-permute-done.2.refs_2_) | copy-start | bytes 1572868
  95.0 21.1 %all-to-all-start.4 = ((bf16[4,320,256]{2,1,0:T(8,128)(2,1)}), bf16[4,320,256]{2,1,0:T(8,128)(2,1)S(1)}, u32[]{:S(2)}, u32[]{:S(2)}) async-start(bf16[4,320,256]{2,1,0:T(8,128)(2,1)} %get-tuple-element.43), calls=%async_computation.4 | async-start | bytes 1310720 | tf_op jit(solution)/shard_map/all_to_all | solution.py:416
  101.6 0.9 copy-start.1
  102.5 0.9 copy-start.3
  104.3 5.4 %collective-permute-start.3 = (f32[1,128]{1,0:T(1,128)S(1)}, f32[1,128]{1,0:T(1,128)S(1)}, u32[]{:S(2)}, u32[]{:S(2)}) collective-permute-start(f32[1,128]{1,0:T(1,128)S(1)} %get-tuple-element.42), channel_id=1, source_target_pairs={{0,32},{32,0},{64,96},{96,64},{1,33},{33,1},{65,97},{97,65},{2,34}... | collective-permute-start | bytes 1544 | tf_op jit(solution)/shard_map/ppermute | solution.py:419
  109.7 6.3 %collective-permute-start.4 = (f32[1,128]{1,0:T(1,128)S(1)}, f32[1,128]{1,0:T(1,128)S(1)}, u32[]{:S(2)}, u32[]{:S(2)}) collective-permute-start(f32[1,128]{1,0:T(1,128)S(1)} %add.58), channel_id=1, source_target_pairs={{0,64},{32,96},{64,0},{96,32},{1,65},{33,97},{65,1},{97,33},{2,66}... | collective-permute-start | bytes 1544 | tf_op jit(solution)/shard_map/ppermute | solution.py:419
  116.1 0.8 copy-start.11
  121.8 37.0 %all-to-all-start.5 = ((bf16[4,272,256]{2,1,0:T(8,128)(2,1)}), bf16[4,272,256]{2,1,0:T(8,128)(2,1)S(1)}, u32[]{:S(2)}, u32[]{:S(2)}) async-start(bf16[4,272,256]{2,1,0:T(8,128)(2,1)} %shard_map.145), calls=%async_computation.5 | async-start | bytes 1114112 | tf_op jit(solution)/shard_map/all_to_all | solution.py:425
  129.0 3.0 %collective-permute-start.5 = (f32[1,128]{1,0:T(1,128)S(1)}, f32[1,128]{1,0:T(1,128)S(1)}, u32[]{:S(2)}, u32[]{:S(2)}) collective-permute-start(f32[1,128]{1,0:T(1,128)S(1)} %add.59), channel_id=1, source_target_pairs={{0,16},{16,0},{1,17},{17,1},{2,18},{18,2},{3,19},{19,3},{4,20},{20... | collective-permute-start | bytes 1544 | tf_op jit(solution)/shard_map/ppermute | solution.py:424
  132.0 5.4 %collective-permute-start.6 = (f32[1,128]{1,0:T(1,128)S(1)}, f32[1,128]{1,0:T(1,128)S(1)}, u32[]{:S(2)}, u32[]{:S(2)}) collective-permute-start(f32[1,128]{1,0:T(1,128)S(1)} %add.60), channel_id=1, source_target_pairs={{0,128},{128,0},{256,384},{384,256},{1,129},{129,1},{257,385},{385... | collective-permute-start | bytes 1544 | tf_op jit(solution)/shard_map/ppermute | solution.py:424
  137.4 6.9 %collective-permute-start.7 = (f32[1,128]{1,0:T(1,128)S(1)}, f32[1,128]{1,0:T(1,128)S(1)}, u32[]{:S(2)}, u32[]{:S(2)}) collective-permute-start(f32[1,128]{1,0:T(1,128)S(1)} %add.61), channel_id=1, source_target_pairs={{0,256},{128,384},{256,0},{384,128},{1,257},{129,385},{257,1},{385... | collective-permute-start | bytes 1544 | tf_op jit(solution)/shard_map/ppermute | solution.py:424
  (1 other events, 0.7 us)

commit v5 on v4

--- a/solution.py
+++ b/solution.py
@@ -248,7 +248,6 @@
     return pl.pallas_call(
         dt_kernel,
         out_shape=(jax.ShapeDtypeStruct(dt_raw.shape, f32), jax.ShapeDtypeStruct((1, 128), f32)),
-        compiler_params=small(),
         cost_estimate=cost(1 << 22, 1 << 20),
     )(back, half, rows, part, carried, states, dt_raw, scalars)
 
@@ -300,58 +299,34 @@
     )(carried, b_in, wide, half, rows)
 
 
-def in_kernel(y_ref, got_ref, own_hbm, *refs):
-    *held_hbm, out_hbm, w_ref, out_ref, w_sems, out_sems = refs
-    _, _, feats, inner = w_ref.shape
+def in_kernel(y_ref, got_ref, *refs):
+    *w_refs, out_ref = refs
+    quarter, inner = w_refs[0].shape
+    feats = quarter // 4
     rows = out_ref.shape[1] - feats
     y = y_ref[0]
-
-    def fetch(z, s):
-        at = pl.multiple_of((4 * y + z) * feats, feats) if s == 0 else z * feats
-        source = own_hbm if s == 0 else held_hbm[s - 1]
-        return pltpu.make_async_copy(source.at[pl.ds(at, feats)], w_ref.at[z, s], w_sems.at[z, s])
-
-    def store(z):
-        return pltpu.make_async_copy(out_ref.at[z], out_hbm.at[z], out_sems.at[z])
-
-    for z in range(4):
-        for s in range(4):
-            fetch(z, s).start()
+    x_grad = jnp.concatenate([got_ref[lax.rem(y + 4 - s, 4), :inner] for s in range(4)], axis=0)
     for z in range(4):
         at = slice(inner + z * rows, inner + (z + 1) * rows)
         bc = got_ref[0, at].astype(f32)
         for other in range(1, 4):
             bc = bc + got_ref[other, at].astype(f32)
         out_ref[z, feats:] = bc.astype(bf16)
-        total = jnp.zeros((feats, got_ref.shape[2]), f32)
-        for s in range(4):
-            fetch(z, s).wait()
-            total = total + jnp.dot(w_ref[z, s], got_ref[lax.rem(y + 4 - s, 4), :inner], preferred_element_type=f32)
-        out_ref[z, :feats] = total.astype(bf16)
-        store(z).start()
-    for z in range(4):
-        store(z).wait()
-
-
-def in_products(y, got, w_in, held):
-    features, inner = w_in.shape
+        w = jnp.concatenate([w_ref[z * feats:(z + 1) * feats] for w_ref in w_refs], axis=1)
+        out_ref[z, :feats] = jnp.dot(w, x_grad, preferred_element_type=f32).astype(bf16)
+
+
+def in_products(y, got, pieces):
+    quarter, inner = pieces[0].shape
     _, height, tokens = got.shape
-    feats, rows = features // 16, (height - inner) // 4
-    out = (4, feats + rows, tokens)
+    feats, rows = quarter // 4, (height - inner) // 4
     return pl.pallas_call(
         in_kernel,
-        in_specs=[pl.BlockSpec(memory_space=pltpu.SMEM), pl.BlockSpec(memory_space=pltpu.VMEM)]
-        + [pl.BlockSpec(memory_space=pltpu.HBM)] * 4,
-        out_specs=pl.BlockSpec(memory_space=pltpu.HBM),
-        out_shape=jax.ShapeDtypeStruct(out, bf16),
-        scratch_shapes=[
-            pltpu.VMEM((4, 4, feats, inner), w_in.dtype),
-            pltpu.VMEM(out, bf16),
-            pltpu.SemaphoreType.DMA((4, 4)),
-            pltpu.SemaphoreType.DMA((4,)),
-        ],
-        cost_estimate=cost(8 * features * inner * tokens // 4, 4 << 20),
-    )(y.reshape(1), got, w_in, *held)
+        in_specs=[pl.BlockSpec(memory_space=pltpu.SMEM)] + [pl.BlockSpec(memory_space=pltpu.VMEM)] * 5,
+        out_shape=pltpu.HBM((4, feats + rows, tokens), bf16),
+        compiler_params=small(),
+        cost_estimate=cost(8 * quarter * inner * tokens, 4 << 20),
+    )(y.reshape(1), got, *pieces)
 
 
 def sum_kernel(terms_ref, in_ref, bc_ref):
@@ -388,7 +363,12 @@
 
     w_out_y = lax.all_to_all(regrouped(w_out), "y", 0, 0)
     near = lax.all_gather(out_grad, "zh", axis=1, tiled=True)
-    head_parts = lax.all_to_all(partial_products(near, w_out_y), "y", 0, 0)
+    products = partial_products(near, w_out_y)
+    w_in_held, products = lax.optimization_barrier((w_in, products))
+    quarter = w_in.shape[0] // 4
+    pieces = [lax.dynamic_slice_in_dim(w_in_held, lax.rem(y + s, 4) * quarter, quarter) for s in range(4)]
+    held = [pieces[0]] + [lax.ppermute(pieces[s], "y", [(i, (i + s) % 4) for i in range(4)]) for s in range(1, 4)]
+    head_parts = lax.all_to_all(products, "y", 0, 0)
 
     decay_rate = jnp.exp(a_log)
     step_size = jax.nn.softplus(dt_raw + dt_bias[:, None])
@@ -401,26 +381,19 @@
     ends = jnp.broadcast_to(ends[:, None, :, None], (group_heads, blocks // group_heads, 8, state_dim))
     scalars = jnp.pad(jnp.stack([decay_rate, dt_bias], axis=1), ((0, 0), (0, 126)))
     skip = jnp.repeat(d_skip, head_dim)[None]
-    w_in_held, head_parts = lax.optimization_barrier((w_in, head_parts))
-    quarter = w_in.shape[0] // 4
-    pieces = [lax.dynamic_slice_in_dim(w_in_held, lax.rem(y + s, 4) * quarter, quarter) for s in range(1, 4)]
-    shift = [[(i, (i + s) % 4) for i in range(4)] for s in range(1, 4)]
     dy, sent = local_states(head_parts, rows, c_in, ends.reshape(blocks, 8, state_dim))
-    held = [lax.ppermute(pieces[1], "y", shift[1]), lax.ppermute(pieces[0], "y", shift[0])]
     ahead = suffix_scan(lax.all_to_all(sent, SEQ, 0, 0))
-    ahead, dy, piece = lax.optimization_barrier((ahead, dy, pieces[2]))
-    held.append(lax.ppermute(piece, "y", shift[2]))
+    ahead, dy, held[2] = lax.optimization_barrier((ahead, dy, held[2]))
     wide, half, part = intra_terms(dy, x_in, b_in, c_in, entry_state, rows, skip)
     *held, carried, wide = lax.optimization_barrier((*held, lax.all_to_all(ahead, SEQ, 0, 0), wide))
     sent_y, back = x_grads(carried, b_in, wide, half, rows)
     got = lax.all_to_all(sent_y, "y", 0, 0)
     dt_grad, row = dt_terms(back, half, rows, part, carried, entry_state, dt_raw, scalars)
-    for flip in (1, 2):
-        row = row + lax.ppermute(row, "zl", [(i, i ^ flip) for i in range(4)])
+    row = row + lax.ppermute(row, "zl", [(i, i ^ 1) for i in range(4)])
     row, got = lax.optimization_barrier((row, got))
-    terms = in_products(y, got, w_in, (held[1], held[0], held[2]))
+    terms = in_products(y, got, held)
     row, terms = lax.optimization_barrier((row, terms))
-    for axis, flip in (("core", 1), ("x", 1), ("x", 2)):
+    for axis, flip in (("zl", 2), ("x", 1), ("x", 2), ("core", 1)):
         row = row + lax.ppermute(row, axis, [(i, i ^ flip) for i in range(lax.axis_size(axis))])
     in_grad, bc_grad = final_sums(lax.all_to_all(terms, "zh", 0, 0), w_in.shape[0] // 16)
     norm_scale = (blocks * tokens_here * head_dim) ** (-0.5)

time: 161 us -> 160 us (level)
  the two profiles are of different devices: /device:TPU:54 before, /device:TPU:257 now
where the time goes in v5:
time: 160 us; the launch traced here: 159 us
  starting transfers between devices  86.2 us (54%)
  waiting for transfers between devices  23.5 us (15%)
  blocking collectives  23 us (14%)
  Pallas kernels  18.6 us (12%)
  local copies, waits for them, and re-layouts  4.82 us (3%)
  other arithmetic  1.62 us (1%)
    ppermute x4, starting transfers between devices, shards(): lax.ppermute(row, axis, [(i, i ^ flip) for i in range(lax.axis_size(axis))])  29.7 us
    all_gather x1, blocking collectives, shards(): near = lax.all_gather(out_grad, 'zh', axis=1, tiled=True)  23 us
    all_to_all x1, starting transfers between devices, shards(): lax.all_to_all(terms, 'zh', 0, 0)  15.8 us
    ppermute x3, starting transfers between devices, shards(): lax.ppermute(pieces[s], 'y', [(i, (i + s) % 4) for i in range(4)])  11.3 us
    ppermute x4, waiting for transfers between devices, shards(): lax.ppermute(row, axis, [(i, i ^ flip) for i in range(lax.axis_size(axis))])  11.2 us
    all_to_all x1, starting transfers between devices, shards(): ahead = suffix_scan(lax.all_to_all(sent, SEQ, 0, 0))  9.97 us
    all_to_all x1, starting transfers between devices, shards(): lax.all_to_all(ahead, SEQ, 0, 0)  6.06 us
    pallas_call x1, Pallas kernels, intra_terms(): pl.pallas_call(intra_kernel, out_shape=(pltpu.HBM((height, tokens), f32),...  4.69 us
  transfers between devices with their start and end apart: 14, of which 9 were waited for; matrix products, arithmetic and copies ran while one was open for 4% of the time, Pallas kernels for 5%

profile of v5, /device:TPU:257, one launch (start us, length us, event | category | flops | bytes accessed | tf_op | source)
XLA Modules:
  0.0 158.8 jit_solution(6948926802549126796)
XLA Ops:
  0.6 2.6 %shard_map.138 = bf16[4,256,1024]{2,1,0:T(8,128)(2,1)} custom-call(bf16[256,4096]{1,0:T(8,128)(2,1)} %w_ref.1), custom_call_target="tpu_custom_call" | custom-call | bytes 4194304 | tf_op jit(solution)/shard_map/pallas_call | solution.py:74
  3.3 4.3 %all-to-all-start = ((bf16[4,256,1024]{2,1,0:T(8,128)(2,1)}), bf16[4,256,1024]{2,1,0:T(8,128)(2,1)S(1)}, u32[]{:S(2)}, u32[]{:S(2)}) async-start(bf16[4,256,1024]{2,1,0:T(8,128)(2,1)} %shard_map.138), calls=%async_computation | async-start | bytes 4194304 | tf_op jit(solution)/shard_map/all_to_all | solution.py:364
  8.2 23.0 %all_gather.3.near_ref = bf16[256,1024]{1,0:T(8,128)(2,1)S(1)} all-gather(bf16[256,256]{1,0:T(8,128)(2,1)S(1)} %copy-done.3), channel_id=1, replica_groups=mesh['x'=4,'zl'=4,'core'=2,'y'=4,'zh'=4] {'zh'}, dimensions={1}, use_global_device_ids=true | all-gather | bytes 655360 | tf_op jit(solution)/shard_map/all_gather | solution.py:365
  31.2 1.9 %all-to-all-done.w_ref = bf16[4,256,1024]{2,1,0:T(8,128)(2,1)S(1)} async-done(((bf16[4,256,1024]{2,1,0:T(8,128)(2,1)}), bf16[4,256,1024]{2,1,0:T(8,128)(2,1)S(1)}, u32[]{:S(2)}, u32[]{:S(2)}) %all-to-all-start) | async-done | bytes 2097184 | tf_op jit(solution)/shard_map/all_to_all | solution.py:364
  33.1 2.3 %shard_map.139 = bf16[4,256,256]{2,1,0:T(8,128)(2,1)} custom-call(bf16[256,1024]{1,0:T(8,128)(2,1)S(1)} %all_gather.3.near_ref, bf16[4,256,1024]{2,1,0:T(8,128)(2,1)S(1)} %all-to-all-done.w_ref), custom_call_target="tpu_custom_call" | custom-call | flops 536870912 | bytes 4194304 | tf_op jit(solution)/shard_map/pallas_call | solution.py:95
  35.4 3.5 %all-to-all-start.1 = ((bf16[4,256,256]{2,1,0:T(8,128)(2,1)}), bf16[4,256,256]{2,1,0:T(8,128)(2,1)S(1)}, u32[]{:S(2)}, u32[]{:S(2)}) async-start(bf16[4,256,256]{2,1,0:T(8,128)(2,1)} %shard_map.139), calls=%async_computation.1 | async-start | bytes 1048576 | tf_op jit(solution)/shard_map/all_to_all | solution.py:371
  38.9 2.5 %constant_dynamic-slice_fusion = (bf16[1024,256]{1,0:T(8,128)(2,1)S(1)}, bf16[1024,256]{1,0:T(8,128)(2,1)}, bf16[1024,256]{1,0:T(8,128)(2,1)S(1)}, bf16[1024,256]{1,0:T(8,128)(2,1)S(1)}) fusion(bf16[4096,256]{1,0:T(8,128)(2,1)} %param.21, s32[]{:T(128)S(6)} %select_n.20, s32[]{:T(128)S(6)} %select_n.19, s32[]{:T(128)S(6)} %select_n.17, s32[]{:T(128)S(6)} %select_n.16), kind=kLoop, calls=%fused_computation.18 | loop fusion | bytes 4194320 | tf_op jit(solution)/shard_map/dynamic_slice | solution.py:369
  41.4 4.8 %collective-permute-start.1 = (bf16[1024,256]{1,0:T(8,128)(2,1)}, bf16[1024,256]{1,0:T(8,128)(2,1)S(1)}, u32[]{:S(2)}, u32[]{:S(2)}) collective-permute-start(bf16[1024,256]{1,0:T(8,128)(2,1)} %get-tuple-element.57), channel_id=1, source_target_pairs={{0,8},{4,12},{8,0},{12,4},{1,9},{5,13},{9,1},{13,5},{2,10},{6,14},... | collective-permute-start | bytes 1572872 | tf_op jit(solution)/shard_map/ppermute | solution.py:370
  46.4 0.9 shard_map.140
  47.2 10.0 %all-to-all-start.2 = ((bf16[32,16,128]{2,1,0:T(8,128)(2,1)}), bf16[32,16,128]{2,1,0:T(8,128)(2,1)S(1)}, u32[]{:S(2)}, u32[]{:S(2)}) async-start(bf16[32,16,128]{2,1,0:T(8,128)(2,1)} %get-tuple-element.32), calls=%async_computation.2 | async-start | bytes 262144 | tf_op jit(solution)/shard_map/all_to_all | solution.py:385
  57.2 1.9 %collective-permute-start = (bf16[1024,256]{1,0:T(8,128)(2,1)S(1)}, bf16[1024,256]{1,0:T(8,128)(2,1)S(1)}, u32[]{:S(2)}, u32[]{:S(2)}) collective-permute-start(bf16[1024,256]{1,0:T(8,128)(2,1)S(1)} %get-tuple-element.58), channel_id=1, source_target_pairs={{0,4},{4,8},{8,12},{12,0},{1,5},{5,9},{9,13},{13,1},{2,6},{6,10},{... | collective-permute-start | bytes 1572872 | tf_op jit(solution)/shard_map/ppermute | solution.py:370
  59.1 4.6 %collective-permute-start.2 = (bf16[1024,256]{1,0:T(8,128)(2,1)S(1)}, bf16[1024,256]{1,0:T(8,128)(2,1)S(1)}, u32[]{:S(2)}, u32[]{:S(2)}) collective-permute-start(bf16[1024,256]{1,0:T(8,128)(2,1)S(1)} %get-tuple-element.56), channel_id=1, source_target_pairs={{0,12},{4,0},{8,4},{12,8},{1,13},{5,1},{9,5},{13,9},{2,14},{6,2},{... | collective-permute-start | bytes 1572872 | tf_op jit(solution)/shard_map/ppermute | solution.py:370
  63.7 2.2 %all-to-all-done.2.parts_ref = bf16[32,16,128]{2,1,0:T(8,128)(2,1)S(1)} async-done(((bf16[32,16,128]{2,1,0:T(8,128)(2,1)}), bf16[32,16,128]{2,1,0:T(8,128)(2,1)S(1)}, u32[]{:S(2)}, u32[]{:S(2)}) %all-to-all-start.2) | async-done | bytes 131104 | tf_op jit(solution)/shard_map/all_to_all | solution.py:385
  66.6 6.1 %all-to-all-start.3 = ((f32[32,8,128]{2,1,0:T(8,128)}), f32[32,8,128]{2,1,0:T(8,128)S(1)}, u32[]{:S(2)}, u32[]{:S(2)}) async-start(f32[32,8,128]{2,1,0:T(8,128)} %shard_map.141), calls=%async_computation.3 | async-start | bytes 262144 | tf_op jit(solution)/shard_map/all_to_all | solution.py:388
  73.4 4.7 %shard_map.142 = (f32[384,256]{1,0:T(8,128)}, bf16[384,256]{1,0:T(8,128)(2,1)}, f32[16,256]{1,0:T(8,128)}) custom-call(bf16[256,256]{1,0:T(8,128)(2,1)} %get-tuple-element.36.dy_ref, bf16[256,256]{1,0:T(8,128)(2,1)} %x_ref.1, bf16[256,128]{1,0:T(8,128)(2,1)} %b_ref.3, bf16[256,128]{1,0:T(8,128)(2,1)} %c_ref.3, bf16[256,128]{1,0:T(8,128)(2,1)} %bitcast.7, ...), custom_call_target="tpu_custom_call" | custom-call | flops 234881024 | bytes 2097152 | tf_op jit(solution)/shard_map/pallas_call | solution.py:209
  78.1 3.3 %all-to-all-done.3.carried_ref = f32[32,8,128]{2,1,0:T(8,128)S(1)} async-done(((f32[32,8,128]{2,1,0:T(8,128)}), f32[32,8,128]{2,1,0:T(8,128)S(1)}, u32[]{:S(2)}, u32[]{:S(2)}) %all-to-all-start.3) | async-done | bytes 131104 | tf_op jit(solution)/shard_map/all_to_all | solution.py:388
  82.1 3.0 %shard_map.143 = (bf16[4,320,256]{2,1,0:T(8,128)(2,1)}, f32[256,256]{1,0:T(8,128)}) custom-call(f32[32,8,128]{2,1,0:T(8,128)} %copy-done.2, bf16[256,128]{1,0:T(8,128)(2,1)} %b_ref.3, f32[384,256]{1,0:T(8,128)} %get-tuple-element.39.wide_hbm, bf16[384,256]{1,0:T(8,128)(2,1)} %get-tuple-element.40.half_hbm.half_ref, f32[8,256]{1,0:T(8,128)} %copy-done), custom_call_target="tpu_custom_call" | custom-call | flops 33554432 | bytes 2097152 | tf_op jit(solution)/shard_map/pallas_call | solution.py:289
  85.1 3.5 %all-to-all-start.4 = ((bf16[4,320,256]{2,1,0:T(8,128)(2,1)}), bf16[4,320,256]{2,1,0:T(8,128)(2,1)S(1)}, u32[]{:S(2)}, u32[]{:S(2)}) async-start(bf16[4,320,256]{2,1,0:T(8,128)(2,1)} %get-tuple-element.44), calls=%async_computation.4 | async-start | bytes 1310720 | tf_op jit(solution)/shard_map/all_to_all | solution.py:390
  89.5 2.1 %shard_map.144 = (f32[4,256]{1,0:T(4,128)}, f32[1,128]{1,0:T(1,128)}) custom-call(f32[256,256]{1,0:T(8,128)} %get-tuple-element.41.back_ref, bf16[384,256]{1,0:T(8,128)(2,1)} %get-tuple-element.40.half_hbm.half_ref, f32[8,256]{1,0:T(8,128)} %copy-done, f32[16,256]{1,0:T(8,128)} %get-tuple-element.42.part_ref, f32[32,8,128]{2,1,0:T(8,128)} %copy-done.2, ...), custom_call_target="tpu_custom_call" | custom-call | flops 4194304 | bytes 1048576 | tf_op jit(solution)/shard_map/pallas_call | solution.py:248
  91.5 2.1 %collective-permute-start.3 = (f32[1,128]{1,0:T(1,128)}, f32[1,128]{1,0:T(1,128)S(1)}, u32[]{:S(2)}, u32[]{:S(2)}) collective-permute-start(f32[1,128]{1,0:T(1,128)} %get-tuple-element.43), channel_id=1, source_target_pairs={{0,32},{32,0},{64,96},{96,64},{1,33},{33,1},{65,97},{97,65},{2,34}... | collective-permute-start | bytes 1544 | tf_op jit(solution)/shard_map/ppermute | solution.py:392
  93.7 2.6 %collective-permute-done.3 = f32[1,128]{1,0:T(1,128)S(1)} collective-permute-done((f32[1,128]{1,0:T(1,128)}, f32[1,128]{1,0:T(1,128)S(1)}, u32[]{:S(2)}, u32[]{:S(2)}) %collective-permute-start.3) | collective-permute-done | bytes 544 | tf_op jit(solution)/shard_map/ppermute | solution.py:392
  96.9 2.2 %all-to-all-done.4.got_ref = bf16[4,320,256]{2,1,0:T(8,128)(2,1)S(1)} async-done(((bf16[4,320,256]{2,1,0:T(8,128)(2,1)}), bf16[4,320,256]{2,1,0:T(8,128)(2,1)S(1)}, u32[]{:S(2)}, u32[]{:S(2)}) %all-to-all-start.4) | async-done | bytes 655392 | tf_op jit(solution)/shard_map/all_to_all | solution.py:390
  99.2 1.5 shard_map.145
  100.7 15.8 %all-to-all-start.5 = ((bf16[4,272,256]{2,1,0:T(8,128)(2,1)}), bf16[4,272,256]{2,1,0:T(8,128)(2,1)S(1)}, u32[]{:S(2)}, u32[]{:S(2)}) async-start(bf16[4,272,256]{2,1,0:T(8,128)(2,1)} %shard_map.145), calls=%async_computation.5 | async-start | bytes 1114112 | tf_op jit(solution)/shard_map/all_to_all | solution.py:398
  116.5 2.1 %collective-permute-start.4 = (f32[1,128]{1,0:T(1,128)S(1)}, f32[1,128]{1,0:T(1,128)S(1)}, u32[]{:S(2)}, u32[]{:S(2)}) collective-permute-start(f32[1,128]{1,0:T(1,128)S(1)} %add.62), channel_id=1, source_target_pairs={{0,64},{32,96},{64,0},{96,32},{1,65},{33,97},{65,1},{97,33},{2,66}... | collective-permute-start | bytes 1544 | tf_op jit(solution)/shard_map/ppermute | solution.py:397
  118.5 5.6 %collective-permute-done.4 = f32[1,128]{1,0:T(1,128)S(1)} collective-permute-done((f32[1,128]{1,0:T(1,128)S(1)}, f32[1,128]{1,0:T(1,128)S(1)}, u32[]{:S(2)}, u32[]{:S(2)}) %collective-permute-start.4) | collective-permute-done | bytes 544 | tf_op jit(solution)/shard_map/ppermute | solution.py:397
  124.1 2.1 %collective-permute-start.5 = (f32[1,128]{1,0:T(1,128)S(1)}, f32[1,128]{1,0:T(1,128)S(1)}, u32[]{:S(2)}, u32[]{:S(2)}) collective-permute-start(f32[1,128]{1,0:T(1,128)S(1)} %add.63), channel_id=1, source_target_pairs={{0,128},{128,0},{256,384},{384,256},{1,129},{129,1},{257,385},{385... | collective-permute-start | bytes 1544 | tf_op jit(solution)/shard_map/ppermute | solution.py:397
  126.3 2.4 %collective-permute-done.5 = f32[1,128]{1,0:T(1,128)S(1)} collective-permute-done((f32[1,128]{1,0:T(1,128)S(1)}, f32[1,128]{1,0:T(1,128)S(1)}, u32[]{:S(2)}, u32[]{:S(2)}) %collective-permute-start.5) | collective-permute-done | bytes 544 | tf_op jit(solution)/shard_map/ppermute | solution.py:397
  128.7 3.6 %collective-permute-start.6 = (f32[1,128]{1,0:T(1,128)S(1)}, f32[1,128]{1,0:T(1,128)S(1)}, u32[]{:S(2)}, u32[]{:S(2)}) collective-permute-start(f32[1,128]{1,0:T(1,128)S(1)} %add.64), channel_id=1, source_target_pairs={{0,256},{128,384},{256,0},{384,128},{1,257},{129,385},{257,1},{385... | collective-permute-start | bytes 1544 | tf_op jit(solution)/shard_map/ppermute | solution.py:397
  132.3 2.4 %collective-permute-done.6 = f32[1,128]{1,0:T(1,128)S(1)} collective-permute-done((f32[1,128]{1,0:T(1,128)S(1)}, f32[1,128]{1,0:T(1,128)S(1)}, u32[]{:S(2)}, u32[]{:S(2)}) %collective-permute-start.6) | collective-permute-done | bytes 544 | tf_op jit(solution)/shard_map/ppermute | solution.py:397
  134.8 21.8 %collective-permute-start.7 = (f32[1,128]{1,0:T(1,128)S(1)}, f32[1,128]{1,0:T(1,128)S(1)}, u32[]{:S(2)}, u32[]{:S(2)}) collective-permute-start(f32[1,128]{1,0:T(1,128)S(1)} %add.65), channel_id=1, source_target_pairs={{0,16},{16,0},{1,17},{17,1},{2,18},{18,2},{3,19},{19,3},{4,20},{20... | collective-permute-start | bytes 1544 | tf_op jit(solution)/shard_map/ppermute | solution.py:397
  156.6 0.8 collective-permute-done.7
  (43 shorter events, 5.6 us)
Async XLA Ops:
  3.3 4.4 %copy-start.7 = (f32[4]{0:T(128)S(1)}, f32[4]{0:T(128)}, u32[]{:S(2)}) copy-start(f32[4]{0:T(128)} %param.17) | copy-start | bytes 52
  3.3 4.4 %copy-start.4 = (f32[4,256]{1,0:T(4,128)S(1)}, f32[4,256]{1,0:T(4,128)}, u32[]{:S(2)}) copy-start(f32[4,256]{1,0:T(4,128)} %raw_ref.1) | copy-start | bytes 12292
  3.3 4.4 %copy-start.5 = (f32[4]{0:T(128)S(1)}, f32[4]{0:T(128)}, u32[]{:S(2)}) copy-start(f32[4]{0:T(128)} %param.16) | copy-start | bytes 52
  3.3 4.8 %copy-start.3 = (bf16[256,256]{1,0:T(8,128)(2,1)S(1)}, bf16[256,256]{1,0:T(8,128)(2,1)}, u32[]{:S(2)}) copy-start(bf16[256,256]{1,0:T(8,128)(2,1)} %param.11) | copy-start | bytes 393220
  3.3 29.7 %all-to-all-start = ((bf16[4,256,1024]{2,1,0:T(8,128)(2,1)}), bf16[4,256,1024]{2,1,0:T(8,128)(2,1)S(1)}, u32[]{:S(2)}, u32[]{:S(2)}) async-start(bf16[4,256,1024]{2,1,0:T(8,128)(2,1)} %shard_map.138), calls=%async_computation | async-start | bytes 4194304 | tf_op jit(solution)/shard_map/all_to_all | solution.py:364
  35.4 10.8 %all-to-all-start.1 = ((bf16[4,256,256]{2,1,0:T(8,128)(2,1)}), bf16[4,256,256]{2,1,0:T(8,128)(2,1)S(1)}, u32[]{:S(2)}, u32[]{:S(2)}) async-start(bf16[4,256,256]{2,1,0:T(8,128)(2,1)} %shard_map.139), calls=%async_computation.1 | async-start | bytes 1048576 | tf_op jit(solution)/shard_map/all_to_all | solution.py:371
  38.9 7.4 %copy-start.1 = (bf16[256,128]{1,0:T(8,128)(2,1)S(1)}, bf16[256,128]{1,0:T(8,128)(2,1)}, u32[]{:S(2)}) copy-start(bf16[256,128]{1,0:T(8,128)(2,1)} %c_ref.3) | copy-start | bytes 196612
  38.9 33.8 %copy-start.6 = (f32[4]{0:T(128)S(1)}, f32[4]{0:T(128)}, u32[]{:S(2)}) copy-start(f32[4]{0:T(128)} %param.18) | copy-start | bytes 52
  41.4 25.3 %collective-permute-start.1 = (bf16[1024,256]{1,0:T(8,128)(2,1)}, bf16[1024,256]{1,0:T(8,128)(2,1)S(1)}, u32[]{:S(2)}, u32[]{:S(2)}) collective-permute-start(bf16[1024,256]{1,0:T(8,128)(2,1)} %get-tuple-element.57), channel_id=1, source_target_pairs={{0,8},{4,12},{8,0},{12,4},{1,9},{5,13},{9,1},{13,5},{2,10},{6,14},... | collective-permute-start | bytes 1572872 | tf_op jit(solution)/shard_map/ppermute | solution.py:370
  46.2 27.2 %copy-start = (f32[8,256]{1,0:T(8,128)}, f32[8,256]{1,0:T(8,128)S(1)}, u32[]{:S(2)}) copy-start(f32[8,256]{1,0:T(8,128)S(1)} %pad_maximum_fusion.rows_ref) | copy-start | bytes 24580
  47.2 18.7 %all-to-all-start.2 = ((bf16[32,16,128]{2,1,0:T(8,128)(2,1)}), bf16[32,16,128]{2,1,0:T(8,128)(2,1)S(1)}, u32[]{:S(2)}, u32[]{:S(2)}) async-start(bf16[32,16,128]{2,1,0:T(8,128)(2,1)} %get-tuple-element.32), calls=%async_computation.2 | async-start | bytes 262144 | tf_op jit(solution)/shard_map/all_to_all | solution.py:385
  57.2 20.9 %collective-permute-start = (bf16[1024,256]{1,0:T(8,128)(2,1)S(1)}, bf16[1024,256]{1,0:T(8,128)(2,1)S(1)}, u32[]{:S(2)}, u32[]{:S(2)}) collective-permute-start(bf16[1024,256]{1,0:T(8,128)(2,1)S(1)} %get-tuple-element.58), channel_id=1, source_target_pairs={{0,4},{4,8},{8,12},{12,0},{1,5},{5,9},{9,13},{13,1},{2,6},{6,10},{... | collective-permute-start | bytes 1572872 | tf_op jit(solution)/shard_map/ppermute | solution.py:370
  59.1 19.0 %collective-permute-start.2 = (bf16[1024,256]{1,0:T(8,128)(2,1)S(1)}, bf16[1024,256]{1,0:T(8,128)(2,1)S(1)}, u32[]{:S(2)}, u32[]{:S(2)}) collective-permute-start(bf16[1024,256]{1,0:T(8,128)(2,1)S(1)} %get-tuple-element.56), channel_id=1, source_target_pairs={{0,12},{4,0},{8,4},{12,8},{1,13},{5,1},{9,5},{13,9},{2,14},{6,2},{... | collective-permute-start | bytes 1572872 | tf_op jit(solution)/shard_map/ppermute | solution.py:370
  66.6 14.8 %all-to-all-start.3 = ((f32[32,8,128]{2,1,0:T(8,128)}), f32[32,8,128]{2,1,0:T(8,128)S(1)}, u32[]{:S(2)}, u32[]{:S(2)}) async-start(f32[32,8,128]{2,1,0:T(8,128)} %shard_map.141), calls=%async_computation.3 | async-start | bytes 262144 | tf_op jit(solution)/shard_map/all_to_all | solution.py:388
  81.4 0.7 copy-start.2
  85.1 14.1 %all-to-all-start.4 = ((bf16[4,320,256]{2,1,0:T(8,128)(2,1)}), bf16[4,320,256]{2,1,0:T(8,128)(2,1)S(1)}, u32[]{:S(2)}, u32[]{:S(2)}) async-start(bf16[4,320,256]{2,1,0:T(8,128)(2,1)} %get-tuple-element.44), calls=%async_computation.4 | async-start | bytes 1310720 | tf_op jit(solution)/shard_map/all_to_all | solution.py:390
  91.5 4.8 %collective-permute-start.3 = (f32[1,128]{1,0:T(1,128)}, f32[1,128]{1,0:T(1,128)S(1)}, u32[]{:S(2)}, u32[]{:S(2)}) collective-permute-start(f32[1,128]{1,0:T(1,128)} %get-tuple-element.43), channel_id=1, source_target_pairs={{0,32},{32,0},{64,96},{96,64},{1,33},{33,1},{65,97},{97,65},{2,34}... | collective-permute-start | bytes 1544 | tf_op jit(solution)/shard_map/ppermute | solution.py:392
  100.7 57.4 %all-to-all-start.5 = ((bf16[4,272,256]{2,1,0:T(8,128)(2,1)}), bf16[4,272,256]{2,1,0:T(8,128)(2,1)S(1)}, u32[]{:S(2)}, u32[]{:S(2)}) async-start(bf16[4,272,256]{2,1,0:T(8,128)(2,1)} %shard_map.145), calls=%async_computation.5 | async-start | bytes 1114112 | tf_op jit(solution)/shard_map/all_to_all | solution.py:398
  116.5 7.7 %collective-permute-start.4 = (f32[1,128]{1,0:T(1,128)S(1)}, f32[1,128]{1,0:T(1,128)S(1)}, u32[]{:S(2)}, u32[]{:S(2)}) collective-permute-start(f32[1,128]{1,0:T(1,128)S(1)} %add.62), channel_id=1, source_target_pairs={{0,64},{32,96},{64,0},{96,32},{1,65},{33,97},{65,1},{97,33},{2,66}... | collective-permute-start | bytes 1544 | tf_op jit(solution)/shard_map/ppermute | solution.py:397
  124.1 4.6 %collective-permute-start.5 = (f32[1,128]{1,0:T(1,128)S(1)}, f32[1,128]{1,0:T(1,128)S(1)}, u32[]{:S(2)}, u32[]{:S(2)}) collective-permute-start(f32[1,128]{1,0:T(1,128)S(1)} %add.63), channel_id=1, source_target_pairs={{0,128},{128,0},{256,384},{384,256},{1,129},{129,1},{257,385},{385... | collective-permute-start | bytes 1544 | tf_op jit(solution)/shard_map/ppermute | solution.py:397
  128.7 6.1 %collective-permute-start.6 = (f32[1,128]{1,0:T(1,128)S(1)}, f32[1,128]{1,0:T(1,128)S(1)}, u32[]{:S(2)}, u32[]{:S(2)}) collective-permute-start(f32[1,128]{1,0:T(1,128)S(1)} %add.64), channel_id=1, source_target_pairs={{0,256},{128,384},{256,0},{384,128},{1,257},{129,385},{257,1},{385... | collective-permute-start | bytes 1544 | tf_op jit(solution)/shard_map/ppermute | solution.py:397
  134.8 22.6 %collective-permute-start.7 = (f32[1,128]{1,0:T(1,128)S(1)}, f32[1,128]{1,0:T(1,128)S(1)}, u32[]{:S(2)}, u32[]{:S(2)}) collective-permute-start(f32[1,128]{1,0:T(1,128)S(1)} %add.65), channel_id=1, source_target_pairs={{0,16},{16,0},{1,17},{17,1},{2,18},{18,2},{3,19},{19,3},{4,20},{20... | collective-permute-start | bytes 1544 | tf_op jit(solution)/shard_map/ppermute | solution.py:397

commit v6 on v5

--- a/solution.py
+++ b/solution.py
@@ -86,7 +86,9 @@
 
 
 def partial_kernel(near_ref, w_ref, out_ref):
-    out_ref[0] = dot_last(w_ref[0], near_ref[...]).astype(bf16)
+    groups, inner, depth = w_ref.shape
+    out = dot_last(w_ref[...].reshape(groups * inner, depth), near_ref[...]).astype(bf16)
+    out_ref[...] = out.reshape(out_ref.shape)
 
 
 def partial_products(near, w_mine):
@@ -94,13 +96,7 @@
     tokens = near.shape[0]
     return pl.pallas_call(
         partial_kernel,
-        grid=(groups,),
-        in_specs=[
-            pl.BlockSpec((tokens, depth), lambda g: (0, 0)),
-            pl.BlockSpec((1, inner, depth), lambda g: (g, 0, 0)),
-        ],
-        out_specs=pl.BlockSpec((1, inner, tokens), lambda g: (g, 0, 0)),
-        out_shape=jax.ShapeDtypeStruct((groups, inner, tokens), bf16),
+        out_shape=pltpu.HBM((groups, inner, tokens), bf16),
         compiler_params=small(),
         cost_estimate=cost(2 * groups * tokens * inner * depth, 4 << 20),
     )(near, w_mine)
@@ -163,7 +159,7 @@
     width, tokens = dy_ref.shape
     head_dim = width // 4
     cum = rows_ref[:4]
-    columns = rows_ref[...].T
+    columns = rows_ref[:8].T
     step = widened(columns[:, 4:], width)
     start = widened(jnp.exp(columns[:, :4]), width)
     b, c, states = b_ref[...], c_ref[...], states_ref[...]
@@ -208,17 +204,18 @@
     height = width + b_in.shape[1]
     return pl.pallas_call(
         intra_kernel,
-        out_shape=(pltpu.HBM((height, tokens), f32), pltpu.HBM((height, tokens), bf16), pltpu.HBM((16, tokens), f32)),
+        out_shape=(jax.ShapeDtypeStruct((height, tokens), f32), jax.ShapeDtypeStruct((height, tokens), bf16), jax.ShapeDtypeStruct((16, tokens), f32)),
+        compiler_params=small(),
         cost_estimate=cost(14 * tokens * tokens * width, 2 << 20),
     )(dy, x_in, b_in, c_in, states, rows, skip)
 
 
-def dt_kernel(back_ref, half_ref, rows_ref, part_ref, carried_ref, states_ref, raw_ref, scal_ref, dt_ref, param_ref):
+def dt_kernel(back_ref, half_ref, rows_ref, part_ref, carried_ref, states_ref, raw_ref, dt_ref, param_ref):
     width, tokens = back_ref.shape
     head_dim = width // 4
-    cum, step = rows_ref[:4], rows_ref[4:]
+    cum, step = rows_ref[:4], rows_ref[4:8]
     last = cum[:, tokens - 1:]
-    rate, bias = scal_ref[:, 0:1], scal_ref[:, 1:2]
+    rate, bias = rows_ref[8:12], rows_ref[12:]
     dots = jnp.sum((half_ref[:width].astype(f32) * back_ref[...]).reshape(4, head_dim, tokens), axis=1)
     end_decay = jnp.exp(last - cum)
     end_terms = step * end_decay * dots
@@ -244,21 +241,15 @@
     param_ref[...] = jnp.sum(placed, axis=0, keepdims=True)
 
 
-def dt_terms(back, half, rows, part, carried, states, dt_raw, scalars):
+def dt_terms(back, half, rows, part, carried, states, dt_raw):
     return pl.pallas_call(
         dt_kernel,
         out_shape=(jax.ShapeDtypeStruct(dt_raw.shape, f32), jax.ShapeDtypeStruct((1, 128), f32)),
         cost_estimate=cost(1 << 22, 1 << 20),
-    )(back, half, rows, part, carried, states, dt_raw, scalars)
-
-
-def x_grad_kernel(carried_ref, b_ref, wide_hbm, half_hbm, rows_ref, sent_ref, back_ref, wide_ref, half_ref, sems):
-    fetches = [
-        pltpu.make_async_copy(wide_hbm, wide_ref, sems.at[0]),
-        pltpu.make_async_copy(half_hbm, half_ref, sems.at[1]),
-    ]
-    for fetch in fetches:
-        fetch.start()
+    )(back, half, rows, part, carried, states, dt_raw)
+
+
+def x_grad_kernel(carried_ref, b_ref, wide_ref, half_ref, rows_ref, sent_ref, back_ref):
     blocks, height, state_dim = carried_ref.shape
     width = blocks * height
     tokens = b_ref.shape[0]
@@ -266,9 +257,7 @@
     back = dot_last(carried, b_ref[...])
     back_ref[...] = back
     cum = rows_ref[:4]
-    weight = over_channels(rows_ref[4:] * jnp.exp(cum[:, tokens - 1:] - cum), width)
-    for fetch in fetches:
-        fetch.wait()
+    weight = over_channels(rows_ref[4:8] * jnp.exp(cum[:, tokens - 1:] - cum), width)
     x_grad = (wide_ref[:width] + weight * back).astype(bf16)
     x_end = (half_ref[:width].astype(f32) * weight).astype(bf16)
     entry = lax.dot_general(carried, x_end, (((0,), (0,)), ((), ())), preferred_element_type=f32)
@@ -285,16 +274,10 @@
 def x_grads(carried, b_in, wide, half, rows):
     tokens, state_dim = b_in.shape
     inner = wide.shape[0] - state_dim
-    at_vmem, at_hbm = pl.BlockSpec(memory_space=pltpu.VMEM), pl.BlockSpec(memory_space=pltpu.HBM)
     return pl.pallas_call(
         x_grad_kernel,
-        in_specs=[at_vmem, at_vmem, at_hbm, at_hbm, at_vmem],
-        scratch_shapes=[
-            pltpu.VMEM(wide.shape, wide.dtype),
-            pltpu.VMEM(half.shape, half.dtype),
-            pltpu.SemaphoreType.DMA((2,)),
-        ],
         out_shape=(pltpu.HBM((4, inner + state_dim // 2, tokens), bf16), pltpu.HBM((inner, tokens), f32)),
+        compiler_params=small(),
         cost_estimate=cost(4 * tokens * inner * 128, 2 << 20),
     )(carried, b_in, wide, half, rows)
 
@@ -352,6 +335,11 @@
     )(terms)
 
 
+def summed_over(row, axis):
+    first, second, third = (lax.ppermute(row, axis, [(i, (i + s) % 4) for i in range(4)]) for s in (1, 2, 3))
+    return (row + second) + (first + third)
+
+
 def shards(out_grad, x_in, b_in, c_in, dt_raw, dt_bias, a_log, d_skip, states, w_out, w_in):
     tokens_here, inner_here = x_in.shape
     group_heads = dt_raw.shape[0]
@@ -376,25 +364,25 @@
     positions = jnp.arange(tokens_here)
     upto = (positions[:, None] <= positions[None, :]).astype(f32)
     cumlog = jnp.dot(log_step, upto, precision=lax.Precision.HIGHEST)
-    rows = jnp.concatenate([cumlog, step_size], axis=0)
+    wide_scalars = jnp.broadcast_to(jnp.concatenate([decay_rate, dt_bias])[:, None], (2 * group_heads, tokens_here))
+    rows = jnp.concatenate([cumlog, step_size, wide_scalars], axis=0)
     ends = jnp.pad(three_parts(jnp.exp(cumlog[:, -1])), ((0, 0), (0, 5)))
     ends = jnp.broadcast_to(ends[:, None, :, None], (group_heads, blocks // group_heads, 8, state_dim))
-    scalars = jnp.pad(jnp.stack([decay_rate, dt_bias], axis=1), ((0, 0), (0, 126)))
     skip = jnp.repeat(d_skip, head_dim)[None]
     dy, sent = local_states(head_parts, rows, c_in, ends.reshape(blocks, 8, state_dim))
     ahead = suffix_scan(lax.all_to_all(sent, SEQ, 0, 0))
     ahead, dy, held[2] = lax.optimization_barrier((ahead, dy, held[2]))
     wide, half, part = intra_terms(dy, x_in, b_in, c_in, entry_state, rows, skip)
-    *held, carried, wide = lax.optimization_barrier((*held, lax.all_to_all(ahead, SEQ, 0, 0), wide))
+    *held, carried = lax.optimization_barrier((*held, lax.all_to_all(ahead, SEQ, 0, 0)))
     sent_y, back = x_grads(carried, b_in, wide, half, rows)
     got = lax.all_to_all(sent_y, "y", 0, 0)
-    dt_grad, row = dt_terms(back, half, rows, part, carried, entry_state, dt_raw, scalars)
-    row = row + lax.ppermute(row, "zl", [(i, i ^ 1) for i in range(4)])
+    dt_grad, row = dt_terms(back, half, rows, part, carried, entry_state, dt_raw)
+    row = summed_over(row, "zl")
     row, got = lax.optimization_barrier((row, got))
     terms = in_products(y, got, held)
     row, terms = lax.optimization_barrier((row, terms))
-    for axis, flip in (("zl", 2), ("x", 1), ("x", 2), ("core", 1)):
-        row = row + lax.ppermute(row, axis, [(i, i ^ flip) for i in range(lax.axis_size(axis))])
+    row = summed_over(row, "x")
+    row = row + lax.ppermute(row, "core", [(0, 1), (1, 0)])
     in_grad, bc_grad = final_sums(lax.all_to_all(terms, "zh", 0, 0), w_in.shape[0] // 16)
     norm_scale = (blocks * tokens_here * head_dim) ** (-0.5)
     param_grad = row[0, : 3 * group_heads].reshape(3, group_heads) * norm_scale

time: 160 us -> 153 us (0.956)
  the two profiles are of different devices: /device:TPU:257 before, /device:TPU:10 now
where the time goes in v6:
time: 153 us; the launch traced here: 152 us
  starting transfers between devices  63.2 us (41%)
  waiting for transfers between devices  35.1 us (23%)
  blocking collectives  32.3 us (21%)
  Pallas kernels  14 us (9%)
  local copies, waits for them, and re-layouts  5.17 us (3%)
    all_gather x1, blocking collectives, shards(): near = lax.all_gather(out_grad, 'zh', axis=1, tiled=True)  32.3 us
    ppermute x6, starting transfers between devices, summed_over(): lax.ppermute(row, axis, [(i, (i + s) % 4) for i in range(4)])  19.2 us
    all_to_all x1, waiting for transfers between devices, shards(): lax.all_to_all(terms, 'zh', 0, 0)  16.4 us
    ppermute x3, starting transfers between devices, shards(): lax.ppermute(pieces[s], 'y', [(i, (i + s) % 4) for i in range(4)])  10.1 us
    all_to_all x1, waiting for transfers between devices, shards(): head_parts = lax.all_to_all(products, 'y', 0, 0)  8.61 us
    all_to_all x1, starting transfers between devices, shards(): ahead = suffix_scan(lax.all_to_all(sent, SEQ, 0, 0))  6.2 us
    all_to_all x1, starting transfers between devices, shards(): lax.all_to_all(ahead, SEQ, 0, 0)  6.19 us
    all_to_all x1, starting transfers between devices, shards(): head_parts = lax.all_to_all(products, 'y', 0, 0)  5.66 us
  transfers between devices with their start and end apart: 16, of which 8 were waited for; matrix products, arithmetic and copies ran while one was open for 3% of the time, Pallas kernels for 4%

profile of v6, /device:TPU:10, one launch (start us, length us, event | category | flops | bytes accessed | tf_op | source)
XLA Modules:
  0.0 151.9 jit_solution(9786419938945483125)
XLA Ops:
  0.6 2.6 %shard_map.138 = bf16[4,256,1024]{2,1,0:T(8,128)(2,1)} custom-call(bf16[256,4096]{1,0:T(8,128)(2,1)} %w_ref.1), custom_call_target="tpu_custom_call" | custom-call | bytes 4194304 | tf_op jit(solution)/shard_map/pallas_call | solution.py:74
  3.3 5.1 %all-to-all-start = ((bf16[4,256,1024]{2,1,0:T(8,128)(2,1)}), bf16[4,256,1024]{2,1,0:T(8,128)(2,1)S(1)}, u32[]{:S(2)}, u32[]{:S(2)}) async-start(bf16[4,256,1024]{2,1,0:T(8,128)(2,1)} %shard_map.138), calls=%async_computation | async-start | bytes 4194304 | tf_op jit(solution)/shard_map/all_to_all | solution.py:352
  8.9 32.3 %all_gather.3.near_ref = bf16[256,1024]{1,0:T(8,128)(2,1)S(1)} all-gather(bf16[256,256]{1,0:T(8,128)(2,1)S(1)} %copy-done.9), channel_id=1, replica_groups=mesh['x'=4,'zl'=4,'core'=2,'y'=4,'zh'=4] {'zh'}, dimensions={1}, use_global_device_ids=true | all-gather | bytes 655360 | tf_op jit(solution)/shard_map/all_gather | solution.py:353
  41.1 1.5 %shard_map.139 = bf16[4,256,256]{2,1,0:T(8,128)(2,1)} custom-call(bf16[256,1024]{1,0:T(8,128)(2,1)S(1)} %all_gather.3.near_ref, bf16[4,256,1024]{2,1,0:T(8,128)(2,1)S(1)} %all-to-all-done.w_ref), custom_call_target="tpu_custom_call" | custom-call | flops 536870912 | bytes 4194304 | tf_op jit(solution)/shard_map/pallas_call | solution.py:97
  42.7 5.7 %all-to-all-start.1 = ((bf16[4,256,256]{2,1,0:T(8,128)(2,1)}), bf16[4,256,256]{2,1,0:T(8,128)(2,1)S(1)}, u32[]{:S(2)}, u32[]{:S(2)}) async-start(bf16[4,256,256]{2,1,0:T(8,128)(2,1)} %shard_map.139), calls=%async_computation.1 | async-start | bytes 1048576 | tf_op jit(solution)/shard_map/all_to_all | solution.py:359
  48.4 2.7 %constant_dynamic-slice_fusion = (bf16[1024,256]{1,0:T(8,128)(2,1)}, bf16[1024,256]{1,0:T(8,128)(2,1)S(1)}, bf16[1024,256]{1,0:T(8,128)(2,1)}, bf16[1024,256]{1,0:T(8,128)(2,1)S(1)}) fusion(bf16[4096,256]{1,0:T(8,128)(2,1)} %param.21, s32[]{:T(128)S(6)} %select_n.20, s32[]{:T(128)S(6)} %select_n.19, s32[]{:T(128)S(6)} %select_n.17, s32[]{:T(128)S(6)} %select_n.16), kind=kLoop, calls=%fused_computation.16 | loop fusion | bytes 4194320 | tf_op jit(solution)/shard_map/dynamic_slice | solution.py:357
  51.1 4.0 %collective-permute-start.1 = (bf16[1024,256]{1,0:T(8,128)(2,1)S(1)}, bf16[1024,256]{1,0:T(8,128)(2,1)S(1)}, u32[]{:S(2)}, u32[]{:S(2)}) collective-permute-start(bf16[1024,256]{1,0:T(8,128)(2,1)S(1)} %get-tuple-element.55), channel_id=1, source_target_pairs={{0,8},{4,12},{8,0},{12,4},{1,9},{5,13},{9,1},{13,5},{2,10},{6,14},... | collective-permute-start | bytes 1572872 | tf_op jit(solution)/shard_map/ppermute | solution.py:358
  55.2 8.6 %all-to-all-done.1.parts_ref = bf16[4,256,256]{2,1,0:T(8,128)(2,1)S(1)} async-done(((bf16[4,256,256]{2,1,0:T(8,128)(2,1)}), bf16[4,256,256]{2,1,0:T(8,128)(2,1)S(1)}, u32[]{:S(2)}, u32[]{:S(2)}) %all-to-all-start.1) | async-done | bytes 524320 | tf_op jit(solution)/shard_map/all_to_all | solution.py:359
  64.8 6.2 %all-to-all-start.2 = ((bf16[32,16,128]{2,1,0:T(8,128)(2,1)}), bf16[32,16,128]{2,1,0:T(8,128)(2,1)S(1)}, u32[]{:S(2)}, u32[]{:S(2)}) async-start(bf16[32,16,128]{2,1,0:T(8,128)(2,1)} %get-tuple-element.31), calls=%async_computation.2 | async-start | bytes 262144 | tf_op jit(solution)/shard_map/all_to_all | solution.py:373
  71.0 4.3 %collective-permute-start = (bf16[1024,256]{1,0:T(8,128)(2,1)}, bf16[1024,256]{1,0:T(8,128)(2,1)S(1)}, u32[]{:S(2)}, u32[]{:S(2)}) collective-permute-start(bf16[1024,256]{1,0:T(8,128)(2,1)} %get-tuple-element.56), channel_id=1, source_target_pairs={{0,4},{4,8},{8,12},{12,0},{1,5},{5,9},{9,13},{13,1},{2,6},{6,10},{... | collective-permute-start | bytes 1572872 | tf_op jit(solution)/shard_map/ppermute | solution.py:358
  75.2 1.9 %collective-permute-start.2 = (bf16[1024,256]{1,0:T(8,128)(2,1)}, bf16[1024,256]{1,0:T(8,128)(2,1)S(1)}, u32[]{:S(2)}, u32[]{:S(2)}) collective-permute-start(bf16[1024,256]{1,0:T(8,128)(2,1)} %get-tuple-element.54), channel_id=1, source_target_pairs={{0,12},{4,0},{8,4},{12,8},{1,13},{5,1},{9,5},{13,9},{2,14},{6,2},{... | collective-permute-start | bytes 1572872 | tf_op jit(solution)/shard_map/ppermute | solution.py:358
  77.2 1.5 all-to-all-done.2.parts_ref
  79.4 6.2 %all-to-all-start.3 = ((f32[32,8,128]{2,1,0:T(8,128)}), f32[32,8,128]{2,1,0:T(8,128)S(1)}, u32[]{:S(2)}, u32[]{:S(2)}) async-start(f32[32,8,128]{2,1,0:T(8,128)} %shard_map.141), calls=%async_computation.3 | async-start | bytes 262144 | tf_op jit(solution)/shard_map/all_to_all | solution.py:376
  86.7 2.8 %shard_map.142 = (f32[384,256]{1,0:T(8,128)S(1)}, bf16[384,256]{1,0:T(8,128)(2,1)S(1)}, f32[16,256]{1,0:T(8,128)S(1)}) custom-call(bf16[256,256]{1,0:T(8,128)(2,1)S(1)} %copy-done.8, bf16[256,256]{1,0:T(8,128)(2,1)S(1)} %copy-done.7, bf16[256,128]{1,0:T(8,128)(2,1)S(1)} %copy-done.4, bf16[256,128]{1,0:T(8,128)(2,1)S(1)} %copy-done.3, ...), custom_call_target="tpu_custom_call" | custom-call | flops 234881024 | bytes 2097152 | tf_op jit(solution)/shard_map/pallas_call | solution.py:205
  90.1 0.9 collective-permute-done.2.refs_3_
  91.0 2.3 %all-to-all-done.3.carried_ref = f32[32,8,128]{2,1,0:T(8,128)S(1)} async-done(((f32[32,8,128]{2,1,0:T(8,128)}), f32[32,8,128]{2,1,0:T(8,128)S(1)}, u32[]{:S(2)}, u32[]{:S(2)}) %all-to-all-start.3) | async-done | bytes 131104 | tf_op jit(solution)/shard_map/all_to_all | solution.py:376
  93.3 1.2 shard_map.143
  94.5 5.3 %all-to-all-start.4 = ((bf16[4,320,256]{2,1,0:T(8,128)(2,1)}), bf16[4,320,256]{2,1,0:T(8,128)(2,1)S(1)}, u32[]{:S(2)}, u32[]{:S(2)}) async-start(bf16[4,320,256]{2,1,0:T(8,128)(2,1)} %get-tuple-element.42), calls=%async_computation.4 | async-start | bytes 1310720 | tf_op jit(solution)/shard_map/all_to_all | solution.py:378
  99.8 2.0 %shard_map.144 = (f32[4,256]{1,0:T(4,128)}, f32[1,128]{1,0:T(1,128)}) custom-call(f32[256,256]{1,0:T(8,128)} %get-tuple-element.39.back_ref, bf16[384,256]{1,0:T(8,128)(2,1)} %copy-done.1, f32[16,256]{1,0:T(8,128)} %copy-done.2, f32[16,256]{1,0:T(8,128)} %copy-done.6, f32[32,8,128]{2,1,0:T(8,128)} %copy-done, bf16[256,128]{1,0:T(8,128)(2,1)} %bitcast.4, ...), custom_call_target="tpu_custom_call" | custom-call | flops 4194304 | bytes 1048576 | tf_op jit(solution)/shard_map/pallas_call | solution.py:245
  101.9 2.4 %collective-permute-start.3 = (f32[1,128]{1,0:T(1,128)}, f32[1,128]{1,0:T(1,128)S(1)}, u32[]{:S(2)}, u32[]{:S(2)}) collective-permute-start(f32[1,128]{1,0:T(1,128)} %get-tuple-element.41), channel_id=1, source_target_pairs={{0,64},{32,96},{64,0},{96,32},{1,65},{33,97},{65,1},{97,33},{2,66}... | collective-permute-start | bytes 1544 | tf_op jit(solution)/shard_map/ppermute | solution.py:339
  104.2 2.9 %collective-permute-start.4 = (f32[1,128]{1,0:T(1,128)}, f32[1,128]{1,0:T(1,128)S(1)}, u32[]{:S(2)}, u32[]{:S(2)}) collective-permute-start(f32[1,128]{1,0:T(1,128)} %get-tuple-element.41), channel_id=1, source_target_pairs={{0,32},{32,64},{64,96},{96,0},{1,33},{33,65},{65,97},{97,1},{2,34}... | collective-permute-start | bytes 1544 | tf_op jit(solution)/shard_map/ppermute | solution.py:339
  107.2 4.7 %collective-permute-start.5 = (f32[1,128]{1,0:T(1,128)}, f32[1,128]{1,0:T(1,128)S(1)}, u32[]{:S(2)}, u32[]{:S(2)}) collective-permute-start(f32[1,128]{1,0:T(1,128)} %get-tuple-element.41), channel_id=1, source_target_pairs={{0,96},{32,0},{64,32},{96,64},{1,97},{33,1},{65,33},{97,65},{2,98}... | collective-permute-start | bytes 1544 | tf_op jit(solution)/shard_map/ppermute | solution.py:339
  111.9 1.4 collective-permute-done.5
  114.0 1.5 shard_map.145
  115.5 3.5 %all-to-all-start.5 = ((bf16[4,272,256]{2,1,0:T(8,128)(2,1)}), bf16[4,272,256]{2,1,0:T(8,128)(2,1)S(1)}, u32[]{:S(2)}, u32[]{:S(2)}) async-start(bf16[4,272,256]{2,1,0:T(8,128)(2,1)} %shard_map.145), calls=%async_computation.5 | async-start | bytes 1114112 | tf_op jit(solution)/shard_map/all_to_all | solution.py:386
  119.0 3.4 %collective-permute-start.6 = (f32[1,128]{1,0:T(1,128)S(1)}, f32[1,128]{1,0:T(1,128)S(1)}, u32[]{:S(2)}, u32[]{:S(2)}) collective-permute-start(f32[1,128]{1,0:T(1,128)S(1)} %add_add_fusion.1), channel_id=1, source_target_pairs={{0,256},{128,384},{256,0},{384,128},{1,257},{129,385},{257,1},{385... | collective-permute-start | bytes 1544 | tf_op jit(solution)/shard_map/ppermute | solution.py:339
  122.3 3.3 %collective-permute-start.7 = (f32[1,128]{1,0:T(1,128)S(1)}, f32[1,128]{1,0:T(1,128)S(1)}, u32[]{:S(2)}, u32[]{:S(2)}) collective-permute-start(f32[1,128]{1,0:T(1,128)S(1)} %add_add_fusion.1), channel_id=1, source_target_pairs={{0,128},{128,256},{256,384},{384,0},{1,129},{129,257},{257,385},{3... | collective-permute-start | bytes 1544 | tf_op jit(solution)/shard_map/ppermute | solution.py:339
  125.7 2.5 %collective-permute-start.8 = (f32[1,128]{1,0:T(1,128)S(1)}, f32[1,128]{1,0:T(1,128)S(1)}, u32[]{:S(2)}, u32[]{:S(2)}) collective-permute-start(f32[1,128]{1,0:T(1,128)S(1)} %add_add_fusion.1), channel_id=1, source_target_pairs={{0,384},{128,0},{256,128},{384,256},{1,385},{129,1},{257,129},{385... | collective-permute-start | bytes 1544 | tf_op jit(solution)/shard_map/ppermute | solution.py:339
  128.2 2.9 %collective-permute-done.8 = f32[1,128]{1,0:T(1,128)S(1)} collective-permute-done((f32[1,128]{1,0:T(1,128)S(1)}, f32[1,128]{1,0:T(1,128)S(1)}, u32[]{:S(2)}, u32[]{:S(2)}) %collective-permute-start.8) | collective-permute-done | bytes 544 | tf_op jit(solution)/shard_map/ppermute | solution.py:339
  131.1 1.9 %collective-permute-start.9 = (f32[1,128]{1,0:T(1,128)S(1)}, f32[1,128]{1,0:T(1,128)S(1)}, u32[]{:S(2)}, u32[]{:S(2)}) collective-permute-start(f32[1,128]{1,0:T(1,128)S(1)} %add_add_fusion), channel_id=1, source_target_pairs={{0,16},{16,0},{1,17},{17,1},{2,18},{18,2},{3,19},{19,3},{4,20},{20... | collective-permute-start | bytes 1544 | tf_op jit(solution)/shard_map/ppermute | solution.py:385
  133.0 1.1 collective-permute-done.9
  134.8 16.4 %all-to-all-done.5.terms_ref = bf16[4,272,256]{2,1,0:T(8,128)(2,1)S(1)} async-done(((bf16[4,272,256]{2,1,0:T(8,128)(2,1)}), bf16[4,272,256]{2,1,0:T(8,128)(2,1)S(1)}, u32[]{:S(2)}, u32[]{:S(2)}) %all-to-all-start.5) | async-done | bytes 557088 | tf_op jit(solution)/shard_map/all_to_all | solution.py:386
  (55 shorter events, 6.1 us)
Async XLA Ops:
  3.3 5.1 %copy-start.13 = (f32[4]{0:T(128)S(1)}, f32[4]{0:T(128)}, u32[]{:S(2)}) copy-start(f32[4]{0:T(128)} %param.17) | copy-start | bytes 52
  3.3 5.1 %copy-start.10 = (f32[4,256]{1,0:T(4,128)S(1)}, f32[4,256]{1,0:T(4,128)}, u32[]{:S(2)}) copy-start(f32[4,256]{1,0:T(4,128)} %raw_ref.1) | copy-start | bytes 12292
  3.3 5.1 %copy-start.11 = (f32[4]{0:T(128)S(1)}, f32[4]{0:T(128)}, u32[]{:S(2)}) copy-start(f32[4]{0:T(128)} %param.16) | copy-start | bytes 52
  3.3 5.6 %copy-start.9 = (bf16[256,256]{1,0:T(8,128)(2,1)S(1)}, bf16[256,256]{1,0:T(8,128)(2,1)}, u32[]{:S(2)}) copy-start(bf16[256,256]{1,0:T(8,128)(2,1)} %param.11) | copy-start | bytes 393220
  3.3 37.8 %all-to-all-start = ((bf16[4,256,1024]{2,1,0:T(8,128)(2,1)}), bf16[4,256,1024]{2,1,0:T(8,128)(2,1)S(1)}, u32[]{:S(2)}, u32[]{:S(2)}) async-start(bf16[4,256,1024]{2,1,0:T(8,128)(2,1)} %shard_map.138), calls=%async_computation | async-start | bytes 4194304 | tf_op jit(solution)/shard_map/all_to_all | solution.py:352
  42.7 21.1 %all-to-all-start.1 = ((bf16[4,256,256]{2,1,0:T(8,128)(2,1)}), bf16[4,256,256]{2,1,0:T(8,128)(2,1)S(1)}, u32[]{:S(2)}, u32[]{:S(2)}) async-start(bf16[4,256,256]{2,1,0:T(8,128)(2,1)} %shard_map.139), calls=%async_computation.1 | async-start | bytes 1048576 | tf_op jit(solution)/shard_map/all_to_all | solution.py:359
  48.4 15.5 %copy-start.3 = (bf16[256,128]{1,0:T(8,128)(2,1)S(1)}, bf16[256,128]{1,0:T(8,128)(2,1)}, u32[]{:S(2)}) copy-start(bf16[256,128]{1,0:T(8,128)(2,1)} %c_ref.3) | copy-start | bytes 196612
  48.4 37.2 %copy-start.12 = (f32[4]{0:T(128)S(1)}, f32[4]{0:T(128)}, u32[]{:S(2)}) copy-start(f32[4]{0:T(128)} %param.18) | copy-start | bytes 52
  48.4 37.4 %copy-start.4 = (bf16[256,128]{1,0:T(8,128)(2,1)S(1)}, bf16[256,128]{1,0:T(8,128)(2,1)}, u32[]{:S(2)}) copy-start(bf16[256,128]{1,0:T(8,128)(2,1)} %b_ref.3) | copy-start | bytes 196612
  48.4 37.4 %copy-start.5 = (bf16[1,256,128]{2,1,0:T(8,128)(2,1)S(1)}, bf16[1,256,128]{2,1,0:T(8,128)(2,1)}, u32[]{:S(2)}) copy-start(bf16[1,256,128]{2,1,0:T(8,128)(2,1)} %param.19) | copy-start | bytes 196612
  48.4 37.4 %copy-start.7 = (bf16[256,256]{1,0:T(8,128)(2,1)S(1)}, bf16[256,256]{1,0:T(8,128)(2,1)}, u32[]{:S(2)}) copy-start(bf16[256,256]{1,0:T(8,128)(2,1)} %x_ref.1) | copy-start | bytes 393220
  51.1 28.3 %collective-permute-start.1 = (bf16[1024,256]{1,0:T(8,128)(2,1)S(1)}, bf16[1024,256]{1,0:T(8,128)(2,1)S(1)}, u32[]{:S(2)}, u32[]{:S(2)}) collective-permute-start(bf16[1024,256]{1,0:T(8,128)(2,1)S(1)} %get-tuple-element.55), channel_id=1, source_target_pairs={{0,8},{4,12},{8,0},{12,4},{1,9},{5,13},{9,1},{13,5},{2,10},{6,14},... | collective-permute-start | bytes 1572872 | tf_op jit(solution)/shard_map/ppermute | solution.py:358
  55.2 39.3 %copy-start.2 = (f32[16,256]{1,0:T(8,128)}, f32[16,256]{1,0:T(8,128)S(1)}, u32[]{:S(2)}) copy-start(f32[16,256]{1,0:T(8,128)S(1)} %maximum_maximum_fusion.rows_ref) | copy-start | bytes 49156
  64.8 13.9 %all-to-all-start.2 = ((bf16[32,16,128]{2,1,0:T(8,128)(2,1)}), bf16[32,16,128]{2,1,0:T(8,128)(2,1)S(1)}, u32[]{:S(2)}, u32[]{:S(2)}) async-start(bf16[32,16,128]{2,1,0:T(8,128)(2,1)} %get-tuple-element.31), calls=%async_computation.2 | async-start | bytes 262144 | tf_op jit(solution)/shard_map/all_to_all | solution.py:373
  71.0 19.1 %collective-permute-start = (bf16[1024,256]{1,0:T(8,128)(2,1)}, bf16[1024,256]{1,0:T(8,128)(2,1)S(1)}, u32[]{:S(2)}, u32[]{:S(2)}) collective-permute-start(bf16[1024,256]{1,0:T(8,128)(2,1)} %get-tuple-element.56), channel_id=1, source_target_pairs={{0,4},{4,8},{8,12},{12,0},{1,5},{5,9},{9,13},{13,1},{2,6},{6,10},{... | collective-permute-start | bytes 1572872 | tf_op jit(solution)/shard_map/ppermute | solution.py:358
  75.2 15.8 %collective-permute-start.2 = (bf16[1024,256]{1,0:T(8,128)(2,1)}, bf16[1024,256]{1,0:T(8,128)(2,1)S(1)}, u32[]{:S(2)}, u32[]{:S(2)}) collective-permute-start(bf16[1024,256]{1,0:T(8,128)(2,1)} %get-tuple-element.54), channel_id=1, source_target_pairs={{0,12},{4,0},{8,4},{12,8},{1,13},{5,1},{9,5},{13,9},{2,14},{6,2},{... | collective-permute-start | bytes 1572872 | tf_op jit(solution)/shard_map/ppermute | solution.py:358
  79.4 13.9 %all-to-all-start.3 = ((f32[32,8,128]{2,1,0:T(8,128)}), f32[32,8,128]{2,1,0:T(8,128)S(1)}, u32[]{:S(2)}, u32[]{:S(2)}) async-start(f32[32,8,128]{2,1,0:T(8,128)} %shard_map.141), calls=%async_computation.3 | async-start | bytes 262144 | tf_op jit(solution)/shard_map/all_to_all | solution.py:376
  85.8 0.9 copy-start.8
  89.5 0.6 copy-start.6
  90.1 9.7 %copy-start.1 = (bf16[384,256]{1,0:T(8,128)(2,1)}, bf16[384,256]{1,0:T(8,128)(2,1)S(1)}, u32[]{:S(2)}) copy-start(bf16[384,256]{1,0:T(8,128)(2,1)S(1)} %get-tuple-element.38.half_ref) | copy-start | bytes 589828
  93.3 6.5 %copy-start = (f32[32,8,128]{2,1,0:T(8,128)}, f32[32,8,128]{2,1,0:T(8,128)S(1)}, u32[]{:S(2)}) copy-start(f32[32,8,128]{2,1,0:T(8,128)S(1)} %all-to-all-done.3.carried_ref) | copy-start | bytes 393220
  94.5 19.5 %all-to-all-start.4 = ((bf16[4,320,256]{2,1,0:T(8,128)(2,1)}), bf16[4,320,256]{2,1,0:T(8,128)(2,1)S(1)}, u32[]{:S(2)}, u32[]{:S(2)}) async-start(bf16[4,320,256]{2,1,0:T(8,128)(2,1)} %get-tuple-element.42), calls=%async_computation.4 | async-start | bytes 1310720 | tf_op jit(solution)/shard_map/all_to_all | solution.py:378
  101.9 10.0 %collective-permute-start.3 = (f32[1,128]{1,0:T(1,128)}, f32[1,128]{1,0:T(1,128)S(1)}, u32[]{:S(2)}, u32[]{:S(2)}) collective-permute-start(f32[1,128]{1,0:T(1,128)} %get-tuple-element.41), channel_id=1, source_target_pairs={{0,64},{32,96},{64,0},{96,32},{1,65},{33,97},{65,1},{97,33},{2,66}... | collective-permute-start | bytes 1544 | tf_op jit(solution)/shard_map/ppermute | solution.py:339
  104.2 7.7 %collective-permute-start.4 = (f32[1,128]{1,0:T(1,128)}, f32[1,128]{1,0:T(1,128)S(1)}, u32[]{:S(2)}, u32[]{:S(2)}) collective-permute-start(f32[1,128]{1,0:T(1,128)} %get-tuple-element.41), channel_id=1, source_target_pairs={{0,32},{32,64},{64,96},{96,0},{1,33},{33,65},{65,97},{97,1},{2,34}... | collective-permute-start | bytes 1544 | tf_op jit(solution)/shard_map/ppermute | solution.py:339
  107.2 6.1 %collective-permute-start.5 = (f32[1,128]{1,0:T(1,128)}, f32[1,128]{1,0:T(1,128)S(1)}, u32[]{:S(2)}, u32[]{:S(2)}) collective-permute-start(f32[1,128]{1,0:T(1,128)} %get-tuple-element.41), channel_id=1, source_target_pairs={{0,96},{32,0},{64,32},{96,64},{1,97},{33,1},{65,33},{97,65},{2,98}... | collective-permute-start | bytes 1544 | tf_op jit(solution)/shard_map/ppermute | solution.py:339
  115.5 35.7 %all-to-all-start.5 = ((bf16[4,272,256]{2,1,0:T(8,128)(2,1)}), bf16[4,272,256]{2,1,0:T(8,128)(2,1)S(1)}, u32[]{:S(2)}, u32[]{:S(2)}) async-start(bf16[4,272,256]{2,1,0:T(8,128)(2,1)} %shard_map.145), calls=%async_computation.5 | async-start | bytes 1114112 | tf_op jit(solution)/shard_map/all_to_all | solution.py:386
  119.0 9.2 %collective-permute-start.6 = (f32[1,128]{1,0:T(1,128)S(1)}, f32[1,128]{1,0:T(1,128)S(1)}, u32[]{:S(2)}, u32[]{:S(2)}) collective-permute-start(f32[1,128]{1,0:T(1,128)S(1)} %add_add_fusion.1), channel_id=1, source_target_pairs={{0,256},{128,384},{256,0},{384,128},{1,257},{129,385},{257,1},{385... | collective-permute-start | bytes 1544 | tf_op jit(solution)/shard_map/ppermute | solution.py:339
  122.3 5.9 %collective-permute-start.7 = (f32[1,128]{1,0:T(1,128)S(1)}, f32[1,128]{1,0:T(1,128)S(1)}, u32[]{:S(2)}, u32[]{:S(2)}) collective-permute-start(f32[1,128]{1,0:T(1,128)S(1)} %add_add_fusion.1), channel_id=1, source_target_pairs={{0,128},{128,256},{256,384},{384,0},{1,129},{129,257},{257,385},{3... | collective-permute-start | bytes 1544 | tf_op jit(solution)/shard_map/ppermute | solution.py:339
  125.7 5.4 %collective-permute-start.8 = (f32[1,128]{1,0:T(1,128)S(1)}, f32[1,128]{1,0:T(1,128)S(1)}, u32[]{:S(2)}, u32[]{:S(2)}) collective-permute-start(f32[1,128]{1,0:T(1,128)S(1)} %add_add_fusion.1), channel_id=1, source_target_pairs={{0,384},{128,0},{256,128},{384,256},{1,385},{129,1},{257,129},{385... | collective-permute-start | bytes 1544 | tf_op jit(solution)/shard_map/ppermute | solution.py:339
  131.1 3.0 %collective-permute-start.9 = (f32[1,128]{1,0:T(1,128)S(1)}, f32[1,128]{1,0:T(1,128)S(1)}, u32[]{:S(2)}, u32[]{:S(2)}) collective-permute-start(f32[1,128]{1,0:T(1,128)S(1)} %add_add_fusion), channel_id=1, source_target_pairs={{0,16},{16,0},{1,17},{17,1},{2,18},{18,2},{3,19},{19,3},{4,20},{20... | collective-permute-start | bytes 1544 | tf_op jit(solution)/shard_map/ppermute | solution.py:385

commit v7 on v6

--- a/solution.py
+++ b/solution.py
@@ -335,8 +335,12 @@
     )(terms)
 
 
-def summed_over(row, axis):
-    first, second, third = (lax.ppermute(row, axis, [(i, (i + s) % 4) for i in range(4)]) for s in (1, 2, 3))
+def shifted(row, axis):
+    return [lax.ppermute(row, axis, [(i, (i + s) % 4) for i in range(4)]) for s in (1, 2, 3)]
+
+
+def paired(row, rounds):
+    first, second, third = rounds
     return (row + second) + (first + third)
 
 
@@ -354,8 +358,11 @@
     products = partial_products(near, w_out_y)
     w_in_held, products = lax.optimization_barrier((w_in, products))
     quarter = w_in.shape[0] // 4
-    pieces = [lax.dynamic_slice_in_dim(w_in_held, lax.rem(y + s, 4) * quarter, quarter) for s in range(4)]
-    held = [pieces[0]] + [lax.ppermute(pieces[s], "y", [(i, (i + s) % 4) for i in range(4)]) for s in range(1, 4)]
+
+    def exchanged(source, s):
+        piece = lax.dynamic_slice_in_dim(source, lax.rem(y + s, 4) * quarter, quarter)
+        return lax.ppermute(piece, "y", [(i, (i + s) % 4) for i in range(4)])
+
     head_parts = lax.all_to_all(products, "y", 0, 0)
 
     decay_rate = jnp.exp(a_log)
@@ -371,17 +378,20 @@
     skip = jnp.repeat(d_skip, head_dim)[None]
     dy, sent = local_states(head_parts, rows, c_in, ends.reshape(blocks, 8, state_dim))
     ahead = suffix_scan(lax.all_to_all(sent, SEQ, 0, 0))
-    ahead, dy, held[2] = lax.optimization_barrier((ahead, dy, held[2]))
+    held = [None, None, exchanged(w_in_held, 2), exchanged(w_in_held, 3)]
+    ahead, dy, w_in_late = lax.optimization_barrier((ahead, dy, w_in_held))
+    held[0] = lax.dynamic_slice_in_dim(w_in_late, y * quarter, quarter)
+    held[1] = exchanged(w_in_late, 1)
     wide, half, part = intra_terms(dy, x_in, b_in, c_in, entry_state, rows, skip)
-    *held, carried = lax.optimization_barrier((*held, lax.all_to_all(ahead, SEQ, 0, 0)))
+    held[2], held[3], carried = lax.optimization_barrier((held[2], held[3], lax.all_to_all(ahead, SEQ, 0, 0)))
     sent_y, back = x_grads(carried, b_in, wide, half, rows)
     got = lax.all_to_all(sent_y, "y", 0, 0)
     dt_grad, row = dt_terms(back, half, rows, part, carried, entry_state, dt_raw)
-    row = summed_over(row, "zl")
-    row, got = lax.optimization_barrier((row, got))
+    *rounds, got = lax.optimization_barrier((*shifted(row, "zl"), got))
     terms = in_products(y, got, held)
-    row, terms = lax.optimization_barrier((row, terms))
-    row = summed_over(row, "x")
+    *rounds, terms = lax.optimization_barrier((*rounds, terms))
+    row = paired(row, rounds)
+    row = paired(row, shifted(row, "x"))
     row = row + lax.ppermute(row, "core", [(0, 1), (1, 0)])
     in_grad, bc_grad = final_sums(lax.all_to_all(terms, "zh", 0, 0), w_in.shape[0] // 16)
     norm_scale = (blocks * tokens_here * head_dim) ** (-0.5)

time: 153 us -> 155 us (1.013)
  the two profiles are of different devices: /device:TPU:10 before, /device:TPU:18 now
where the time goes in v7:
time: 155 us; the launch traced here: 154 us
  starting transfers between devices  69.8 us (45%)
  blocking collectives  32.3 us (21%)
  waiting for transfers between devices  30.4 us (20%)
  Pallas kernels  14 us (9%)
  local copies, waits for them, and re-layouts  6 us (4%)
    all_gather x1, blocking collectives, shards(): near = lax.all_gather(out_grad, 'zh', axis=1, tiled=True)  32.3 us
    ppermute x6, starting transfers between devices, shifted(): lax.ppermute(row, axis, [(i, (i + s) % 4) for i in range(4)])  20.9 us
    all_to_all x1, waiting for transfers between devices, shards(): lax.all_to_all(terms, 'zh', 0, 0)  16 us
    ppermute x3, starting transfers between devices, exchanged(): return lax.ppermute(piece, 'y', [(i, (i + s) % 4) for i in range(4)])  10.7 us
    all_to_all x1, starting transfers between devices, shards(): lax.all_to_all(ahead, SEQ, 0, 0)  7.69 us
    all_to_all x1, starting transfers between devices, shards(): lax.all_to_all(terms, 'zh', 0, 0)  7.01 us
    all_to_all x1, starting transfers between devices, shards(): ahead = suffix_scan(lax.all_to_all(sent, SEQ, 0, 0))  6.2 us
    all_to_all x1, starting transfers between devices, shards(): head_parts = lax.all_to_all(products, 'y', 0, 0)  5.67 us
  transfers between devices with their start and end apart: 16, of which 6 were waited for; matrix products, arithmetic and copies ran while one was open for 4% of the time, Pallas kernels for 4%

profile of v7, /device:TPU:18, one launch (start us, length us, event | category | flops | bytes accessed | tf_op | source)
XLA Modules:
  0.0 154.1 jit_solution(7324077271297270135)
XLA Ops:
  0.6 2.6 %shard_map.138 = bf16[4,256,1024]{2,1,0:T(8,128)(2,1)} custom-call(bf16[256,4096]{1,0:T(8,128)(2,1)} %w_ref.1), custom_call_target="tpu_custom_call" | custom-call | bytes 4194304 | tf_op jit(solution)/shard_map/pallas_call | solution.py:74
  3.3 4.9 %all-to-all-start = ((bf16[4,256,1024]{2,1,0:T(8,128)(2,1)}), bf16[4,256,1024]{2,1,0:T(8,128)(2,1)S(1)}, u32[]{:S(2)}, u32[]{:S(2)}) async-start(bf16[4,256,1024]{2,1,0:T(8,128)(2,1)} %shard_map.138), calls=%async_computation | async-start | bytes 4194304 | tf_op jit(solution)/shard_map/all_to_all | solution.py:356
  8.8 32.3 %all_gather.3.near_ref = bf16[256,1024]{1,0:T(8,128)(2,1)S(1)} all-gather(bf16[256,256]{1,0:T(8,128)(2,1)S(1)} %copy-done.9), channel_id=1, replica_groups=mesh['x'=4,'zl'=4,'core'=2,'y'=4,'zh'=4] {'zh'}, dimensions={1}, use_global_device_ids=true | all-gather | bytes 655360 | tf_op jit(solution)/shard_map/all_gather | solution.py:357
  41.1 1.5 shard_map.139
  42.6 5.7 %all-to-all-start.1 = ((bf16[4,256,256]{2,1,0:T(8,128)(2,1)}), bf16[4,256,256]{2,1,0:T(8,128)(2,1)S(1)}, u32[]{:S(2)}, u32[]{:S(2)}) async-start(bf16[4,256,256]{2,1,0:T(8,128)(2,1)} %shard_map.139), calls=%async_computation.1 | async-start | bytes 1048576 | tf_op jit(solution)/shard_map/all_to_all | solution.py:366
  48.4 5.0 %all-to-all-done.1.parts_ref = bf16[4,256,256]{2,1,0:T(8,128)(2,1)S(1)} async-done(((bf16[4,256,256]{2,1,0:T(8,128)(2,1)}), bf16[4,256,256]{2,1,0:T(8,128)(2,1)S(1)}, u32[]{:S(2)}, u32[]{:S(2)}) %all-to-all-start.1) | async-done | bytes 524320 | tf_op jit(solution)/shard_map/all_to_all | solution.py:366
  53.5 0.9 shard_map.140
  54.4 6.2 %all-to-all-start.2 = ((bf16[32,16,128]{2,1,0:T(8,128)(2,1)}), bf16[32,16,128]{2,1,0:T(8,128)(2,1)S(1)}, u32[]{:S(2)}, u32[]{:S(2)}) async-start(bf16[32,16,128]{2,1,0:T(8,128)(2,1)} %get-tuple-element.33), calls=%async_computation.2 | async-start | bytes 262144 | tf_op jit(solution)/shard_map/all_to_all | solution.py:380
  60.6 2.3 %constant_dynamic-slice_fusion.2 = (bf16[1024,256]{1,0:T(8,128)(2,1)}, bf16[1024,256]{1,0:T(8,128)(2,1)}) fusion(bf16[4096,256]{1,0:T(8,128)(2,1)} %param.21, s32[]{:T(128)S(6)} %select_n.17, s32[]{:T(128)S(6)} %select_n.16), kind=kLoop, calls=%fused_computation.18 | loop fusion | bytes 2097160 | tf_op jit(solution)/shard_map/dynamic_slice | solution.py:363
  63.0 4.9 %collective-permute-start = (bf16[1024,256]{1,0:T(8,128)(2,1)}, bf16[1024,256]{1,0:T(8,128)(2,1)S(1)}, u32[]{:S(2)}, u32[]{:S(2)}) collective-permute-start(bf16[1024,256]{1,0:T(8,128)(2,1)} %get-tuple-element.61), channel_id=1, source_target_pairs={{0,8},{4,12},{8,0},{12,4},{1,9},{5,13},{9,1},{13,5},{2,10},{6,14},... | collective-permute-start | bytes 1572872 | tf_op jit(solution)/shard_map/ppermute | solution.py:364
  67.8 2.5 %collective-permute-start.1 = (bf16[1024,256]{1,0:T(8,128)(2,1)}, bf16[1024,256]{1,0:T(8,128)(2,1)S(1)}, u32[]{:S(2)}, u32[]{:S(2)}) collective-permute-start(bf16[1024,256]{1,0:T(8,128)(2,1)} %get-tuple-element.60), channel_id=1, source_target_pairs={{0,12},{4,0},{8,4},{12,8},{1,13},{5,1},{9,5},{13,9},{2,14},{6,2},{... | collective-permute-start | bytes 1572872 | tf_op jit(solution)/shard_map/ppermute | solution.py:364
  71.0 7.7 %all-to-all-start.3 = ((f32[32,8,128]{2,1,0:T(8,128)}), f32[32,8,128]{2,1,0:T(8,128)S(1)}, u32[]{:S(2)}, u32[]{:S(2)}) async-start(f32[32,8,128]{2,1,0:T(8,128)} %shard_map.141), calls=%async_computation.3 | async-start | bytes 262144 | tf_op jit(solution)/shard_map/all_to_all | solution.py:386
  78.7 2.1 %constant_dynamic-slice_fusion = (bf16[1024,256]{1,0:T(8,128)(2,1)}, bf16[1024,256]{1,0:T(8,128)(2,1)S(1)}) fusion(bf16[4096,256]{1,0:T(8,128)(2,1)} %param.21, s32[]{:T(128)S(6)} %select_n.20, s32[]{:T(128)S(6)} %select_n.19), kind=kLoop, calls=%fused_computation.16 | loop fusion | bytes 2097160 | tf_op jit(solution)/shard_map/dynamic_slice | solution.py:363
  80.8 3.4 %collective-permute-start.5 = (bf16[1024,256]{1,0:T(8,128)(2,1)}, bf16[1024,256]{1,0:T(8,128)(2,1)S(1)}, u32[]{:S(2)}, u32[]{:S(2)}) collective-permute-start(bf16[1024,256]{1,0:T(8,128)(2,1)} %get-tuple-element.58), channel_id=1, source_target_pairs={{0,4},{4,8},{8,12},{12,0},{1,5},{5,9},{9,13},{13,1},{2,6},{6,10},{... | collective-permute-start | bytes 1572872 | tf_op jit(solution)/shard_map/ppermute | solution.py:364
  84.4 2.8 %shard_map.142 = (f32[384,256]{1,0:T(8,128)S(1)}, bf16[384,256]{1,0:T(8,128)(2,1)S(1)}, f32[16,256]{1,0:T(8,128)S(1)}) custom-call(bf16[256,256]{1,0:T(8,128)(2,1)S(1)} %copy-done.8, bf16[256,256]{1,0:T(8,128)(2,1)S(1)} %copy-done.7, bf16[256,128]{1,0:T(8,128)(2,1)S(1)} %copy-done.4, bf16[256,128]{1,0:T(8,128)(2,1)S(1)} %copy-done.3, ...), custom_call_target="tpu_custom_call" | custom-call | flops 234881024 | bytes 2097152 | tf_op jit(solution)/shard_map/pallas_call | solution.py:205
  87.8 4.6 %collective-permute-done.1.refs_3_ = bf16[1024,256]{1,0:T(8,128)(2,1)S(1)} collective-permute-done((bf16[1024,256]{1,0:T(8,128)(2,1)}, bf16[1024,256]{1,0:T(8,128)(2,1)S(1)}, u32[]{:S(2)}, u32[]{:S(2)}) %collective-permute-start.1) | collective-permute-done | bytes 524320 | tf_op jit(solution)/shard_map/ppermute | solution.py:364
  92.4 1.1 shard_map.143
  93.6 4.8 %all-to-all-start.4 = ((bf16[4,320,256]{2,1,0:T(8,128)(2,1)}), bf16[4,320,256]{2,1,0:T(8,128)(2,1)S(1)}, u32[]{:S(2)}, u32[]{:S(2)}) async-start(bf16[4,320,256]{2,1,0:T(8,128)(2,1)} %get-tuple-element.43), calls=%async_computation.4 | async-start | bytes 1310720 | tf_op jit(solution)/shard_map/all_to_all | solution.py:388
  98.4 2.0 %shard_map.144 = (f32[4,256]{1,0:T(4,128)}, f32[1,128]{1,0:T(1,128)}) custom-call(f32[256,256]{1,0:T(8,128)} %get-tuple-element.40.back_ref, bf16[384,256]{1,0:T(8,128)(2,1)} %copy-done.1, f32[16,256]{1,0:T(8,128)} %copy-done.2, f32[16,256]{1,0:T(8,128)} %copy-done.6, f32[32,8,128]{2,1,0:T(8,128)} %copy-done, bf16[256,128]{1,0:T(8,128)(2,1)} %bitcast.4, ...), custom_call_target="tpu_custom_call" | custom-call | flops 4194304 | bytes 1048576 | tf_op jit(solution)/shard_map/pallas_call | solution.py:245
  100.4 3.4 %collective-permute-start.2 = (f32[1,128]{1,0:T(1,128)}, f32[1,128]{1,0:T(1,128)S(1)}, u32[]{:S(2)}, u32[]{:S(2)}) collective-permute-start(f32[1,128]{1,0:T(1,128)} %get-tuple-element.42), channel_id=1, source_target_pairs={{0,32},{32,64},{64,96},{96,0},{1,33},{33,65},{65,97},{97,1},{2,34}... | collective-permute-start | bytes 1544 | tf_op jit(solution)/shard_map/ppermute | solution.py:339
  103.8 4.3 %collective-permute-start.3 = (f32[1,128]{1,0:T(1,128)}, f32[1,128]{1,0:T(1,128)S(1)}, u32[]{:S(2)}, u32[]{:S(2)}) collective-permute-start(f32[1,128]{1,0:T(1,128)} %get-tuple-element.42), channel_id=1, source_target_pairs={{0,64},{32,96},{64,0},{96,32},{1,65},{33,97},{65,1},{97,33},{2,66}... | collective-permute-start | bytes 1544 | tf_op jit(solution)/shard_map/ppermute | solution.py:339
  108.1 3.4 %collective-permute-start.4 = (f32[1,128]{1,0:T(1,128)}, f32[1,128]{1,0:T(1,128)S(1)}, u32[]{:S(2)}, u32[]{:S(2)}) collective-permute-start(f32[1,128]{1,0:T(1,128)} %get-tuple-element.42), channel_id=1, source_target_pairs={{0,96},{32,0},{64,32},{96,64},{1,97},{33,1},{65,33},{97,65},{2,98}... | collective-permute-start | bytes 1544 | tf_op jit(solution)/shard_map/ppermute | solution.py:339
  111.5 2.2 %collective-permute-done.4 = f32[1,128]{1,0:T(1,128)S(1)} collective-permute-done((f32[1,128]{1,0:T(1,128)}, f32[1,128]{1,0:T(1,128)S(1)}, u32[]{:S(2)}, u32[]{:S(2)}) %collective-permute-start.4) | collective-permute-done | bytes 544 | tf_op jit(solution)/shard_map/ppermute | solution.py:339
  113.7 1.5 shard_map.145
  115.2 7.0 %all-to-all-start.5 = ((bf16[4,272,256]{2,1,0:T(8,128)(2,1)}), bf16[4,272,256]{2,1,0:T(8,128)(2,1)S(1)}, u32[]{:S(2)}, u32[]{:S(2)}) async-start(bf16[4,272,256]{2,1,0:T(8,128)(2,1)} %shard_map.145), calls=%async_computation.5 | async-start | bytes 1114112 | tf_op jit(solution)/shard_map/all_to_all | solution.py:396
  122.2 4.1 %collective-permute-start.6 = (f32[1,128]{1,0:T(1,128)S(1)}, f32[1,128]{1,0:T(1,128)S(1)}, u32[]{:S(2)}, u32[]{:S(2)}) collective-permute-start(f32[1,128]{1,0:T(1,128)S(1)} %add_add_fusion.1), channel_id=1, source_target_pairs={{0,256},{128,384},{256,0},{384,128},{1,257},{129,385},{257,1},{385... | collective-permute-start | bytes 1544 | tf_op jit(solution)/shard_map/ppermute | solution.py:339
  126.3 1.9 %collective-permute-start.7 = (f32[1,128]{1,0:T(1,128)S(1)}, f32[1,128]{1,0:T(1,128)S(1)}, u32[]{:S(2)}, u32[]{:S(2)}) collective-permute-start(f32[1,128]{1,0:T(1,128)S(1)} %add_add_fusion.1), channel_id=1, source_target_pairs={{0,128},{128,256},{256,384},{384,0},{1,129},{129,257},{257,385},{3... | collective-permute-start | bytes 1544 | tf_op jit(solution)/shard_map/ppermute | solution.py:339
  128.2 3.9 %collective-permute-start.8 = (f32[1,128]{1,0:T(1,128)S(1)}, f32[1,128]{1,0:T(1,128)S(1)}, u32[]{:S(2)}, u32[]{:S(2)}) collective-permute-start(f32[1,128]{1,0:T(1,128)S(1)} %add_add_fusion.1), channel_id=1, source_target_pairs={{0,384},{128,0},{256,128},{384,256},{1,385},{129,1},{257,129},{385... | collective-permute-start | bytes 1544 | tf_op jit(solution)/shard_map/ppermute | solution.py:339
  132.1 1.5 collective-permute-done.8
  133.6 1.9 %collective-permute-start.9 = (f32[1,128]{1,0:T(1,128)S(1)}, f32[1,128]{1,0:T(1,128)S(1)}, u32[]{:S(2)}, u32[]{:S(2)}) collective-permute-start(f32[1,128]{1,0:T(1,128)S(1)} %add_add_fusion), channel_id=1, source_target_pairs={{0,16},{16,0},{1,17},{17,1},{2,18},{18,2},{3,19},{19,3},{4,20},{20... | collective-permute-start | bytes 1544 | tf_op jit(solution)/shard_map/ppermute | solution.py:395
  135.5 1.1 collective-permute-done.9
  137.3 16.0 %all-to-all-done.5.terms_ref = bf16[4,272,256]{2,1,0:T(8,128)(2,1)S(1)} async-done(((bf16[4,272,256]{2,1,0:T(8,128)(2,1)}), bf16[4,272,256]{2,1,0:T(8,128)(2,1)S(1)}, u32[]{:S(2)}, u32[]{:S(2)}) %all-to-all-start.5) | async-done | bytes 557088 | tf_op jit(solution)/shard_map/all_to_all | solution.py:396
  (58 shorter events, 3.7 us)
Async XLA Ops:
  3.3 5.0 %copy-start.14 = (f32[4]{0:T(128)S(1)}, f32[4]{0:T(128)}, u32[]{:S(2)}) copy-start(f32[4]{0:T(128)} %param.17) | copy-start | bytes 52
  3.3 5.0 %copy-start.11 = (f32[4]{0:T(128)S(1)}, f32[4]{0:T(128)}, u32[]{:S(2)}) copy-start(f32[4]{0:T(128)} %param.16) | copy-start | bytes 52
  3.3 5.1 %copy-start.10 = (f32[4,256]{1,0:T(4,128)S(1)}, f32[4,256]{1,0:T(4,128)}, u32[]{:S(2)}) copy-start(f32[4,256]{1,0:T(4,128)} %raw_ref.1) | copy-start | bytes 12292
  3.3 5.5 %copy-start.9 = (bf16[256,256]{1,0:T(8,128)(2,1)S(1)}, bf16[256,256]{1,0:T(8,128)(2,1)}, u32[]{:S(2)}) copy-start(bf16[256,256]{1,0:T(8,128)(2,1)} %param.11) | copy-start | bytes 393220
  3.3 37.8 %all-to-all-start = ((bf16[4,256,1024]{2,1,0:T(8,128)(2,1)}), bf16[4,256,1024]{2,1,0:T(8,128)(2,1)S(1)}, u32[]{:S(2)}, u32[]{:S(2)}) async-start(bf16[4,256,1024]{2,1,0:T(8,128)(2,1)} %shard_map.138), calls=%async_computation | async-start | bytes 4194304 | tf_op jit(solution)/shard_map/all_to_all | solution.py:356
  41.1 12.4 %copy-start.3 = (bf16[256,128]{1,0:T(8,128)(2,1)S(1)}, bf16[256,128]{1,0:T(8,128)(2,1)}, u32[]{:S(2)}) copy-start(bf16[256,128]{1,0:T(8,128)(2,1)} %c_ref.3) | copy-start | bytes 196612
  42.6 10.8 %all-to-all-start.1 = ((bf16[4,256,256]{2,1,0:T(8,128)(2,1)}), bf16[4,256,256]{2,1,0:T(8,128)(2,1)S(1)}, u32[]{:S(2)}, u32[]{:S(2)}) async-start(bf16[4,256,256]{2,1,0:T(8,128)(2,1)} %shard_map.139), calls=%async_computation.1 | async-start | bytes 1048576 | tf_op jit(solution)/shard_map/all_to_all | solution.py:366
  48.3 44.1 %copy-start.2 = (f32[16,256]{1,0:T(8,128)}, f32[16,256]{1,0:T(8,128)S(1)}, u32[]{:S(2)}) copy-start(f32[16,256]{1,0:T(8,128)S(1)} %maximum_maximum_fusion.rows_ref) | copy-start | bytes 49156
  54.4 16.0 %all-to-all-start.2 = ((bf16[32,16,128]{2,1,0:T(8,128)(2,1)}), bf16[32,16,128]{2,1,0:T(8,128)(2,1)S(1)}, u32[]{:S(2)}, u32[]{:S(2)}) async-start(bf16[32,16,128]{2,1,0:T(8,128)(2,1)} %get-tuple-element.33), calls=%async_computation.2 | async-start | bytes 262144 | tf_op jit(solution)/shard_map/all_to_all | solution.py:380
  60.6 23.6 %copy-start.12 = (f32[4]{0:T(128)S(1)}, f32[4]{0:T(128)}, u32[]{:S(2)}) copy-start(f32[4]{0:T(128)} %param.18) | copy-start | bytes 52
  60.6 23.8 %copy-start.4 = (bf16[256,128]{1,0:T(8,128)(2,1)S(1)}, bf16[256,128]{1,0:T(8,128)(2,1)}, u32[]{:S(2)}) copy-start(bf16[256,128]{1,0:T(8,128)(2,1)} %b_ref.3) | copy-start | bytes 196612
  60.6 23.8 %copy-start.5 = (bf16[1,256,128]{2,1,0:T(8,128)(2,1)S(1)}, bf16[1,256,128]{2,1,0:T(8,128)(2,1)}, u32[]{:S(2)}) copy-start(bf16[1,256,128]{2,1,0:T(8,128)(2,1)} %param.19) | copy-start | bytes 196612
  60.6 23.8 %copy-start.7 = (bf16[256,256]{1,0:T(8,128)(2,1)S(1)}, bf16[256,256]{1,0:T(8,128)(2,1)}, u32[]{:S(2)}) copy-start(bf16[256,256]{1,0:T(8,128)(2,1)} %x_ref.1) | copy-start | bytes 393220
  60.6 23.8 %copy-start.8 = (bf16[256,256]{1,0:T(8,128)(2,1)S(1)}, bf16[256,256]{1,0:T(8,128)(2,1)}, u32[]{:S(2)}) copy-start(bf16[256,256]{1,0:T(8,128)(2,1)} %get-tuple-element.37.dy_ref) | copy-start | bytes 393220
  63.0 24.9 %collective-permute-start = (bf16[1024,256]{1,0:T(8,128)(2,1)}, bf16[1024,256]{1,0:T(8,128)(2,1)S(1)}, u32[]{:S(2)}, u32[]{:S(2)}) collective-permute-start(bf16[1024,256]{1,0:T(8,128)(2,1)} %get-tuple-element.61), channel_id=1, source_target_pairs={{0,8},{4,12},{8,0},{12,4},{1,9},{5,13},{9,1},{13,5},{2,10},{6,14},... | collective-permute-start | bytes 1572872 | tf_op jit(solution)/shard_map/ppermute | solution.py:364
  67.8 24.6 %collective-permute-start.1 = (bf16[1024,256]{1,0:T(8,128)(2,1)}, bf16[1024,256]{1,0:T(8,128)(2,1)S(1)}, u32[]{:S(2)}, u32[]{:S(2)}) collective-permute-start(bf16[1024,256]{1,0:T(8,128)(2,1)} %get-tuple-element.60), channel_id=1, source_target_pairs={{0,12},{4,0},{8,4},{12,8},{1,13},{5,1},{9,5},{13,9},{2,14},{6,2},{... | collective-permute-start | bytes 1572872 | tf_op jit(solution)/shard_map/ppermute | solution.py:364
  71.0 21.4 %all-to-all-start.3 = ((f32[32,8,128]{2,1,0:T(8,128)}), f32[32,8,128]{2,1,0:T(8,128)S(1)}, u32[]{:S(2)}, u32[]{:S(2)}) async-start(f32[32,8,128]{2,1,0:T(8,128)} %shard_map.141), calls=%async_computation.3 | async-start | bytes 262144 | tf_op jit(solution)/shard_map/all_to_all | solution.py:386
  80.8 32.8 %collective-permute-start.5 = (bf16[1024,256]{1,0:T(8,128)(2,1)}, bf16[1024,256]{1,0:T(8,128)(2,1)S(1)}, u32[]{:S(2)}, u32[]{:S(2)}) collective-permute-start(bf16[1024,256]{1,0:T(8,128)(2,1)} %get-tuple-element.58), channel_id=1, source_target_pairs={{0,4},{4,8},{8,12},{12,0},{1,5},{5,9},{9,13},{13,1},{2,6},{6,10},{... | collective-permute-start | bytes 1572872 | tf_op jit(solution)/shard_map/ppermute | solution.py:364
  87.2 0.6 copy-start.6
  87.8 10.6 %copy-start.1 = (bf16[384,256]{1,0:T(8,128)(2,1)}, bf16[384,256]{1,0:T(8,128)(2,1)S(1)}, u32[]{:S(2)}) copy-start(bf16[384,256]{1,0:T(8,128)(2,1)S(1)} %get-tuple-element.39.half_ref) | copy-start | bytes 589828
  92.4 6.0 %copy-start = (f32[32,8,128]{2,1,0:T(8,128)}, f32[32,8,128]{2,1,0:T(8,128)S(1)}, u32[]{:S(2)}) copy-start(f32[32,8,128]{2,1,0:T(8,128)S(1)} %all-to-all-done.3.carried_ref) | copy-start | bytes 393220
  93.6 20.1 %all-to-all-start.4 = ((bf16[4,320,256]{2,1,0:T(8,128)(2,1)}), bf16[4,320,256]{2,1,0:T(8,128)(2,1)S(1)}, u32[]{:S(2)}, u32[]{:S(2)}) async-start(bf16[4,320,256]{2,1,0:T(8,128)(2,1)} %get-tuple-element.43), calls=%async_computation.4 | async-start | bytes 1310720 | tf_op jit(solution)/shard_map/all_to_all | solution.py:388
  100.4 11.0 %collective-permute-start.2 = (f32[1,128]{1,0:T(1,128)}, f32[1,128]{1,0:T(1,128)S(1)}, u32[]{:S(2)}, u32[]{:S(2)}) collective-permute-start(f32[1,128]{1,0:T(1,128)} %get-tuple-element.42), channel_id=1, source_target_pairs={{0,32},{32,64},{64,96},{96,0},{1,33},{33,65},{65,97},{97,1},{2,34}... | collective-permute-start | bytes 1544 | tf_op jit(solution)/shard_map/ppermute | solution.py:339
  103.8 7.7 %collective-permute-start.3 = (f32[1,128]{1,0:T(1,128)}, f32[1,128]{1,0:T(1,128)S(1)}, u32[]{:S(2)}, u32[]{:S(2)}) collective-permute-start(f32[1,128]{1,0:T(1,128)} %get-tuple-element.42), channel_id=1, source_target_pairs={{0,64},{32,96},{64,0},{96,32},{1,65},{33,97},{65,1},{97,33},{2,66}... | collective-permute-start | bytes 1544 | tf_op jit(solution)/shard_map/ppermute | solution.py:339
  108.1 5.6 %collective-permute-start.4 = (f32[1,128]{1,0:T(1,128)}, f32[1,128]{1,0:T(1,128)S(1)}, u32[]{:S(2)}, u32[]{:S(2)}) collective-permute-start(f32[1,128]{1,0:T(1,128)} %get-tuple-element.42), channel_id=1, source_target_pairs={{0,96},{32,0},{64,32},{96,64},{1,97},{33,1},{65,33},{97,65},{2,98}... | collective-permute-start | bytes 1544 | tf_op jit(solution)/shard_map/ppermute | solution.py:339
  113.7 8.5 %copy-start.13 = (f32[1,128]{1,0:T(1,128)S(1)}, f32[1,128]{1,0:T(1,128)}, u32[]{:S(2)}) copy-start(f32[1,128]{1,0:T(1,128)} %get-tuple-element.42) | copy-start | bytes 1540
  115.2 38.2 %all-to-all-start.5 = ((bf16[4,272,256]{2,1,0:T(8,128)(2,1)}), bf16[4,272,256]{2,1,0:T(8,128)(2,1)S(1)}, u32[]{:S(2)}, u32[]{:S(2)}) async-start(bf16[4,272,256]{2,1,0:T(8,128)(2,1)} %shard_map.145), calls=%async_computation.5 | async-start | bytes 1114112 | tf_op jit(solution)/shard_map/all_to_all | solution.py:396
  122.2 9.9 %collective-permute-start.6 = (f32[1,128]{1,0:T(1,128)S(1)}, f32[1,128]{1,0:T(1,128)S(1)}, u32[]{:S(2)}, u32[]{:S(2)}) collective-permute-start(f32[1,128]{1,0:T(1,128)S(1)} %add_add_fusion.1), channel_id=1, source_target_pairs={{0,256},{128,384},{256,0},{384,128},{1,257},{129,385},{257,1},{385... | collective-permute-start | bytes 1544 | tf_op jit(solution)/shard_map/ppermute | solution.py:339
  126.3 5.9 %collective-permute-start.7 = (f32[1,128]{1,0:T(1,128)S(1)}, f32[1,128]{1,0:T(1,128)S(1)}, u32[]{:S(2)}, u32[]{:S(2)}) collective-permute-start(f32[1,128]{1,0:T(1,128)S(1)} %add_add_fusion.1), channel_id=1, source_target_pairs={{0,128},{128,256},{256,384},{384,0},{1,129},{129,257},{257,385},{3... | collective-permute-start | bytes 1544 | tf_op jit(solution)/shard_map/ppermute | solution.py:339
  128.2 5.4 %collective-permute-start.8 = (f32[1,128]{1,0:T(1,128)S(1)}, f32[1,128]{1,0:T(1,128)S(1)}, u32[]{:S(2)}, u32[]{:S(2)}) collective-permute-start(f32[1,128]{1,0:T(1,128)S(1)} %add_add_fusion.1), channel_id=1, source_target_pairs={{0,384},{128,0},{256,128},{384,256},{1,385},{129,1},{257,129},{385... | collective-permute-start | bytes 1544 | tf_op jit(solution)/shard_map/ppermute | solution.py:339
  133.6 3.0 %collective-permute-start.9 = (f32[1,128]{1,0:T(1,128)S(1)}, f32[1,128]{1,0:T(1,128)S(1)}, u32[]{:S(2)}, u32[]{:S(2)}) collective-permute-start(f32[1,128]{1,0:T(1,128)S(1)} %add_add_fusion), channel_id=1, source_target_pairs={{0,16},{16,0},{1,17},{17,1},{2,18},{18,2},{3,19},{19,3},{4,20},{20... | collective-permute-start | bytes 1544 | tf_op jit(solution)/shard_map/ppermute | solution.py:395

commit v8 on v7

--- a/solution.py
+++ b/solution.py
@@ -210,16 +210,16 @@
     )(dy, x_in, b_in, c_in, states, rows, skip)
 
 
-def dt_kernel(back_ref, half_ref, rows_ref, part_ref, carried_ref, states_ref, raw_ref, dt_ref, param_ref):
-    width, tokens = back_ref.shape
+def dt_rows(back, carried, half_ref, rows_ref, part_ref, states_ref, raw_ref, dt_ref, param_ref):
+    width, tokens = back.shape
     head_dim = width // 4
     cum, step = rows_ref[:4], rows_ref[4:8]
     last = cum[:, tokens - 1:]
     rate, bias = rows_ref[8:12], rows_ref[12:]
-    dots = jnp.sum((half_ref[:width].astype(f32) * back_ref[...]).reshape(4, head_dim, tokens), axis=1)
+    dots = jnp.sum((half_ref[:width].astype(f32) * back).reshape(4, head_dim, tokens), axis=1)
     end_decay = jnp.exp(last - cum)
     end_terms = step * end_decay * dots
-    carried = carried_ref[...].reshape(4, head_dim, -1)
+    carried = carried.reshape(4, head_dim, -1)
     held = jnp.sum(carried * states_ref[...].astype(f32).reshape(4, head_dim, -1), axis=1)
     tail = jnp.sum(end_terms, axis=1, keepdims=True) + jnp.exp(last) * jnp.sum(held, axis=1, keepdims=True)
     below = lax.broadcasted_iota(jnp.int32, (tokens, tokens), 0) >= lax.broadcasted_iota(jnp.int32, (tokens, tokens), 1)
@@ -241,21 +241,15 @@
     param_ref[...] = jnp.sum(placed, axis=0, keepdims=True)
 
 
-def dt_terms(back, half, rows, part, carried, states, dt_raw):
-    return pl.pallas_call(
-        dt_kernel,
-        out_shape=(jax.ShapeDtypeStruct(dt_raw.shape, f32), jax.ShapeDtypeStruct((1, 128), f32)),
-        cost_estimate=cost(1 << 22, 1 << 20),
-    )(back, half, rows, part, carried, states, dt_raw)
-
-
-def x_grad_kernel(carried_ref, b_ref, wide_ref, half_ref, rows_ref, sent_ref, back_ref):
+def x_grad_kernel(
+    carried_ref, b_ref, wide_ref, half_ref, rows_ref, part_ref, states_ref, raw_ref, sent_ref, dt_ref, param_ref
+):
     blocks, height, state_dim = carried_ref.shape
     width = blocks * height
     tokens = b_ref.shape[0]
-    carried = carried_ref[...].reshape(width, state_dim).astype(bf16)
+    carried_wide = carried_ref[...].reshape(width, state_dim)
+    carried = carried_wide.astype(bf16)
     back = dot_last(carried, b_ref[...])
-    back_ref[...] = back
     cum = rows_ref[:4]
     weight = over_channels(rows_ref[4:8] * jnp.exp(cum[:, tokens - 1:] - cum), width)
     x_grad = (wide_ref[:width] + weight * back).astype(bf16)
@@ -269,47 +263,55 @@
             sent_ref[y, width:] = db[y * rows:(y + 1) * rows]
         else:
             sent_ref[y, width:] = half_ref[width + (y - 2) * rows:width + (y - 1) * rows]
-
-
-def x_grads(carried, b_in, wide, half, rows):
+    dt_rows(back, carried_wide, half_ref, rows_ref, part_ref, states_ref, raw_ref, dt_ref, param_ref)
+
+
+def x_grads(carried, b_in, wide, half, rows, part, states, dt_raw):
     tokens, state_dim = b_in.shape
     inner = wide.shape[0] - state_dim
     return pl.pallas_call(
         x_grad_kernel,
-        out_shape=(pltpu.HBM((4, inner + state_dim // 2, tokens), bf16), pltpu.HBM((inner, tokens), f32)),
+        out_shape=(
+            pltpu.HBM((4, inner + state_dim // 2, tokens), bf16),
+            jax.ShapeDtypeStruct(dt_raw.shape, f32),
+            jax.ShapeDtypeStruct((1, 128), f32),
+        ),
         compiler_params=small(),
         cost_estimate=cost(4 * tokens * inner * 128, 2 << 20),
-    )(carried, b_in, wide, half, rows)
-
-
-def in_kernel(y_ref, got_ref, *refs):
-    *w_refs, out_ref = refs
-    quarter, inner = w_refs[0].shape
+    )(carried, b_in, wide, half, rows, part, states, dt_raw)
+
+
+def in_kernel(place_ref, got_ref, own_ref, near_ref, other_ref, half_ref, rest_ref, out_ref):
+    quarter, inner = own_ref.shape
     feats = quarter // 4
     rows = out_ref.shape[1] - feats
-    y = y_ref[0]
-    x_grad = jnp.concatenate([got_ref[lax.rem(y + 4 - s, 4), :inner] for s in range(4)], axis=0)
+    y, core = place_ref[0], place_ref[1]
+    sources = [y, lax.rem(y + 3 + 2 * core, 4), lax.rem(y + 5 - 2 * core, 4), lax.rem(y + 2, 4)]
+    x_grad = jnp.concatenate([got_ref[source, :inner] for source in sources], axis=0)
     for z in range(4):
         at = slice(inner + z * rows, inner + (z + 1) * rows)
         bc = got_ref[0, at].astype(f32)
         for other in range(1, 4):
             bc = bc + got_ref[other, at].astype(f32)
         out_ref[z, feats:] = bc.astype(bf16)
-        w = jnp.concatenate([w_ref[z * feats:(z + 1) * feats] for w_ref in w_refs], axis=1)
+        mine = slice(z * feats, (z + 1) * feats)
+        part = slice((z % 2) * feats, (z % 2 + 1) * feats)
+        far = jnp.where(core == z // 2, half_ref[part], rest_ref[part])
+        w = jnp.concatenate([own_ref[mine], near_ref[mine], other_ref[mine], far], axis=1)
         out_ref[z, :feats] = jnp.dot(w, x_grad, preferred_element_type=f32).astype(bf16)
 
 
-def in_products(y, got, pieces):
+def in_products(place, got, pieces):
     quarter, inner = pieces[0].shape
     _, height, tokens = got.shape
     feats, rows = quarter // 4, (height - inner) // 4
     return pl.pallas_call(
         in_kernel,
-        in_specs=[pl.BlockSpec(memory_space=pltpu.SMEM)] + [pl.BlockSpec(memory_space=pltpu.VMEM)] * 5,
+        in_specs=[pl.BlockSpec(memory_space=pltpu.SMEM)] + [pl.BlockSpec(memory_space=pltpu.VMEM)] * 6,
         out_shape=pltpu.HBM((4, feats + rows, tokens), bf16),
         compiler_params=small(),
         cost_estimate=cost(8 * quarter * inner * tokens, 4 << 20),
-    )(y.reshape(1), got, *pieces)
+    )(place, got, *pieces)
 
 
 def sum_kernel(terms_ref, in_ref, bc_ref):
@@ -358,11 +360,11 @@
     products = partial_products(near, w_out_y)
     w_in_held, products = lax.optimization_barrier((w_in, products))
     quarter = w_in.shape[0] // 4
-
-    def exchanged(source, s):
-        piece = lax.dynamic_slice_in_dim(source, lax.rem(y + s, 4) * quarter, quarter)
-        return lax.ppermute(piece, "y", [(i, (i + s) % 4) for i in range(4)])
-
+    core = lax.axis_index("core")
+    own = lax.dynamic_slice_in_dim(w_in_held, y * quarter, quarter)
+    near_piece = lax.dynamic_slice_in_dim(w_in_held, lax.rem(y + 1 + 2 * core, 4) * quarter, quarter)
+    far_at = lax.rem(y + 2, 4) * quarter + core * (quarter // 2)
+    far_half = lax.dynamic_slice_in_dim(w_in_held, far_at, quarter // 2)
     head_parts = lax.all_to_all(products, "y", 0, 0)
 
     decay_rate = jnp.exp(a_log)
@@ -376,19 +378,21 @@
     ends = jnp.pad(three_parts(jnp.exp(cumlog[:, -1])), ((0, 0), (0, 5)))
     ends = jnp.broadcast_to(ends[:, None, :, None], (group_heads, blocks // group_heads, 8, state_dim))
     skip = jnp.repeat(d_skip, head_dim)[None]
+    own, far_half, head_parts = lax.optimization_barrier((own, far_half, head_parts))
+    one_step = [((c, i), (c, (i + 1 + 2 * c) % 4)) for c in range(2) for i in range(4)]
+    near_piece = lax.ppermute(near_piece, ("core", "y"), [(4 * a[0] + a[1], 4 * b[0] + b[1]) for a, b in one_step])
+    far_half = lax.ppermute(far_half, "y", [(i, (i + 2) % 4) for i in range(4)])
+    swap = [(0, 1), (1, 0)]
+    held = [own, near_piece, lax.ppermute(near_piece, "core", swap), far_half, lax.ppermute(far_half, "core", swap)]
     dy, sent = local_states(head_parts, rows, c_in, ends.reshape(blocks, 8, state_dim))
     ahead = suffix_scan(lax.all_to_all(sent, SEQ, 0, 0))
-    held = [None, None, exchanged(w_in_held, 2), exchanged(w_in_held, 3)]
-    ahead, dy, w_in_late = lax.optimization_barrier((ahead, dy, w_in_held))
-    held[0] = lax.dynamic_slice_in_dim(w_in_late, y * quarter, quarter)
-    held[1] = exchanged(w_in_late, 1)
+    ahead, dy = lax.optimization_barrier((ahead, dy))
     wide, half, part = intra_terms(dy, x_in, b_in, c_in, entry_state, rows, skip)
-    held[2], held[3], carried = lax.optimization_barrier((held[2], held[3], lax.all_to_all(ahead, SEQ, 0, 0)))
-    sent_y, back = x_grads(carried, b_in, wide, half, rows)
+    *held, carried = lax.optimization_barrier((*held, lax.all_to_all(ahead, SEQ, 0, 0)))
+    sent_y, dt_grad, row = x_grads(carried, b_in, wide, half, rows, part, entry_state, dt_raw)
     got = lax.all_to_all(sent_y, "y", 0, 0)
-    dt_grad, row = dt_terms(back, half, rows, part, carried, entry_state, dt_raw)
     *rounds, got = lax.optimization_barrier((*shifted(row, "zl"), got))
-    terms = in_products(y, got, held)
+    terms = in_products(jnp.stack([y, core]), got, held)
     *rounds, terms = lax.optimization_barrier((*rounds, terms))
     row = paired(row, rounds)
     row = paired(row, shifted(row, "x"))

time: 155 us -> 146 us (0.942)
  the two profiles are of different devices: /device:TPU:18 before, /device:TPU:1 now
where the time goes in v8:
time: 146 us; the launch traced here: 143 us
  starting transfers between devices  72.3 us (50%)
  blocking collectives  30.9 us (21%)
  waiting for transfers between devices  21.5 us (15%)
  Pallas kernels  12.7 us (9%)
  local copies, waits for them, and re-layouts  4.14 us (3%)
    all_gather x1, blocking collectives, shards(): near = lax.all_gather(out_grad, 'zh', axis=1, tiled=True)  30.9 us
    ppermute x6, starting transfers between devices, shifted(): lax.ppermute(row, axis, [(i, (i + s) % 4) for i in range(4)])  18.9 us
    all_to_all x1, waiting for transfers between devices, shards(): lax.all_to_all(terms, 'zh', 0, 0)  12.5 us
    all_to_all x1, starting transfers between devices, shards(): ahead = suffix_scan(lax.all_to_all(sent, SEQ, 0, 0))  11.3 us
    all_to_all x1, starting transfers between devices, shards(): got = lax.all_to_all(sent_y, 'y', 0, 0)  5.87 us
    all_to_all x1, starting transfers between devices, shards(): lax.all_to_all(terms, 'zh', 0, 0)  5.76 us
    ppermute x1, starting transfers between devices, shards(): row = row + lax.ppermute(row, 'core', [(0, 1), (1, 0)])  5.57 us
    all_to_all x1, starting transfers between devices, shards(): w_out_y = lax.all_to_all(regrouped(w_out), 'y', 0, 0)  5.16 us
  transfers between devices with their start and end apart: 17, of which 6 were waited for; matrix products, arithmetic and copies ran while one was open for 3% of the time, Pallas kernels for 3%

profile of v8, /device:TPU:1, one launch (start us, length us, event | category | flops | bytes accessed | tf_op | source)
XLA Modules:
  0.0 143.1 jit_solution(7472012601335964081)
XLA Ops:
  0.6 2.6 %shard_map.138 = bf16[4,256,1024]{2,1,0:T(8,128)(2,1)} custom-call(bf16[256,4096]{1,0:T(8,128)(2,1)} %w_ref.1), custom_call_target="tpu_custom_call" | custom-call | bytes 4194304 | tf_op jit(solution)/shard_map/pallas_call | solution.py:74
  3.3 5.2 %all-to-all-start = ((bf16[4,256,1024]{2,1,0:T(8,128)(2,1)}), bf16[4,256,1024]{2,1,0:T(8,128)(2,1)S(1)}, u32[]{:S(2)}, u32[]{:S(2)}) async-start(bf16[4,256,1024]{2,1,0:T(8,128)(2,1)} %shard_map.138), calls=%async_computation | async-start | bytes 4194304 | tf_op jit(solution)/shard_map/all_to_all | solution.py:358
  9.0 30.9 %all_gather.3.near_ref = bf16[256,1024]{1,0:T(8,128)(2,1)S(1)} all-gather(bf16[256,256]{1,0:T(8,128)(2,1)S(1)} %copy-done.6), channel_id=1, replica_groups=mesh['x'=4,'zl'=4,'core'=2,'y'=4,'zh'=4] {'zh'}, dimensions={1}, use_global_device_ids=true | all-gather | bytes 655360 | tf_op jit(solution)/shard_map/all_gather | solution.py:359
  39.9 1.5 %shard_map.139 = bf16[4,256,256]{2,1,0:T(8,128)(2,1)} custom-call(bf16[256,1024]{1,0:T(8,128)(2,1)S(1)} %all_gather.3.near_ref, bf16[4,256,1024]{2,1,0:T(8,128)(2,1)S(1)} %all-to-all-done.w_ref), custom_call_target="tpu_custom_call" | custom-call | flops 536870912 | bytes 4194304 | tf_op jit(solution)/shard_map/pallas_call | solution.py:97
  41.4 3.6 %all-to-all-start.1 = ((bf16[4,256,256]{2,1,0:T(8,128)(2,1)}), bf16[4,256,256]{2,1,0:T(8,128)(2,1)S(1)}, u32[]{:S(2)}, u32[]{:S(2)}) async-start(bf16[4,256,256]{2,1,0:T(8,128)(2,1)} %shard_map.139), calls=%async_computation.1 | async-start | bytes 1048576 | tf_op jit(solution)/shard_map/all_to_all | solution.py:368
  45.1 1.3 constant_dynamic-slice_fusion
  46.5 4.5 %collective-permute-start = (bf16[1024,256]{1,0:T(8,128)(2,1)S(1)}, bf16[1024,256]{1,0:T(8,128)(2,1)S(1)}, u32[]{:S(2)}, u32[]{:S(2)}) collective-permute-start(bf16[1024,256]{1,0:T(8,128)(2,1)S(1)} %get-tuple-element.66), channel_id=1, source_target_pairs={{0,4},{4,8},{8,12},{12,0},{16,28},{20,16},{24,20},{28,24},{1,5},{5... | collective-permute-start | bytes 1572872 | tf_op jit(solution)/shard_map/ppermute | solution.py:383
  51.0 1.0 constant_dynamic-slice_fusion.1
  52.1 0.9 shard_map.140
  53.0 11.3 %all-to-all-start.2 = ((bf16[32,16,128]{2,1,0:T(8,128)(2,1)}), bf16[32,16,128]{2,1,0:T(8,128)(2,1)S(1)}, u32[]{:S(2)}, u32[]{:S(2)}) async-start(bf16[32,16,128]{2,1,0:T(8,128)(2,1)} %get-tuple-element.40), calls=%async_computation.2 | async-start | bytes 262144 | tf_op jit(solution)/shard_map/all_to_all | solution.py:388
  64.3 2.9 %collective-permute-start.2 = (bf16[512,256]{1,0:T(8,128)(2,1)S(1)}, bf16[512,256]{1,0:T(8,128)(2,1)S(1)}, u32[]{:S(2)}, u32[]{:S(2)}) collective-permute-start(bf16[512,256]{1,0:T(8,128)(2,1)S(1)} %constant_dynamic-slice_fusion.1), channel_id=1, source_target_pairs={{0,8},{4,12},{8,0},{12,4},{1,9},{5,13},{9,1},{13,5},{2,10},{6,14},... | collective-permute-start | bytes 786440 | tf_op jit(solution)/shard_map/ppermute | solution.py:384
  67.2 2.4 %collective-permute-start.1 = (bf16[1024,256]{1,0:T(8,128)(2,1)S(1)}, bf16[1024,256]{1,0:T(8,128)(2,1)S(1)}, u32[]{:S(2)}, u32[]{:S(2)}) collective-permute-start(bf16[1024,256]{1,0:T(8,128)(2,1)S(1)} %collective-permute-done.near_ref), channel_id=1, source_target_pairs={{0,16},{16,0},{1,17},{17,1},{2,18},{18,2},{3,19},{19,3},{4,20},{20... | collective-permute-start | bytes 1572872 | tf_op jit(solution)/shard_map/ppermute | solution.py:386
  69.6 3.4 %all-to-all-done.2.parts_ref = bf16[32,16,128]{2,1,0:T(8,128)(2,1)S(1)} async-done(((bf16[32,16,128]{2,1,0:T(8,128)(2,1)}), bf16[32,16,128]{2,1,0:T(8,128)(2,1)S(1)}, u32[]{:S(2)}, u32[]{:S(2)}) %all-to-all-start.2) | async-done | bytes 131104 | tf_op jit(solution)/shard_map/all_to_all | solution.py:388
  73.7 4.2 %all-to-all-start.3 = ((f32[32,8,128]{2,1,0:T(8,128)}), f32[32,8,128]{2,1,0:T(8,128)S(1)}, u32[]{:S(2)}, u32[]{:S(2)}) async-start(f32[32,8,128]{2,1,0:T(8,128)} %shard_map.141), calls=%async_computation.3 | async-start | bytes 262144 | tf_op jit(solution)/shard_map/all_to_all | solution.py:391
  77.9 2.1 %collective-permute-start.3 = (bf16[512,256]{1,0:T(8,128)(2,1)S(1)}, bf16[512,256]{1,0:T(8,128)(2,1)S(1)}, u32[]{:S(2)}, u32[]{:S(2)}) collective-permute-start(bf16[512,256]{1,0:T(8,128)(2,1)S(1)} %collective-permute-done.2.half_ref), channel_id=1, source_target_pairs={{0,16},{16,0},{1,17},{17,1},{2,18},{18,2},{3,19},{19,3},{4,20},{20... | collective-permute-start | bytes 786440 | tf_op jit(solution)/shard_map/ppermute | solution.py:386
  80.3 0.9 copy-done.5
  81.2 2.8 %shard_map.142 = (f32[384,256]{1,0:T(8,128)S(1)}, bf16[384,256]{1,0:T(8,128)(2,1)S(1)}, f32[16,256]{1,0:T(8,128)S(1)}) custom-call(bf16[256,256]{1,0:T(8,128)(2,1)S(1)} %copy-done.5, bf16[256,256]{1,0:T(8,128)(2,1)S(1)} %copy-done.4, bf16[256,128]{1,0:T(8,128)(2,1)S(1)} %copy-done.1, bf16[256,128]{1,0:T(8,128)(2,1)S(1)} %copy-done, ...), custom_call_target="tpu_custom_call" | custom-call | flops 234881024 | bytes 2097152 | tf_op jit(solution)/shard_map/pallas_call | solution.py:205
  84.0 2.6 %all-to-all-done.3.carried_ref = f32[32,8,128]{2,1,0:T(8,128)S(1)} async-done(((f32[32,8,128]{2,1,0:T(8,128)}), f32[32,8,128]{2,1,0:T(8,128)S(1)}, u32[]{:S(2)}, u32[]{:S(2)}) %all-to-all-start.3) | async-done | bytes 131104 | tf_op jit(solution)/shard_map/all_to_all | solution.py:391
  86.6 1.3 shard_map.143
  88.0 5.9 %all-to-all-start.4 = ((bf16[4,320,256]{2,1,0:T(8,128)(2,1)}), bf16[4,320,256]{2,1,0:T(8,128)(2,1)S(1)}, u32[]{:S(2)}, u32[]{:S(2)}) async-start(bf16[4,320,256]{2,1,0:T(8,128)(2,1)} %get-tuple-element.49), calls=%async_computation.4 | async-start | bytes 1310720 | tf_op jit(solution)/shard_map/all_to_all | solution.py:393
  93.8 2.1 %collective-permute-start.4 = (f32[1,128]{1,0:T(1,128)S(1)}, f32[1,128]{1,0:T(1,128)S(1)}, u32[]{:S(2)}, u32[]{:S(2)}) collective-permute-start(f32[1,128]{1,0:T(1,128)S(1)} %get-tuple-element.48), channel_id=1, source_target_pairs={{0,32},{32,64},{64,96},{96,0},{1,33},{33,65},{65,97},{97,1},{2,34}... | collective-permute-start | bytes 1544 | tf_op jit(solution)/shard_map/ppermute | solution.py:341
  96.0 2.9 %collective-permute-start.5 = (f32[1,128]{1,0:T(1,128)S(1)}, f32[1,128]{1,0:T(1,128)S(1)}, u32[]{:S(2)}, u32[]{:S(2)}) collective-permute-start(f32[1,128]{1,0:T(1,128)S(1)} %get-tuple-element.48), channel_id=1, source_target_pairs={{0,64},{32,96},{64,0},{96,32},{1,65},{33,97},{65,1},{97,33},{2,66}... | collective-permute-start | bytes 1544 | tf_op jit(solution)/shard_map/ppermute | solution.py:341
  98.9 3.9 %collective-permute-start.6 = (f32[1,128]{1,0:T(1,128)S(1)}, f32[1,128]{1,0:T(1,128)S(1)}, u32[]{:S(2)}, u32[]{:S(2)}) collective-permute-start(f32[1,128]{1,0:T(1,128)S(1)} %get-tuple-element.48), channel_id=1, source_target_pairs={{0,96},{32,0},{64,32},{96,64},{1,97},{33,1},{65,33},{97,65},{2,98}... | collective-permute-start | bytes 1544 | tf_op jit(solution)/shard_map/ppermute | solution.py:341
  102.9 1.4 collective-permute-done.6
  104.3 2.1 %shard_map.144 = bf16[4,272,256]{2,1,0:T(8,128)(2,1)} custom-call(s32[2]{0:T(128)S(1)} %pad_add_fusion.place_ref, bf16[4,320,256]{2,1,0:T(8,128)(2,1)S(1)} %all-to-all-done.4.got_ref, bf16[1024,256]{1,0:T(8,128)(2,1)S(1)} %get-tuple-element.54.own_ref, bf16[1024,256]{1,0:T(8,128)(2,1)S(1)} %collective-permute-done.near_ref, ...), custom_call_target="tpu_custom_call" | custom-call | flops 536870912 | bytes 4194304 | tf_op jit(solution)/shard_map/pallas_call | solution.py:308
  106.4 5.8 %all-to-all-start.5 = ((bf16[4,272,256]{2,1,0:T(8,128)(2,1)}), bf16[4,272,256]{2,1,0:T(8,128)(2,1)S(1)}, u32[]{:S(2)}, u32[]{:S(2)}) async-start(bf16[4,272,256]{2,1,0:T(8,128)(2,1)} %shard_map.144), calls=%async_computation.5 | async-start | bytes 1114112 | tf_op jit(solution)/shard_map/all_to_all | solution.py:400
  112.2 3.4 %collective-permute-start.7 = (f32[1,128]{1,0:T(1,128)S(1)}, f32[1,128]{1,0:T(1,128)S(1)}, u32[]{:S(2)}, u32[]{:S(2)}) collective-permute-start(f32[1,128]{1,0:T(1,128)S(1)} %add_add_fusion.1), channel_id=1, source_target_pairs={{0,256},{128,384},{256,0},{384,128},{1,257},{129,385},{257,1},{385... | collective-permute-start | bytes 1544 | tf_op jit(solution)/shard_map/ppermute | solution.py:341
  115.6 2.4 %collective-permute-start.8 = (f32[1,128]{1,0:T(1,128)S(1)}, f32[1,128]{1,0:T(1,128)S(1)}, u32[]{:S(2)}, u32[]{:S(2)}) collective-permute-start(f32[1,128]{1,0:T(1,128)S(1)} %add_add_fusion.1), channel_id=1, source_target_pairs={{0,128},{128,256},{256,384},{384,0},{1,129},{129,257},{257,385},{3... | collective-permute-start | bytes 1544 | tf_op jit(solution)/shard_map/ppermute | solution.py:341
  117.9 4.1 %collective-permute-start.9 = (f32[1,128]{1,0:T(1,128)S(1)}, f32[1,128]{1,0:T(1,128)S(1)}, u32[]{:S(2)}, u32[]{:S(2)}) collective-permute-start(f32[1,128]{1,0:T(1,128)S(1)} %add_add_fusion.1), channel_id=1, source_target_pairs={{0,384},{128,0},{256,128},{384,256},{1,385},{129,1},{257,129},{385... | collective-permute-start | bytes 1544 | tf_op jit(solution)/shard_map/ppermute | solution.py:341
  122.8 5.6 %collective-permute-start.10 = (f32[1,128]{1,0:T(1,128)S(1)}, f32[1,128]{1,0:T(1,128)S(1)}, u32[]{:S(2)}, u32[]{:S(2)}) collective-permute-start(f32[1,128]{1,0:T(1,128)S(1)} %add_add_fusion), channel_id=1, source_target_pairs={{0,16},{16,0},{1,17},{17,1},{2,18},{18,2},{3,19},{19,3},{4,20},{20... | collective-permute-start | bytes 1544 | tf_op jit(solution)/shard_map/ppermute | solution.py:399
  128.4 0.8 collective-permute-done.10
  129.8 12.5 %all-to-all-done.5.terms_ref = bf16[4,272,256]{2,1,0:T(8,128)(2,1)S(1)} async-done(((bf16[4,272,256]{2,1,0:T(8,128)(2,1)}), bf16[4,272,256]{2,1,0:T(8,128)(2,1)S(1)}, u32[]{:S(2)}, u32[]{:S(2)}) %all-to-all-start.5) | async-done | bytes 557088 | tf_op jit(solution)/shard_map/all_to_all | solution.py:400
  (50 shorter events, 3.8 us)
Async XLA Ops:
  3.3 5.2 %copy-start.9 = (f32[4]{0:T(128)S(1)}, f32[4]{0:T(128)}, u32[]{:S(2)}) copy-start(f32[4]{0:T(128)} %param.17) | copy-start | bytes 52
  3.3 5.2 %copy-start.7 = (f32[4]{0:T(128)S(1)}, f32[4]{0:T(128)}, u32[]{:S(2)}) copy-start(f32[4]{0:T(128)} %param.16) | copy-start | bytes 52
  3.3 5.3 %copy-start.3 = (f32[4,256]{1,0:T(4,128)S(1)}, f32[4,256]{1,0:T(4,128)}, u32[]{:S(2)}) copy-start(f32[4,256]{1,0:T(4,128)} %raw_ref.1) | copy-start | bytes 12292
  3.3 5.7 %copy-start.6 = (bf16[256,256]{1,0:T(8,128)(2,1)S(1)}, bf16[256,256]{1,0:T(8,128)(2,1)}, u32[]{:S(2)}) copy-start(bf16[256,256]{1,0:T(8,128)(2,1)} %param.11) | copy-start | bytes 393220
  3.3 36.6 %all-to-all-start = ((bf16[4,256,1024]{2,1,0:T(8,128)(2,1)}), bf16[4,256,1024]{2,1,0:T(8,128)(2,1)S(1)}, u32[]{:S(2)}, u32[]{:S(2)}) async-start(bf16[4,256,1024]{2,1,0:T(8,128)(2,1)} %shard_map.138), calls=%async_computation | async-start | bytes 4194304 | tf_op jit(solution)/shard_map/all_to_all | solution.py:358
  41.4 10.7 %copy-start = (bf16[256,128]{1,0:T(8,128)(2,1)S(1)}, bf16[256,128]{1,0:T(8,128)(2,1)}, u32[]{:S(2)}) copy-start(bf16[256,128]{1,0:T(8,128)(2,1)} %c_ref.3) | copy-start | bytes 196612
  41.4 10.6 %all-to-all-start.1 = ((bf16[4,256,256]{2,1,0:T(8,128)(2,1)}), bf16[4,256,256]{2,1,0:T(8,128)(2,1)S(1)}, u32[]{:S(2)}, u32[]{:S(2)}) async-start(bf16[4,256,256]{2,1,0:T(8,128)(2,1)} %shard_map.139), calls=%async_computation.1 | async-start | bytes 1048576 | tf_op jit(solution)/shard_map/all_to_all | solution.py:368
  45.1 35.0 %copy-start.8 = (f32[4]{0:T(128)S(1)}, f32[4]{0:T(128)}, u32[]{:S(2)}) copy-start(f32[4]{0:T(128)} %param.18) | copy-start | bytes 52
  45.1 35.1 %copy-start.1 = (bf16[256,128]{1,0:T(8,128)(2,1)S(1)}, bf16[256,128]{1,0:T(8,128)(2,1)}, u32[]{:S(2)}) copy-start(bf16[256,128]{1,0:T(8,128)(2,1)} %b_ref.3) | copy-start | bytes 196612
  45.1 35.1 %copy-start.2 = (bf16[1,256,128]{2,1,0:T(8,128)(2,1)S(1)}, bf16[1,256,128]{2,1,0:T(8,128)(2,1)}, u32[]{:S(2)}) copy-start(bf16[1,256,128]{2,1,0:T(8,128)(2,1)} %param.19) | copy-start | bytes 196612
  45.1 35.1 %copy-start.4 = (bf16[256,256]{1,0:T(8,128)(2,1)S(1)}, bf16[256,256]{1,0:T(8,128)(2,1)}, u32[]{:S(2)}) copy-start(bf16[256,256]{1,0:T(8,128)(2,1)} %x_ref.1) | copy-start | bytes 393220
  46.5 20.7 %collective-permute-start = (bf16[1024,256]{1,0:T(8,128)(2,1)S(1)}, bf16[1024,256]{1,0:T(8,128)(2,1)S(1)}, u32[]{:S(2)}, u32[]{:S(2)}) collective-permute-start(bf16[1024,256]{1,0:T(8,128)(2,1)S(1)} %get-tuple-element.66), channel_id=1, source_target_pairs={{0,4},{4,8},{8,12},{12,0},{16,28},{20,16},{24,20},{28,24},{1,5},{5... | collective-permute-start | bytes 1572872 | tf_op jit(solution)/shard_map/ppermute | solution.py:383
  53.0 20.0 %all-to-all-start.2 = ((bf16[32,16,128]{2,1,0:T(8,128)(2,1)}), bf16[32,16,128]{2,1,0:T(8,128)(2,1)S(1)}, u32[]{:S(2)}, u32[]{:S(2)}) async-start(bf16[32,16,128]{2,1,0:T(8,128)(2,1)} %get-tuple-element.40), calls=%async_computation.2 | async-start | bytes 262144 | tf_op jit(solution)/shard_map/all_to_all | solution.py:388
  64.3 13.6 %collective-permute-start.2 = (bf16[512,256]{1,0:T(8,128)(2,1)S(1)}, bf16[512,256]{1,0:T(8,128)(2,1)S(1)}, u32[]{:S(2)}, u32[]{:S(2)}) collective-permute-start(bf16[512,256]{1,0:T(8,128)(2,1)S(1)} %constant_dynamic-slice_fusion.1), channel_id=1, source_target_pairs={{0,8},{4,12},{8,0},{12,4},{1,9},{5,13},{9,1},{13,5},{2,10},{6,14},... | collective-permute-start | bytes 786440 | tf_op jit(solution)/shard_map/ppermute | solution.py:384
  67.2 16.8 %collective-permute-start.1 = (bf16[1024,256]{1,0:T(8,128)(2,1)S(1)}, bf16[1024,256]{1,0:T(8,128)(2,1)S(1)}, u32[]{:S(2)}, u32[]{:S(2)}) collective-permute-start(bf16[1024,256]{1,0:T(8,128)(2,1)S(1)} %collective-permute-done.near_ref), channel_id=1, source_target_pairs={{0,16},{16,0},{1,17},{17,1},{2,18},{18,2},{3,19},{19,3},{4,20},{20... | collective-permute-start | bytes 1572872 | tf_op jit(solution)/shard_map/ppermute | solution.py:386
  73.7 12.9 %all-to-all-start.3 = ((f32[32,8,128]{2,1,0:T(8,128)}), f32[32,8,128]{2,1,0:T(8,128)S(1)}, u32[]{:S(2)}, u32[]{:S(2)}) async-start(f32[32,8,128]{2,1,0:T(8,128)} %shard_map.141), calls=%async_computation.3 | async-start | bytes 262144 | tf_op jit(solution)/shard_map/all_to_all | solution.py:391
  77.9 6.1 %collective-permute-start.3 = (bf16[512,256]{1,0:T(8,128)(2,1)S(1)}, bf16[512,256]{1,0:T(8,128)(2,1)S(1)}, u32[]{:S(2)}, u32[]{:S(2)}) collective-permute-start(bf16[512,256]{1,0:T(8,128)(2,1)S(1)} %collective-permute-done.2.half_ref), channel_id=1, source_target_pairs={{0,16},{16,0},{1,17},{17,1},{2,18},{18,2},{3,19},{19,3},{4,20},{20... | collective-permute-start | bytes 786440 | tf_op jit(solution)/shard_map/ppermute | solution.py:386
  80.3 0.9 copy-start.5
  88.0 16.4 %all-to-all-start.4 = ((bf16[4,320,256]{2,1,0:T(8,128)(2,1)}), bf16[4,320,256]{2,1,0:T(8,128)(2,1)S(1)}, u32[]{:S(2)}, u32[]{:S(2)}) async-start(bf16[4,320,256]{2,1,0:T(8,128)(2,1)} %get-tuple-element.49), calls=%async_computation.4 | async-start | bytes 1310720 | tf_op jit(solution)/shard_map/all_to_all | solution.py:393
  93.8 9.1 %collective-permute-start.4 = (f32[1,128]{1,0:T(1,128)S(1)}, f32[1,128]{1,0:T(1,128)S(1)}, u32[]{:S(2)}, u32[]{:S(2)}) collective-permute-start(f32[1,128]{1,0:T(1,128)S(1)} %get-tuple-element.48), channel_id=1, source_target_pairs={{0,32},{32,64},{64,96},{96,0},{1,33},{33,65},{65,97},{97,1},{2,34}... | collective-permute-start | bytes 1544 | tf_op jit(solution)/shard_map/ppermute | solution.py:341
  96.0 7.0 %collective-permute-start.5 = (f32[1,128]{1,0:T(1,128)S(1)}, f32[1,128]{1,0:T(1,128)S(1)}, u32[]{:S(2)}, u32[]{:S(2)}) collective-permute-start(f32[1,128]{1,0:T(1,128)S(1)} %get-tuple-element.48), channel_id=1, source_target_pairs={{0,64},{32,96},{64,0},{96,32},{1,65},{33,97},{65,1},{97,33},{2,66}... | collective-permute-start | bytes 1544 | tf_op jit(solution)/shard_map/ppermute | solution.py:341
  98.9 5.4 %collective-permute-start.6 = (f32[1,128]{1,0:T(1,128)S(1)}, f32[1,128]{1,0:T(1,128)S(1)}, u32[]{:S(2)}, u32[]{:S(2)}) collective-permute-start(f32[1,128]{1,0:T(1,128)S(1)} %get-tuple-element.48), channel_id=1, source_target_pairs={{0,96},{32,0},{64,32},{96,64},{1,97},{33,1},{65,33},{97,65},{2,98}... | collective-permute-start | bytes 1544 | tf_op jit(solution)/shard_map/ppermute | solution.py:341
  106.4 36.0 %all-to-all-start.5 = ((bf16[4,272,256]{2,1,0:T(8,128)(2,1)}), bf16[4,272,256]{2,1,0:T(8,128)(2,1)S(1)}, u32[]{:S(2)}, u32[]{:S(2)}) async-start(bf16[4,272,256]{2,1,0:T(8,128)(2,1)} %shard_map.144), calls=%async_computation.5 | async-start | bytes 1114112 | tf_op jit(solution)/shard_map/all_to_all | solution.py:400
  112.2 9.9 %collective-permute-start.7 = (f32[1,128]{1,0:T(1,128)S(1)}, f32[1,128]{1,0:T(1,128)S(1)}, u32[]{:S(2)}, u32[]{:S(2)}) collective-permute-start(f32[1,128]{1,0:T(1,128)S(1)} %add_add_fusion.1), channel_id=1, source_target_pairs={{0,256},{128,384},{256,0},{384,128},{1,257},{129,385},{257,1},{385... | collective-permute-start | bytes 1544 | tf_op jit(solution)/shard_map/ppermute | solution.py:341
  115.6 6.5 %collective-permute-start.8 = (f32[1,128]{1,0:T(1,128)S(1)}, f32[1,128]{1,0:T(1,128)S(1)}, u32[]{:S(2)}, u32[]{:S(2)}) collective-permute-start(f32[1,128]{1,0:T(1,128)S(1)} %add_add_fusion.1), channel_id=1, source_target_pairs={{0,128},{128,256},{256,384},{384,0},{1,129},{129,257},{257,385},{3... | collective-permute-start | bytes 1544 | tf_op jit(solution)/shard_map/ppermute | solution.py:341
  117.9 4.8 %collective-permute-start.9 = (f32[1,128]{1,0:T(1,128)S(1)}, f32[1,128]{1,0:T(1,128)S(1)}, u32[]{:S(2)}, u32[]{:S(2)}) collective-permute-start(f32[1,128]{1,0:T(1,128)S(1)} %add_add_fusion.1), channel_id=1, source_target_pairs={{0,384},{128,0},{256,128},{384,256},{1,385},{129,1},{257,129},{385... | collective-permute-start | bytes 1544 | tf_op jit(solution)/shard_map/ppermute | solution.py:341
  122.8 6.4 %collective-permute-start.10 = (f32[1,128]{1,0:T(1,128)S(1)}, f32[1,128]{1,0:T(1,128)S(1)}, u32[]{:S(2)}, u32[]{:S(2)}) collective-permute-start(f32[1,128]{1,0:T(1,128)S(1)} %add_add_fusion), channel_id=1, source_target_pairs={{0,16},{16,0},{1,17},{17,1},{2,18},{18,2},{3,19},{19,3},{4,20},{20... | collective-permute-start | bytes 1544 | tf_op jit(solution)/shard_map/ppermute | solution.py:399

commit v9 on v8

--- a/solution.py
+++ b/solution.py
@@ -281,24 +281,25 @@
     )(carried, b_in, wide, half, rows, part, states, dt_raw)
 
 
-def in_kernel(place_ref, got_ref, own_ref, near_ref, other_ref, half_ref, rest_ref, out_ref):
+def in_kernel(place_ref, got_ref, own_ref, near_ref, other_ref, half_ref, rest_ref, *out_refs):
     quarter, inner = own_ref.shape
     feats = quarter // 4
-    rows = out_ref.shape[1] - feats
-    y, core = place_ref[0], place_ref[1]
+    rows = out_refs[0].shape[0] - feats
+    y, core, zh = place_ref[0], place_ref[1], place_ref[2]
     sources = [y, lax.rem(y + 3 + 2 * core, 4), lax.rem(y + 5 - 2 * core, 4), lax.rem(y + 2, 4)]
     x_grad = jnp.concatenate([got_ref[source, :inner] for source in sources], axis=0)
-    for z in range(4):
-        at = slice(inner + z * rows, inner + (z + 1) * rows)
+    targets = [zh, lax.rem(zh + 1 + 2 * core, 4), lax.rem(zh + 2, 4), lax.rem(zh + 3 + 2 * core, 4)]
+    for z, out_ref in zip(targets, out_refs):
+        at = pl.ds(pl.multiple_of(inner + z * rows, rows), rows)
         bc = got_ref[0, at].astype(f32)
         for other in range(1, 4):
             bc = bc + got_ref[other, at].astype(f32)
-        out_ref[z, feats:] = bc.astype(bf16)
-        mine = slice(z * feats, (z + 1) * feats)
-        part = slice((z % 2) * feats, (z % 2 + 1) * feats)
+        out_ref[feats:] = bc.astype(bf16)
+        mine = pl.ds(pl.multiple_of(z * feats, feats), feats)
+        part = pl.ds(pl.multiple_of(lax.rem(z, 2) * feats, feats), feats)
         far = jnp.where(core == z // 2, half_ref[part], rest_ref[part])
         w = jnp.concatenate([own_ref[mine], near_ref[mine], other_ref[mine], far], axis=1)
-        out_ref[z, :feats] = jnp.dot(w, x_grad, preferred_element_type=f32).astype(bf16)
+        out_ref[:feats] = jnp.dot(w, x_grad, preferred_element_type=f32).astype(bf16)
 
 
 def in_products(place, got, pieces):
@@ -308,24 +309,22 @@
     return pl.pallas_call(
         in_kernel,
         in_specs=[pl.BlockSpec(memory_space=pltpu.SMEM)] + [pl.BlockSpec(memory_space=pltpu.VMEM)] * 6,
-        out_shape=pltpu.HBM((4, feats + rows, tokens), bf16),
+        out_shape=[jax.ShapeDtypeStruct((feats + rows, tokens), bf16)] * 4,
         compiler_params=small(),
         cost_estimate=cost(8 * quarter * inner * tokens, 4 << 20),
     )(place, got, *pieces)
 
 
-def sum_kernel(terms_ref, in_ref, bc_ref):
+def sum_kernel(own_ref, chain_ref, direct_ref, in_ref, bc_ref):
     feats = in_ref.shape[0]
-    total = terms_ref[0].astype(f32)
-    for z in range(1, 4):
-        total = total + terms_ref[z].astype(f32)
+    total = own_ref[...].astype(f32) + chain_ref[...].astype(f32) + direct_ref[...].astype(f32)
     total = total.astype(bf16)
     in_ref[...] = total[:feats]
     bc_ref[...] = total[feats:]
 
 
-def final_sums(terms, feats):
-    _, height, tokens = terms.shape
+def final_sums(own, chain, direct, feats):
+    height, tokens = own.shape
     return pl.pallas_call(
         sum_kernel,
         out_shape=(
@@ -334,7 +333,12 @@
         ),
         compiler_params=small(),
         cost_estimate=cost(4 * height * tokens, 1 << 20),
-    )(terms)
+    )(own, chain, direct)
+
+
+def ring_step(value, axis, way):
+    pairs = [(c, i, (i + (way if c == 0 else -way)) % 4) for c in range(2) for i in range(4)]
+    return lax.ppermute(value, ("core", axis), [(4 * c + i, 4 * c + j) for c, i, j in pairs])
 
 
 def shifted(row, axis):
@@ -392,12 +396,18 @@
     sent_y, dt_grad, row = x_grads(carried, b_in, wide, half, rows, part, entry_state, dt_raw)
     got = lax.all_to_all(sent_y, "y", 0, 0)
     *rounds, got = lax.optimization_barrier((*shifted(row, "zl"), got))
-    terms = in_products(jnp.stack([y, core]), got, held)
-    *rounds, terms = lax.optimization_barrier((*rounds, terms))
+    place = jnp.stack([y, core, lax.axis_index("zh")])
+    mine, near_terms, far_terms, direct_terms = in_products(place, got, held)
+    relayed = ring_step(far_terms, "zh", 1)
+    direct = ring_step(direct_terms, "zh", -1)
     row = paired(row, rounds)
-    row = paired(row, shifted(row, "x"))
+    relayed, direct, *rounds = lax.optimization_barrier((relayed, direct, *shifted(row, "x")))
+    onward = (near_terms.astype(f32) + relayed.astype(f32)).astype(bf16)
+    *rounds, onward = lax.optimization_barrier((*rounds, onward))
+    chain = ring_step(onward, "zh", 1)
+    row = paired(row, rounds)
     row = row + lax.ppermute(row, "core", [(0, 1), (1, 0)])
-    in_grad, bc_grad = final_sums(lax.all_to_all(terms, "zh", 0, 0), w_in.shape[0] // 16)
+    in_grad, bc_grad = final_sums(mine, chain, direct, w_in.shape[0] // 16)
     norm_scale = (blocks * tokens_here * head_dim) ** (-0.5)
     param_grad = row[0, : 3 * group_heads].reshape(3, group_heads) * norm_scale
     return (in_grad, bc_grad, dt_grad, param_grad)

time: 146 us -> 146 us (level)
  the two profiles are of different devices: /device:TPU:1 before, /device:TPU:40 now
where the time goes in v9:
time: 146 us; the launch traced here: 145 us
  starting transfers between devices  73.9 us (51%)
  blocking collectives  32 us (22%)
  waiting for transfers between devices  21.4 us (15%)
  Pallas kernels  11.9 us (8%)
  local copies, waits for them, and re-layouts  4.14 us (3%)
    all_gather x1, blocking collectives, shards(): near = lax.all_gather(out_grad, 'zh', axis=1, tiled=True)  32 us
    ppermute x6, starting transfers between devices, shifted(): lax.ppermute(row, axis, [(i, (i + s) % 4) for i in range(4)])  19 us
    ppermute x3, starting transfers between devices, ring_step(): lax.ppermute(value, ('core', axis), [(4 * c + i, 4 * c + j) for c, i, j i...  15 us
    ppermute x6, waiting for transfers between devices, shifted(): lax.ppermute(row, axis, [(i, (i + s) % 4) for i in range(4)])  8.05 us
    all_to_all x1, starting transfers between devices, shards(): ahead = suffix_scan(lax.all_to_all(sent, SEQ, 0, 0))  6.9 us
    all_to_all x1, starting transfers between devices, shards(): lax.all_to_all(ahead, SEQ, 0, 0)  5.9 us
    ppermute x3, waiting for transfers between devices, ring_step(): lax.ppermute(value, ('core', axis), [(4 * c + i, 4 * c + j) for c, i, j i...  5.34 us
    all_to_all x1, starting transfers between devices, shards(): w_out_y = lax.all_to_all(regrouped(w_out), 'y', 0, 0)  5.05 us
  transfers between devices with their start and end apart: 19, of which 7 were waited for; matrix products, arithmetic and copies ran while one was open for 3% of the time, Pallas kernels for 3%

profile of v9, /device:TPU:40, one launch (start us, length us, event | category | flops | bytes accessed | tf_op | source)
XLA Modules:
  0.0 145.1 jit_solution(11771683732194224156)
XLA Ops:
  0.6 2.6 %shard_map.138 = bf16[4,256,1024]{2,1,0:T(8,128)(2,1)} custom-call(bf16[256,4096]{1,0:T(8,128)(2,1)} %w_ref.1), custom_call_target="tpu_custom_call" | custom-call | bytes 4194304 | tf_op jit(solution)/shard_map/pallas_call | solution.py:74
  3.3 5.1 %all-to-all-start = ((bf16[4,256,1024]{2,1,0:T(8,128)(2,1)}), bf16[4,256,1024]{2,1,0:T(8,128)(2,1)S(1)}, u32[]{:S(2)}, u32[]{:S(2)}) async-start(bf16[4,256,1024]{2,1,0:T(8,128)(2,1)} %shard_map.138), calls=%async_computation | async-start | bytes 4194304 | tf_op jit(solution)/shard_map/all_to_all | solution.py:362
  8.9 32.0 %all_gather.3.near_ref = bf16[256,1024]{1,0:T(8,128)(2,1)S(1)} all-gather(bf16[256,256]{1,0:T(8,128)(2,1)S(1)} %copy-done.6), channel_id=1, replica_groups=mesh['x'=4,'zl'=4,'core'=2,'y'=4,'zh'=4] {'zh'}, dimensions={1}, use_global_device_ids=true | all-gather | bytes 655360 | tf_op jit(solution)/shard_map/all_gather | solution.py:363
  40.9 1.5 %shard_map.139 = bf16[4,256,256]{2,1,0:T(8,128)(2,1)} custom-call(bf16[256,1024]{1,0:T(8,128)(2,1)S(1)} %all_gather.3.near_ref, bf16[4,256,1024]{2,1,0:T(8,128)(2,1)S(1)} %all-to-all-done.w_ref), custom_call_target="tpu_custom_call" | custom-call | flops 536870912 | bytes 4194304 | tf_op jit(solution)/shard_map/pallas_call | solution.py:97
  42.5 4.9 %all-to-all-start.1 = ((bf16[4,256,256]{2,1,0:T(8,128)(2,1)}), bf16[4,256,256]{2,1,0:T(8,128)(2,1)S(1)}, u32[]{:S(2)}, u32[]{:S(2)}) async-start(bf16[4,256,256]{2,1,0:T(8,128)(2,1)} %shard_map.139), calls=%async_computation.1 | async-start | bytes 1048576 | tf_op jit(solution)/shard_map/all_to_all | solution.py:372
  47.5 1.3 constant_dynamic-slice_fusion
  48.8 3.4 %collective-permute-start = (bf16[1024,256]{1,0:T(8,128)(2,1)S(1)}, bf16[1024,256]{1,0:T(8,128)(2,1)S(1)}, u32[]{:S(2)}, u32[]{:S(2)}) collective-permute-start(bf16[1024,256]{1,0:T(8,128)(2,1)S(1)} %get-tuple-element.84), channel_id=1, source_target_pairs={{0,4},{4,8},{8,12},{12,0},{16,28},{20,16},{24,20},{28,24},{1,5},{5... | collective-permute-start | bytes 1572872 | tf_op jit(solution)/shard_map/ppermute | solution.py:387
  53.2 3.7 %all-to-all-done.1.parts_ref = bf16[4,256,256]{2,1,0:T(8,128)(2,1)S(1)} async-done(((bf16[4,256,256]{2,1,0:T(8,128)(2,1)}), bf16[4,256,256]{2,1,0:T(8,128)(2,1)S(1)}, u32[]{:S(2)}, u32[]{:S(2)}) %all-to-all-start.1) | async-done | bytes 524320 | tf_op jit(solution)/shard_map/all_to_all | solution.py:372
  57.9 6.9 %all-to-all-start.2 = ((bf16[32,16,128]{2,1,0:T(8,128)(2,1)}), bf16[32,16,128]{2,1,0:T(8,128)(2,1)S(1)}, u32[]{:S(2)}, u32[]{:S(2)}) async-start(bf16[32,16,128]{2,1,0:T(8,128)(2,1)} %get-tuple-element.49), calls=%async_computation.2 | async-start | bytes 262144 | tf_op jit(solution)/shard_map/all_to_all | solution.py:392
  64.8 3.4 %collective-permute-start.2 = (bf16[512,256]{1,0:T(8,128)(2,1)S(1)}, bf16[512,256]{1,0:T(8,128)(2,1)S(1)}, u32[]{:S(2)}, u32[]{:S(2)}) collective-permute-start(bf16[512,256]{1,0:T(8,128)(2,1)S(1)} %constant_dynamic-slice_fusion.1), channel_id=1, source_target_pairs={{0,8},{4,12},{8,0},{12,4},{1,9},{5,13},{9,1},{13,5},{2,10},{6,14},... | collective-permute-start | bytes 786440 | tf_op jit(solution)/shard_map/ppermute | solution.py:388
  68.2 1.9 %collective-permute-start.1 = (bf16[1024,256]{1,0:T(8,128)(2,1)S(1)}, bf16[1024,256]{1,0:T(8,128)(2,1)S(1)}, u32[]{:S(2)}, u32[]{:S(2)}) collective-permute-start(bf16[1024,256]{1,0:T(8,128)(2,1)S(1)} %collective-permute-done.near_ref), channel_id=1, source_target_pairs={{0,16},{16,0},{1,17},{17,1},{2,18},{18,2},{3,19},{19,3},{4,20},{20... | collective-permute-start | bytes 1572872 | tf_op jit(solution)/shard_map/ppermute | solution.py:390
  70.2 1.9 %all-to-all-done.2.parts_ref = bf16[32,16,128]{2,1,0:T(8,128)(2,1)S(1)} async-done(((bf16[32,16,128]{2,1,0:T(8,128)(2,1)}), bf16[32,16,128]{2,1,0:T(8,128)(2,1)S(1)}, u32[]{:S(2)}, u32[]{:S(2)}) %all-to-all-start.2) | async-done | bytes 131104 | tf_op jit(solution)/shard_map/all_to_all | solution.py:392
  72.8 5.9 %all-to-all-start.3 = ((f32[32,8,128]{2,1,0:T(8,128)}), f32[32,8,128]{2,1,0:T(8,128)S(1)}, u32[]{:S(2)}, u32[]{:S(2)}) async-start(f32[32,8,128]{2,1,0:T(8,128)} %shard_map.141), calls=%async_computation.3 | async-start | bytes 262144 | tf_op jit(solution)/shard_map/all_to_all | solution.py:395
  78.7 2.1 %collective-permute-start.3 = (bf16[512,256]{1,0:T(8,128)(2,1)S(1)}, bf16[512,256]{1,0:T(8,128)(2,1)S(1)}, u32[]{:S(2)}, u32[]{:S(2)}) collective-permute-start(bf16[512,256]{1,0:T(8,128)(2,1)S(1)} %collective-permute-done.2.half_ref), channel_id=1, source_target_pairs={{0,16},{16,0},{1,17},{17,1},{2,18},{18,2},{3,19},{19,3},{4,20},{20... | collective-permute-start | bytes 786440 | tf_op jit(solution)/shard_map/ppermute | solution.py:390
  81.8 2.8 %shard_map.142 = (f32[384,256]{1,0:T(8,128)S(1)}, bf16[384,256]{1,0:T(8,128)(2,1)S(1)}, f32[16,256]{1,0:T(8,128)S(1)}) custom-call(bf16[256,256]{1,0:T(8,128)(2,1)S(1)} %copy-done.5, bf16[256,256]{1,0:T(8,128)(2,1)S(1)} %copy-done.4, bf16[256,128]{1,0:T(8,128)(2,1)S(1)} %copy-done.1, bf16[256,128]{1,0:T(8,128)(2,1)S(1)} %copy-done, ...), custom_call_target="tpu_custom_call" | custom-call | flops 234881024 | bytes 2097152 | tf_op jit(solution)/shard_map/pallas_call | solution.py:205
  84.7 1.3 all-to-all-done.3.carried_ref
  86.0 1.3 shard_map.143
  87.3 4.4 %all-to-all-start.4 = ((bf16[4,320,256]{2,1,0:T(8,128)(2,1)}), bf16[4,320,256]{2,1,0:T(8,128)(2,1)S(1)}, u32[]{:S(2)}, u32[]{:S(2)}) async-start(bf16[4,320,256]{2,1,0:T(8,128)(2,1)} %get-tuple-element.58), calls=%async_computation.4 | async-start | bytes 1310720 | tf_op jit(solution)/shard_map/all_to_all | solution.py:397
  91.7 2.7 %collective-permute-start.4 = (f32[1,128]{1,0:T(1,128)S(1)}, f32[1,128]{1,0:T(1,128)S(1)}, u32[]{:S(2)}, u32[]{:S(2)}) collective-permute-start(f32[1,128]{1,0:T(1,128)S(1)} %get-tuple-element.57), channel_id=1, source_target_pairs={{0,32},{32,64},{64,96},{96,0},{1,33},{33,65},{65,97},{97,1},{2,34}... | collective-permute-start | bytes 1544 | tf_op jit(solution)/shard_map/ppermute | solution.py:345
  94.5 5.3 %collective-permute-start.5 = (f32[1,128]{1,0:T(1,128)S(1)}, f32[1,128]{1,0:T(1,128)S(1)}, u32[]{:S(2)}, u32[]{:S(2)}) collective-permute-start(f32[1,128]{1,0:T(1,128)S(1)} %get-tuple-element.57), channel_id=1, source_target_pairs={{0,64},{32,96},{64,0},{96,32},{1,65},{33,97},{65,1},{97,33},{2,66}... | collective-permute-start | bytes 1544 | tf_op jit(solution)/shard_map/ppermute | solution.py:345
  99.8 1.9 %collective-permute-start.6 = (f32[1,128]{1,0:T(1,128)S(1)}, f32[1,128]{1,0:T(1,128)S(1)}, u32[]{:S(2)}, u32[]{:S(2)}) collective-permute-start(f32[1,128]{1,0:T(1,128)S(1)} %get-tuple-element.57), channel_id=1, source_target_pairs={{0,96},{32,0},{64,32},{96,64},{1,97},{33,1},{65,33},{97,65},{2,98}... | collective-permute-start | bytes 1544 | tf_op jit(solution)/shard_map/ppermute | solution.py:345
  101.8 3.4 %collective-permute-done.6 = f32[1,128]{1,0:T(1,128)S(1)} collective-permute-done((f32[1,128]{1,0:T(1,128)S(1)}, f32[1,128]{1,0:T(1,128)S(1)}, u32[]{:S(2)}, u32[]{:S(2)}) %collective-permute-start.6) | collective-permute-done | bytes 544 | tf_op jit(solution)/shard_map/ppermute | solution.py:345
  105.2 1.3 shard_map.144
  106.5 5.2 %collective-permute-start.7 = (bf16[272,256]{1,0:T(8,128)(2,1)S(1)}, bf16[272,256]{1,0:T(8,128)(2,1)S(1)}, u32[]{:S(2)}, u32[]{:S(2)}) collective-permute-start(bf16[272,256]{1,0:T(8,128)(2,1)S(1)} %get-tuple-element.66), channel_id=1, source_target_pairs={{0,1},{1,2},{2,3},{3,0},{16,19},{17,16},{18,17},{19,18},{4,5},{5,6... | collective-permute-start | bytes 417800 | tf_op jit(solution)/shard_map/ppermute | solution.py:341
  111.7 4.5 %collective-permute-start.8 = (bf16[272,256]{1,0:T(8,128)(2,1)S(1)}, bf16[272,256]{1,0:T(8,128)(2,1)S(1)}, u32[]{:S(2)}, u32[]{:S(2)}) collective-permute-start(bf16[272,256]{1,0:T(8,128)(2,1)S(1)} %get-tuple-element.67), channel_id=1, source_target_pairs={{0,3},{1,0},{2,1},{3,2},{16,17},{17,18},{18,19},{19,16},{4,7},{5,4... | collective-permute-start | bytes 417800 | tf_op jit(solution)/shard_map/ppermute | solution.py:341
  116.2 3.3 %collective-permute-start.10 = (f32[1,128]{1,0:T(1,128)S(1)}, f32[1,128]{1,0:T(1,128)S(1)}, u32[]{:S(2)}, u32[]{:S(2)}) collective-permute-start(f32[1,128]{1,0:T(1,128)S(1)} %add_add_fusion.1), channel_id=1, source_target_pairs={{0,256},{128,384},{256,0},{384,128},{1,257},{129,385},{257,1},{385... | collective-permute-start | bytes 1544 | tf_op jit(solution)/shard_map/ppermute | solution.py:345
  119.5 3.8 %collective-permute-start.11 = (f32[1,128]{1,0:T(1,128)S(1)}, f32[1,128]{1,0:T(1,128)S(1)}, u32[]{:S(2)}, u32[]{:S(2)}) collective-permute-start(f32[1,128]{1,0:T(1,128)S(1)} %add_add_fusion.1), channel_id=1, source_target_pairs={{0,384},{128,0},{256,128},{384,256},{1,385},{129,1},{257,129},{385... | collective-permute-start | bytes 1544 | tf_op jit(solution)/shard_map/ppermute | solution.py:345
  123.4 2.0 %collective-permute-start.9 = (f32[1,128]{1,0:T(1,128)S(1)}, f32[1,128]{1,0:T(1,128)S(1)}, u32[]{:S(2)}, u32[]{:S(2)}) collective-permute-start(f32[1,128]{1,0:T(1,128)S(1)} %add_add_fusion.1), channel_id=1, source_target_pairs={{0,128},{128,256},{256,384},{384,0},{1,129},{129,257},{257,385},{3... | collective-permute-start | bytes 1544 | tf_op jit(solution)/shard_map/ppermute | solution.py:345
  125.4 4.6 %collective-permute-done.9 = f32[1,128]{1,0:T(1,128)S(1)} collective-permute-done((f32[1,128]{1,0:T(1,128)S(1)}, f32[1,128]{1,0:T(1,128)S(1)}, u32[]{:S(2)}, u32[]{:S(2)}) %collective-permute-start.9) | collective-permute-done | bytes 544 | tf_op jit(solution)/shard_map/ppermute | solution.py:345
  130.1 5.2 %collective-permute-start.12 = (bf16[272,256]{1,0:T(8,128)(2,1)S(1)}, bf16[272,256]{1,0:T(8,128)(2,1)S(1)}, u32[]{:S(2)}, u32[]{:S(2)}) collective-permute-start(bf16[272,256]{1,0:T(8,128)(2,1)S(1)} %add_convert_fusion), channel_id=1, source_target_pairs={{0,1},{1,2},{2,3},{3,0},{16,19},{17,16},{18,17},{19,18},{4,5},{5,6... | collective-permute-start | bytes 417800 | tf_op jit(solution)/shard_map/ppermute | solution.py:341
  135.3 1.9 %collective-permute-start.13 = (f32[1,128]{1,0:T(1,128)S(1)}, f32[1,128]{1,0:T(1,128)S(1)}, u32[]{:S(2)}, u32[]{:S(2)}) collective-permute-start(f32[1,128]{1,0:T(1,128)S(1)} %add_add_fusion), channel_id=1, source_target_pairs={{0,16},{16,0},{1,17},{17,1},{2,18},{18,2},{3,19},{19,3},{4,20},{20... | collective-permute-start | bytes 1544 | tf_op jit(solution)/shard_map/ppermute | solution.py:409
  139.0 5.3 %collective-permute-done.12.chain_ref = bf16[272,256]{1,0:T(8,128)(2,1)S(1)} collective-permute-done((bf16[272,256]{1,0:T(8,128)(2,1)S(1)}, bf16[272,256]{1,0:T(8,128)(2,1)S(1)}, u32[]{:S(2)}, u32[]{:S(2)}) %collective-permute-start.12) | collective-permute-done | bytes 139296 | tf_op jit(solution)/shard_map/ppermute | solution.py:341
  (55 shorter events, 7.0 us)
Async XLA Ops:
  3.3 5.1 %copy-start.9 = (f32[4]{0:T(128)S(1)}, f32[4]{0:T(128)}, u32[]{:S(2)}) copy-start(f32[4]{0:T(128)} %param.17) | copy-start | bytes 52
  3.3 5.1 %copy-start.7 = (f32[4]{0:T(128)S(1)}, f32[4]{0:T(128)}, u32[]{:S(2)}) copy-start(f32[4]{0:T(128)} %param.16) | copy-start | bytes 52
  3.3 5.2 %copy-start.3 = (f32[4,256]{1,0:T(4,128)S(1)}, f32[4,256]{1,0:T(4,128)}, u32[]{:S(2)}) copy-start(f32[4,256]{1,0:T(4,128)} %raw_ref.1) | copy-start | bytes 12292
  3.3 5.6 %copy-start.6 = (bf16[256,256]{1,0:T(8,128)(2,1)S(1)}, bf16[256,256]{1,0:T(8,128)(2,1)}, u32[]{:S(2)}) copy-start(bf16[256,256]{1,0:T(8,128)(2,1)} %param.11) | copy-start | bytes 393220
  3.3 37.6 %all-to-all-start = ((bf16[4,256,1024]{2,1,0:T(8,128)(2,1)}), bf16[4,256,1024]{2,1,0:T(8,128)(2,1)S(1)}, u32[]{:S(2)}, u32[]{:S(2)}) async-start(bf16[4,256,1024]{2,1,0:T(8,128)(2,1)} %shard_map.138), calls=%async_computation | async-start | bytes 4194304 | tf_op jit(solution)/shard_map/all_to_all | solution.py:362
  42.5 14.5 %copy-start = (bf16[256,128]{1,0:T(8,128)(2,1)S(1)}, bf16[256,128]{1,0:T(8,128)(2,1)}, u32[]{:S(2)}) copy-start(bf16[256,128]{1,0:T(8,128)(2,1)} %c_ref.3) | copy-start | bytes 196612
  42.5 14.4 %all-to-all-start.1 = ((bf16[4,256,256]{2,1,0:T(8,128)(2,1)}), bf16[4,256,256]{2,1,0:T(8,128)(2,1)S(1)}, u32[]{:S(2)}, u32[]{:S(2)}) async-start(bf16[4,256,256]{2,1,0:T(8,128)(2,1)} %shard_map.139), calls=%async_computation.1 | async-start | bytes 1048576 | tf_op jit(solution)/shard_map/all_to_all | solution.py:372
  47.5 33.3 %copy-start.8 = (f32[4]{0:T(128)S(1)}, f32[4]{0:T(128)}, u32[]{:S(2)}) copy-start(f32[4]{0:T(128)} %param.18) | copy-start | bytes 52
  47.5 33.4 %copy-start.1 = (bf16[256,128]{1,0:T(8,128)(2,1)S(1)}, bf16[256,128]{1,0:T(8,128)(2,1)}, u32[]{:S(2)}) copy-start(bf16[256,128]{1,0:T(8,128)(2,1)} %b_ref.3) | copy-start | bytes 196612
  47.5 33.4 %copy-start.2 = (bf16[1,256,128]{2,1,0:T(8,128)(2,1)S(1)}, bf16[1,256,128]{2,1,0:T(8,128)(2,1)}, u32[]{:S(2)}) copy-start(bf16[1,256,128]{2,1,0:T(8,128)(2,1)} %param.19) | copy-start | bytes 196612
  47.5 33.4 %copy-start.4 = (bf16[256,256]{1,0:T(8,128)(2,1)S(1)}, bf16[256,256]{1,0:T(8,128)(2,1)}, u32[]{:S(2)}) copy-start(bf16[256,256]{1,0:T(8,128)(2,1)} %x_ref.1) | copy-start | bytes 393220
  48.8 19.4 %collective-permute-start = (bf16[1024,256]{1,0:T(8,128)(2,1)S(1)}, bf16[1024,256]{1,0:T(8,128)(2,1)S(1)}, u32[]{:S(2)}, u32[]{:S(2)}) collective-permute-start(bf16[1024,256]{1,0:T(8,128)(2,1)S(1)} %get-tuple-element.84), channel_id=1, source_target_pairs={{0,4},{4,8},{8,12},{12,0},{16,28},{20,16},{24,20},{28,24},{1,5},{5... | collective-permute-start | bytes 1572872 | tf_op jit(solution)/shard_map/ppermute | solution.py:387
  57.9 14.2 %all-to-all-start.2 = ((bf16[32,16,128]{2,1,0:T(8,128)(2,1)}), bf16[32,16,128]{2,1,0:T(8,128)(2,1)S(1)}, u32[]{:S(2)}, u32[]{:S(2)}) async-start(bf16[32,16,128]{2,1,0:T(8,128)(2,1)} %get-tuple-element.49), calls=%async_computation.2 | async-start | bytes 262144 | tf_op jit(solution)/shard_map/all_to_all | solution.py:392
  64.8 13.9 %collective-permute-start.2 = (bf16[512,256]{1,0:T(8,128)(2,1)S(1)}, bf16[512,256]{1,0:T(8,128)(2,1)S(1)}, u32[]{:S(2)}, u32[]{:S(2)}) collective-permute-start(bf16[512,256]{1,0:T(8,128)(2,1)S(1)} %constant_dynamic-slice_fusion.1), channel_id=1, source_target_pairs={{0,8},{4,12},{8,0},{12,4},{1,9},{5,13},{9,1},{13,5},{2,10},{6,14},... | collective-permute-start | bytes 786440 | tf_op jit(solution)/shard_map/ppermute | solution.py:388
  68.2 16.5 %collective-permute-start.1 = (bf16[1024,256]{1,0:T(8,128)(2,1)S(1)}, bf16[1024,256]{1,0:T(8,128)(2,1)S(1)}, u32[]{:S(2)}, u32[]{:S(2)}) collective-permute-start(bf16[1024,256]{1,0:T(8,128)(2,1)S(1)} %collective-permute-done.near_ref), channel_id=1, source_target_pairs={{0,16},{16,0},{1,17},{17,1},{2,18},{18,2},{3,19},{19,3},{4,20},{20... | collective-permute-start | bytes 1572872 | tf_op jit(solution)/shard_map/ppermute | solution.py:390
  72.8 13.2 %all-to-all-start.3 = ((f32[32,8,128]{2,1,0:T(8,128)}), f32[32,8,128]{2,1,0:T(8,128)S(1)}, u32[]{:S(2)}, u32[]{:S(2)}) async-start(f32[32,8,128]{2,1,0:T(8,128)} %shard_map.141), calls=%async_computation.3 | async-start | bytes 262144 | tf_op jit(solution)/shard_map/all_to_all | solution.py:395
  78.7 6.0 %collective-permute-start.3 = (bf16[512,256]{1,0:T(8,128)(2,1)S(1)}, bf16[512,256]{1,0:T(8,128)(2,1)S(1)}, u32[]{:S(2)}, u32[]{:S(2)}) collective-permute-start(bf16[512,256]{1,0:T(8,128)(2,1)S(1)} %collective-permute-done.2.half_ref), channel_id=1, source_target_pairs={{0,16},{16,0},{1,17},{17,1},{2,18},{18,2},{3,19},{19,3},{4,20},{20... | collective-permute-start | bytes 786440 | tf_op jit(solution)/shard_map/ppermute | solution.py:390
  80.9 0.9 copy-start.5
  87.3 17.9 %all-to-all-start.4 = ((bf16[4,320,256]{2,1,0:T(8,128)(2,1)}), bf16[4,320,256]{2,1,0:T(8,128)(2,1)S(1)}, u32[]{:S(2)}, u32[]{:S(2)}) async-start(bf16[4,320,256]{2,1,0:T(8,128)(2,1)} %get-tuple-element.58), calls=%async_computation.4 | async-start | bytes 1310720 | tf_op jit(solution)/shard_map/all_to_all | solution.py:397
  91.7 10.0 %collective-permute-start.4 = (f32[1,128]{1,0:T(1,128)S(1)}, f32[1,128]{1,0:T(1,128)S(1)}, u32[]{:S(2)}, u32[]{:S(2)}) collective-permute-start(f32[1,128]{1,0:T(1,128)S(1)} %get-tuple-element.57), channel_id=1, source_target_pairs={{0,32},{32,64},{64,96},{96,0},{1,33},{33,65},{65,97},{97,1},{2,34}... | collective-permute-start | bytes 1544 | tf_op jit(solution)/shard_map/ppermute | solution.py:345
  94.5 7.3 %collective-permute-start.5 = (f32[1,128]{1,0:T(1,128)S(1)}, f32[1,128]{1,0:T(1,128)S(1)}, u32[]{:S(2)}, u32[]{:S(2)}) collective-permute-start(f32[1,128]{1,0:T(1,128)S(1)} %get-tuple-element.57), channel_id=1, source_target_pairs={{0,64},{32,96},{64,0},{96,32},{1,65},{33,97},{65,1},{97,33},{2,66}... | collective-permute-start | bytes 1544 | tf_op jit(solution)/shard_map/ppermute | solution.py:345
  99.8 5.4 %collective-permute-start.6 = (f32[1,128]{1,0:T(1,128)S(1)}, f32[1,128]{1,0:T(1,128)S(1)}, u32[]{:S(2)}, u32[]{:S(2)}) collective-permute-start(f32[1,128]{1,0:T(1,128)S(1)} %get-tuple-element.57), channel_id=1, source_target_pairs={{0,96},{32,0},{64,32},{96,64},{1,97},{33,1},{65,33},{97,65},{2,98}... | collective-permute-start | bytes 1544 | tf_op jit(solution)/shard_map/ppermute | solution.py:345
  106.5 23.6 %collective-permute-start.7 = (bf16[272,256]{1,0:T(8,128)(2,1)S(1)}, bf16[272,256]{1,0:T(8,128)(2,1)S(1)}, u32[]{:S(2)}, u32[]{:S(2)}) collective-permute-start(bf16[272,256]{1,0:T(8,128)(2,1)S(1)} %get-tuple-element.66), channel_id=1, source_target_pairs={{0,1},{1,2},{2,3},{3,0},{16,19},{17,16},{18,17},{19,18},{4,5},{5,6... | collective-permute-start | bytes 417800 | tf_op jit(solution)/shard_map/ppermute | solution.py:341
  111.7 18.3 %collective-permute-start.8 = (bf16[272,256]{1,0:T(8,128)(2,1)S(1)}, bf16[272,256]{1,0:T(8,128)(2,1)S(1)}, u32[]{:S(2)}, u32[]{:S(2)}) collective-permute-start(bf16[272,256]{1,0:T(8,128)(2,1)S(1)} %get-tuple-element.67), channel_id=1, source_target_pairs={{0,3},{1,0},{2,1},{3,2},{16,17},{17,18},{18,19},{19,16},{4,7},{5,4... | collective-permute-start | bytes 417800 | tf_op jit(solution)/shard_map/ppermute | solution.py:341
  116.2 9.1 %collective-permute-start.10 = (f32[1,128]{1,0:T(1,128)S(1)}, f32[1,128]{1,0:T(1,128)S(1)}, u32[]{:S(2)}, u32[]{:S(2)}) collective-permute-start(f32[1,128]{1,0:T(1,128)S(1)} %add_add_fusion.1), channel_id=1, source_target_pairs={{0,256},{128,384},{256,0},{384,128},{1,257},{129,385},{257,1},{385... | collective-permute-start | bytes 1544 | tf_op jit(solution)/shard_map/ppermute | solution.py:345
  119.5 5.9 %collective-permute-start.11 = (f32[1,128]{1,0:T(1,128)S(1)}, f32[1,128]{1,0:T(1,128)S(1)}, u32[]{:S(2)}, u32[]{:S(2)}) collective-permute-start(f32[1,128]{1,0:T(1,128)S(1)} %add_add_fusion.1), channel_id=1, source_target_pairs={{0,384},{128,0},{256,128},{384,256},{1,385},{129,1},{257,129},{385... | collective-permute-start | bytes 1544 | tf_op jit(solution)/shard_map/ppermute | solution.py:345
  123.4 6.6 %collective-permute-start.9 = (f32[1,128]{1,0:T(1,128)S(1)}, f32[1,128]{1,0:T(1,128)S(1)}, u32[]{:S(2)}, u32[]{:S(2)}) collective-permute-start(f32[1,128]{1,0:T(1,128)S(1)} %add_add_fusion.1), channel_id=1, source_target_pairs={{0,128},{128,256},{256,384},{384,0},{1,129},{129,257},{257,385},{3... | collective-permute-start | bytes 1544 | tf_op jit(solution)/shard_map/ppermute | solution.py:345
  130.1 14.3 %collective-permute-start.12 = (bf16[272,256]{1,0:T(8,128)(2,1)S(1)}, bf16[272,256]{1,0:T(8,128)(2,1)S(1)}, u32[]{:S(2)}, u32[]{:S(2)}) collective-permute-start(bf16[272,256]{1,0:T(8,128)(2,1)S(1)} %add_convert_fusion), channel_id=1, source_target_pairs={{0,1},{1,2},{2,3},{3,0},{16,19},{17,16},{18,17},{19,18},{4,5},{5,6... | collective-permute-start | bytes 417800 | tf_op jit(solution)/shard_map/ppermute | solution.py:341
  135.3 3.0 %collective-permute-start.13 = (f32[1,128]{1,0:T(1,128)S(1)}, f32[1,128]{1,0:T(1,128)S(1)}, u32[]{:S(2)}, u32[]{:S(2)}) collective-permute-start(f32[1,128]{1,0:T(1,128)S(1)} %add_add_fusion), channel_id=1, source_target_pairs={{0,16},{16,0},{1,17},{17,1},{2,18},{18,2},{3,19},{19,3},{4,20},{20... | collective-permute-start | bytes 1544 | tf_op jit(solution)/shard_map/ppermute | solution.py:409

commit v10 on v9

--- a/solution.py
+++ b/solution.py
@@ -400,13 +400,13 @@
     mine, near_terms, far_terms, direct_terms = in_products(place, got, held)
     relayed = ring_step(far_terms, "zh", 1)
     direct = ring_step(direct_terms, "zh", -1)
-    row = paired(row, rounds)
-    relayed, direct, *rounds = lax.optimization_barrier((relayed, direct, *shifted(row, "x")))
+    relayed, direct = lax.optimization_barrier((relayed, direct))
     onward = (near_terms.astype(f32) + relayed.astype(f32)).astype(bf16)
     *rounds, onward = lax.optimization_barrier((*rounds, onward))
     chain = ring_step(onward, "zh", 1)
     row = paired(row, rounds)
-    row = row + lax.ppermute(row, "core", [(0, 1), (1, 0)])
+    peers = lax.axis_size(("x", "core"))
+    row = lax.all_to_all(jnp.broadcast_to(row[None], (peers,) + row.shape), ("x", "core"), 0, 0).sum(axis=0)
     in_grad, bc_grad = final_sums(mine, chain, direct, w_in.shape[0] // 16)
     norm_scale = (blocks * tokens_here * head_dim) ** (-0.5)
     param_grad = row[0, : 3 * group_heads].reshape(3, group_heads) * norm_scale

time: 146 us -> 143 us (0.979)
  the two profiles are of different devices: /device:TPU:40 before, /device:TPU:1 now
where the time goes in v10:
time: 143 us; the launch traced here: 142 us
  starting transfers between devices  65.5 us (46%)
  blocking collectives  44.1 us (31%)
  waiting for transfers between devices  14.7 us (10%)
  Pallas kernels  11.9 us (8%)
  local copies, waits for them, and re-layouts  4.15 us (3%)
    all_gather x1, blocking collectives, shards(): near = lax.all_gather(out_grad, 'zh', axis=1, tiled=True)  30.9 us
    ppermute x3, starting transfers between devices, ring_step(): lax.ppermute(value, ('core', axis), [(4 * c + i, 4 * c + j) for c, i, j i...  14.4 us
    all_to_all x1, blocking collectives, shards(): lax.all_to_all(jnp.broadcast_to(row[None], (peers,) + row.shape), ('x', '...  13.2 us
    all_to_all x1, starting transfers between devices, shards(): ahead = suffix_scan(lax.all_to_all(sent, SEQ, 0, 0))  11.3 us
    ppermute x3, starting transfers between devices, shifted(): lax.ppermute(row, axis, [(i, (i + s) % 4) for i in range(4)])  8.99 us
    ppermute x3, waiting for transfers between devices, ring_step(): lax.ppermute(value, ('core', axis), [(4 * c + i, 4 * c + j) for c, i, j i...  7.32 us
    all_to_all x1, starting transfers between devices, shards(): got = lax.all_to_all(sent_y, 'y', 0, 0)  5.87 us
    all_to_all x1, starting transfers between devices, shards(): w_out_y = lax.all_to_all(regrouped(w_out), 'y', 0, 0)  5.16 us
  transfers between devices with their start and end apart: 15, of which 5 were waited for; matrix products, arithmetic and copies ran while one was open for 3% of the time, Pallas kernels for 3%

profile of v10, /device:TPU:1, one launch (start us, length us, event | category | flops | bytes accessed | tf_op | source)
XLA Modules:
  0.0 142.1 jit_solution(12456451935896575285)
XLA Ops:
  0.6 2.6 %shard_map.138 = bf16[4,256,1024]{2,1,0:T(8,128)(2,1)} custom-call(bf16[256,4096]{1,0:T(8,128)(2,1)} %w_ref.1), custom_call_target="tpu_custom_call" | custom-call | bytes 4194304 | tf_op jit(solution)/shard_map/pallas_call | solution.py:74
  3.3 5.2 %all-to-all-start = ((bf16[4,256,1024]{2,1,0:T(8,128)(2,1)}), bf16[4,256,1024]{2,1,0:T(8,128)(2,1)S(1)}, u32[]{:S(2)}, u32[]{:S(2)}) async-start(bf16[4,256,1024]{2,1,0:T(8,128)(2,1)} %shard_map.138), calls=%async_computation | async-start | bytes 4194304 | tf_op jit(solution)/shard_map/all_to_all | solution.py:362
  9.1 30.9 %all_gather.3.near_ref = bf16[256,1024]{1,0:T(8,128)(2,1)S(1)} all-gather(bf16[256,256]{1,0:T(8,128)(2,1)S(1)} %copy-done.6), channel_id=1, replica_groups=mesh['x'=4,'zl'=4,'core'=2,'y'=4,'zh'=4] {'zh'}, dimensions={1}, use_global_device_ids=true | all-gather | bytes 655360 | tf_op jit(solution)/shard_map/all_gather | solution.py:363
  39.9 1.6 %shard_map.139 = bf16[4,256,256]{2,1,0:T(8,128)(2,1)} custom-call(bf16[256,1024]{1,0:T(8,128)(2,1)S(1)} %all_gather.3.near_ref, bf16[4,256,1024]{2,1,0:T(8,128)(2,1)S(1)} %all-to-all-done.w_ref), custom_call_target="tpu_custom_call" | custom-call | flops 536870912 | bytes 4194304 | tf_op jit(solution)/shard_map/pallas_call | solution.py:97
  41.5 3.6 %all-to-all-start.1 = ((bf16[4,256,256]{2,1,0:T(8,128)(2,1)}), bf16[4,256,256]{2,1,0:T(8,128)(2,1)S(1)}, u32[]{:S(2)}, u32[]{:S(2)}) async-start(bf16[4,256,256]{2,1,0:T(8,128)(2,1)} %shard_map.139), calls=%async_computation.1 | async-start | bytes 1048576 | tf_op jit(solution)/shard_map/all_to_all | solution.py:372
  45.2 1.3 constant_dynamic-slice_fusion
  46.5 4.5 %collective-permute-start = (bf16[1024,256]{1,0:T(8,128)(2,1)S(1)}, bf16[1024,256]{1,0:T(8,128)(2,1)S(1)}, u32[]{:S(2)}, u32[]{:S(2)}) collective-permute-start(bf16[1024,256]{1,0:T(8,128)(2,1)S(1)} %get-tuple-element.78), channel_id=1, source_target_pairs={{0,4},{4,8},{8,12},{12,0},{16,28},{20,16},{24,20},{28,24},{1,5},{5... | collective-permute-start | bytes 1572872 | tf_op jit(solution)/shard_map/ppermute | solution.py:387
  51.1 1.0 constant_dynamic-slice_fusion.1
  52.1 0.9 shard_map.140
  53.0 11.3 %all-to-all-start.2 = ((bf16[32,16,128]{2,1,0:T(8,128)(2,1)}), bf16[32,16,128]{2,1,0:T(8,128)(2,1)S(1)}, u32[]{:S(2)}, u32[]{:S(2)}) async-start(bf16[32,16,128]{2,1,0:T(8,128)(2,1)} %get-tuple-element.46), calls=%async_computation.2 | async-start | bytes 262144 | tf_op jit(solution)/shard_map/all_to_all | solution.py:392
  64.3 2.9 %collective-permute-start.2 = (bf16[512,256]{1,0:T(8,128)(2,1)S(1)}, bf16[512,256]{1,0:T(8,128)(2,1)S(1)}, u32[]{:S(2)}, u32[]{:S(2)}) collective-permute-start(bf16[512,256]{1,0:T(8,128)(2,1)S(1)} %constant_dynamic-slice_fusion.1), channel_id=1, source_target_pairs={{0,8},{4,12},{8,0},{12,4},{1,9},{5,13},{9,1},{13,5},{2,10},{6,14},... | collective-permute-start | bytes 786440 | tf_op jit(solution)/shard_map/ppermute | solution.py:388
  67.2 2.4 %collective-permute-start.1 = (bf16[1024,256]{1,0:T(8,128)(2,1)S(1)}, bf16[1024,256]{1,0:T(8,128)(2,1)S(1)}, u32[]{:S(2)}, u32[]{:S(2)}) collective-permute-start(bf16[1024,256]{1,0:T(8,128)(2,1)S(1)} %collective-permute-done.near_ref), channel_id=1, source_target_pairs={{0,16},{16,0},{1,17},{17,1},{2,18},{18,2},{3,19},{19,3},{4,20},{20... | collective-permute-start | bytes 1572872 | tf_op jit(solution)/shard_map/ppermute | solution.py:390
  69.7 3.4 %all-to-all-done.2.parts_ref = bf16[32,16,128]{2,1,0:T(8,128)(2,1)S(1)} async-done(((bf16[32,16,128]{2,1,0:T(8,128)(2,1)}), bf16[32,16,128]{2,1,0:T(8,128)(2,1)S(1)}, u32[]{:S(2)}, u32[]{:S(2)}) %all-to-all-start.2) | async-done | bytes 131104 | tf_op jit(solution)/shard_map/all_to_all | solution.py:392
  73.1 0.7 shard_map.141
  73.8 4.2 %all-to-all-start.3 = ((f32[32,8,128]{2,1,0:T(8,128)}), f32[32,8,128]{2,1,0:T(8,128)S(1)}, u32[]{:S(2)}, u32[]{:S(2)}) async-start(f32[32,8,128]{2,1,0:T(8,128)} %shard_map.141), calls=%async_computation.3 | async-start | bytes 262144 | tf_op jit(solution)/shard_map/all_to_all | solution.py:395
  78.0 2.1 %collective-permute-start.3 = (bf16[512,256]{1,0:T(8,128)(2,1)S(1)}, bf16[512,256]{1,0:T(8,128)(2,1)S(1)}, u32[]{:S(2)}, u32[]{:S(2)}) collective-permute-start(bf16[512,256]{1,0:T(8,128)(2,1)S(1)} %collective-permute-done.2.half_ref), channel_id=1, source_target_pairs={{0,16},{16,0},{1,17},{17,1},{2,18},{18,2},{3,19},{19,3},{4,20},{20... | collective-permute-start | bytes 786440 | tf_op jit(solution)/shard_map/ppermute | solution.py:390
  80.3 0.9 copy-done.5
  81.2 2.8 %shard_map.142 = (f32[384,256]{1,0:T(8,128)S(1)}, bf16[384,256]{1,0:T(8,128)(2,1)S(1)}, f32[16,256]{1,0:T(8,128)S(1)}) custom-call(bf16[256,256]{1,0:T(8,128)(2,1)S(1)} %copy-done.5, bf16[256,256]{1,0:T(8,128)(2,1)S(1)} %copy-done.4, bf16[256,128]{1,0:T(8,128)(2,1)S(1)} %copy-done.1, bf16[256,128]{1,0:T(8,128)(2,1)S(1)} %copy-done, ...), custom_call_target="tpu_custom_call" | custom-call | flops 234881024 | bytes 2097152 | tf_op jit(solution)/shard_map/pallas_call | solution.py:205
  84.1 2.6 %all-to-all-done.3.carried_ref = f32[32,8,128]{2,1,0:T(8,128)S(1)} async-done(((f32[32,8,128]{2,1,0:T(8,128)}), f32[32,8,128]{2,1,0:T(8,128)S(1)}, u32[]{:S(2)}, u32[]{:S(2)}) %all-to-all-start.3) | async-done | bytes 131104 | tf_op jit(solution)/shard_map/all_to_all | solution.py:395
  86.7 1.3 shard_map.143
  88.0 5.9 %all-to-all-start.4 = ((bf16[4,320,256]{2,1,0:T(8,128)(2,1)}), bf16[4,320,256]{2,1,0:T(8,128)(2,1)S(1)}, u32[]{:S(2)}, u32[]{:S(2)}) async-start(bf16[4,320,256]{2,1,0:T(8,128)(2,1)} %get-tuple-element.55), calls=%async_computation.4 | async-start | bytes 1310720 | tf_op jit(solution)/shard_map/all_to_all | solution.py:397
  93.9 2.1 %collective-permute-start.4 = (f32[1,128]{1,0:T(1,128)S(1)}, f32[1,128]{1,0:T(1,128)S(1)}, u32[]{:S(2)}, u32[]{:S(2)}) collective-permute-start(f32[1,128]{1,0:T(1,128)S(1)} %get-tuple-element.54), channel_id=1, source_target_pairs={{0,32},{32,64},{64,96},{96,0},{1,33},{33,65},{65,97},{97,1},{2,34}... | collective-permute-start | bytes 1544 | tf_op jit(solution)/shard_map/ppermute | solution.py:345
  96.0 2.9 %collective-permute-start.5 = (f32[1,128]{1,0:T(1,128)S(1)}, f32[1,128]{1,0:T(1,128)S(1)}, u32[]{:S(2)}, u32[]{:S(2)}) collective-permute-start(f32[1,128]{1,0:T(1,128)S(1)} %get-tuple-element.54), channel_id=1, source_target_pairs={{0,64},{32,96},{64,0},{96,32},{1,65},{33,97},{65,1},{97,33},{2,66}... | collective-permute-start | bytes 1544 | tf_op jit(solution)/shard_map/ppermute | solution.py:345
  99.0 3.9 %collective-permute-start.6 = (f32[1,128]{1,0:T(1,128)S(1)}, f32[1,128]{1,0:T(1,128)S(1)}, u32[]{:S(2)}, u32[]{:S(2)}) collective-permute-start(f32[1,128]{1,0:T(1,128)S(1)} %get-tuple-element.54), channel_id=1, source_target_pairs={{0,96},{32,0},{64,32},{96,64},{1,97},{33,1},{65,33},{97,65},{2,98}... | collective-permute-start | bytes 1544 | tf_op jit(solution)/shard_map/ppermute | solution.py:345
  103.0 1.4 collective-permute-done.6
  104.4 1.3 shard_map.144
  105.7 4.6 %collective-permute-start.7 = (bf16[272,256]{1,0:T(8,128)(2,1)S(1)}, bf16[272,256]{1,0:T(8,128)(2,1)S(1)}, u32[]{:S(2)}, u32[]{:S(2)}) collective-permute-start(bf16[272,256]{1,0:T(8,128)(2,1)S(1)} %get-tuple-element.67), channel_id=1, source_target_pairs={{0,1},{1,2},{2,3},{3,0},{16,19},{17,16},{18,17},{19,18},{4,5},{5,6... | collective-permute-start | bytes 417800 | tf_op jit(solution)/shard_map/ppermute | solution.py:341
  110.2 4.6 %collective-permute-start.8 = (bf16[272,256]{1,0:T(8,128)(2,1)S(1)}, bf16[272,256]{1,0:T(8,128)(2,1)S(1)}, u32[]{:S(2)}, u32[]{:S(2)}) collective-permute-start(bf16[272,256]{1,0:T(8,128)(2,1)S(1)} %get-tuple-element.68), channel_id=1, source_target_pairs={{0,3},{1,0},{2,1},{3,2},{16,17},{17,18},{18,19},{19,16},{4,7},{5,4... | collective-permute-start | bytes 417800 | tf_op jit(solution)/shard_map/ppermute | solution.py:341
  114.9 4.3 %collective-permute-done.7 = bf16[272,256]{1,0:T(8,128)(2,1)S(1)} collective-permute-done((bf16[272,256]{1,0:T(8,128)(2,1)S(1)}, bf16[272,256]{1,0:T(8,128)(2,1)S(1)}, u32[]{:S(2)}, u32[]{:S(2)}) %collective-permute-start.7) | collective-permute-done | bytes 139296 | tf_op jit(solution)/shard_map/ppermute | solution.py:341
  119.2 3.0 %collective-permute-done.8.direct_ref = bf16[272,256]{1,0:T(8,128)(2,1)S(1)} collective-permute-done((bf16[272,256]{1,0:T(8,128)(2,1)S(1)}, bf16[272,256]{1,0:T(8,128)(2,1)S(1)}, u32[]{:S(2)}, u32[]{:S(2)}) %collective-permute-start.8) | collective-permute-done | bytes 139296 | tf_op jit(solution)/shard_map/ppermute | solution.py:341
  122.2 5.2 %collective-permute-start.9 = (bf16[272,256]{1,0:T(8,128)(2,1)S(1)}, bf16[272,256]{1,0:T(8,128)(2,1)S(1)}, u32[]{:S(2)}, u32[]{:S(2)}) collective-permute-start(bf16[272,256]{1,0:T(8,128)(2,1)S(1)} %add_convert_fusion), channel_id=1, source_target_pairs={{0,1},{1,2},{2,3},{3,0},{16,19},{17,16},{18,17},{19,18},{4,5},{5,6... | collective-permute-start | bytes 417800 | tf_op jit(solution)/shard_map/ppermute | solution.py:341
  127.5 13.2 %all_to_all.30 = f32[8,1,128]{2,1,0:T(1,128)S(1)} all-to-all(f32[8,1,128]{2,1,0:T(1,128)S(1)} %broadcast_in_dim.37), channel_id=1, replica_groups=mesh['x'=4,'zl'=4,'core'=2,'y'=4,'zh'=4] {'x','core'}, dimensions={0} | all-to-all | bytes 8192 | tf_op jit(solution)/shard_map/all_to_all | solution.py:409
  (48 shorter events, 2.5 us)
Async XLA Ops:
  3.3 5.2 %copy-start.9 = (f32[4]{0:T(128)S(1)}, f32[4]{0:T(128)}, u32[]{:S(2)}) copy-start(f32[4]{0:T(128)} %param.17) | copy-start | bytes 52
  3.3 5.2 %copy-start.7 = (f32[4]{0:T(128)S(1)}, f32[4]{0:T(128)}, u32[]{:S(2)}) copy-start(f32[4]{0:T(128)} %param.16) | copy-start | bytes 52
  3.3 5.3 %copy-start.3 = (f32[4,256]{1,0:T(4,128)S(1)}, f32[4,256]{1,0:T(4,128)}, u32[]{:S(2)}) copy-start(f32[4,256]{1,0:T(4,128)} %raw_ref.1) | copy-start | bytes 12292
  3.3 5.7 %copy-start.6 = (bf16[256,256]{1,0:T(8,128)(2,1)S(1)}, bf16[256,256]{1,0:T(8,128)(2,1)}, u32[]{:S(2)}) copy-start(bf16[256,256]{1,0:T(8,128)(2,1)} %param.11) | copy-start | bytes 393220
  3.3 36.6 %all-to-all-start = ((bf16[4,256,1024]{2,1,0:T(8,128)(2,1)}), bf16[4,256,1024]{2,1,0:T(8,128)(2,1)S(1)}, u32[]{:S(2)}, u32[]{:S(2)}) async-start(bf16[4,256,1024]{2,1,0:T(8,128)(2,1)} %shard_map.138), calls=%async_computation | async-start | bytes 4194304 | tf_op jit(solution)/shard_map/all_to_all | solution.py:362
  41.5 10.7 %copy-start = (bf16[256,128]{1,0:T(8,128)(2,1)S(1)}, bf16[256,128]{1,0:T(8,128)(2,1)}, u32[]{:S(2)}) copy-start(bf16[256,128]{1,0:T(8,128)(2,1)} %c_ref.3) | copy-start | bytes 196612
  41.5 10.6 %all-to-all-start.1 = ((bf16[4,256,256]{2,1,0:T(8,128)(2,1)}), bf16[4,256,256]{2,1,0:T(8,128)(2,1)S(1)}, u32[]{:S(2)}, u32[]{:S(2)}) async-start(bf16[4,256,256]{2,1,0:T(8,128)(2,1)} %shard_map.139), calls=%async_computation.1 | async-start | bytes 1048576 | tf_op jit(solution)/shard_map/all_to_all | solution.py:372
  45.2 35.0 %copy-start.8 = (f32[4]{0:T(128)S(1)}, f32[4]{0:T(128)}, u32[]{:S(2)}) copy-start(f32[4]{0:T(128)} %param.18) | copy-start | bytes 52
  45.2 35.1 %copy-start.1 = (bf16[256,128]{1,0:T(8,128)(2,1)S(1)}, bf16[256,128]{1,0:T(8,128)(2,1)}, u32[]{:S(2)}) copy-start(bf16[256,128]{1,0:T(8,128)(2,1)} %b_ref.3) | copy-start | bytes 196612
  45.2 35.1 %copy-start.2 = (bf16[1,256,128]{2,1,0:T(8,128)(2,1)S(1)}, bf16[1,256,128]{2,1,0:T(8,128)(2,1)}, u32[]{:S(2)}) copy-start(bf16[1,256,128]{2,1,0:T(8,128)(2,1)} %param.19) | copy-start | bytes 196612
  45.2 35.1 %copy-start.4 = (bf16[256,256]{1,0:T(8,128)(2,1)S(1)}, bf16[256,256]{1,0:T(8,128)(2,1)}, u32[]{:S(2)}) copy-start(bf16[256,256]{1,0:T(8,128)(2,1)} %x_ref.1) | copy-start | bytes 393220
  46.5 20.7 %collective-permute-start = (bf16[1024,256]{1,0:T(8,128)(2,1)S(1)}, bf16[1024,256]{1,0:T(8,128)(2,1)S(1)}, u32[]{:S(2)}, u32[]{:S(2)}) collective-permute-start(bf16[1024,256]{1,0:T(8,128)(2,1)S(1)} %get-tuple-element.78), channel_id=1, source_target_pairs={{0,4},{4,8},{8,12},{12,0},{16,28},{20,16},{24,20},{28,24},{1,5},{5... | collective-permute-start | bytes 1572872 | tf_op jit(solution)/shard_map/ppermute | solution.py:387
  53.0 20.0 %all-to-all-start.2 = ((bf16[32,16,128]{2,1,0:T(8,128)(2,1)}), bf16[32,16,128]{2,1,0:T(8,128)(2,1)S(1)}, u32[]{:S(2)}, u32[]{:S(2)}) async-start(bf16[32,16,128]{2,1,0:T(8,128)(2,1)} %get-tuple-element.46), calls=%async_computation.2 | async-start | bytes 262144 | tf_op jit(solution)/shard_map/all_to_all | solution.py:392
  64.3 13.6 %collective-permute-start.2 = (bf16[512,256]{1,0:T(8,128)(2,1)S(1)}, bf16[512,256]{1,0:T(8,128)(2,1)S(1)}, u32[]{:S(2)}, u32[]{:S(2)}) collective-permute-start(bf16[512,256]{1,0:T(8,128)(2,1)S(1)} %constant_dynamic-slice_fusion.1), channel_id=1, source_target_pairs={{0,8},{4,12},{8,0},{12,4},{1,9},{5,13},{9,1},{13,5},{2,10},{6,14},... | collective-permute-start | bytes 786440 | tf_op jit(solution)/shard_map/ppermute | solution.py:388
  67.2 16.8 %collective-permute-start.1 = (bf16[1024,256]{1,0:T(8,128)(2,1)S(1)}, bf16[1024,256]{1,0:T(8,128)(2,1)S(1)}, u32[]{:S(2)}, u32[]{:S(2)}) collective-permute-start(bf16[1024,256]{1,0:T(8,128)(2,1)S(1)} %collective-permute-done.near_ref), channel_id=1, source_target_pairs={{0,16},{16,0},{1,17},{17,1},{2,18},{18,2},{3,19},{19,3},{4,20},{20... | collective-permute-start | bytes 1572872 | tf_op jit(solution)/shard_map/ppermute | solution.py:390
  73.8 12.9 %all-to-all-start.3 = ((f32[32,8,128]{2,1,0:T(8,128)}), f32[32,8,128]{2,1,0:T(8,128)S(1)}, u32[]{:S(2)}, u32[]{:S(2)}) async-start(f32[32,8,128]{2,1,0:T(8,128)} %shard_map.141), calls=%async_computation.3 | async-start | bytes 262144 | tf_op jit(solution)/shard_map/all_to_all | solution.py:395
  78.0 6.1 %collective-permute-start.3 = (bf16[512,256]{1,0:T(8,128)(2,1)S(1)}, bf16[512,256]{1,0:T(8,128)(2,1)S(1)}, u32[]{:S(2)}, u32[]{:S(2)}) collective-permute-start(bf16[512,256]{1,0:T(8,128)(2,1)S(1)} %collective-permute-done.2.half_ref), channel_id=1, source_target_pairs={{0,16},{16,0},{1,17},{17,1},{2,18},{18,2},{3,19},{19,3},{4,20},{20... | collective-permute-start | bytes 786440 | tf_op jit(solution)/shard_map/ppermute | solution.py:390
  80.3 0.9 copy-start.5
  88.0 16.4 %all-to-all-start.4 = ((bf16[4,320,256]{2,1,0:T(8,128)(2,1)}), bf16[4,320,256]{2,1,0:T(8,128)(2,1)S(1)}, u32[]{:S(2)}, u32[]{:S(2)}) async-start(bf16[4,320,256]{2,1,0:T(8,128)(2,1)} %get-tuple-element.55), calls=%async_computation.4 | async-start | bytes 1310720 | tf_op jit(solution)/shard_map/all_to_all | solution.py:397
  93.9 9.1 %collective-permute-start.4 = (f32[1,128]{1,0:T(1,128)S(1)}, f32[1,128]{1,0:T(1,128)S(1)}, u32[]{:S(2)}, u32[]{:S(2)}) collective-permute-start(f32[1,128]{1,0:T(1,128)S(1)} %get-tuple-element.54), channel_id=1, source_target_pairs={{0,32},{32,64},{64,96},{96,0},{1,33},{33,65},{65,97},{97,1},{2,34}... | collective-permute-start | bytes 1544 | tf_op jit(solution)/shard_map/ppermute | solution.py:345
  96.0 7.0 %collective-permute-start.5 = (f32[1,128]{1,0:T(1,128)S(1)}, f32[1,128]{1,0:T(1,128)S(1)}, u32[]{:S(2)}, u32[]{:S(2)}) collective-permute-start(f32[1,128]{1,0:T(1,128)S(1)} %get-tuple-element.54), channel_id=1, source_target_pairs={{0,64},{32,96},{64,0},{96,32},{1,65},{33,97},{65,1},{97,33},{2,66}... | collective-permute-start | bytes 1544 | tf_op jit(solution)/shard_map/ppermute | solution.py:345
  99.0 5.4 %collective-permute-start.6 = (f32[1,128]{1,0:T(1,128)S(1)}, f32[1,128]{1,0:T(1,128)S(1)}, u32[]{:S(2)}, u32[]{:S(2)}) collective-permute-start(f32[1,128]{1,0:T(1,128)S(1)} %get-tuple-element.54), channel_id=1, source_target_pairs={{0,96},{32,0},{64,32},{96,64},{1,97},{33,1},{65,33},{97,65},{2,98}... | collective-permute-start | bytes 1544 | tf_op jit(solution)/shard_map/ppermute | solution.py:345
  105.7 13.5 %collective-permute-start.7 = (bf16[272,256]{1,0:T(8,128)(2,1)S(1)}, bf16[272,256]{1,0:T(8,128)(2,1)S(1)}, u32[]{:S(2)}, u32[]{:S(2)}) collective-permute-start(bf16[272,256]{1,0:T(8,128)(2,1)S(1)} %get-tuple-element.67), channel_id=1, source_target_pairs={{0,1},{1,2},{2,3},{3,0},{16,19},{17,16},{18,17},{19,18},{4,5},{5,6... | collective-permute-start | bytes 417800 | tf_op jit(solution)/shard_map/ppermute | solution.py:341
  110.2 11.9 %collective-permute-start.8 = (bf16[272,256]{1,0:T(8,128)(2,1)S(1)}, bf16[272,256]{1,0:T(8,128)(2,1)S(1)}, u32[]{:S(2)}, u32[]{:S(2)}) collective-permute-start(bf16[272,256]{1,0:T(8,128)(2,1)S(1)} %get-tuple-element.68), channel_id=1, source_target_pairs={{0,3},{1,0},{2,1},{3,2},{16,17},{17,18},{18,19},{19,16},{4,7},{5,4... | collective-permute-start | bytes 417800 | tf_op jit(solution)/shard_map/ppermute | solution.py:341
  122.2 19.2 %collective-permute-start.9 = (bf16[272,256]{1,0:T(8,128)(2,1)S(1)}, bf16[272,256]{1,0:T(8,128)(2,1)S(1)}, u32[]{:S(2)}, u32[]{:S(2)}) collective-permute-start(bf16[272,256]{1,0:T(8,128)(2,1)S(1)} %add_convert_fusion), channel_id=1, source_target_pairs={{0,1},{1,2},{2,3},{3,0},{16,19},{17,16},{18,17},{19,18},{4,5},{5,6... | collective-permute-start | bytes 417800 | tf_op jit(solution)/shard_map/ppermute | solution.py:341

commit v11 on v10

--- a/solution.py
+++ b/solution.py
@@ -85,21 +85,27 @@
     )(w)
 
 
-def partial_kernel(near_ref, w_ref, out_ref):
+def partial_kernel(order_ref, *refs):
+    *block_refs, w_ref, out_ref, near_ref = refs
     groups, inner, depth = w_ref.shape
+    width = block_refs[0].shape[1]
+    for k, block_ref in enumerate(block_refs):
+        near_ref[:, pl.ds(pl.multiple_of(order_ref[k] * width, width), width)] = block_ref[...]
     out = dot_last(w_ref[...].reshape(groups * inner, depth), near_ref[...]).astype(bf16)
     out_ref[...] = out.reshape(out_ref.shape)
 
 
-def partial_products(near, w_mine):
+def partial_products(order, near, w_mine):
     groups, inner, depth = w_mine.shape
-    tokens = near.shape[0]
+    tokens = near[0].shape[0]
     return pl.pallas_call(
         partial_kernel,
+        in_specs=[pl.BlockSpec(memory_space=pltpu.SMEM)] + [pl.BlockSpec(memory_space=pltpu.VMEM)] * 5,
         out_shape=pltpu.HBM((groups, inner, tokens), bf16),
+        scratch_shapes=[pltpu.VMEM((tokens, depth), bf16)],
         compiler_params=small(),
         cost_estimate=cost(2 * groups * tokens * inner * depth, 4 << 20),
-    )(near, w_mine)
+    )(order, *near, w_mine)
 
 
 def over_channels(rows, height):
@@ -359,12 +365,16 @@
     y = lax.axis_index("y")
     entry_state = states[0]
 
-    w_out_y = lax.all_to_all(regrouped(w_out), "y", 0, 0)
-    near = lax.all_gather(out_grad, "zh", axis=1, tiled=True)
-    products = partial_products(near, w_out_y)
+    core, zh = lax.axis_index("core"), lax.axis_index("zh")
+    w_out_parts, own_grad = lax.optimization_barrier((regrouped(w_out), out_grad))
+    w_out_y = lax.all_to_all(w_out_parts, "y", 0, 0)
+    behind = ring_step(own_grad, "zh", 1)
+    ahead_grad = ring_step(own_grad, "zh", -1)
+    across_grad = ring_step(behind, "zh", 1)
+    order = jnp.stack([zh, lax.rem(zh + 3 + 2 * core, 4), lax.rem(zh + 1 + 2 * core, 4), lax.rem(zh + 2, 4)])
+    products = partial_products(order, (own_grad, behind, ahead_grad, across_grad), w_out_y)
     w_in_held, products = lax.optimization_barrier((w_in, products))
     quarter = w_in.shape[0] // 4
-    core = lax.axis_index("core")
     own = lax.dynamic_slice_in_dim(w_in_held, y * quarter, quarter)
     near_piece = lax.dynamic_slice_in_dim(w_in_held, lax.rem(y + 1 + 2 * core, 4) * quarter, quarter)
     far_at = lax.rem(y + 2, 4) * quarter + core * (quarter // 2)
@@ -396,15 +406,15 @@
     sent_y, dt_grad, row = x_grads(carried, b_in, wide, half, rows, part, entry_state, dt_raw)
     got = lax.all_to_all(sent_y, "y", 0, 0)
     *rounds, got = lax.optimization_barrier((*shifted(row, "zl"), got))
-    place = jnp.stack([y, core, lax.axis_index("zh")])
+    place = jnp.stack([y, core, zh])
     mine, near_terms, far_terms, direct_terms = in_products(place, got, held)
     relayed = ring_step(far_terms, "zh", 1)
     direct = ring_step(direct_terms, "zh", -1)
-    relayed, direct = lax.optimization_barrier((relayed, direct))
     onward = (near_terms.astype(f32) + relayed.astype(f32)).astype(bf16)
     *rounds, onward = lax.optimization_barrier((*rounds, onward))
     chain = ring_step(onward, "zh", 1)
     row = paired(row, rounds)
+    row, direct = lax.optimization_barrier((row, direct))
     peers = lax.axis_size(("x", "core"))
     row = lax.all_to_all(jnp.broadcast_to(row[None], (peers,) + row.shape), ("x", "core"), 0, 0).sum(axis=0)
     in_grad, bc_grad = final_sums(mine, chain, direct, w_in.shape[0] // 16)

time: 143 us -> 151 us (1.056)
  blocking collectives: 44.1 us -> 12.5 us
  starting transfers between devices: 65.5 us -> 85.6 us
  waiting for transfers between devices: 14.7 us -> 33.3 us
    all_gather x1 -> x0, blocking collectives: 30.9 us -> none  [shards(): near = lax.all_gather(out_grad, 'zh', axis=1, tiled=True)]
    ppermute x3 -> x6, starting transfers between devices: 14.4 us -> 35 us  [ring_step(): lax.ppermute(value, ('core', axis), [(4 * c + i, 4 * c + j) for c, i, j i...]
    ppermute x3 -> x6, waiting for transfers between devices: 7.32 us -> 23.3 us  [ring_step(): lax.ppermute(value, ('core', axis), [(4 * c + i, 4 * c + j) for c, i, j i...]
    ppermute x3, waiting for transfers between devices: 1.4 us -> 3.97 us  [shifted(): lax.ppermute(row, axis, [(i, (i + s) % 4) for i in range(4)])]
    all_to_all x1, starting transfers between devices: 11.3 us -> 13.2 us  [shards(): ahead = suffix_scan(lax.all_to_all(sent, SEQ, 0, 0))]
    ppermute x3, starting transfers between devices: 8.99 us -> 7.37 us  [shifted(): lax.ppermute(row, axis, [(i, (i + s) % 4) for i in range(4)])]
  transfers between devices with their start and end apart: 15 -> 18, of which waited for: 5 -> 8; matrix products, arithmetic and copies ran while one was open for 3% -> 3% of each run, Pallas kernels for 3% -> 3%
where the time goes in v11:
time: 151 us; the launch traced here: 150 us
  starting transfers between devices  85.6 us (57%)
  waiting for transfers between devices  33.3 us (22%)
  blocking collectives  12.5 us (8%)
  Pallas kernels  12.4 us (8%)
  local copies, waits for them, and re-layouts  4.15 us (3%)
    ppermute x6, starting transfers between devices, ring_step(): lax.ppermute(value, ('core', axis), [(4 * c + i, 4 * c + j) for c, i, j i...  35 us
    ppermute x6, waiting for transfers between devices, ring_step(): lax.ppermute(value, ('core', axis), [(4 * c + i, 4 * c + j) for c, i, j i...  23.3 us
    all_to_all x1, starting transfers between devices, shards(): ahead = suffix_scan(lax.all_to_all(sent, SEQ, 0, 0))  13.2 us
    all_to_all x1, blocking collectives, shards(): lax.all_to_all(jnp.broadcast_to(row[None], (peers,) + row.shape), ('x', '...  12.5 us
    ppermute x3, starting transfers between devices, shifted(): lax.ppermute(row, axis, [(i, (i + s) % 4) for i in range(4)])  7.37 us
    all_to_all x1, starting transfers between devices, shards(): w_out_y = lax.all_to_all(w_out_parts, 'y', 0, 0)  5.16 us
    all_to_all x1, starting transfers between devices, shards(): got = lax.all_to_all(sent_y, 'y', 0, 0)  5.15 us
    ppermute x1, starting transfers between devices, shards(): lax.ppermute(near_piece, ('core', 'y'), [(4 * a[0] + a[1], 4 * b[0] + b[1...  4.55 us
  transfers between devices with their start and end apart: 18, of which 8 were waited for; matrix products, arithmetic and copies ran while one was open for 3% of the time, Pallas kernels for 3%

profile of v11, /device:TPU:1, one launch (start us, length us, event | category | flops | bytes accessed | tf_op | source)
XLA Modules:
  0.0 149.8 jit_solution(1275496099688139551)
XLA Ops:
  0.6 2.6 %shard_map.138 = bf16[4,256,1024]{2,1,0:T(8,128)(2,1)} custom-call(bf16[256,4096]{1,0:T(8,128)(2,1)} %w_ref.1), custom_call_target="tpu_custom_call" | custom-call | bytes 4194304 | tf_op jit(solution)/shard_map/pallas_call | solution.py:74
  3.3 5.2 %all-to-all-start = ((bf16[4,256,1024]{2,1,0:T(8,128)(2,1)}), bf16[4,256,1024]{2,1,0:T(8,128)(2,1)S(1)}, u32[]{:S(2)}, u32[]{:S(2)}) async-start(bf16[4,256,1024]{2,1,0:T(8,128)(2,1)} %shard_map.138), calls=%async_computation | async-start | bytes 4194304 | tf_op jit(solution)/shard_map/all_to_all | solution.py:370
  8.5 8.8 %collective-permute-start.1 = (bf16[256,256]{1,0:T(8,128)(2,1)S(1)}, bf16[256,256]{1,0:T(8,128)(2,1)S(1)}, u32[]{:S(2)}, u32[]{:S(2)}) collective-permute-start(bf16[256,256]{1,0:T(8,128)(2,1)S(1)} %copy-done), channel_id=1, source_target_pairs={{0,3},{1,0},{2,1},{3,2},{16,17},{17,18},{18,19},{19,16},{4,7},{5,4... | collective-permute-start | bytes 393224 | tf_op jit(solution)/shard_map/ppermute | solution.py:347
  17.3 5.6 %collective-permute-start = (bf16[256,256]{1,0:T(8,128)(2,1)S(1)}, bf16[256,256]{1,0:T(8,128)(2,1)S(1)}, u32[]{:S(2)}, u32[]{:S(2)}) collective-permute-start(bf16[256,256]{1,0:T(8,128)(2,1)S(1)} %copy-done), channel_id=1, source_target_pairs={{0,1},{1,2},{2,3},{3,0},{16,19},{17,16},{18,17},{19,18},{4,5},{5,6... | collective-permute-start | bytes 393224 | tf_op jit(solution)/shard_map/ppermute | solution.py:347
  23.4 9.2 %collective-permute-done.refs_1_ = bf16[256,256]{1,0:T(8,128)(2,1)S(1)} collective-permute-done((bf16[256,256]{1,0:T(8,128)(2,1)S(1)}, bf16[256,256]{1,0:T(8,128)(2,1)S(1)}, u32[]{:S(2)}, u32[]{:S(2)}) %collective-permute-start) | collective-permute-done | bytes 131104 | tf_op jit(solution)/shard_map/ppermute | solution.py:347
  32.5 6.4 %collective-permute-start.2 = (bf16[256,256]{1,0:T(8,128)(2,1)S(1)}, bf16[256,256]{1,0:T(8,128)(2,1)S(1)}, u32[]{:S(2)}, u32[]{:S(2)}) collective-permute-start(bf16[256,256]{1,0:T(8,128)(2,1)S(1)} %collective-permute-done.refs_1_), channel_id=1, source_target_pairs={{0,1},{1,2},{2,3},{3,0},{16,19},{17,16},{18,17},{19,18},{4,5},{5,6... | collective-permute-start | bytes 393224 | tf_op jit(solution)/shard_map/ppermute | solution.py:347
  39.1 5.5 %collective-permute-done.2.refs_3_ = bf16[256,256]{1,0:T(8,128)(2,1)S(1)} collective-permute-done((bf16[256,256]{1,0:T(8,128)(2,1)S(1)}, bf16[256,256]{1,0:T(8,128)(2,1)S(1)}, u32[]{:S(2)}, u32[]{:S(2)}) %collective-permute-start.2) | collective-permute-done | bytes 131104 | tf_op jit(solution)/shard_map/ppermute | solution.py:347
  44.7 2.1 %shard_map.139 = bf16[4,256,256]{2,1,0:T(8,128)(2,1)} custom-call(s32[4]{0:T(128)S(1)} %pad_add_fusion.1.order_ref, bf16[256,256]{1,0:T(8,128)(2,1)S(1)} %copy-done, bf16[256,256]{1,0:T(8,128)(2,1)S(1)} %collective-permute-done.refs_1_, bf16[256,256]{1,0:T(8,128)(2,1)S(1)} %collective-permute-done.1.refs_2_, ...), custom_call_target="tpu_custom_call" | custom-call | flops 536870912 | bytes 4194304 | tf_op jit(solution)/shard_map/pallas_call | solution.py:101
  46.8 3.6 %all-to-all-start.1 = ((bf16[4,256,256]{2,1,0:T(8,128)(2,1)}), bf16[4,256,256]{2,1,0:T(8,128)(2,1)S(1)}, u32[]{:S(2)}, u32[]{:S(2)}) async-start(bf16[4,256,256]{2,1,0:T(8,128)(2,1)} %shard_map.139), calls=%async_computation.1 | async-start | bytes 1048576 | tf_op jit(solution)/shard_map/all_to_all | solution.py:382
  50.5 1.3 constant_dynamic-slice_fusion
  51.8 4.5 %collective-permute-start.3 = (bf16[1024,256]{1,0:T(8,128)(2,1)S(1)}, bf16[1024,256]{1,0:T(8,128)(2,1)S(1)}, u32[]{:S(2)}, u32[]{:S(2)}) collective-permute-start(bf16[1024,256]{1,0:T(8,128)(2,1)S(1)} %get-tuple-element.82), channel_id=1, source_target_pairs={{0,4},{4,8},{8,12},{12,0},{16,28},{20,16},{24,20},{28,24},{1,5},{5... | collective-permute-start | bytes 1572872 | tf_op jit(solution)/shard_map/ppermute | solution.py:397
  58.4 13.2 %all-to-all-start.2 = ((bf16[32,16,128]{2,1,0:T(8,128)(2,1)}), bf16[32,16,128]{2,1,0:T(8,128)(2,1)S(1)}, u32[]{:S(2)}, u32[]{:S(2)}) async-start(bf16[32,16,128]{2,1,0:T(8,128)(2,1)} %get-tuple-element.50), calls=%async_computation.2 | async-start | bytes 262144 | tf_op jit(solution)/shard_map/all_to_all | solution.py:402
  71.5 2.9 %collective-permute-start.5 = (bf16[512,256]{1,0:T(8,128)(2,1)S(1)}, bf16[512,256]{1,0:T(8,128)(2,1)S(1)}, u32[]{:S(2)}, u32[]{:S(2)}) collective-permute-start(bf16[512,256]{1,0:T(8,128)(2,1)S(1)} %constant_dynamic-slice_fusion.1), channel_id=1, source_target_pairs={{0,8},{4,12},{8,0},{12,4},{1,9},{5,13},{9,1},{13,5},{2,10},{6,14},... | collective-permute-start | bytes 786440 | tf_op jit(solution)/shard_map/ppermute | solution.py:398
  74.4 2.4 %collective-permute-start.4 = (bf16[1024,256]{1,0:T(8,128)(2,1)S(1)}, bf16[1024,256]{1,0:T(8,128)(2,1)S(1)}, u32[]{:S(2)}, u32[]{:S(2)}) collective-permute-start(bf16[1024,256]{1,0:T(8,128)(2,1)S(1)} %collective-permute-done.3.near_ref), channel_id=1, source_target_pairs={{0,16},{16,0},{1,17},{17,1},{2,18},{18,2},{3,19},{19,3},{4,20},{20... | collective-permute-start | bytes 1572872 | tf_op jit(solution)/shard_map/ppermute | solution.py:400
  76.8 3.4 %all-to-all-done.2.parts_ref = bf16[32,16,128]{2,1,0:T(8,128)(2,1)S(1)} async-done(((bf16[32,16,128]{2,1,0:T(8,128)(2,1)}), bf16[32,16,128]{2,1,0:T(8,128)(2,1)S(1)}, u32[]{:S(2)}, u32[]{:S(2)}) %all-to-all-start.2) | async-done | bytes 131104 | tf_op jit(solution)/shard_map/all_to_all | solution.py:402
  81.0 4.2 %all-to-all-start.3 = ((f32[32,8,128]{2,1,0:T(8,128)}), f32[32,8,128]{2,1,0:T(8,128)S(1)}, u32[]{:S(2)}, u32[]{:S(2)}) async-start(f32[32,8,128]{2,1,0:T(8,128)} %shard_map.141), calls=%async_computation.3 | async-start | bytes 262144 | tf_op jit(solution)/shard_map/all_to_all | solution.py:405
  85.1 2.1 %collective-permute-start.6 = (bf16[512,256]{1,0:T(8,128)(2,1)S(1)}, bf16[512,256]{1,0:T(8,128)(2,1)S(1)}, u32[]{:S(2)}, u32[]{:S(2)}) collective-permute-start(bf16[512,256]{1,0:T(8,128)(2,1)S(1)} %collective-permute-done.5.half_ref), channel_id=1, source_target_pairs={{0,16},{16,0},{1,17},{17,1},{2,18},{18,2},{3,19},{19,3},{4,20},{20... | collective-permute-start | bytes 786440 | tf_op jit(solution)/shard_map/ppermute | solution.py:400
  88.4 2.8 %shard_map.142 = (f32[384,256]{1,0:T(8,128)S(1)}, bf16[384,256]{1,0:T(8,128)(2,1)S(1)}, f32[16,256]{1,0:T(8,128)S(1)}) custom-call(bf16[256,256]{1,0:T(8,128)(2,1)S(1)} %copy-done.6, bf16[256,256]{1,0:T(8,128)(2,1)S(1)} %copy-done.5, bf16[256,128]{1,0:T(8,128)(2,1)S(1)} %copy-done.2, bf16[256,128]{1,0:T(8,128)(2,1)S(1)} %copy-done.1, ...), custom_call_target="tpu_custom_call" | custom-call | flops 234881024 | bytes 2097152 | tf_op jit(solution)/shard_map/pallas_call | solution.py:211
  91.2 2.6 %all-to-all-done.3.carried_ref = f32[32,8,128]{2,1,0:T(8,128)S(1)} async-done(((f32[32,8,128]{2,1,0:T(8,128)}), f32[32,8,128]{2,1,0:T(8,128)S(1)}, u32[]{:S(2)}, u32[]{:S(2)}) %all-to-all-start.3) | async-done | bytes 131104 | tf_op jit(solution)/shard_map/all_to_all | solution.py:405
  93.8 1.3 shard_map.143
  95.2 5.2 %all-to-all-start.4 = ((bf16[4,320,256]{2,1,0:T(8,128)(2,1)}), bf16[4,320,256]{2,1,0:T(8,128)(2,1)S(1)}, u32[]{:S(2)}, u32[]{:S(2)}) async-start(bf16[4,320,256]{2,1,0:T(8,128)(2,1)} %get-tuple-element.59), calls=%async_computation.4 | async-start | bytes 1310720 | tf_op jit(solution)/shard_map/all_to_all | solution.py:407
  100.3 2.9 %collective-permute-start.9 = (f32[1,128]{1,0:T(1,128)S(1)}, f32[1,128]{1,0:T(1,128)S(1)}, u32[]{:S(2)}, u32[]{:S(2)}) collective-permute-start(f32[1,128]{1,0:T(1,128)S(1)} %get-tuple-element.58), channel_id=1, source_target_pairs={{0,96},{32,0},{64,32},{96,64},{1,97},{33,1},{65,33},{97,65},{2,98}... | collective-permute-start | bytes 1544 | tf_op jit(solution)/shard_map/ppermute | solution.py:351
  103.2 2.4 %collective-permute-start.8 = (f32[1,128]{1,0:T(1,128)S(1)}, f32[1,128]{1,0:T(1,128)S(1)}, u32[]{:S(2)}, u32[]{:S(2)}) collective-permute-start(f32[1,128]{1,0:T(1,128)S(1)} %get-tuple-element.58), channel_id=1, source_target_pairs={{0,64},{32,96},{64,0},{96,32},{1,65},{33,97},{65,1},{97,33},{2,66}... | collective-permute-start | bytes 1544 | tf_op jit(solution)/shard_map/ppermute | solution.py:351
  105.6 2.1 %collective-permute-start.7 = (f32[1,128]{1,0:T(1,128)S(1)}, f32[1,128]{1,0:T(1,128)S(1)}, u32[]{:S(2)}, u32[]{:S(2)}) collective-permute-start(f32[1,128]{1,0:T(1,128)S(1)} %get-tuple-element.58), channel_id=1, source_target_pairs={{0,32},{32,64},{64,96},{96,0},{1,33},{33,65},{65,97},{97,1},{2,34}... | collective-permute-start | bytes 1544 | tf_op jit(solution)/shard_map/ppermute | solution.py:351
  108.7 3.1 %collective-permute-done.7 = f32[1,128]{1,0:T(1,128)S(1)} collective-permute-done((f32[1,128]{1,0:T(1,128)S(1)}, f32[1,128]{1,0:T(1,128)S(1)}, u32[]{:S(2)}, u32[]{:S(2)}) %collective-permute-start.7) | collective-permute-done | bytes 544 | tf_op jit(solution)/shard_map/ppermute | solution.py:351
  111.8 1.2 shard_map.144
  113.0 5.0 %collective-permute-start.10 = (bf16[272,256]{1,0:T(8,128)(2,1)S(1)}, bf16[272,256]{1,0:T(8,128)(2,1)S(1)}, u32[]{:S(2)}, u32[]{:S(2)}) collective-permute-start(bf16[272,256]{1,0:T(8,128)(2,1)S(1)} %get-tuple-element.71), channel_id=1, source_target_pairs={{0,1},{1,2},{2,3},{3,0},{16,19},{17,16},{18,17},{19,18},{4,5},{5,6... | collective-permute-start | bytes 417800 | tf_op jit(solution)/shard_map/ppermute | solution.py:347
  118.1 4.1 %collective-permute-start.12 = (bf16[272,256]{1,0:T(8,128)(2,1)S(1)}, bf16[272,256]{1,0:T(8,128)(2,1)S(1)}, u32[]{:S(2)}, u32[]{:S(2)}) collective-permute-start(bf16[272,256]{1,0:T(8,128)(2,1)S(1)} %get-tuple-element.76), channel_id=1, source_target_pairs={{0,3},{1,0},{2,1},{3,2},{16,17},{17,18},{18,19},{19,16},{4,7},{5,4... | collective-permute-start | bytes 417800 | tf_op jit(solution)/shard_map/ppermute | solution.py:347
  122.2 4.4 %collective-permute-done.10 = bf16[272,256]{1,0:T(8,128)(2,1)S(1)} collective-permute-done((bf16[272,256]{1,0:T(8,128)(2,1)S(1)}, bf16[272,256]{1,0:T(8,128)(2,1)S(1)}, u32[]{:S(2)}, u32[]{:S(2)}) %collective-permute-start.10) | collective-permute-done | bytes 139296 | tf_op jit(solution)/shard_map/ppermute | solution.py:347
  126.7 5.0 %collective-permute-start.11 = (bf16[272,256]{1,0:T(8,128)(2,1)S(1)}, bf16[272,256]{1,0:T(8,128)(2,1)S(1)}, u32[]{:S(2)}, u32[]{:S(2)}) collective-permute-start(bf16[272,256]{1,0:T(8,128)(2,1)S(1)} %add_convert_fusion), channel_id=1, source_target_pairs={{0,1},{1,2},{2,3},{3,0},{16,19},{17,16},{18,17},{19,18},{4,5},{5,6... | collective-permute-start | bytes 417800 | tf_op jit(solution)/shard_map/ppermute | solution.py:347
  131.8 4.1 %collective-permute-done.12.direct_ref = bf16[272,256]{1,0:T(8,128)(2,1)S(1)} collective-permute-done((bf16[272,256]{1,0:T(8,128)(2,1)S(1)}, bf16[272,256]{1,0:T(8,128)(2,1)S(1)}, u32[]{:S(2)}, u32[]{:S(2)}) %collective-permute-start.12) | collective-permute-done | bytes 139296 | tf_op jit(solution)/shard_map/ppermute | solution.py:347
  135.9 12.5 %all_to_all.30 = f32[8,1,128]{2,1,0:T(1,128)S(1)} all-to-all(f32[8,1,128]{2,1,0:T(1,128)S(1)} %broadcast_in_dim.37), channel_id=1, replica_groups=mesh['x'=4,'zl'=4,'core'=2,'y'=4,'zh'=4] {'x','core'}, dimensions={0} | all-to-all | bytes 8192 | tf_op jit(solution)/shard_map/all_to_all | solution.py:419
  (54 shorter events, 6.9 us)
Async XLA Ops:
  3.3 5.2 %copy-start = (bf16[256,256]{1,0:T(8,128)(2,1)S(1)}, bf16[256,256]{1,0:T(8,128)(2,1)}, u32[]{:S(2)}) copy-start(bf16[256,256]{1,0:T(8,128)(2,1)} %refs_0_) | copy-start | bytes 393220
  3.3 19.6 %copy-start.9 = (f32[4]{0:T(128)S(1)}, f32[4]{0:T(128)}, u32[]{:S(2)}) copy-start(f32[4]{0:T(128)} %param.17) | copy-start | bytes 52
  3.3 19.6 %copy-start.4 = (f32[4,256]{1,0:T(4,128)S(1)}, f32[4,256]{1,0:T(4,128)}, u32[]{:S(2)}) copy-start(f32[4,256]{1,0:T(4,128)} %raw_ref.1) | copy-start | bytes 12292
  3.3 19.6 %copy-start.7 = (f32[4]{0:T(128)S(1)}, f32[4]{0:T(128)}, u32[]{:S(2)}) copy-start(f32[4]{0:T(128)} %param.16) | copy-start | bytes 52
  3.3 41.4 %all-to-all-start = ((bf16[4,256,1024]{2,1,0:T(8,128)(2,1)}), bf16[4,256,1024]{2,1,0:T(8,128)(2,1)S(1)}, u32[]{:S(2)}, u32[]{:S(2)}) async-start(bf16[4,256,1024]{2,1,0:T(8,128)(2,1)} %shard_map.138), calls=%async_computation | async-start | bytes 4194304 | tf_op jit(solution)/shard_map/all_to_all | solution.py:370
  8.5 30.7 %collective-permute-start.1 = (bf16[256,256]{1,0:T(8,128)(2,1)S(1)}, bf16[256,256]{1,0:T(8,128)(2,1)S(1)}, u32[]{:S(2)}, u32[]{:S(2)}) collective-permute-start(bf16[256,256]{1,0:T(8,128)(2,1)S(1)} %copy-done), channel_id=1, source_target_pairs={{0,3},{1,0},{2,1},{3,2},{16,17},{17,18},{18,19},{19,16},{4,7},{5,4... | collective-permute-start | bytes 393224 | tf_op jit(solution)/shard_map/ppermute | solution.py:347
  17.3 15.2 %collective-permute-start = (bf16[256,256]{1,0:T(8,128)(2,1)S(1)}, bf16[256,256]{1,0:T(8,128)(2,1)S(1)}, u32[]{:S(2)}, u32[]{:S(2)}) collective-permute-start(bf16[256,256]{1,0:T(8,128)(2,1)S(1)} %copy-done), channel_id=1, source_target_pairs={{0,1},{1,2},{2,3},{3,0},{16,19},{17,16},{18,17},{19,18},{4,5},{5,6... | collective-permute-start | bytes 393224 | tf_op jit(solution)/shard_map/ppermute | solution.py:347
  32.5 12.2 %collective-permute-start.2 = (bf16[256,256]{1,0:T(8,128)(2,1)S(1)}, bf16[256,256]{1,0:T(8,128)(2,1)S(1)}, u32[]{:S(2)}, u32[]{:S(2)}) collective-permute-start(bf16[256,256]{1,0:T(8,128)(2,1)S(1)} %collective-permute-done.refs_1_), channel_id=1, source_target_pairs={{0,1},{1,2},{2,3},{3,0},{16,19},{17,16},{18,17},{19,18},{4,5},{5,6... | collective-permute-start | bytes 393224 | tf_op jit(solution)/shard_map/ppermute | solution.py:347
  46.8 10.7 %copy-start.1 = (bf16[256,128]{1,0:T(8,128)(2,1)S(1)}, bf16[256,128]{1,0:T(8,128)(2,1)}, u32[]{:S(2)}) copy-start(bf16[256,128]{1,0:T(8,128)(2,1)} %c_ref.3) | copy-start | bytes 196612
  46.8 10.6 %all-to-all-start.1 = ((bf16[4,256,256]{2,1,0:T(8,128)(2,1)}), bf16[4,256,256]{2,1,0:T(8,128)(2,1)S(1)}, u32[]{:S(2)}, u32[]{:S(2)}) async-start(bf16[4,256,256]{2,1,0:T(8,128)(2,1)} %shard_map.139), calls=%async_computation.1 | async-start | bytes 1048576 | tf_op jit(solution)/shard_map/all_to_all | solution.py:382
  50.5 36.8 %copy-start.8 = (f32[4]{0:T(128)S(1)}, f32[4]{0:T(128)}, u32[]{:S(2)}) copy-start(f32[4]{0:T(128)} %param.18) | copy-start | bytes 52
  50.5 37.0 %copy-start.2 = (bf16[256,128]{1,0:T(8,128)(2,1)S(1)}, bf16[256,128]{1,0:T(8,128)(2,1)}, u32[]{:S(2)}) copy-start(bf16[256,128]{1,0:T(8,128)(2,1)} %b_ref.3) | copy-start | bytes 196612
  50.5 37.0 %copy-start.3 = (bf16[1,256,128]{2,1,0:T(8,128)(2,1)S(1)}, bf16[1,256,128]{2,1,0:T(8,128)(2,1)}, u32[]{:S(2)}) copy-start(bf16[1,256,128]{2,1,0:T(8,128)(2,1)} %param.19) | copy-start | bytes 196612
  50.5 37.0 %copy-start.5 = (bf16[256,256]{1,0:T(8,128)(2,1)S(1)}, bf16[256,256]{1,0:T(8,128)(2,1)}, u32[]{:S(2)}) copy-start(bf16[256,256]{1,0:T(8,128)(2,1)} %x_ref.1) | copy-start | bytes 393220
  51.8 22.5 %collective-permute-start.3 = (bf16[1024,256]{1,0:T(8,128)(2,1)S(1)}, bf16[1024,256]{1,0:T(8,128)(2,1)S(1)}, u32[]{:S(2)}, u32[]{:S(2)}) collective-permute-start(bf16[1024,256]{1,0:T(8,128)(2,1)S(1)} %get-tuple-element.82), channel_id=1, source_target_pairs={{0,4},{4,8},{8,12},{12,0},{16,28},{20,16},{24,20},{28,24},{1,5},{5... | collective-permute-start | bytes 1572872 | tf_op jit(solution)/shard_map/ppermute | solution.py:397
  58.4 21.9 %all-to-all-start.2 = ((bf16[32,16,128]{2,1,0:T(8,128)(2,1)}), bf16[32,16,128]{2,1,0:T(8,128)(2,1)S(1)}, u32[]{:S(2)}, u32[]{:S(2)}) async-start(bf16[32,16,128]{2,1,0:T(8,128)(2,1)} %get-tuple-element.50), calls=%async_computation.2 | async-start | bytes 262144 | tf_op jit(solution)/shard_map/all_to_all | solution.py:402
  71.5 13.6 %collective-permute-start.5 = (bf16[512,256]{1,0:T(8,128)(2,1)S(1)}, bf16[512,256]{1,0:T(8,128)(2,1)S(1)}, u32[]{:S(2)}, u32[]{:S(2)}) collective-permute-start(bf16[512,256]{1,0:T(8,128)(2,1)S(1)} %constant_dynamic-slice_fusion.1), channel_id=1, source_target_pairs={{0,8},{4,12},{8,0},{12,4},{1,9},{5,13},{9,1},{13,5},{2,10},{6,14},... | collective-permute-start | bytes 786440 | tf_op jit(solution)/shard_map/ppermute | solution.py:398
  74.4 16.8 %collective-permute-start.4 = (bf16[1024,256]{1,0:T(8,128)(2,1)S(1)}, bf16[1024,256]{1,0:T(8,128)(2,1)S(1)}, u32[]{:S(2)}, u32[]{:S(2)}) collective-permute-start(bf16[1024,256]{1,0:T(8,128)(2,1)S(1)} %collective-permute-done.3.near_ref), channel_id=1, source_target_pairs={{0,16},{16,0},{1,17},{17,1},{2,18},{18,2},{3,19},{19,3},{4,20},{20... | collective-permute-start | bytes 1572872 | tf_op jit(solution)/shard_map/ppermute | solution.py:400
  81.0 12.9 %all-to-all-start.3 = ((f32[32,8,128]{2,1,0:T(8,128)}), f32[32,8,128]{2,1,0:T(8,128)S(1)}, u32[]{:S(2)}, u32[]{:S(2)}) async-start(f32[32,8,128]{2,1,0:T(8,128)} %shard_map.141), calls=%async_computation.3 | async-start | bytes 262144 | tf_op jit(solution)/shard_map/all_to_all | solution.py:405
  85.1 6.1 %collective-permute-start.6 = (bf16[512,256]{1,0:T(8,128)(2,1)S(1)}, bf16[512,256]{1,0:T(8,128)(2,1)S(1)}, u32[]{:S(2)}, u32[]{:S(2)}) collective-permute-start(bf16[512,256]{1,0:T(8,128)(2,1)S(1)} %collective-permute-done.5.half_ref), channel_id=1, source_target_pairs={{0,16},{16,0},{1,17},{17,1},{2,18},{18,2},{3,19},{19,3},{4,20},{20... | collective-permute-start | bytes 786440 | tf_op jit(solution)/shard_map/ppermute | solution.py:400
  87.5 0.9 copy-start.6
  95.2 16.6 %all-to-all-start.4 = ((bf16[4,320,256]{2,1,0:T(8,128)(2,1)}), bf16[4,320,256]{2,1,0:T(8,128)(2,1)S(1)}, u32[]{:S(2)}, u32[]{:S(2)}) async-start(bf16[4,320,256]{2,1,0:T(8,128)(2,1)} %get-tuple-element.59), calls=%async_computation.4 | async-start | bytes 1310720 | tf_op jit(solution)/shard_map/all_to_all | solution.py:407
  100.3 7.5 %collective-permute-start.9 = (f32[1,128]{1,0:T(1,128)S(1)}, f32[1,128]{1,0:T(1,128)S(1)}, u32[]{:S(2)}, u32[]{:S(2)}) collective-permute-start(f32[1,128]{1,0:T(1,128)S(1)} %get-tuple-element.58), channel_id=1, source_target_pairs={{0,96},{32,0},{64,32},{96,64},{1,97},{33,1},{65,33},{97,65},{2,98}... | collective-permute-start | bytes 1544 | tf_op jit(solution)/shard_map/ppermute | solution.py:351
  103.2 5.5 %collective-permute-start.8 = (f32[1,128]{1,0:T(1,128)S(1)}, f32[1,128]{1,0:T(1,128)S(1)}, u32[]{:S(2)}, u32[]{:S(2)}) collective-permute-start(f32[1,128]{1,0:T(1,128)S(1)} %get-tuple-element.58), channel_id=1, source_target_pairs={{0,64},{32,96},{64,0},{96,32},{1,65},{33,97},{65,1},{97,33},{2,66}... | collective-permute-start | bytes 1544 | tf_op jit(solution)/shard_map/ppermute | solution.py:351
  105.6 6.2 %collective-permute-start.7 = (f32[1,128]{1,0:T(1,128)S(1)}, f32[1,128]{1,0:T(1,128)S(1)}, u32[]{:S(2)}, u32[]{:S(2)}) collective-permute-start(f32[1,128]{1,0:T(1,128)S(1)} %get-tuple-element.58), channel_id=1, source_target_pairs={{0,32},{32,64},{64,96},{96,0},{1,33},{33,65},{65,97},{97,1},{2,34}... | collective-permute-start | bytes 1544 | tf_op jit(solution)/shard_map/ppermute | solution.py:351
  113.0 13.6 %collective-permute-start.10 = (bf16[272,256]{1,0:T(8,128)(2,1)S(1)}, bf16[272,256]{1,0:T(8,128)(2,1)S(1)}, u32[]{:S(2)}, u32[]{:S(2)}) collective-permute-start(bf16[272,256]{1,0:T(8,128)(2,1)S(1)} %get-tuple-element.71), channel_id=1, source_target_pairs={{0,1},{1,2},{2,3},{3,0},{16,19},{17,16},{18,17},{19,18},{4,5},{5,6... | collective-permute-start | bytes 417800 | tf_op jit(solution)/shard_map/ppermute | solution.py:347
  118.1 17.8 %collective-permute-start.12 = (bf16[272,256]{1,0:T(8,128)(2,1)S(1)}, bf16[272,256]{1,0:T(8,128)(2,1)S(1)}, u32[]{:S(2)}, u32[]{:S(2)}) collective-permute-start(bf16[272,256]{1,0:T(8,128)(2,1)S(1)} %get-tuple-element.76), channel_id=1, source_target_pairs={{0,3},{1,0},{2,1},{3,2},{16,17},{17,18},{18,19},{19,16},{4,7},{5,4... | collective-permute-start | bytes 417800 | tf_op jit(solution)/shard_map/ppermute | solution.py:347
  126.7 22.3 %collective-permute-start.11 = (bf16[272,256]{1,0:T(8,128)(2,1)S(1)}, bf16[272,256]{1,0:T(8,128)(2,1)S(1)}, u32[]{:S(2)}, u32[]{:S(2)}) collective-permute-start(bf16[272,256]{1,0:T(8,128)(2,1)S(1)} %add_convert_fusion), channel_id=1, source_target_pairs={{0,1},{1,2},{2,3},{3,0},{16,19},{17,16},{18,17},{19,18},{4,5},{5,6... | collective-permute-start | bytes 417800 | tf_op jit(solution)/shard_map/ppermute | solution.py:347

commit v12 on v10

--- a/solution.py
+++ b/solution.py
@@ -399,11 +399,11 @@
     place = jnp.stack([y, core, lax.axis_index("zh")])
     mine, near_terms, far_terms, direct_terms = in_products(place, got, held)
     relayed = ring_step(far_terms, "zh", 1)
-    direct = ring_step(direct_terms, "zh", -1)
-    relayed, direct = lax.optimization_barrier((relayed, direct))
+    relayed, direct_terms = lax.optimization_barrier((relayed, direct_terms))
     onward = (near_terms.astype(f32) + relayed.astype(f32)).astype(bf16)
     *rounds, onward = lax.optimization_barrier((*rounds, onward))
     chain = ring_step(onward, "zh", 1)
+    direct = ring_step(direct_terms, "zh", -1)
     row = paired(row, rounds)
     peers = lax.axis_size(("x", "core"))
     row = lax.all_to_all(jnp.broadcast_to(row[None], (peers,) + row.shape), ("x", "core"), 0, 0).sum(axis=0)

time: 143 us -> 142 us (level)
  blocking collectives: 44.1 us -> 41.4 us
  waiting for transfers between devices: 14.7 us -> 16.4 us
    all_to_all x1, blocking collectives: 13.2 us -> 10.5 us  [shards(): lax.all_to_all(jnp.broadcast_to(row[None], (peers,) + row.shape), ('x', '...]
    ppermute x3, waiting for transfers between devices: 7.32 us -> 8.94 us  [ring_step(): lax.ppermute(value, ('core', axis), [(4 * c + i, 4 * c + j) for c, i, j i...]
  transfers between devices with their start and end apart: 15 -> 15, of which waited for: 5 -> 4; matrix products, arithmetic and copies ran while one was open for 3% -> 3% of each run, Pallas kernels for 3% -> 3%
where the time goes in v12:
time: 142 us; the launch traced here: 140 us
  starting transfers between devices  64.8 us (46%)
  blocking collectives  41.4 us (29%)
  waiting for transfers between devices  16.4 us (12%)
  Pallas kernels  11.9 us (8%)
  local copies, waits for them, and re-layouts  4.15 us (3%)
    all_gather x1, blocking collectives, shards(): near = lax.all_gather(out_grad, 'zh', axis=1, tiled=True)  30.9 us
    ppermute x3, starting transfers between devices, ring_step(): lax.ppermute(value, ('core', axis), [(4 * c + i, 4 * c + j) for c, i, j i...  13.8 us
    all_to_all x1, starting transfers between devices, shards(): ahead = suffix_scan(lax.all_to_all(sent, SEQ, 0, 0))  11.3 us
    all_to_all x1, blocking collectives, shards(): lax.all_to_all(jnp.broadcast_to(row[None], (peers,) + row.shape), ('x', '...  10.5 us
    ppermute x3, starting transfers between devices, shifted(): lax.ppermute(row, axis, [(i, (i + s) % 4) for i in range(4)])  8.99 us
    ppermute x3, waiting for transfers between devices, ring_step(): lax.ppermute(value, ('core', axis), [(4 * c + i, 4 * c + j) for c, i, j i...  8.94 us
    all_to_all x1, starting transfers between devices, shards(): got = lax.all_to_all(sent_y, 'y', 0, 0)  5.87 us
    all_to_all x1, starting transfers between devices, shards(): w_out_y = lax.all_to_all(regrouped(w_out), 'y', 0, 0)  5.16 us
  transfers between devices with their start and end apart: 15, of which 4 were waited for; matrix products, arithmetic and copies ran while one was open for 3% of the time, Pallas kernels for 3%

profile of v12, /device:TPU:1, one launch (start us, length us, event | category | flops | bytes accessed | tf_op | source)
XLA Modules:
  0.0 140.4 jit_solution(15624009738579507551)
XLA Ops:
  0.6 2.6 %shard_map.138 = bf16[4,256,1024]{2,1,0:T(8,128)(2,1)} custom-call(bf16[256,4096]{1,0:T(8,128)(2,1)} %w_ref.1), custom_call_target="tpu_custom_call" | custom-call | bytes 4194304 | tf_op jit(solution)/shard_map/pallas_call | solution.py:74
  3.3 5.2 %all-to-all-start = ((bf16[4,256,1024]{2,1,0:T(8,128)(2,1)}), bf16[4,256,1024]{2,1,0:T(8,128)(2,1)S(1)}, u32[]{:S(2)}, u32[]{:S(2)}) async-start(bf16[4,256,1024]{2,1,0:T(8,128)(2,1)} %shard_map.138), calls=%async_computation | async-start | bytes 4194304 | tf_op jit(solution)/shard_map/all_to_all | solution.py:362
  9.1 30.9 %all_gather.3.near_ref = bf16[256,1024]{1,0:T(8,128)(2,1)S(1)} all-gather(bf16[256,256]{1,0:T(8,128)(2,1)S(1)} %copy-done.6), channel_id=1, replica_groups=mesh['x'=4,'zl'=4,'core'=2,'y'=4,'zh'=4] {'zh'}, dimensions={1}, use_global_device_ids=true | all-gather | bytes 655360 | tf_op jit(solution)/shard_map/all_gather | solution.py:363
  39.9 1.6 %shard_map.139 = bf16[4,256,256]{2,1,0:T(8,128)(2,1)} custom-call(bf16[256,1024]{1,0:T(8,128)(2,1)S(1)} %all_gather.3.near_ref, bf16[4,256,1024]{2,1,0:T(8,128)(2,1)S(1)} %all-to-all-done.w_ref), custom_call_target="tpu_custom_call" | custom-call | flops 536870912 | bytes 4194304 | tf_op jit(solution)/shard_map/pallas_call | solution.py:97
  41.5 3.6 %all-to-all-start.1 = ((bf16[4,256,256]{2,1,0:T(8,128)(2,1)}), bf16[4,256,256]{2,1,0:T(8,128)(2,1)S(1)}, u32[]{:S(2)}, u32[]{:S(2)}) async-start(bf16[4,256,256]{2,1,0:T(8,128)(2,1)} %shard_map.139), calls=%async_computation.1 | async-start | bytes 1048576 | tf_op jit(solution)/shard_map/all_to_all | solution.py:372
  45.2 1.3 constant_dynamic-slice_fusion
  46.5 4.5 %collective-permute-start = (bf16[1024,256]{1,0:T(8,128)(2,1)S(1)}, bf16[1024,256]{1,0:T(8,128)(2,1)S(1)}, u32[]{:S(2)}, u32[]{:S(2)}) collective-permute-start(bf16[1024,256]{1,0:T(8,128)(2,1)S(1)} %get-tuple-element.78), channel_id=1, source_target_pairs={{0,4},{4,8},{8,12},{12,0},{16,28},{20,16},{24,20},{28,24},{1,5},{5... | collective-permute-start | bytes 1572872 | tf_op jit(solution)/shard_map/ppermute | solution.py:387
  51.1 1.0 constant_dynamic-slice_fusion.1
  52.1 0.9 shard_map.140
  53.0 11.3 %all-to-all-start.2 = ((bf16[32,16,128]{2,1,0:T(8,128)(2,1)}), bf16[32,16,128]{2,1,0:T(8,128)(2,1)S(1)}, u32[]{:S(2)}, u32[]{:S(2)}) async-start(bf16[32,16,128]{2,1,0:T(8,128)(2,1)} %get-tuple-element.46), calls=%async_computation.2 | async-start | bytes 262144 | tf_op jit(solution)/shard_map/all_to_all | solution.py:392
  64.3 2.9 %collective-permute-start.2 = (bf16[512,256]{1,0:T(8,128)(2,1)S(1)}, bf16[512,256]{1,0:T(8,128)(2,1)S(1)}, u32[]{:S(2)}, u32[]{:S(2)}) collective-permute-start(bf16[512,256]{1,0:T(8,128)(2,1)S(1)} %constant_dynamic-slice_fusion.1), channel_id=1, source_target_pairs={{0,8},{4,12},{8,0},{12,4},{1,9},{5,13},{9,1},{13,5},{2,10},{6,14},... | collective-permute-start | bytes 786440 | tf_op jit(solution)/shard_map/ppermute | solution.py:388
  67.2 2.4 %collective-permute-start.1 = (bf16[1024,256]{1,0:T(8,128)(2,1)S(1)}, bf16[1024,256]{1,0:T(8,128)(2,1)S(1)}, u32[]{:S(2)}, u32[]{:S(2)}) collective-permute-start(bf16[1024,256]{1,0:T(8,128)(2,1)S(1)} %collective-permute-done.near_ref), channel_id=1, source_target_pairs={{0,16},{16,0},{1,17},{17,1},{2,18},{18,2},{3,19},{19,3},{4,20},{20... | collective-permute-start | bytes 1572872 | tf_op jit(solution)/shard_map/ppermute | solution.py:390
  69.7 3.4 %all-to-all-done.2.parts_ref = bf16[32,16,128]{2,1,0:T(8,128)(2,1)S(1)} async-done(((bf16[32,16,128]{2,1,0:T(8,128)(2,1)}), bf16[32,16,128]{2,1,0:T(8,128)(2,1)S(1)}, u32[]{:S(2)}, u32[]{:S(2)}) %all-to-all-start.2) | async-done | bytes 131104 | tf_op jit(solution)/shard_map/all_to_all | solution.py:392
  73.1 0.7 shard_map.141
  73.8 4.2 %all-to-all-start.3 = ((f32[32,8,128]{2,1,0:T(8,128)}), f32[32,8,128]{2,1,0:T(8,128)S(1)}, u32[]{:S(2)}, u32[]{:S(2)}) async-start(f32[32,8,128]{2,1,0:T(8,128)} %shard_map.141), calls=%async_computation.3 | async-start | bytes 262144 | tf_op jit(solution)/shard_map/all_to_all | solution.py:395
  78.0 2.1 %collective-permute-start.3 = (bf16[512,256]{1,0:T(8,128)(2,1)S(1)}, bf16[512,256]{1,0:T(8,128)(2,1)S(1)}, u32[]{:S(2)}, u32[]{:S(2)}) collective-permute-start(bf16[512,256]{1,0:T(8,128)(2,1)S(1)} %collective-permute-done.2.half_ref), channel_id=1, source_target_pairs={{0,16},{16,0},{1,17},{17,1},{2,18},{18,2},{3,19},{19,3},{4,20},{20... | collective-permute-start | bytes 786440 | tf_op jit(solution)/shard_map/ppermute | solution.py:390
  80.3 0.9 copy-done.5
  81.2 2.8 %shard_map.142 = (f32[384,256]{1,0:T(8,128)S(1)}, bf16[384,256]{1,0:T(8,128)(2,1)S(1)}, f32[16,256]{1,0:T(8,128)S(1)}) custom-call(bf16[256,256]{1,0:T(8,128)(2,1)S(1)} %copy-done.5, bf16[256,256]{1,0:T(8,128)(2,1)S(1)} %copy-done.4, bf16[256,128]{1,0:T(8,128)(2,1)S(1)} %copy-done.1, bf16[256,128]{1,0:T(8,128)(2,1)S(1)} %copy-done, ...), custom_call_target="tpu_custom_call" | custom-call | flops 234881024 | bytes 2097152 | tf_op jit(solution)/shard_map/pallas_call | solution.py:205
  84.1 2.6 %all-to-all-done.3.carried_ref = f32[32,8,128]{2,1,0:T(8,128)S(1)} async-done(((f32[32,8,128]{2,1,0:T(8,128)}), f32[32,8,128]{2,1,0:T(8,128)S(1)}, u32[]{:S(2)}, u32[]{:S(2)}) %all-to-all-start.3) | async-done | bytes 131104 | tf_op jit(solution)/shard_map/all_to_all | solution.py:395
  86.7 1.3 shard_map.143
  88.0 5.9 %all-to-all-start.4 = ((bf16[4,320,256]{2,1,0:T(8,128)(2,1)}), bf16[4,320,256]{2,1,0:T(8,128)(2,1)S(1)}, u32[]{:S(2)}, u32[]{:S(2)}) async-start(bf16[4,320,256]{2,1,0:T(8,128)(2,1)} %get-tuple-element.55), calls=%async_computation.4 | async-start | bytes 1310720 | tf_op jit(solution)/shard_map/all_to_all | solution.py:397
  93.9 2.1 %collective-permute-start.4 = (f32[1,128]{1,0:T(1,128)S(1)}, f32[1,128]{1,0:T(1,128)S(1)}, u32[]{:S(2)}, u32[]{:S(2)}) collective-permute-start(f32[1,128]{1,0:T(1,128)S(1)} %get-tuple-element.54), channel_id=1, source_target_pairs={{0,32},{32,64},{64,96},{96,0},{1,33},{33,65},{65,97},{97,1},{2,34}... | collective-permute-start | bytes 1544 | tf_op jit(solution)/shard_map/ppermute | solution.py:345
  96.0 2.9 %collective-permute-start.5 = (f32[1,128]{1,0:T(1,128)S(1)}, f32[1,128]{1,0:T(1,128)S(1)}, u32[]{:S(2)}, u32[]{:S(2)}) collective-permute-start(f32[1,128]{1,0:T(1,128)S(1)} %get-tuple-element.54), channel_id=1, source_target_pairs={{0,64},{32,96},{64,0},{96,32},{1,65},{33,97},{65,1},{97,33},{2,66}... | collective-permute-start | bytes 1544 | tf_op jit(solution)/shard_map/ppermute | solution.py:345
  99.0 3.9 %collective-permute-start.6 = (f32[1,128]{1,0:T(1,128)S(1)}, f32[1,128]{1,0:T(1,128)S(1)}, u32[]{:S(2)}, u32[]{:S(2)}) collective-permute-start(f32[1,128]{1,0:T(1,128)S(1)} %get-tuple-element.54), channel_id=1, source_target_pairs={{0,96},{32,0},{64,32},{96,64},{1,97},{33,1},{65,33},{97,65},{2,98}... | collective-permute-start | bytes 1544 | tf_op jit(solution)/shard_map/ppermute | solution.py:345
  103.0 1.4 collective-permute-done.6
  104.4 1.3 shard_map.144
  105.7 4.6 %collective-permute-start.7 = (bf16[272,256]{1,0:T(8,128)(2,1)S(1)}, bf16[272,256]{1,0:T(8,128)(2,1)S(1)}, u32[]{:S(2)}, u32[]{:S(2)}) collective-permute-start(bf16[272,256]{1,0:T(8,128)(2,1)S(1)} %get-tuple-element.67), channel_id=1, source_target_pairs={{0,1},{1,2},{2,3},{3,0},{16,19},{17,16},{18,17},{19,18},{4,5},{5,6... | collective-permute-start | bytes 417800 | tf_op jit(solution)/shard_map/ppermute | solution.py:341
  110.2 8.9 %collective-permute-done.7 = bf16[272,256]{1,0:T(8,128)(2,1)S(1)} collective-permute-done((bf16[272,256]{1,0:T(8,128)(2,1)S(1)}, bf16[272,256]{1,0:T(8,128)(2,1)S(1)}, u32[]{:S(2)}, u32[]{:S(2)}) %collective-permute-start.7) | collective-permute-done | bytes 139296 | tf_op jit(solution)/shard_map/ppermute | solution.py:341
  119.2 4.2 %collective-permute-start.8 = (bf16[272,256]{1,0:T(8,128)(2,1)S(1)}, bf16[272,256]{1,0:T(8,128)(2,1)S(1)}, u32[]{:S(2)}, u32[]{:S(2)}) collective-permute-start(bf16[272,256]{1,0:T(8,128)(2,1)S(1)} %add_convert_fusion), channel_id=1, source_target_pairs={{0,1},{1,2},{2,3},{3,0},{16,19},{17,16},{18,17},{19,18},{4,5},{5,6... | collective-permute-start | bytes 417800 | tf_op jit(solution)/shard_map/ppermute | solution.py:341
  123.4 5.0 %collective-permute-start.9 = (bf16[272,256]{1,0:T(8,128)(2,1)S(1)}, bf16[272,256]{1,0:T(8,128)(2,1)S(1)}, u32[]{:S(2)}, u32[]{:S(2)}) collective-permute-start(bf16[272,256]{1,0:T(8,128)(2,1)S(1)} %get-tuple-element.71), channel_id=1, source_target_pairs={{0,3},{1,0},{2,1},{3,2},{16,17},{17,18},{18,19},{19,16},{4,7},{5,4... | collective-permute-start | bytes 417800 | tf_op jit(solution)/shard_map/ppermute | solution.py:341
  128.4 10.5 %all_to_all.30 = f32[8,1,128]{2,1,0:T(1,128)S(1)} all-to-all(f32[8,1,128]{2,1,0:T(1,128)S(1)} %broadcast_in_dim.37), channel_id=1, replica_groups=mesh['x'=4,'zl'=4,'core'=2,'y'=4,'zh'=4] {'x','core'}, dimensions={0} | all-to-all | bytes 8192 | tf_op jit(solution)/shard_map/all_to_all | solution.py:409
  139.7 0.7 shard_map.145
  (48 shorter events, 1.8 us)
Async XLA Ops:
  3.3 5.2 %copy-start.9 = (f32[4]{0:T(128)S(1)}, f32[4]{0:T(128)}, u32[]{:S(2)}) copy-start(f32[4]{0:T(128)} %param.17) | copy-start | bytes 52
  3.3 5.2 %copy-start.7 = (f32[4]{0:T(128)S(1)}, f32[4]{0:T(128)}, u32[]{:S(2)}) copy-start(f32[4]{0:T(128)} %param.16) | copy-start | bytes 52
  3.3 5.3 %copy-start.3 = (f32[4,256]{1,0:T(4,128)S(1)}, f32[4,256]{1,0:T(4,128)}, u32[]{:S(2)}) copy-start(f32[4,256]{1,0:T(4,128)} %raw_ref.1) | copy-start | bytes 12292
  3.3 5.7 %copy-start.6 = (bf16[256,256]{1,0:T(8,128)(2,1)S(1)}, bf16[256,256]{1,0:T(8,128)(2,1)}, u32[]{:S(2)}) copy-start(bf16[256,256]{1,0:T(8,128)(2,1)} %param.11) | copy-start | bytes 393220
  3.3 36.6 %all-to-all-start = ((bf16[4,256,1024]{2,1,0:T(8,128)(2,1)}), bf16[4,256,1024]{2,1,0:T(8,128)(2,1)S(1)}, u32[]{:S(2)}, u32[]{:S(2)}) async-start(bf16[4,256,1024]{2,1,0:T(8,128)(2,1)} %shard_map.138), calls=%async_computation | async-start | bytes 4194304 | tf_op jit(solution)/shard_map/all_to_all | solution.py:362
  41.5 10.7 %copy-start = (bf16[256,128]{1,0:T(8,128)(2,1)S(1)}, bf16[256,128]{1,0:T(8,128)(2,1)}, u32[]{:S(2)}) copy-start(bf16[256,128]{1,0:T(8,128)(2,1)} %c_ref.3) | copy-start | bytes 196612
  41.5 10.6 %all-to-all-start.1 = ((bf16[4,256,256]{2,1,0:T(8,128)(2,1)}), bf16[4,256,256]{2,1,0:T(8,128)(2,1)S(1)}, u32[]{:S(2)}, u32[]{:S(2)}) async-start(bf16[4,256,256]{2,1,0:T(8,128)(2,1)} %shard_map.139), calls=%async_computation.1 | async-start | bytes 1048576 | tf_op jit(solution)/shard_map/all_to_all | solution.py:372
  45.2 35.0 %copy-start.8 = (f32[4]{0:T(128)S(1)}, f32[4]{0:T(128)}, u32[]{:S(2)}) copy-start(f32[4]{0:T(128)} %param.18) | copy-start | bytes 52
  45.2 35.1 %copy-start.1 = (bf16[256,128]{1,0:T(8,128)(2,1)S(1)}, bf16[256,128]{1,0:T(8,128)(2,1)}, u32[]{:S(2)}) copy-start(bf16[256,128]{1,0:T(8,128)(2,1)} %b_ref.3) | copy-start | bytes 196612
  45.2 35.1 %copy-start.2 = (bf16[1,256,128]{2,1,0:T(8,128)(2,1)S(1)}, bf16[1,256,128]{2,1,0:T(8,128)(2,1)}, u32[]{:S(2)}) copy-start(bf16[1,256,128]{2,1,0:T(8,128)(2,1)} %param.19) | copy-start | bytes 196612
  45.2 35.1 %copy-start.4 = (bf16[256,256]{1,0:T(8,128)(2,1)S(1)}, bf16[256,256]{1,0:T(8,128)(2,1)}, u32[]{:S(2)}) copy-start(bf16[256,256]{1,0:T(8,128)(2,1)} %x_ref.1) | copy-start | bytes 393220
  46.5 20.7 %collective-permute-start = (bf16[1024,256]{1,0:T(8,128)(2,1)S(1)}, bf16[1024,256]{1,0:T(8,128)(2,1)S(1)}, u32[]{:S(2)}, u32[]{:S(2)}) collective-permute-start(bf16[1024,256]{1,0:T(8,128)(2,1)S(1)} %get-tuple-element.78), channel_id=1, source_target_pairs={{0,4},{4,8},{8,12},{12,0},{16,28},{20,16},{24,20},{28,24},{1,5},{5... | collective-permute-start | bytes 1572872 | tf_op jit(solution)/shard_map/ppermute | solution.py:387
  53.0 20.0 %all-to-all-start.2 = ((bf16[32,16,128]{2,1,0:T(8,128)(2,1)}), bf16[32,16,128]{2,1,0:T(8,128)(2,1)S(1)}, u32[]{:S(2)}, u32[]{:S(2)}) async-start(bf16[32,16,128]{2,1,0:T(8,128)(2,1)} %get-tuple-element.46), calls=%async_computation.2 | async-start | bytes 262144 | tf_op jit(solution)/shard_map/all_to_all | solution.py:392
  64.3 13.6 %collective-permute-start.2 = (bf16[512,256]{1,0:T(8,128)(2,1)S(1)}, bf16[512,256]{1,0:T(8,128)(2,1)S(1)}, u32[]{:S(2)}, u32[]{:S(2)}) collective-permute-start(bf16[512,256]{1,0:T(8,128)(2,1)S(1)} %constant_dynamic-slice_fusion.1), channel_id=1, source_target_pairs={{0,8},{4,12},{8,0},{12,4},{1,9},{5,13},{9,1},{13,5},{2,10},{6,14},... | collective-permute-start | bytes 786440 | tf_op jit(solution)/shard_map/ppermute | solution.py:388
  67.2 16.8 %collective-permute-start.1 = (bf16[1024,256]{1,0:T(8,128)(2,1)S(1)}, bf16[1024,256]{1,0:T(8,128)(2,1)S(1)}, u32[]{:S(2)}, u32[]{:S(2)}) collective-permute-start(bf16[1024,256]{1,0:T(8,128)(2,1)S(1)} %collective-permute-done.near_ref), channel_id=1, source_target_pairs={{0,16},{16,0},{1,17},{17,1},{2,18},{18,2},{3,19},{19,3},{4,20},{20... | collective-permute-start | bytes 1572872 | tf_op jit(solution)/shard_map/ppermute | solution.py:390
  73.8 12.9 %all-to-all-start.3 = ((f32[32,8,128]{2,1,0:T(8,128)}), f32[32,8,128]{2,1,0:T(8,128)S(1)}, u32[]{:S(2)}, u32[]{:S(2)}) async-start(f32[32,8,128]{2,1,0:T(8,128)} %shard_map.141), calls=%async_computation.3 | async-start | bytes 262144 | tf_op jit(solution)/shard_map/all_to_all | solution.py:395
  78.0 6.1 %collective-permute-start.3 = (bf16[512,256]{1,0:T(8,128)(2,1)S(1)}, bf16[512,256]{1,0:T(8,128)(2,1)S(1)}, u32[]{:S(2)}, u32[]{:S(2)}) collective-permute-start(bf16[512,256]{1,0:T(8,128)(2,1)S(1)} %collective-permute-done.2.half_ref), channel_id=1, source_target_pairs={{0,16},{16,0},{1,17},{17,1},{2,18},{18,2},{3,19},{19,3},{4,20},{20... | collective-permute-start | bytes 786440 | tf_op jit(solution)/shard_map/ppermute | solution.py:390
  80.3 0.9 copy-start.5
  88.0 16.4 %all-to-all-start.4 = ((bf16[4,320,256]{2,1,0:T(8,128)(2,1)}), bf16[4,320,256]{2,1,0:T(8,128)(2,1)S(1)}, u32[]{:S(2)}, u32[]{:S(2)}) async-start(bf16[4,320,256]{2,1,0:T(8,128)(2,1)} %get-tuple-element.55), calls=%async_computation.4 | async-start | bytes 1310720 | tf_op jit(solution)/shard_map/all_to_all | solution.py:397
  93.9 9.1 %collective-permute-start.4 = (f32[1,128]{1,0:T(1,128)S(1)}, f32[1,128]{1,0:T(1,128)S(1)}, u32[]{:S(2)}, u32[]{:S(2)}) collective-permute-start(f32[1,128]{1,0:T(1,128)S(1)} %get-tuple-element.54), channel_id=1, source_target_pairs={{0,32},{32,64},{64,96},{96,0},{1,33},{33,65},{65,97},{97,1},{2,34}... | collective-permute-start | bytes 1544 | tf_op jit(solution)/shard_map/ppermute | solution.py:345
  96.0 7.0 %collective-permute-start.5 = (f32[1,128]{1,0:T(1,128)S(1)}, f32[1,128]{1,0:T(1,128)S(1)}, u32[]{:S(2)}, u32[]{:S(2)}) collective-permute-start(f32[1,128]{1,0:T(1,128)S(1)} %get-tuple-element.54), channel_id=1, source_target_pairs={{0,64},{32,96},{64,0},{96,32},{1,65},{33,97},{65,1},{97,33},{2,66}... | collective-permute-start | bytes 1544 | tf_op jit(solution)/shard_map/ppermute | solution.py:345
  99.0 5.4 %collective-permute-start.6 = (f32[1,128]{1,0:T(1,128)S(1)}, f32[1,128]{1,0:T(1,128)S(1)}, u32[]{:S(2)}, u32[]{:S(2)}) collective-permute-start(f32[1,128]{1,0:T(1,128)S(1)} %get-tuple-element.54), channel_id=1, source_target_pairs={{0,96},{32,0},{64,32},{96,64},{1,97},{33,1},{65,33},{97,65},{2,98}... | collective-permute-start | bytes 1544 | tf_op jit(solution)/shard_map/ppermute | solution.py:345
  105.7 13.5 %collective-permute-start.7 = (bf16[272,256]{1,0:T(8,128)(2,1)S(1)}, bf16[272,256]{1,0:T(8,128)(2,1)S(1)}, u32[]{:S(2)}, u32[]{:S(2)}) collective-permute-start(bf16[272,256]{1,0:T(8,128)(2,1)S(1)} %get-tuple-element.67), channel_id=1, source_target_pairs={{0,1},{1,2},{2,3},{3,0},{16,19},{17,16},{18,17},{19,18},{4,5},{5,6... | collective-permute-start | bytes 417800 | tf_op jit(solution)/shard_map/ppermute | solution.py:341
  119.2 20.5 %collective-permute-start.8 = (bf16[272,256]{1,0:T(8,128)(2,1)S(1)}, bf16[272,256]{1,0:T(8,128)(2,1)S(1)}, u32[]{:S(2)}, u32[]{:S(2)}) collective-permute-start(bf16[272,256]{1,0:T(8,128)(2,1)S(1)} %add_convert_fusion), channel_id=1, source_target_pairs={{0,1},{1,2},{2,3},{3,0},{16,19},{17,16},{18,17},{19,18},{4,5},{5,6... | collective-permute-start | bytes 417800 | tf_op jit(solution)/shard_map/ppermute | solution.py:341
  123.4 16.2 %collective-permute-start.9 = (bf16[272,256]{1,0:T(8,128)(2,1)S(1)}, bf16[272,256]{1,0:T(8,128)(2,1)S(1)}, u32[]{:S(2)}, u32[]{:S(2)}) collective-permute-start(bf16[272,256]{1,0:T(8,128)(2,1)S(1)} %get-tuple-element.71), channel_id=1, source_target_pairs={{0,3},{1,0},{2,1},{3,2},{16,17},{17,18},{18,19},{19,16},{4,7},{5,4... | collective-permute-start | bytes 417800 | tf_op jit(solution)/shard_map/ppermute | solution.py:341

commit v13 on v12

--- a/solution.py
+++ b/solution.py
@@ -399,14 +399,14 @@
     place = jnp.stack([y, core, lax.axis_index("zh")])
     mine, near_terms, far_terms, direct_terms = in_products(place, got, held)
     relayed = ring_step(far_terms, "zh", 1)
-    relayed, direct_terms = lax.optimization_barrier((relayed, direct_terms))
+    row = paired(row, rounds)
+    peers = lax.axis_size(("x", "core"))
+    spread = lax.all_to_all(jnp.broadcast_to(row[None], (peers,) + row.shape), ("x", "core"), 0, 0)
+    relayed, direct_terms, spread = lax.optimization_barrier((relayed, direct_terms, spread))
     onward = (near_terms.astype(f32) + relayed.astype(f32)).astype(bf16)
-    *rounds, onward = lax.optimization_barrier((*rounds, onward))
     chain = ring_step(onward, "zh", 1)
     direct = ring_step(direct_terms, "zh", -1)
-    row = paired(row, rounds)
-    peers = lax.axis_size(("x", "core"))
-    row = lax.all_to_all(jnp.broadcast_to(row[None], (peers,) + row.shape), ("x", "core"), 0, 0).sum(axis=0)
+    row = spread.sum(axis=0)
     in_grad, bc_grad = final_sums(mine, chain, direct, w_in.shape[0] // 16)
     norm_scale = (blocks * tokens_here * head_dim) ** (-0.5)
     param_grad = row[0, : 3 * group_heads].reshape(3, group_heads) * norm_scale

time: 142 us -> 143 us (level)
  the two profiles are of different devices: /device:TPU:1 before, /device:TPU:41 now
where the time goes in v13:
time: 143 us; the launch traced here: 142 us
  starting transfers between devices  67.4 us (47%)
  blocking collectives  38.5 us (27%)
  waiting for transfers between devices  18.3 us (13%)
  Pallas kernels  11.9 us (8%)
  local copies, waits for them, and re-layouts  4.15 us (3%)
    all_gather x1, blocking collectives, shards(): near = lax.all_gather(out_grad, 'zh', axis=1, tiled=True)  27.8 us
    all_to_all x1, starting transfers between devices, shards(): ahead = suffix_scan(lax.all_to_all(sent, SEQ, 0, 0))  16.2 us
    ppermute x3, starting transfers between devices, ring_step(): lax.ppermute(value, ('core', axis), [(4 * c + i, 4 * c + j) for c, i, j i...  13.8 us
    ppermute x3, waiting for transfers between devices, ring_step(): lax.ppermute(value, ('core', axis), [(4 * c + i, 4 * c + j) for c, i, j i...  11.4 us
    all_to_all x1, blocking collectives, shards(): lax.all_to_all(jnp.broadcast_to(row[None], (peers,) + row.shape), ('x', '...  10.6 us
    ppermute x3, starting transfers between devices, shifted(): lax.ppermute(row, axis, [(i, (i + s) % 4) for i in range(4)])  9.04 us
    all_to_all x1, starting transfers between devices, shards(): lax.all_to_all(ahead, SEQ, 0, 0)  5.65 us
    all_to_all x1, starting transfers between devices, shards(): w_out_y = lax.all_to_all(regrouped(w_out), 'y', 0, 0)  4.49 us
  transfers between devices with their start and end apart: 15, of which 6 were waited for; matrix products, arithmetic and copies ran while one was open for 3% of the time, Pallas kernels for 3%

profile of v13, /device:TPU:41, one launch (start us, length us, event | category | flops | bytes accessed | tf_op | source)
XLA Modules:
  0.0 141.8 jit_solution(11602610328762748195)
XLA Ops:
  0.6 2.6 %shard_map.138 = bf16[4,256,1024]{2,1,0:T(8,128)(2,1)} custom-call(bf16[256,4096]{1,0:T(8,128)(2,1)} %w_ref.1), custom_call_target="tpu_custom_call" | custom-call | bytes 4194304 | tf_op jit(solution)/shard_map/pallas_call | solution.py:74
  3.3 4.5 %all-to-all-start = ((bf16[4,256,1024]{2,1,0:T(8,128)(2,1)}), bf16[4,256,1024]{2,1,0:T(8,128)(2,1)S(1)}, u32[]{:S(2)}, u32[]{:S(2)}) async-start(bf16[4,256,1024]{2,1,0:T(8,128)(2,1)} %shard_map.138), calls=%async_computation | async-start | bytes 4194304 | tf_op jit(solution)/shard_map/all_to_all | solution.py:362
  8.4 27.8 %all_gather.3.near_ref = bf16[256,1024]{1,0:T(8,128)(2,1)S(1)} all-gather(bf16[256,256]{1,0:T(8,128)(2,1)S(1)} %copy-done.6), channel_id=1, replica_groups=mesh['x'=4,'zl'=4,'core'=2,'y'=4,'zh'=4] {'zh'}, dimensions={1}, use_global_device_ids=true | all-gather | bytes 655360 | tf_op jit(solution)/shard_map/all_gather | solution.py:363
  36.2 1.6 %shard_map.139 = bf16[4,256,256]{2,1,0:T(8,128)(2,1)} custom-call(bf16[256,1024]{1,0:T(8,128)(2,1)S(1)} %all_gather.3.near_ref, bf16[4,256,1024]{2,1,0:T(8,128)(2,1)S(1)} %all-to-all-done.w_ref), custom_call_target="tpu_custom_call" | custom-call | flops 536870912 | bytes 4194304 | tf_op jit(solution)/shard_map/pallas_call | solution.py:97
  37.8 4.4 %all-to-all-start.1 = ((bf16[4,256,256]{2,1,0:T(8,128)(2,1)}), bf16[4,256,256]{2,1,0:T(8,128)(2,1)S(1)}, u32[]{:S(2)}, u32[]{:S(2)}) async-start(bf16[4,256,256]{2,1,0:T(8,128)(2,1)} %shard_map.139), calls=%async_computation.1 | async-start | bytes 1048576 | tf_op jit(solution)/shard_map/all_to_all | solution.py:372
  42.2 1.3 constant_dynamic-slice_fusion
  43.5 1.9 %collective-permute-start = (bf16[1024,256]{1,0:T(8,128)(2,1)S(1)}, bf16[1024,256]{1,0:T(8,128)(2,1)S(1)}, u32[]{:S(2)}, u32[]{:S(2)}) collective-permute-start(bf16[1024,256]{1,0:T(8,128)(2,1)S(1)} %get-tuple-element.72), channel_id=1, source_target_pairs={{0,4},{4,8},{8,12},{12,0},{16,28},{20,16},{24,20},{28,24},{1,5},{5... | collective-permute-start | bytes 1572872 | tf_op jit(solution)/shard_map/ppermute | solution.py:387
  45.5 1.0 constant_dynamic-slice_fusion.1
  46.5 1.4 %all-to-all-done.1.parts_ref = bf16[4,256,256]{2,1,0:T(8,128)(2,1)S(1)} async-done(((bf16[4,256,256]{2,1,0:T(8,128)(2,1)}), bf16[4,256,256]{2,1,0:T(8,128)(2,1)S(1)}, u32[]{:S(2)}, u32[]{:S(2)}) %all-to-all-start.1) | async-done | bytes 524320 | tf_op jit(solution)/shard_map/all_to_all | solution.py:372
  48.0 0.9 shard_map.140
  48.9 16.2 %all-to-all-start.2 = ((bf16[32,16,128]{2,1,0:T(8,128)(2,1)}), bf16[32,16,128]{2,1,0:T(8,128)(2,1)S(1)}, u32[]{:S(2)}, u32[]{:S(2)}) async-start(bf16[32,16,128]{2,1,0:T(8,128)(2,1)} %get-tuple-element.43), calls=%async_computation.2 | async-start | bytes 262144 | tf_op jit(solution)/shard_map/all_to_all | solution.py:392
  65.1 3.2 %collective-permute-start.2 = (bf16[512,256]{1,0:T(8,128)(2,1)S(1)}, bf16[512,256]{1,0:T(8,128)(2,1)S(1)}, u32[]{:S(2)}, u32[]{:S(2)}) collective-permute-start(bf16[512,256]{1,0:T(8,128)(2,1)S(1)} %constant_dynamic-slice_fusion.1), channel_id=1, source_target_pairs={{0,8},{4,12},{8,0},{12,4},{1,9},{5,13},{9,1},{13,5},{2,10},{6,14},... | collective-permute-start | bytes 786440 | tf_op jit(solution)/shard_map/ppermute | solution.py:388
  68.3 2.5 %collective-permute-start.1 = (bf16[1024,256]{1,0:T(8,128)(2,1)S(1)}, bf16[1024,256]{1,0:T(8,128)(2,1)S(1)}, u32[]{:S(2)}, u32[]{:S(2)}) collective-permute-start(bf16[1024,256]{1,0:T(8,128)(2,1)S(1)} %collective-permute-done.near_ref), channel_id=1, source_target_pairs={{0,16},{16,0},{1,17},{17,1},{2,18},{18,2},{3,19},{19,3},{4,20},{20... | collective-permute-start | bytes 1572872 | tf_op jit(solution)/shard_map/ppermute | solution.py:390
  70.9 1.8 %all-to-all-done.2.parts_ref = bf16[32,16,128]{2,1,0:T(8,128)(2,1)S(1)} async-done(((bf16[32,16,128]{2,1,0:T(8,128)(2,1)}), bf16[32,16,128]{2,1,0:T(8,128)(2,1)S(1)}, u32[]{:S(2)}, u32[]{:S(2)}) %all-to-all-start.2) | async-done | bytes 131104 | tf_op jit(solution)/shard_map/all_to_all | solution.py:392
  72.7 0.7 shard_map.141
  73.4 5.6 %all-to-all-start.3 = ((f32[32,8,128]{2,1,0:T(8,128)}), f32[32,8,128]{2,1,0:T(8,128)S(1)}, u32[]{:S(2)}, u32[]{:S(2)}) async-start(f32[32,8,128]{2,1,0:T(8,128)} %shard_map.141), calls=%async_computation.3 | async-start | bytes 262144 | tf_op jit(solution)/shard_map/all_to_all | solution.py:395
  79.1 2.3 %collective-permute-start.3 = (bf16[512,256]{1,0:T(8,128)(2,1)S(1)}, bf16[512,256]{1,0:T(8,128)(2,1)S(1)}, u32[]{:S(2)}, u32[]{:S(2)}) collective-permute-start(bf16[512,256]{1,0:T(8,128)(2,1)S(1)} %collective-permute-done.2.half_ref), channel_id=1, source_target_pairs={{0,16},{16,0},{1,17},{17,1},{2,18},{18,2},{3,19},{19,3},{4,20},{20... | collective-permute-start | bytes 786440 | tf_op jit(solution)/shard_map/ppermute | solution.py:390
  81.5 0.9 copy-done.5
  82.4 2.8 %shard_map.142 = (f32[384,256]{1,0:T(8,128)S(1)}, bf16[384,256]{1,0:T(8,128)(2,1)S(1)}, f32[16,256]{1,0:T(8,128)S(1)}) custom-call(bf16[256,256]{1,0:T(8,128)(2,1)S(1)} %copy-done.5, bf16[256,256]{1,0:T(8,128)(2,1)S(1)} %copy-done.4, bf16[256,128]{1,0:T(8,128)(2,1)S(1)} %copy-done.1, bf16[256,128]{1,0:T(8,128)(2,1)S(1)} %copy-done, ...), custom_call_target="tpu_custom_call" | custom-call | flops 234881024 | bytes 2097152 | tf_op jit(solution)/shard_map/pallas_call | solution.py:205
  85.3 1.3 all-to-all-done.3.carried_ref
  86.6 1.3 shard_map.143
  87.9 3.9 %all-to-all-start.4 = ((bf16[4,320,256]{2,1,0:T(8,128)(2,1)}), bf16[4,320,256]{2,1,0:T(8,128)(2,1)S(1)}, u32[]{:S(2)}, u32[]{:S(2)}) async-start(bf16[4,320,256]{2,1,0:T(8,128)(2,1)} %get-tuple-element.52), calls=%async_computation.4 | async-start | bytes 1310720 | tf_op jit(solution)/shard_map/all_to_all | solution.py:397
  91.8 2.1 %collective-permute-start.4 = (f32[1,128]{1,0:T(1,128)S(1)}, f32[1,128]{1,0:T(1,128)S(1)}, u32[]{:S(2)}, u32[]{:S(2)}) collective-permute-start(f32[1,128]{1,0:T(1,128)S(1)} %get-tuple-element.51), channel_id=1, source_target_pairs={{0,32},{32,64},{64,96},{96,0},{1,33},{33,65},{65,97},{97,1},{2,34}... | collective-permute-start | bytes 1544 | tf_op jit(solution)/shard_map/ppermute | solution.py:345
  94.0 5.0 %collective-permute-start.5 = (f32[1,128]{1,0:T(1,128)S(1)}, f32[1,128]{1,0:T(1,128)S(1)}, u32[]{:S(2)}, u32[]{:S(2)}) collective-permute-start(f32[1,128]{1,0:T(1,128)S(1)} %get-tuple-element.51), channel_id=1, source_target_pairs={{0,64},{32,96},{64,0},{96,32},{1,65},{33,97},{65,1},{97,33},{2,66}... | collective-permute-start | bytes 1544 | tf_op jit(solution)/shard_map/ppermute | solution.py:345
  99.0 1.9 %collective-permute-start.6 = (f32[1,128]{1,0:T(1,128)S(1)}, f32[1,128]{1,0:T(1,128)S(1)}, u32[]{:S(2)}, u32[]{:S(2)}) collective-permute-start(f32[1,128]{1,0:T(1,128)S(1)} %get-tuple-element.51), channel_id=1, source_target_pairs={{0,96},{32,0},{64,32},{96,64},{1,97},{33,1},{65,33},{97,65},{2,98}... | collective-permute-start | bytes 1544 | tf_op jit(solution)/shard_map/ppermute | solution.py:345
  101.0 2.3 %collective-permute-done.6 = f32[1,128]{1,0:T(1,128)S(1)} collective-permute-done((f32[1,128]{1,0:T(1,128)S(1)}, f32[1,128]{1,0:T(1,128)S(1)}, u32[]{:S(2)}, u32[]{:S(2)}) %collective-permute-start.6) | collective-permute-done | bytes 544 | tf_op jit(solution)/shard_map/ppermute | solution.py:345
  103.2 1.3 shard_map.144
  104.5 4.6 %collective-permute-start.7 = (bf16[272,256]{1,0:T(8,128)(2,1)S(1)}, bf16[272,256]{1,0:T(8,128)(2,1)S(1)}, u32[]{:S(2)}, u32[]{:S(2)}) collective-permute-start(bf16[272,256]{1,0:T(8,128)(2,1)S(1)} %get-tuple-element.61), channel_id=1, source_target_pairs={{0,1},{1,2},{2,3},{3,0},{16,19},{17,16},{18,17},{19,18},{4,5},{5,6... | collective-permute-start | bytes 417800 | tf_op jit(solution)/shard_map/ppermute | solution.py:341
  109.1 10.6 %all_to_all.30 = f32[8,1,128]{2,1,0:T(1,128)S(1)} all-to-all(f32[8,1,128]{2,1,0:T(1,128)S(1)} %broadcast_in_dim.37), channel_id=1, replica_groups=mesh['x'=4,'zl'=4,'core'=2,'y'=4,'zh'=4] {'x','core'}, dimensions={0} | all-to-all | bytes 8192 | tf_op jit(solution)/shard_map/all_to_all | solution.py:404
  119.8 4.2 %collective-permute-start.8 = (bf16[272,256]{1,0:T(8,128)(2,1)S(1)}, bf16[272,256]{1,0:T(8,128)(2,1)S(1)}, u32[]{:S(2)}, u32[]{:S(2)}) collective-permute-start(bf16[272,256]{1,0:T(8,128)(2,1)S(1)} %add_convert_fusion), channel_id=1, source_target_pairs={{0,1},{1,2},{2,3},{3,0},{16,19},{17,16},{18,17},{19,18},{4,5},{5,6... | collective-permute-start | bytes 417800 | tf_op jit(solution)/shard_map/ppermute | solution.py:341
  124.0 5.0 %collective-permute-start.9 = (bf16[272,256]{1,0:T(8,128)(2,1)S(1)}, bf16[272,256]{1,0:T(8,128)(2,1)S(1)}, u32[]{:S(2)}, u32[]{:S(2)}) collective-permute-start(bf16[272,256]{1,0:T(8,128)(2,1)S(1)} %get-tuple-element.67), channel_id=1, source_target_pairs={{0,3},{1,0},{2,1},{3,2},{16,17},{17,18},{18,19},{19,16},{4,7},{5,4... | collective-permute-start | bytes 417800 | tf_op jit(solution)/shard_map/ppermute | solution.py:341
  130.2 10.9 %collective-permute-done.9.direct_ref = bf16[272,256]{1,0:T(8,128)(2,1)S(1)} collective-permute-done((bf16[272,256]{1,0:T(8,128)(2,1)S(1)}, bf16[272,256]{1,0:T(8,128)(2,1)S(1)}, u32[]{:S(2)}, u32[]{:S(2)}) %collective-permute-start.9) | collective-permute-done | bytes 139296 | tf_op jit(solution)/shard_map/ppermute | solution.py:341
  (48 shorter events, 3.0 us)
Async XLA Ops:
  3.3 4.5 %copy-start.9 = (f32[4]{0:T(128)S(1)}, f32[4]{0:T(128)}, u32[]{:S(2)}) copy-start(f32[4]{0:T(128)} %param.17) | copy-start | bytes 52
  3.3 4.5 %copy-start.7 = (f32[4]{0:T(128)S(1)}, f32[4]{0:T(128)}, u32[]{:S(2)}) copy-start(f32[4]{0:T(128)} %param.16) | copy-start | bytes 52
  3.3 4.6 %copy-start.3 = (f32[4,256]{1,0:T(4,128)S(1)}, f32[4,256]{1,0:T(4,128)}, u32[]{:S(2)}) copy-start(f32[4,256]{1,0:T(4,128)} %raw_ref.1) | copy-start | bytes 12292
  3.3 5.1 %copy-start.6 = (bf16[256,256]{1,0:T(8,128)(2,1)S(1)}, bf16[256,256]{1,0:T(8,128)(2,1)}, u32[]{:S(2)}) copy-start(bf16[256,256]{1,0:T(8,128)(2,1)} %param.11) | copy-start | bytes 393220
  3.3 32.9 %all-to-all-start = ((bf16[4,256,1024]{2,1,0:T(8,128)(2,1)}), bf16[4,256,1024]{2,1,0:T(8,128)(2,1)S(1)}, u32[]{:S(2)}, u32[]{:S(2)}) async-start(bf16[4,256,1024]{2,1,0:T(8,128)(2,1)} %shard_map.138), calls=%async_computation | async-start | bytes 4194304 | tf_op jit(solution)/shard_map/all_to_all | solution.py:362
  37.8 10.2 %copy-start = (bf16[256,128]{1,0:T(8,128)(2,1)S(1)}, bf16[256,128]{1,0:T(8,128)(2,1)}, u32[]{:S(2)}) copy-start(bf16[256,128]{1,0:T(8,128)(2,1)} %c_ref.3) | copy-start | bytes 196612
  37.8 10.1 %all-to-all-start.1 = ((bf16[4,256,256]{2,1,0:T(8,128)(2,1)}), bf16[4,256,256]{2,1,0:T(8,128)(2,1)S(1)}, u32[]{:S(2)}, u32[]{:S(2)}) async-start(bf16[4,256,256]{2,1,0:T(8,128)(2,1)} %shard_map.139), calls=%async_computation.1 | async-start | bytes 1048576 | tf_op jit(solution)/shard_map/all_to_all | solution.py:372
  42.2 39.1 %copy-start.8 = (f32[4]{0:T(128)S(1)}, f32[4]{0:T(128)}, u32[]{:S(2)}) copy-start(f32[4]{0:T(128)} %param.18) | copy-start | bytes 52
  42.2 39.3 %copy-start.1 = (bf16[256,128]{1,0:T(8,128)(2,1)S(1)}, bf16[256,128]{1,0:T(8,128)(2,1)}, u32[]{:S(2)}) copy-start(bf16[256,128]{1,0:T(8,128)(2,1)} %b_ref.3) | copy-start | bytes 196612
  42.2 39.3 %copy-start.2 = (bf16[1,256,128]{2,1,0:T(8,128)(2,1)S(1)}, bf16[1,256,128]{2,1,0:T(8,128)(2,1)}, u32[]{:S(2)}) copy-start(bf16[1,256,128]{2,1,0:T(8,128)(2,1)} %param.19) | copy-start | bytes 196612
  42.2 39.3 %copy-start.4 = (bf16[256,256]{1,0:T(8,128)(2,1)S(1)}, bf16[256,256]{1,0:T(8,128)(2,1)}, u32[]{:S(2)}) copy-start(bf16[256,256]{1,0:T(8,128)(2,1)} %x_ref.1) | copy-start | bytes 393220
  43.5 24.7 %collective-permute-start = (bf16[1024,256]{1,0:T(8,128)(2,1)S(1)}, bf16[1024,256]{1,0:T(8,128)(2,1)S(1)}, u32[]{:S(2)}, u32[]{:S(2)}) collective-permute-start(bf16[1024,256]{1,0:T(8,128)(2,1)S(1)} %get-tuple-element.72), channel_id=1, source_target_pairs={{0,4},{4,8},{8,12},{12,0},{16,28},{20,16},{24,20},{28,24},{1,5},{5... | collective-permute-start | bytes 1572872 | tf_op jit(solution)/shard_map/ppermute | solution.py:387
  48.9 23.8 %all-to-all-start.2 = ((bf16[32,16,128]{2,1,0:T(8,128)(2,1)}), bf16[32,16,128]{2,1,0:T(8,128)(2,1)S(1)}, u32[]{:S(2)}, u32[]{:S(2)}) async-start(bf16[32,16,128]{2,1,0:T(8,128)(2,1)} %get-tuple-element.43), calls=%async_computation.2 | async-start | bytes 262144 | tf_op jit(solution)/shard_map/all_to_all | solution.py:392
  65.1 13.9 %collective-permute-start.2 = (bf16[512,256]{1,0:T(8,128)(2,1)S(1)}, bf16[512,256]{1,0:T(8,128)(2,1)S(1)}, u32[]{:S(2)}, u32[]{:S(2)}) collective-permute-start(bf16[512,256]{1,0:T(8,128)(2,1)S(1)} %constant_dynamic-slice_fusion.1), channel_id=1, source_target_pairs={{0,8},{4,12},{8,0},{12,4},{1,9},{5,13},{9,1},{13,5},{2,10},{6,14},... | collective-permute-start | bytes 786440 | tf_op jit(solution)/shard_map/ppermute | solution.py:388
  68.3 17.0 %collective-permute-start.1 = (bf16[1024,256]{1,0:T(8,128)(2,1)S(1)}, bf16[1024,256]{1,0:T(8,128)(2,1)S(1)}, u32[]{:S(2)}, u32[]{:S(2)}) collective-permute-start(bf16[1024,256]{1,0:T(8,128)(2,1)S(1)} %collective-permute-done.near_ref), channel_id=1, source_target_pairs={{0,16},{16,0},{1,17},{17,1},{2,18},{18,2},{3,19},{19,3},{4,20},{20... | collective-permute-start | bytes 1572872 | tf_op jit(solution)/shard_map/ppermute | solution.py:390
  73.4 13.2 %all-to-all-start.3 = ((f32[32,8,128]{2,1,0:T(8,128)}), f32[32,8,128]{2,1,0:T(8,128)S(1)}, u32[]{:S(2)}, u32[]{:S(2)}) async-start(f32[32,8,128]{2,1,0:T(8,128)} %shard_map.141), calls=%async_computation.3 | async-start | bytes 262144 | tf_op jit(solution)/shard_map/all_to_all | solution.py:395
  79.1 6.2 %collective-permute-start.3 = (bf16[512,256]{1,0:T(8,128)(2,1)S(1)}, bf16[512,256]{1,0:T(8,128)(2,1)S(1)}, u32[]{:S(2)}, u32[]{:S(2)}) collective-permute-start(bf16[512,256]{1,0:T(8,128)(2,1)S(1)} %collective-permute-done.2.half_ref), channel_id=1, source_target_pairs={{0,16},{16,0},{1,17},{17,1},{2,18},{18,2},{3,19},{19,3},{4,20},{20... | collective-permute-start | bytes 786440 | tf_op jit(solution)/shard_map/ppermute | solution.py:390
  81.5 0.9 copy-start.5
  87.9 15.3 %all-to-all-start.4 = ((bf16[4,320,256]{2,1,0:T(8,128)(2,1)}), bf16[4,320,256]{2,1,0:T(8,128)(2,1)S(1)}, u32[]{:S(2)}, u32[]{:S(2)}) async-start(bf16[4,320,256]{2,1,0:T(8,128)(2,1)} %get-tuple-element.52), calls=%async_computation.4 | async-start | bytes 1310720 | tf_op jit(solution)/shard_map/all_to_all | solution.py:397
  91.8 9.1 %collective-permute-start.4 = (f32[1,128]{1,0:T(1,128)S(1)}, f32[1,128]{1,0:T(1,128)S(1)}, u32[]{:S(2)}, u32[]{:S(2)}) collective-permute-start(f32[1,128]{1,0:T(1,128)S(1)} %get-tuple-element.51), channel_id=1, source_target_pairs={{0,32},{32,64},{64,96},{96,0},{1,33},{33,65},{65,97},{97,1},{2,34}... | collective-permute-start | bytes 1544 | tf_op jit(solution)/shard_map/ppermute | solution.py:345
  94.0 7.0 %collective-permute-start.5 = (f32[1,128]{1,0:T(1,128)S(1)}, f32[1,128]{1,0:T(1,128)S(1)}, u32[]{:S(2)}, u32[]{:S(2)}) collective-permute-start(f32[1,128]{1,0:T(1,128)S(1)} %get-tuple-element.51), channel_id=1, source_target_pairs={{0,64},{32,96},{64,0},{96,32},{1,65},{33,97},{65,1},{97,33},{2,66}... | collective-permute-start | bytes 1544 | tf_op jit(solution)/shard_map/ppermute | solution.py:345
  99.0 4.3 %collective-permute-start.6 = (f32[1,128]{1,0:T(1,128)S(1)}, f32[1,128]{1,0:T(1,128)S(1)}, u32[]{:S(2)}, u32[]{:S(2)}) collective-permute-start(f32[1,128]{1,0:T(1,128)S(1)} %get-tuple-element.51), channel_id=1, source_target_pairs={{0,96},{32,0},{64,32},{96,64},{1,97},{33,1},{65,33},{97,65},{2,98}... | collective-permute-start | bytes 1544 | tf_op jit(solution)/shard_map/ppermute | solution.py:345
  104.5 15.2 %collective-permute-start.7 = (bf16[272,256]{1,0:T(8,128)(2,1)S(1)}, bf16[272,256]{1,0:T(8,128)(2,1)S(1)}, u32[]{:S(2)}, u32[]{:S(2)}) collective-permute-start(bf16[272,256]{1,0:T(8,128)(2,1)S(1)} %get-tuple-element.61), channel_id=1, source_target_pairs={{0,1},{1,2},{2,3},{3,0},{16,19},{17,16},{18,17},{19,18},{4,5},{5,6... | collective-permute-start | bytes 417800 | tf_op jit(solution)/shard_map/ppermute | solution.py:341
  119.8 10.4 %collective-permute-start.8 = (bf16[272,256]{1,0:T(8,128)(2,1)S(1)}, bf16[272,256]{1,0:T(8,128)(2,1)S(1)}, u32[]{:S(2)}, u32[]{:S(2)}) collective-permute-start(bf16[272,256]{1,0:T(8,128)(2,1)S(1)} %add_convert_fusion), channel_id=1, source_target_pairs={{0,1},{1,2},{2,3},{3,0},{16,19},{17,16},{18,17},{19,18},{4,5},{5,6... | collective-permute-start | bytes 417800 | tf_op jit(solution)/shard_map/ppermute | solution.py:341
  124.0 17.1 %collective-permute-start.9 = (bf16[272,256]{1,0:T(8,128)(2,1)S(1)}, bf16[272,256]{1,0:T(8,128)(2,1)S(1)}, u32[]{:S(2)}, u32[]{:S(2)}) collective-permute-start(bf16[272,256]{1,0:T(8,128)(2,1)S(1)} %get-tuple-element.67), channel_id=1, source_target_pairs={{0,3},{1,0},{2,1},{3,2},{16,17},{17,18},{18,19},{19,16},{4,7},{5,4... | collective-permute-start | bytes 417800 | tf_op jit(solution)/shard_map/ppermute | solution.py:341
